TPU v7x, 128 devices: a whole 4x4x4 slice. The times are simulated.
128 devices in a mesh: freq: 8 (over z_hi, y), shot: 16 (over z_lo, x, core).
Axes of the slice: x: 4, y: 4, z: 4 (z_hi: 2, z_lo: 2; z = z_hi * 2 + z_lo), core: 2. Of those that a mesh axis runs over, the one named last changes fastest.
Arguments:
- source_field: bfloat16 [16, 16, 2, 128, 4096], P('freq', 'shot'), may hold values from -6 to 6
- receiver_field: bfloat16 [16, 16, 2, 128, 4096], P('freq', 'shot'), may hold values from -6 to 6
- angular_freq: float32 [16], P('freq'), may hold values from 2 to 40
- x_correction: bfloat16 [16, 2, 128, 128], P('freq'), may hold values from -0.25 to 0.25
- y_correction: bfloat16 [16, 2, 128, 128], P('freq'), may hold values from -0.25 to 0.25
- velocity: float32 [16, 128, 4096], P('shot'), may hold values from -1.2 to 1.2
- slab_owner: int32 [2], replicated, may hold values from 0 to 15, as said below
- apertures: int32 [16, 2], P('shot'), may hold values from 0 to 63
- tile_order: int32 [64], replicated, may hold values from 0 to 63, each once
Outputs:
- source_out: bfloat16 [16, 16, 2, 128, 4096], P('freq', 'shot')
- receiver_out: bfloat16 [16, 16, 2, 128, 4096], P('freq', 'shot')
- image: float32 [64, 2, 8192], P('shot', None, 'freq')
Inputs may be any that keep to these rules, and one draw needn't show every extreme that they name: `slab_owner`: the 2 entries are all different. `tile_order`: a permutation of all tiles.
All inputs are finite; a program needn't handle non-finite values.
Results may differ from a plain program's by a relative error of at most 0.0094.
Values sent between devices are 32-bit elements; how exact they have to be, the bound alone decides.
No kernel may reach another device: no remote copies, remote signals or barrier semaphores. Data moves between devices by JAX's collectives and lax.ppermute only.
A program may use at most 128 MiB of HBM per device.

v0:
```python
import jax
import jax.numpy as jnp
from jax import lax
from jax.sharding import PartitionSpec as P

DEPTH = 2
TILE_DEV = 4


def spread(shard, axis, root):
    mine = lax.axis_index(axis) == root
    return lax.psum(jnp.where(mine, shard, jnp.zeros_like(shard)), axis)


def lens(field, phase_angle, conj_sign):
    real_part = field[:, :, 0].astype(jnp.float32)
    imag_part = field[:, :, 1].astype(jnp.float32)
    cosine = jnp.cos(phase_angle)
    sine = conj_sign * jnp.sin(phase_angle)
    new_real = real_part * cosine - imag_part * sine
    new_imag = real_part * sine + imag_part * cosine
    return jnp.stack([new_real, new_imag], axis=2).astype(jnp.bfloat16)


def sweep_x(field, correction, conj_sign):
    shape = field.shape
    width = correction.shape[-1]
    blocks = field.reshape(shape[:-1] + (shape[-1] // width, width))
    real_part = blocks[:, :, 0]
    imag_part = blocks[:, :, 1]
    c_real = correction[:, 0]
    c_imag = correction[:, 1]
    form = "fsynk,fkj->fsynj"
    new_real = (
        real_part.astype(jnp.float32)
        + jnp.einsum(form, real_part, c_real, preferred_element_type=jnp.float32)
        - conj_sign * jnp.einsum(form, imag_part, c_imag, preferred_element_type=jnp.float32)
    )
    new_imag = (
        imag_part.astype(jnp.float32)
        + jnp.einsum(form, imag_part, c_real, preferred_element_type=jnp.float32)
        + conj_sign * jnp.einsum(form, real_part, c_imag, preferred_element_type=jnp.float32)
    )
    return jnp.stack([new_real, new_imag], axis=2).reshape(shape).astype(jnp.bfloat16)


def sweep_y(field, correction, conj_sign):
    shape = field.shape
    width = correction.shape[-1]
    blocks = field.reshape(shape[:3] + (shape[3] // width, width, shape[4]))
    real_part = blocks[:, :, 0]
    imag_part = blocks[:, :, 1]
    c_real = correction[:, 0]
    c_imag = correction[:, 1]
    form = "fsnkx,fkj->fsnjx"
    new_real = (
        real_part.astype(jnp.float32)
        + jnp.einsum(form, real_part, c_real, preferred_element_type=jnp.float32)
        - conj_sign * jnp.einsum(form, imag_part, c_imag, preferred_element_type=jnp.float32)
    )
    new_imag = (
        imag_part.astype(jnp.float32)
        + jnp.einsum(form, imag_part, c_real, preferred_element_type=jnp.float32)
        + conj_sign * jnp.einsum(form, real_part, c_imag, preferred_element_type=jnp.float32)
    )
    return jnp.stack([new_real, new_imag], axis=2).reshape(shape).astype(jnp.bfloat16)


def fetch_slab(velocity, owner):
    return spread(velocity[0], "shot", owner)


def local(
    source_field,
    receiver_field,
    angular_freq,
    x_correction,
    y_correction,
    velocity,
    slab_owner,
    apertures,
    tile_order,
):
    shot_count = lax.axis_size("shot")
    freq_total = angular_freq.shape[0] * lax.axis_size("freq")
    tile_total = TILE_DEV * shot_count
    height = source_field.shape[3]
    width = source_field.shape[4]
    tile_width = width // tile_total
    tile_ids = apertures[0]
    collected = []
    for depth_step in range(DEPTH):
        velocity_slab = fetch_slab(velocity, slab_owner[depth_step])
        phase_angle = angular_freq[:, None, None, None] * velocity_slab[None, None]
        source_field = sweep_y(
            sweep_x(lens(source_field, phase_angle, 1.0), x_correction, 1.0), y_correction, 1.0
        )
        receiver_field = sweep_y(
            sweep_x(lens(receiver_field, phase_angle, -1.0), x_correction, -1.0), y_correction, -1.0
        )
        product_sum = source_field[:, 0, 0].astype(jnp.float32) * receiver_field[:, 0, 0].astype(
            jnp.float32
        ) + source_field[:, 0, 1].astype(jnp.float32) * receiver_field[:, 0, 1].astype(jnp.float32)
        image_term = jnp.sum(product_sum, axis=0) / freq_total
        blocks = image_term.reshape(height, tile_total, tile_width)
        picked = jnp.take(blocks, tile_ids, axis=1)
        collected.append(jnp.transpose(picked, (1, 0, 2)))
    stacked = jnp.stack(collected, axis=1)
    tile_parts = lax.psum_scatter(stacked, "freq", scatter_dimension=2, tiled=True)
    flat_parts = tile_parts.reshape(tile_parts.shape[0], tile_parts.shape[1], -1)
    match_table = (tile_order[:, None] == tile_ids[None, :]).astype(jnp.float32)
    dense_image = jnp.einsum(
        "pa,adl->pdl", match_table, flat_parts, precision=lax.Precision.HIGHEST
    )
    image = lax.psum_scatter(dense_image, "shot", scatter_dimension=0, tiled=True)
    return (source_field, receiver_field, image)


def solution(mesh):
    in_specs = (
        P("freq", "shot", None, None, None),
        P("freq", "shot", None, None, None),
        P("freq"),
        P("freq", None, None, None),
        P("freq", None, None, None),
        P("shot", None, None),
        P(),
        P("shot", None),
        P(),
    )
    out_specs = (
        P("freq", "shot", None, None, None),
        P("freq", "shot", None, None, None),
        P("shot", None, "freq"),
    )
    return jax.shard_map(local, mesh=mesh, in_specs=in_specs, out_specs=out_specs, check_vma=False)
```

profile of v0, /device:TPU:1, one launch (start us, length us, event | category | flops | bytes accessed | tf_op | source)
XLA Modules:
  0.0 447.2 jit_solution(12388754440919761226)
XLA Ops:
  7.2 1.3 fusion.143
  9.8 4.1 select_bitcast_fusion.1
  14.0 4.0 fusion.142
  17.9 4.1 copy.159
  22.0 2.5 copy.160
  24.5 4.1 fusion.141
  28.6 4.1 copy.165
  32.7 2.4 copy.166
  35.2 111.3 %all-reduce.11.cloned.1.call-done = (f32[128,4096]{1,0:T(8,128)}, f32[128,4096]{1,0:T(8,128)}) async-done(((f32[128,4096]{1,0:T(8,128)}, f32[128,4096]{1,0:T(8,128)}), (f32[128,4096]{1,0:T(8,128)}, f32[128,4096]{1,0:T(8,128)})) %all-reduce.11.cloned.1.call-update) | async-done | bytes 4194320 | tf_op jit(solution)/shard_map/psum | solution.py:12
  146.5 3.0 copy.105
  149.5 20.8 %fusion.47 = (bf16[2,1,1,128,4096]{3,4,0,2,1:T(8,128)(2,1)S(1)}, bf16[2,1,1,128,4096]{3,4,0,2,1:T(8,128)(2,1)S(1)}, bf16[2,1,1,128,4096]{3,4,0,2,1:T(8,128)(2,1)S(1)}, bf16[2,1,1,128,4096]{3,4,0,2,1:T(8,128)(2,1)S(1)}) fusion(bf16[2,1,1,128,4096]{3,4,0,2,1:T(8,128)(2,1)} %copy.166, bf16[2,1,1,128,4096]{3,4,0,2,1:T(8,128)(2,1)} %copy.165, ...), kind=kLoop, calls=%fused_computation.79 | loop fusion | flops 23068672 | bytes 18874376 | tf_op jit(solution)/shard_map/convert.23
  170.4 0.7 fusion.78
  171.1 0.7 fusion.76
  171.8 1.0 subtract_convert_fusion.1
  172.8 1.0 add_convert_fusion.1
  173.8 0.7 fusion.21
  174.5 0.7 fusion.18
  175.2 2.0 fusion.41
  177.2 2.0 fusion.40
  179.2 0.7 fusion.86
  180.0 0.7 fusion.84
  180.7 0.8 subtract_convert_fusion.3
  181.6 0.7 fusion.29
  182.2 0.8 add_convert_fusion.3
  183.1 0.7 fusion.27
  183.8 2.0 fusion.45
  185.8 2.0 fusion.44
  187.8 1.9 copy.115
  189.7 2.8 maximum_bitcast_fusion.2
  192.6 0.6 copy-done.5
  193.6 19.2 %fusion.55 = (bf16[2,1,1,128,4096]{3,4,0,2,1:T(8,128)(2,1)S(1)}, bf16[2,1,1,128,4096]{3,4,0,2,1:T(8,128)(2,1)S(1)}, f32[128,4096]{0,1:T(8,128)S(1)}, bf16[2,1,1,...) fusion(f32[128,4096]{0,1:T(8,128)S(1)} %copy.115, f32[2]{0:T(128)S(1)} %copy-done.7, ...), kind=kLoop, calls=%fused_computation.87 | loop fusion | flops 26738688 | bytes 20971528 | tf_op jit(solution)/shard_map/convert.35
  212.8 0.7 fusion.74
  213.5 0.7 fusion.72
  214.3 1.0 subtract_convert_fusion
  215.2 0.7 fusion.15
  215.9 1.1 add_convert_fusion
  217.0 0.7 fusion.12
  217.7 0.7 fusion.39
  218.4 0.7 fusion.38
  219.1 0.7 fusion.82
  219.9 0.7 fusion.80
  220.6 0.9 subtract_convert_fusion.2
  221.5 0.7 fusion.25
  222.2 0.9 add_convert_fusion.2
  223.2 0.7 fusion.23
  223.9 0.7 fusion.43
  224.6 0.7 fusion.42
  226.1 1.6 copy-done
  227.7 1.4 add_reduce_fusion
  229.0 0.6 copy-done.1
  229.8 1.5 broadcast_multiply_fusion.1
  231.2 0.6 gather_fusion.1
  231.8 2.1 gather_fusion
  234.1 0.8 copy.131
  235.0 0.6 dynamic-slice
  236.2 79.4 %all-reduce.7.cloned.1.call-done = f32[2,2,128,64]{3,1,0,2:T(2,128)} async-done(((f32[2,2,128,64]{3,1,0,2:T(2,128)}), f32[2,2,128,64]{3,1,0,2:T(2,128)}) %all-reduce.7.cloned.1.call-update) | async-done | bytes 131088
  315.6 0.8 constant_dynamic-slice_fusion.1
  316.5 1.3 fusion.136
  317.8 0.6 dynamic-slice.2
  319.1 6.4 %copy.135 = bf16[2,1,2,128,4096]{4,3,2,1,0:T(8,128)(2,1)} copy(bf16[2,1,2,128,4096]{3,4,0,2,1:T(8,128)(2,1)} %copy-done) | data formatting | bytes 8388608
  325.4 6.4 %copy.134 = bf16[2,1,2,128,4096]{4,3,2,1,0:T(8,128)(2,1)} copy(bf16[2,1,2,128,4096]{3,4,0,2,1:T(8,128)(2,1)} %copy-done.1) | data formatting | bytes 8388608
  331.8 107.4 %all-reduce.9.cloned.1.call-done = f32[64,2,1024]{2,0,1:T(8,128)} async-done(((f32[64,2,1024]{2,0,1:T(8,128)}), f32[64,2,1024]{2,0,1:T(8,128)}) %all-reduce.9.cloned.1.call-update) | async-done | bytes 524304
  439.2 0.8 constant_dynamic-slice_fusion
  440.1 0.6 copy.136
  (38 shorter events, 1.8 us)
Async XLA Ops:
  7.2 139.3 %all-reduce.11.cloned.1.call-start = ((), (), s32[]{:S(2)}) async-start(), calls=%async_computation.2 | async-start | bytes 8388608 | tf_op jit(solution)/shard_map/psum | solution.py:12
  13.9 301.7 %all-reduce.7.cloned.1.call-start = ((), (), s32[]{:S(2)}) async-start(), calls=%async_computation | async-start | bytes 524288
  32.7 2.5 copy-start.8
  146.4 3.0 copy-start.6
  146.5 3.0 copy-start.7
  149.5 20.9 %copy-start.2 = (bf16[2,2,128,128]{3,2,1,0:T(8,128)(2,1)S(1)}, bf16[2,2,128,128]{3,2,1,0:T(8,128)(2,1)}, u32[]{:S(2)}) copy-start(bf16[2,2,128,128]{3,2,1,0:T(8,128)(2,1)} %param.14) | copy-start | bytes 393220
  172.8 1.0 copy-start.3
  189.7 2.9 copy-start.4
  189.7 3.5 copy-start.5
  225.6 2.0 copy-start
  227.7 2.0 copy-start.1
  229.8 5.2 %copy-start.11 = (u32[128]{0:T(128)S(1)}, u32[128]{0:T(128)}, u32[]{:S(2)}) copy-start(u32[128]{0:T(128)} %constant.34) | copy-start | bytes 1540
  229.8 86.7 %copy-start.9 = (s32[64]{0:T(128)S(1)}, s32[64]{0:T(128)}, u32[]{:S(2)}) copy-start(s32[64]{0:T(128)} %param.19) | copy-start | bytes 772
  231.2 86.6 %copy-start.10 = (u32[128]{0:T(128)S(1)}, u32[128]{0:T(128)}, u32[]{:S(2)}) copy-start(u32[128]{0:T(128)} %constant.38) | copy-start | bytes 1540
  234.9 204.3 %all-reduce.9.cloned.1.call-start = ((), (), s32[]{:S(2)}) async-start(), calls=%async_computation.1 | async-start | bytes 1048576
Sparse Core Ops, SparseCore 0:
  14.1 132.3 all-reduce.10
  235.0 80.5 all-reduce.6
  318.3 120.9 all-reduce.8
where the time goes:
time: 448 us; the launch traced here: 447 us
  waiting for transfers between devices  298 us (67%)
  other arithmetic  51.1 us (11%)
  local copies, waits for them, and re-layouts  50.1 us (11%)
  matrix products  31 us (7%)
  between operations  16.7 us (4%)
    unnamed x5, waiting for transfers between devices  187 us
    psum x1, waiting for transfers between devices, spread(): return lax.psum(jnp.where(mine, shard, jnp.zeros_like(shard)), axis)  111 us
    another operation x2, other arithmetic  40.1 us
    unnamed x35, local copies, waits for them, and re-layouts  32.2 us
  transfers between devices with their start and end apart: 3, of which 3 were waited for; matrix products, arithmetic and copies ran while one was open for 8% of the time, Pallas kernels for 0%

commit v1 on v0

v1 whole, which is shorter than its diff:
```python
import functools
import math

import jax
import jax.numpy as jnp
from jax import lax
from jax.experimental import pallas as pl
from jax.experimental.pallas import tpu as pltpu
from jax.sharding import PartitionSpec as P

DEPTH = 2
TILE_DEV = 4
BLOCK = 128
SIN = (4.442867755889893, -7.307443618774414, 3.594788074493408, -0.7843739986419678)
COS = (1.4142135381698608, -6.978850841522217, 5.7394609451293945, -1.8835630416870117, 0.31069818139076233)


def poly(u, coefs):
    total = coefs[-1] * u + coefs[-2]
    for c in coefs[-3::-1]:
        total = total * u + c
    return total


def sincos(turns):
    r = turns - jnp.round(turns)
    u = r * r
    s = r * poly(u, SIN)
    c = poly(u, COS)
    return s * c, 1.0 - s * s


def quad(a, b, c, d):
    a, b, c, d = (v.astype(jnp.bfloat16) for v in (a, b, c, d))
    return jnp.concatenate([jnp.concatenate([a, b], 1), jnp.concatenate([c, d], 1)], 0)


def advance(parts, phases, wx, wy):
    freqs, blocks = len(parts), len(parts[0])
    height, width = parts[0][0][0].shape
    out = [[None] * blocks for _ in range(freqs)]
    for f in range(freqs):
        for b in range(blocks):
            sr, si, rr, ri = parts[f][b]
            sin, cos = sincos(phases[f][b])
            out[f][b] = (sr * cos - si * sin, sr * sin + si * cos, rr * cos - ri * sin, rr * sin + ri * cos)
    for f in range(freqs):
        left = jnp.concatenate([quad(*out[f][b]) for b in range(blocks)], 0)
        prod = jnp.dot(left, wx[f], preferred_element_type=jnp.float32)
        for b in range(blocks):
            x = prod[b * 2 * height : (b + 1) * 2 * height]
            sr, si, rr, ri = out[f][b]
            out[f][b] = (
                sr + x[:height, :width],
                si + x[:height, width:],
                rr + x[height:, :width],
                ri + x[height:, width:],
            )
    for f in range(freqs):
        right = jnp.concatenate([quad(v[0], v[2], v[1], v[3]) for v in out[f]], 1)
        prod = jnp.dot(wy[f], right, preferred_element_type=jnp.float32)
        for b in range(blocks):
            y = prod[:, b * 2 * width : (b + 1) * 2 * width]
            sr, si, rr, ri = out[f][b]
            out[f][b] = (
                sr + y[:height, :width],
                si + y[height:, :width],
                rr + y[:height, width:],
                ri + y[height:, width:],
            )
    return out


def load_parts(src, rcv, cols):
    f32 = jnp.float32
    return [
        [
            (
                src[f, 0, 0, :, c].astype(f32),
                src[f, 0, 1, :, c].astype(f32),
                rcv[f, 0, 0, :, c].astype(f32),
                -rcv[f, 0, 1, :, c].astype(f32),
            )
            for c in cols
        ]
        for f in range(src.shape[0])
    ]


def march_body(where, turns, slab, wx, wy, src, rcv, *rest):
    so, ro = rest[-2:]
    freqs = src.shape[0]
    cols = [slice(c, c + BLOCK) for c in range(0, src.shape[-1], BLOCK)]
    parts = load_parts(src, rcv, cols)
    for d in range(slab.shape[1]):
        phases = [[slab[0, d, :, c] * turns[f] for c in cols] for f in range(freqs)]
        parts = advance(parts, phases, wx, wy)
    for f in range(freqs):
        for b, c in enumerate(cols):
            sr, si, rr, ri = parts[f][b]
            so[f, 0, 0, :, c] = sr.astype(so.dtype)
            so[f, 0, 1, :, c] = si.astype(so.dtype)
            ro[f, 0, 0, :, c] = rr.astype(ro.dtype)
            ro[f, 0, 1, :, c] = (-ri).astype(ro.dtype)


def march(where, turns, slabs, wx, wy, src, rcv, done=()):
    count, steps, height, cols = slabs.shape
    freqs = src.shape[0]
    field = pl.BlockSpec((freqs, 1, 2, height, cols), lambda i, w: (0, 0, 0, 0, w[i]))
    whole = lambda a: pl.BlockSpec(a.shape, lambda i, w: (0,) * a.ndim)
    args = [turns, slabs, wx, wy, src, rcv]
    in_specs = [
        pl.BlockSpec(memory_space=pltpu.SMEM),
        pl.BlockSpec((1, steps, height, cols), lambda i, w: (i, 0, 0, 0)),
        whole(wx),
        whole(wy),
        field,
        field,
    ]
    alias = {len(args) + 1 + i: i for i in range(len(done))}
    cells = count * cols * height * freqs
    return pl.pallas_call(
        march_body,
        grid_spec=pltpu.PrefetchScalarGridSpec(
            num_scalar_prefetch=1,
            grid=(count,),
            in_specs=in_specs + [pl.BlockSpec(memory_space=pl.ANY)] * len(done),
            out_specs=[field, field],
        ),
        out_shape=[jax.ShapeDtypeStruct(src.shape, src.dtype), jax.ShapeDtypeStruct(rcv.shape, rcv.dtype)],
        input_output_aliases=alias,
        cost_estimate=pl.CostEstimate(
            flops=cells * steps * 4 * 2 * 4 * BLOCK, bytes_accessed=cells * 16, transcendentals=0
        ),
        compiler_params=pltpu.CompilerParams(vmem_limit_bytes=48 * 1024 * 1024),
    )(where, *args, *done)


def image_body(tiles, slot, turns, wx, wy, src, rcv, *rest, scale, per):
    slabs, out, held, sem = rest[:-3], rest[-3], rest[-2], rest[-1]
    i = pl.program_id(0)
    column = pl.multiple_of(lax.rem(lax.div(tiles[i], 2), per) * BLOCK, BLOCK)
    for k, slab in enumerate(slabs):

        @pl.when(slot[i] == k)
        def _():
            pltpu.make_async_copy(slab.at[:, :, pl.ds(column, BLOCK)], held, sem).start()

    pltpu.make_async_copy(slabs[0].at[:, :, pl.ds(0, BLOCK)], held, sem).wait()
    freqs = src.shape[0]
    parts = load_parts(src, rcv, [slice(0, BLOCK)])
    half = BLOCK // 2
    odd = lax.rem(tiles[i], 2) == 1
    for d in range(held.shape[0]):
        parts = advance(parts, [[held[d] * turns[f]] for f in range(freqs)], wx, wy)
        term = sum(p[0][0] * p[0][2] - p[0][1] * p[0][3] for p in parts) * scale
        out[0, d] = jnp.where(odd, term[:, half:], term[:, :half])


def image_terms(tiles, slot, turns, wx, wy, src, rcv, slabs, scale):
    steps, height, cols = slabs[0].shape
    freqs = src.shape[0]
    field = pl.BlockSpec((freqs, 1, 2, height, BLOCK), lambda i, t, s: (0, 0, 0, 0, lax.div(t[i], 2)))
    whole = lambda a: pl.BlockSpec(a.shape, lambda i, t, s: (0,) * a.ndim)
    return pl.pallas_call(
        functools.partial(image_body, scale=scale, per=cols // BLOCK),
        grid_spec=pltpu.PrefetchScalarGridSpec(
            num_scalar_prefetch=2,
            grid=(tiles.shape[0],),
            in_specs=[pl.BlockSpec(memory_space=pltpu.SMEM), whole(wx), whole(wy), field, field]
            + [pl.BlockSpec(memory_space=pl.ANY)] * len(slabs),
            out_specs=pl.BlockSpec((1, steps, height, BLOCK // 2), lambda i, t, s: (i, 0, 0, 0)),
            scratch_shapes=[pltpu.VMEM((steps, height, BLOCK), jnp.float32), pltpu.SemaphoreType.DMA],
        ),
        out_shape=jax.ShapeDtypeStruct((tiles.shape[0], steps, height, BLOCK // 2), jnp.float32),
        compiler_params=pltpu.CompilerParams(vmem_limit_bytes=48 * 1024 * 1024),
    )(tiles, slot, turns, wx, wy, src, rcv, *slabs)


def sweep_weights(xc, yc):
    xr, xi = xc[:, 0], xc[:, 1]
    yr, yi = jnp.swapaxes(yc[:, 0], 1, 2), jnp.swapaxes(yc[:, 1], 1, 2)
    join = lambda a, b, c, d: jnp.concatenate([jnp.concatenate([a, b], 2), jnp.concatenate([c, d], 2)], 1)
    return join(xr, xi, -xi, xr), join(yr, -yi, yi, yr)


AXES = ("freq", "shot")
YS = 4
XS = 4
CORES = 2


def pairs(mesh_shape, move):
    freq, shot = mesh_shape
    at = lambda zh, y, zl, x, c: ((zh * YS + y) * shot) + (zl * XS + x) * CORES + c
    out = []
    for zh in range(freq // YS):
        for y in range(YS):
            for zl in range(shot // (XS * CORES)):
                for x in range(XS):
                    for c in range(CORES):
                        out.append((at(zh, y, zl, x, c), at(*move(zh, y, zl, x, c))))
    return out


def place(blocks, axis, size):
    shape = list(blocks[0][1].shape)
    shape[axis] = size
    whole = jnp.zeros(shape, blocks[0][1].dtype)
    for index, block in blocks:
        whole = lax.dynamic_update_slice_in_dim(whole, block, index, axis)
    return whole


def local(
    source_field,
    receiver_field,
    angular_freq,
    x_correction,
    y_correction,
    velocity,
    slab_owner,
    apertures,
    tile_order,
):
    freqs_dev, shots = lax.axis_size("freq"), lax.axis_size("shot")
    freq_total = angular_freq.shape[0] * freqs_dev
    height, width = velocity.shape[1:]
    f_id, s_id = lax.axis_index("freq"), lax.axis_index("shot")
    zh, y = f_id // YS, f_id % YS
    zl, x, core = s_id // (XS * CORES), (s_id // CORES) % XS, s_id % CORES
    zhs, zls = freqs_dev // YS, shots // (XS * CORES)
    first = core == 0
    cols = width // (CORES * XS)
    rows = height // (zls * zhs * XS)
    send = lambda v, move: lax.ppermute(v, AXES, pairs((freqs_dev, shots), move))

    half = width // CORES
    slab = velocity[0].reshape(zls, zhs, XS, rows, width)
    slab = lax.dynamic_index_in_dim(slab, zh, 1, keepdims=False)
    to_first = lax.dynamic_slice_in_dim(slab, y * cols, cols, 3)
    to_second = lax.dynamic_index_in_dim(slab, y, 1, keepdims=False)[..., half:]
    to_second = jnp.swapaxes(to_second.reshape(zls, rows, XS, cols), 1, 2)
    outgoing = jnp.stack([to_first, to_second], axis=2).reshape(shots, rows, cols)
    arrived = lax.all_to_all(outgoing, "shot", 0, 0, tiled=True)
    mine = jnp.stack([lax.dynamic_index_in_dim(arrived, slab_owner[d], 0, keepdims=False) for d in range(DEPTH)])

    mine = mine[:, None]
    other = send(mine, lambda zh, y, zl, x, c: (zh, y, 1 - zl, x, c))
    mine = place([(zl, mine), (1 - zl, other)], 1, zls)[:, :, None]
    other = send(mine, lambda zh, y, zl, x, c: (1 - zh, y, zl, x, c))
    mine = place([(zh, mine), (1 - zh, other)], 2, zhs)[:, :, :, None]
    third = jnp.where(first, x, y)
    turn = lambda k: lambda zh, y, zl, x, c: (zh, y, zl, (x + k) % XS, c) if c == 0 else (zh, (y + k) % YS, zl, x, c)
    others = [((third + XS - k) % XS, send(mine, turn(k))) for k in (1, 3, 2)]
    own = place([(third, mine)] + others, 3, XS).reshape(DEPTH, height, cols)

    column = jnp.where(first, y, x)
    partner_column = jnp.where(first, x, y)
    shift = lambda k: lambda zh, y, zl, x, c: (zh, (y + k) % YS, zl, x, c) if c == 0 else (zh, y, zl, (x + k) % XS, c)
    swap = lambda zh, y, zl, x, c: (zh, y, zl, x, 1 - c)
    slabs, where = [], []
    for k in (0, 1, 3, 2):
        block = own if k == 0 else send(own, shift(k))
        slabs += [block, send(block, swap)]
        where += [core * XS + (column + XS - k) % XS, (1 - core) * XS + (partner_column + XS - k) % XS]

    wx, wy = sweep_weights(x_correction, y_correction)
    turns = angular_freq * (0.5 / math.pi)
    places = jnp.stack(where).astype(jnp.int32)
    fields = ()
    for k in range(0, len(slabs), 2):
        fields = march(
            places[k : k + 2], turns, jnp.stack(slabs[k : k + 2]), wx, wy, source_field, receiver_field, tuple(fields)
        )

    tiles = apertures[0]
    tile_width = width // (TILE_DEV * shots)
    held = (tiles * tile_width) // cols
    slot = jnp.argmax(places[None, :] == held[:, None], axis=1).astype(jnp.int32)
    terms = image_terms(tiles, slot, turns, wx, wy, source_field, receiver_field, slabs, 1.0 / freq_total)
    parts = terms.reshape(terms.shape[0], DEPTH, freqs_dev, -1)
    parts = lax.all_to_all(parts, "freq", 2, 2, tiled=True)
    summed = jnp.sum(parts, axis=2)
    match = (tile_order[:, None] == tiles[None, :]).astype(jnp.float32)
    dense = jnp.sum(match[:, :, None, None] * summed[None], axis=1)
    dense = lax.all_to_all(dense, "shot", 0, 0, tiled=True)
    image = jnp.sum(dense.reshape((shots, TILE_DEV) + dense.shape[1:]), axis=0)
    return (*fields, image)


def solution(mesh):
    in_specs = (
        P("freq", "shot", None, None, None),
        P("freq", "shot", None, None, None),
        P("freq"),
        P("freq", None, None, None),
        P("freq", None, None, None),
        P("shot", None, None),
        P(),
        P("shot", None),
        P(),
    )
    out_specs = (
        P("freq", "shot", None, None, None),
        P("freq", "shot", None, None, None),
        P("shot", None, "freq"),
    )
    return jax.shard_map(local, mesh=mesh, in_specs=in_specs, out_specs=out_specs, check_vma=False)
```

time: 448 us -> 122 us (0.27)
  waiting for transfers between devices: 298 us -> 7.59 us
  starting transfers between devices: 0.12 us -> 46.5 us
  other arithmetic: 51.1 us -> 8.29 us
  Pallas kernels: 0 us -> 35.6 us
  local copies, waits for them, and re-layouts: 50.1 us -> 17.9 us
  matrix products: 31 us -> 0 us
  between operations: 16.7 us -> 4.8 us
    unnamed x5 -> x0, waiting for transfers between devices: 187 us -> none
    psum x1 -> x0, waiting for transfers between devices: 111 us -> none  [spread(): return lax.psum(jnp.where(mine, shard, jnp.zeros_like(shard)), axis)]
    pallas_call x0 -> x5, Pallas kernels: none -> 35.6 us  [the longest x4 31.5 us: march(): pl.pallas_call(march_body, grid_spec=pltpu.PrefetchScalarGridSpec(num_sca...]
    another operation x4 -> x10, other arithmetic: 40.2 us -> 5.29 us  [the longest x4 3.56 us: local(): jnp.stack(slabs[k:k + 2])]
    dot_general x33 -> x0, matrix products: 31 us -> none  [the longest x4 5.43 us: sweep_y(): jnp.einsum(form, real_part, c_imag, preferred_element_type=jnp.float32)]
    ppermute x0 -> x12, starting transfers between devices: none -> 28.4 us  [local(): lax.ppermute(v, AXES, pairs((freqs_dev, shots), move))]
    unnamed x35 -> x32, local copies, waits for them, and re-layouts: 32.2 us -> 10.7 us
    all_to_all x0 -> x3, starting transfers between devices: none -> 18.2 us  [the longest x1 7.17 us: local(): arrived = lax.all_to_all(outgoing, 'shot', 0, 0, tiled=True)]
  transfers between devices with their start and end apart: 3 -> 15, of which waited for: 3 -> 4; matrix products, arithmetic and copies ran while one was open for 8% -> 8% of each run, Pallas kernels for 0% -> 26%
where the time goes in v1:
time: 122 us; the launch traced here: 121 us
  starting transfers between devices  46.5 us (38%)
  Pallas kernels  35.6 us (29%)
  local copies, waits for them, and re-layouts  17.9 us (15%)
  other arithmetic  8.29 us (7%)
  waiting for transfers between devices  7.59 us (6%)
  between operations  4.8 us (4%)
    pallas_call x4, Pallas kernels, march(): pl.pallas_call(march_body, grid_spec=pltpu.PrefetchScalarGridSpec(num_sca...  31.5 us
    ppermute x12, starting transfers between devices, local(): lax.ppermute(v, AXES, pairs((freqs_dev, shots), move))  28.4 us
    unnamed x32, local copies, waits for them, and re-layouts  10.7 us
    ppermute x12, waiting for transfers between devices, local(): lax.ppermute(v, AXES, pairs((freqs_dev, shots), move))  7.59 us
    all_to_all x1, starting transfers between devices, local(): arrived = lax.all_to_all(outgoing, 'shot', 0, 0, tiled=True)  7.17 us
    all_to_all x1, starting transfers between devices, local(): parts = lax.all_to_all(parts, 'freq', 2, 2, tiled=True)  6.06 us
    all_to_all x1, starting transfers between devices, local(): dense = lax.all_to_all(dense, 'shot', 0, 0, tiled=True)  4.95 us
    pallas_call x1, Pallas kernels, image_terms(): pl.pallas_call(functools.partial(image_body, scale=scale, per=cols // BLO...  4.07 us
  transfers between devices with their start and end apart: 15, of which 4 were waited for; matrix products, arithmetic and copies ran while one was open for 8% of the time, Pallas kernels for 26%

profile of v1, /device:TPU:1, one launch (start us, length us, event | category | flops | bytes accessed | tf_op | source)
XLA Modules:
  0.0 120.7 jit_solution(7871069381766276564)
XLA Ops:
  0.6 0.0 copy-start
  0.7 1.5 %copy-done = f32[1,128,4096]{2,1,0:T(8,128)S(1)} copy-done((f32[1,128,4096]{2,1,0:T(8,128)S(1)}, f32[1,128,4096]{2,1,0:T(8,128)}, u32[]{:S(2)}) %copy-start) | copy-done | bytes 2097176
  2.2 0.1 dynamic-slice_bitcast_fusion.1
  2.4 0.7 pad_maximum_fusion.4
  3.1 7.2 %all-to-all-start = ((f32[16,8,512]{2,1,0:T(8,128)}), f32[16,8,512]{2,1,0:T(8,128)S(1)}, u32[]{:S(2)}, u32[]{:S(2)}) async-start(f32[16,8,512]{2,1,0:T(8,128)} %bitcast.8), calls=%async_computation | async-start | bytes 524288 | tf_op jit(solution)/shard_map/all_to_all | solution.py:246
  10.3 0.8 fusion.1
  11.1 0.9 slice_bitcast_fusion
  12.1 1.4 %fusion.3 = (s32[1]{0:T(128)}, s32[1]{0:T(128)}) fusion(s32[2]{0:T(128)} %param.15), kind=kLoop, calls=%fused_computation.38 | loop fusion | bytes 16 | tf_op jit(solution)/shard_map/slice | solution.py:247
  13.5 0.9 fusion.2
  14.3 0.1 copy.58
  14.5 0.1 copy.57
  14.6 0.1 pad_add_fusion.where
  14.7 0.1 maximum_maximum_fusion
  14.7 0.1 pad_add_fusion.1.where
  18.6 0.1 compare_convert_fusion
  18.7 0.0 all-to-all-done
  18.7 1.5 %collective-permute-start = (f32[2,1,8,512]{3,2,0,1:T(8,128)S(1)}, f32[2,1,8,512]{3,2,0,1:T(8,128)S(1)}, u32[]{:S(2)}, u32[]{:S(2)}) collective-permute-start(f32[2,1,8,512]{3,2,0,1:T(8,128)S(1)} %fusion), channel_id=1, source_target_pairs={{0,8},{1,9},{2,10},{3,11},{4,12},{5,13},{6,14},{7,15},{8,0},{9,1},... | collective-permute-start | bytes 98312 | tf_op jit(solution)/shard_map/ppermute | solution.py:237
  20.2 1.4 %collective-permute-done = f32[2,1,8,512]{3,2,0,1:T(8,128)S(1)} collective-permute-done((f32[2,1,8,512]{3,2,0,1:T(8,128)S(1)}, f32[2,1,8,512]{3,2,0,1:T(8,128)S(1)}, u32[]{:S(2)}, u32[]{:S(2)}) %collective-permute-start) | collective-permute-done | bytes 32800 | tf_op jit(solution)/shard_map/ppermute | solution.py:237
  21.5 3.3 %collective-permute-start.1 = (f32[2,2,1,8,512]{4,3,1,0,2:T(8,128)S(1)}, f32[2,2,1,8,512]{4,3,1,0,2:T(8,128)S(1)}, u32[]{:S(2)}, u32[]{:S(2)}) collective-permute-start(f32[2,2,1,8,512]{4,3,1,0,2:T(8,128)S(1)} %bitcast_dynamic-update-slice_fusion.3), channel_id=1, source_target_pairs={{0,64},{1,65},{2,66},{3,67},{4,68},{5,69},{6,70},{7,71},{8,72},{9,... | collective-permute-start | bytes 196616 | tf_op jit(solution)/shard_map/ppermute | solution.py:237
  24.9 1.6 %collective-permute-done.1 = f32[2,2,1,8,512]{4,3,1,0,2:T(8,128)S(1)} collective-permute-done((f32[2,2,1,8,512]{4,3,1,0,2:T(8,128)S(1)}, f32[2,2,1,8,512]{4,3,1,0,2:T(8,128)S(1)}, u32[]{:S(2)}, u32[]{:S(2)}) %collective-permute-start.1) | collective-permute-done | bytes 65568 | tf_op jit(solution)/shard_map/ppermute | solution.py:237
  26.5 1.4 %collective-permute-start.2 = (f32[2,2,2,1,8,512]{5,4,3,2,1,0:T(8,128)S(1)}, f32[2,2,2,1,8,512]{5,4,3,2,1,0:T(8,128)S(1)}, u32[]{:S(2)}, u32[]{:S(2)}) collective-permute-start(f32[2,2,2,1,8,512]{5,4,3,2,1,0:T(8,128)S(1)} %bitcast_dynamic-update-slice_fusion.1), channel_id=1, source_target_pairs={{0,2},{1,17},{2,4},{3,19},{4,6},{5,21},{6,0},{7,23},{8,10},{9,25},... | collective-permute-start | bytes 393224 | tf_op jit(solution)/shard_map/ppermute | solution.py:237
  27.9 0.1 pad_add_fusion.2.where
  28.0 0.1 stack.109
  28.0 2.6 %collective-permute-start.4 = (f32[2,2,2,1,8,512]{5,4,3,2,1,0:T(8,128)S(1)}, f32[2,2,2,1,8,512]{5,4,3,2,1,0:T(8,128)S(1)}, u32[]{:S(2)}, u32[]{:S(2)}) collective-permute-start(f32[2,2,2,1,8,512]{5,4,3,2,1,0:T(8,128)S(1)} %bitcast_dynamic-update-slice_fusion.1), channel_id=1, source_target_pairs={{0,4},{1,33},{2,6},{3,35},{4,0},{5,37},{6,2},{7,39},{8,12},{9,41},... | collective-permute-start | bytes 393224 | tf_op jit(solution)/shard_map/ppermute | solution.py:237
  30.7 1.1 collective-permute-start.3
  31.9 2.7 %collective-permute-done.3 = f32[2,2,2,1,8,512]{5,4,3,2,1,0:T(8,128)S(1)} collective-permute-done((f32[2,2,2,1,8,512]{5,4,3,2,1,0:T(8,128)S(1)}, f32[2,2,2,1,8,512]{5,4,3,2,1,0:T(8,128)S(1)}, u32[]{:S(2)}, u32[]{:S(2)}) %collective-permute-start.3) | collective-permute-done | bytes 131104 | tf_op jit(solution)/shard_map/ppermute | solution.py:237
  34.6 0.0 collective-permute-done.4
  34.7 1.6 %collective-permute-start.9 = (f32[2,128,512]{2,1,0:T(8,128)S(1)}, f32[2,128,512]{2,1,0:T(8,128)S(1)}, u32[]{:S(2)}, u32[]{:S(2)}) collective-permute-start(f32[2,128,512]{2,1,0:T(8,128)S(1)} %bitcast.68), channel_id=1, source_target_pairs={{0,16},{1,3},{2,18},{3,5},{4,20},{5,7},{6,22},{7,1},{8,24},{9,11},... | collective-permute-start | bytes 1572872 | tf_op jit(solution)/shard_map/ppermute | solution.py:237
  36.3 1.3 %collective-permute-start.7 = (f32[2,128,512]{2,1,0:T(8,128)S(1)}, f32[2,128,512]{2,1,0:T(8,128)S(1)}, u32[]{:S(2)}, u32[]{:S(2)}) collective-permute-start(f32[2,128,512]{2,1,0:T(8,128)S(1)} %bitcast.69), channel_id=1, source_target_pairs={{0,48},{1,7},{2,50},{3,1},{4,52},{5,3},{6,54},{7,5},{8,56},{9,15},... | collective-permute-start | bytes 1572872 | tf_op jit(solution)/shard_map/ppermute | solution.py:237
  37.6 1.4 %collective-permute-start.5 = (f32[2,128,512]{2,1,0:T(8,128)S(1)}, f32[2,128,512]{2,1,0:T(8,128)S(1)}, u32[]{:S(2)}, u32[]{:S(2)}) collective-permute-start(f32[2,128,512]{2,1,0:T(8,128)S(1)} %bitcast.70), channel_id=1, source_target_pairs={{0,32},{1,5},{2,34},{3,7},{4,36},{5,1},{6,38},{7,3},{8,40},{9,13},... | collective-permute-start | bytes 1572872 | tf_op jit(solution)/shard_map/ppermute | solution.py:237
  39.0 4.9 %collective-permute-start.11 = (f32[2,128,512]{2,1,0:T(8,128)S(1)}, f32[2,128,512]{2,1,0:T(8,128)S(1)}, u32[]{:S(2)}, u32[]{:S(2)}) collective-permute-start(f32[2,128,512]{2,1,0:T(8,128)S(1)} %bitcast.71), channel_id=1, source_target_pairs={{0,1},{1,0},{2,3},{3,2},{4,5},{5,4},{6,7},{7,6},{8,9},{9,8},{10,11... | collective-permute-start | bytes 1572872 | tf_op jit(solution)/shard_map/ppermute | solution.py:237
  43.9 0.1 pad_add_fusion.3.where
  44.0 0.7 compare_reduce_fusion
  44.7 0.0 collective-permute-done.9.rest_2_
  44.7 4.3 %collective-permute-start.10 = (f32[2,128,512]{2,1,0:T(8,128)S(1)}, f32[2,128,512]{2,1,0:T(8,128)S(1)}, u32[]{:S(2)}, u32[]{:S(2)}) collective-permute-start(f32[2,128,512]{2,1,0:T(8,128)S(1)} %collective-permute-done.9.rest_2_), channel_id=1, source_target_pairs={{0,1},{1,0},{2,3},{3,2},{4,5},{5,4},{6,7},{7,6},{8,9},{9,8},{10,11... | collective-permute-start | bytes 1572872 | tf_op jit(solution)/shard_map/ppermute | solution.py:237
  49.0 0.4 collective-permute-start.8
  49.3 1.8 %collective-permute-done.5.rest_6_ = f32[2,128,512]{2,1,0:T(8,128)S(1)} collective-permute-done((f32[2,128,512]{2,1,0:T(8,128)S(1)}, f32[2,128,512]{2,1,0:T(8,128)S(1)}, u32[]{:S(2)}, u32[]{:S(2)}) %collective-permute-start.5) | collective-permute-done | bytes 524320 | tf_op jit(solution)/shard_map/ppermute | solution.py:237
  51.2 4.6 %collective-permute-start.6 = (f32[2,128,512]{2,1,0:T(8,128)S(1)}, f32[2,128,512]{2,1,0:T(8,128)S(1)}, u32[]{:S(2)}, u32[]{:S(2)}) collective-permute-start(f32[2,128,512]{2,1,0:T(8,128)S(1)} %collective-permute-done.5.rest_6_), channel_id=1, source_target_pairs={{0,1},{1,0},{2,3},{3,2},{4,5},{5,4},{6,7},{7,6},{8,9},{9,8},{10,11... | collective-permute-start | bytes 1572872 | tf_op jit(solution)/shard_map/ppermute | solution.py:237
  55.8 0.0 collective-permute-done.11.rest_1_
  55.8 0.1 pad_maximum_fusion.3.slab
  55.9 0.0 copy-start.1
  55.9 2.2 %copy-done.1 = bf16[2,1,2,128,4096]{4,3,2,1,0:T(8,128)(2,1)S(1)} copy-done((bf16[2,1,2,128,4096]{4,3,2,1,0:T(8,128)(2,1)S(1)}, bf16[2,1,2,128,4096]{4,3,2,1,0:T(8,128)(2,1)}, u32[]{:S(2)}) %copy-start.1) | copy-done | bytes 4194328
  58.1 7.9 %shard_map.112 = (bf16[2,1,2,128,4096]{4,3,2,1,0:T(8,128)(2,1)}, bf16[2,1,2,128,4096]{4,3,2,1,0:T(8,128)(2,1)}) custom-call(s32[2]{0:T(128)S(1)} %pad_add_fusion.3.where, f32[2]{0:T(128)S(1)} %broadcast_multiply_fusion.turns, f32[2,2,128,512]{3,2,1,0:T(8,128)S(1)} %pad_maximum_fusion.3.slab, bf16[2,256,256]{2,1,0:T(8,128)(2,1)S(1)} %get-tuple-element.29.wx, ...), custom_call_target="tpu_custom_call" | custom-call | flops 2147483648 | bytes 4194304 | tf_op jit(solution)/shard_map/pallas_call | solution.py:123
  66.0 4.1 %shard_map.116 = f32[2,2,128,64]{3,2,1,0:T(8,128)S(1)} custom-call(s32[2]{0:T(128)S(1)} %bitcast.82, s32[2]{0:T(128)S(1)} %get-tuple-element.20.slot, f32[2]{0:T(128)S(1)} %broadcast_multiply_fusion.turns, bf16[2,256,256]{2,1,0:T(8,128)(2,1)S(1)} %get-tuple-element.29.wx, bf16[2,256,256]{2,1,0:T(8,128)(2,1)S(1)} %get-tuple-element.30.wy, ...), custom_call_target="tpu_custom_call" | custom-call | tf_op jit(solution)/shard_map/pallas_call | solution.py:166
  70.1 0.8 copy-done.8
  70.9 0.8 copy-done.9
  71.7 0.8 copy-done.10
  72.5 0.8 reshape.89
  73.3 1.7 %copy.51 = f32[2,2,8,1024]{3,1,0,2:T(2,128)} copy(f32[2,2,8,1024]{3,2,1,0:T(8,128)} %reshape.89) | data formatting | bytes 262144 | tf_op jit(solution)/shard_map/reshape | solution.py:283
  74.9 6.1 %all-to-all-start.1 = ((f32[2,2,8,1024]{3,1,0,2:T(2,128)}), f32[2,2,8,1024]{3,1,0,2:T(2,128)S(1)}, u32[]{:S(2)}, u32[]{:S(2)}) async-start(f32[2,2,8,1024]{3,1,0,2:T(2,128)} %copy.51), calls=%async_computation.1 | async-start | bytes 262144 | tf_op jit(solution)/shard_map/all_to_all | solution.py:284
  81.0 1.3 %pad_maximum_fusion.2.slab = f32[2,2,128,512]{3,2,1,0:T(8,128)S(1)} fusion(f32[1,2,128,512]{3,2,1,0:T(8,128)} %bitcast.79, f32[1,2,128,512]{3,2,1,0:T(8,128)} %bitcast.76), kind=kLoop, calls=%fused_computation.2 | loop fusion | flops 262144 | bytes 2097152 | tf_op jit(solution)/shard_map/stack | solution.py:275
  82.3 0.0 copy-start.2
  82.3 2.2 %copy-done.2 = bf16[2,1,2,128,4096]{4,3,2,1,0:T(8,128)(2,1)S(1)} copy-done((bf16[2,1,2,128,4096]{4,3,2,1,0:T(8,128)(2,1)S(1)}, bf16[2,1,2,128,4096]{4,3,2,1,0:T(8,128)(2,1)}, u32[]{:S(2)}) %copy-start.2) | copy-done | bytes 4194328
  84.4 7.9 %shard_map.113 = (bf16[2,1,2,128,4096]{4,3,2,1,0:T(8,128)(2,1)}, bf16[2,1,2,128,4096]{4,3,2,1,0:T(8,128)(2,1)}) custom-call(s32[2]{0:T(128)S(1)} %pad_add_fusion.2.where, f32[2]{0:T(128)S(1)} %broadcast_multiply_fusion.turns, f32[2,2,128,512]{3,2,1,0:T(8,128)S(1)} %pad_maximum_fusion.2.slab, ...), custom_call_target="tpu_custom_call", output_to_operand_aliasing={{0}: (7, {}), {1}: (8, {})} | custom-call | flops 2147483648 | bytes 4194304 | tf_op jit(solution)/shard_map/pallas_call | solution.py:123
  92.3 1.1 pad_maximum_fusion.slab
  93.5 0.1 multiply_reduce_fusion
  93.6 1.2 copy.52
  94.8 5.0 %all-to-all-start.2 = ((f32[64,2,1024]{2,1,0:T(2,128)}), f32[64,2,1024]{2,1,0:T(2,128)}, u32[]{:S(2)}, u32[]{:S(2)}) async-start(f32[64,2,1024]{2,1,0:T(2,128)} %copy.52), calls=%async_computation.2 | async-start | bytes 1048576 | tf_op jit(solution)/shard_map/all_to_all | solution.py:288
  99.7 1.2 pad_maximum_fusion.1.slab
  100.9 0.0 copy-start.3
  100.9 2.2 %copy-done.3 = bf16[2,1,2,128,4096]{4,3,2,1,0:T(8,128)(2,1)S(1)} copy-done((bf16[2,1,2,128,4096]{4,3,2,1,0:T(8,128)(2,1)S(1)}, bf16[2,1,2,128,4096]{4,3,2,1,0:T(8,128)(2,1)}, u32[]{:S(2)}) %copy-start.3) | copy-done | bytes 4194328
  103.1 7.9 %shard_map.114 = (bf16[2,1,2,128,4096]{4,3,2,1,0:T(8,128)(2,1)}, bf16[2,1,2,128,4096]{4,3,2,1,0:T(8,128)(2,1)}) custom-call(s32[2]{0:T(128)S(1)} %pad_add_fusion.1.where, f32[2]{0:T(128)S(1)} %broadcast_multiply_fusion.turns, f32[2,2,128,512]{3,2,1,0:T(8,128)S(1)} %pad_maximum_fusion.1.slab, ...), custom_call_target="tpu_custom_call", output_to_operand_aliasing={{0}: (7, {}), {1}: (8, {})} | custom-call | flops 2147483648 | bytes 4194304 | tf_op jit(solution)/shard_map/pallas_call | solution.py:123
  111.0 7.9 %shard_map.115 = (bf16[2,1,2,128,4096]{4,3,2,1,0:T(8,128)(2,1)}, bf16[2,1,2,128,4096]{4,3,2,1,0:T(8,128)(2,1)}) custom-call(s32[2]{0:T(128)S(1)} %pad_add_fusion.where, f32[2]{0:T(128)S(1)} %broadcast_multiply_fusion.turns, f32[2,2,128,512]{3,2,1,0:T(8,128)S(1)} %copy-done.4, ...), custom_call_target="tpu_custom_call", output_to_operand_aliasing={{0}: (7, {}), {1}: (8, {})} | custom-call | flops 2147483648 | bytes 4194304 | tf_op jit(solution)/shard_map/pallas_call | solution.py:123
  118.9 1.8 %reduce_sum.29 = f32[4,2,1024]{2,1,0:T(2,128)} reduce(f32[16,4,2,1024]{3,2,1,0:T(2,128)} %bitcast.42, f32[]{:T(128)} %constant.208.clone.1), dimensions={0}, to_apply=%region_3.4 | reduce | flops 122880 | bytes 557060 | tf_op jit(solution)/shard_map/reduce_sum | solution.py:289
  (45 shorter events, 0.3 us)
Async XLA Ops:
  0.6 1.6 %copy-start = (f32[1,128,4096]{2,1,0:T(8,128)S(1)}, f32[1,128,4096]{2,1,0:T(8,128)}, u32[]{:S(2)}) copy-start(f32[1,128,4096]{2,1,0:T(8,128)} %param.14) | copy-start | bytes 6291460
  0.6 17.9 %copy-start.12 = (s32[1,2]{1,0:T(1,128)S(1)}, s32[1,2]{1,0:T(1,128)}, u32[]{:S(2)}) copy-start(s32[1,2]{1,0:T(1,128)} %param.16) | copy-start | bytes 28
  0.7 17.9 %copy-start.13 = (s32[64]{0:T(128)S(1)}, s32[64]{0:T(128)}, u32[]{:S(2)}) copy-start(s32[64]{0:T(128)} %param.17) | copy-start | bytes 772
  0.7 55.2 %copy-start.14 = (f32[2]{0:T(128)S(1)}, f32[2]{0:T(128)}, u32[]{:S(2)}) copy-start(f32[2]{0:T(128)} %param.11) | copy-start | bytes 28
  3.1 15.6 %all-to-all-start = ((f32[16,8,512]{2,1,0:T(8,128)}), f32[16,8,512]{2,1,0:T(8,128)S(1)}, u32[]{:S(2)}, u32[]{:S(2)}) async-start(f32[16,8,512]{2,1,0:T(8,128)} %bitcast.8), calls=%async_computation | async-start | bytes 524288 | tf_op jit(solution)/shard_map/all_to_all | solution.py:246
  18.7 2.8 %collective-permute-start = (f32[2,1,8,512]{3,2,0,1:T(8,128)S(1)}, f32[2,1,8,512]{3,2,0,1:T(8,128)S(1)}, u32[]{:S(2)}, u32[]{:S(2)}) collective-permute-start(f32[2,1,8,512]{3,2,0,1:T(8,128)S(1)} %fusion), channel_id=1, source_target_pairs={{0,8},{1,9},{2,10},{3,11},{4,12},{5,13},{6,14},{7,15},{8,0},{9,1},... | collective-permute-start | bytes 98312 | tf_op jit(solution)/shard_map/ppermute | solution.py:237
  21.5 5.0 %collective-permute-start.1 = (f32[2,2,1,8,512]{4,3,1,0,2:T(8,128)S(1)}, f32[2,2,1,8,512]{4,3,1,0,2:T(8,128)S(1)}, u32[]{:S(2)}, u32[]{:S(2)}) collective-permute-start(f32[2,2,1,8,512]{4,3,1,0,2:T(8,128)S(1)} %bitcast_dynamic-update-slice_fusion.3), channel_id=1, source_target_pairs={{0,64},{1,65},{2,66},{3,67},{4,68},{5,69},{6,70},{7,71},{8,72},{9,... | collective-permute-start | bytes 196616 | tf_op jit(solution)/shard_map/ppermute | solution.py:237
  26.5 5.3 %collective-permute-start.2 = (f32[2,2,2,1,8,512]{5,4,3,2,1,0:T(8,128)S(1)}, f32[2,2,2,1,8,512]{5,4,3,2,1,0:T(8,128)S(1)}, u32[]{:S(2)}, u32[]{:S(2)}) collective-permute-start(f32[2,2,2,1,8,512]{5,4,3,2,1,0:T(8,128)S(1)} %bitcast_dynamic-update-slice_fusion.1), channel_id=1, source_target_pairs={{0,2},{1,17},{2,4},{3,19},{4,6},{5,21},{6,0},{7,23},{8,10},{9,25},... | collective-permute-start | bytes 393224 | tf_op jit(solution)/shard_map/ppermute | solution.py:237
  28.0 6.6 %collective-permute-start.4 = (f32[2,2,2,1,8,512]{5,4,3,2,1,0:T(8,128)S(1)}, f32[2,2,2,1,8,512]{5,4,3,2,1,0:T(8,128)S(1)}, u32[]{:S(2)}, u32[]{:S(2)}) collective-permute-start(f32[2,2,2,1,8,512]{5,4,3,2,1,0:T(8,128)S(1)} %bitcast_dynamic-update-slice_fusion.1), channel_id=1, source_target_pairs={{0,4},{1,33},{2,6},{3,35},{4,0},{5,37},{6,2},{7,39},{8,12},{9,41},... | collective-permute-start | bytes 393224 | tf_op jit(solution)/shard_map/ppermute | solution.py:237
  30.7 3.9 %collective-permute-start.3 = (f32[2,2,2,1,8,512]{5,4,3,2,1,0:T(8,128)S(1)}, f32[2,2,2,1,8,512]{5,4,3,2,1,0:T(8,128)S(1)}, u32[]{:S(2)}, u32[]{:S(2)}) collective-permute-start(f32[2,2,2,1,8,512]{5,4,3,2,1,0:T(8,128)S(1)} %bitcast_dynamic-update-slice_fusion.1), channel_id=1, source_target_pairs={{0,6},{1,49},{2,0},{3,51},{4,2},{5,53},{6,4},{7,55},{8,14},{9,57},... | collective-permute-start | bytes 393224 | tf_op jit(solution)/shard_map/ppermute | solution.py:237
  34.7 10.0 %collective-permute-start.9 = (f32[2,128,512]{2,1,0:T(8,128)S(1)}, f32[2,128,512]{2,1,0:T(8,128)S(1)}, u32[]{:S(2)}, u32[]{:S(2)}) collective-permute-start(f32[2,128,512]{2,1,0:T(8,128)S(1)} %bitcast.68), channel_id=1, source_target_pairs={{0,16},{1,3},{2,18},{3,5},{4,20},{5,7},{6,22},{7,1},{8,24},{9,11},... | collective-permute-start | bytes 1572872 | tf_op jit(solution)/shard_map/ppermute | solution.py:237
  36.3 12.7 %collective-permute-start.7 = (f32[2,128,512]{2,1,0:T(8,128)S(1)}, f32[2,128,512]{2,1,0:T(8,128)S(1)}, u32[]{:S(2)}, u32[]{:S(2)}) collective-permute-start(f32[2,128,512]{2,1,0:T(8,128)S(1)} %bitcast.69), channel_id=1, source_target_pairs={{0,48},{1,7},{2,50},{3,1},{4,52},{5,3},{6,54},{7,5},{8,56},{9,15},... | collective-permute-start | bytes 1572872 | tf_op jit(solution)/shard_map/ppermute | solution.py:237
  37.6 13.6 %collective-permute-start.5 = (f32[2,128,512]{2,1,0:T(8,128)S(1)}, f32[2,128,512]{2,1,0:T(8,128)S(1)}, u32[]{:S(2)}, u32[]{:S(2)}) collective-permute-start(f32[2,128,512]{2,1,0:T(8,128)S(1)} %bitcast.70), channel_id=1, source_target_pairs={{0,32},{1,5},{2,34},{3,7},{4,36},{5,1},{6,38},{7,3},{8,40},{9,13},... | collective-permute-start | bytes 1572872 | tf_op jit(solution)/shard_map/ppermute | solution.py:237
  39.0 16.8 %collective-permute-start.11 = (f32[2,128,512]{2,1,0:T(8,128)S(1)}, f32[2,128,512]{2,1,0:T(8,128)S(1)}, u32[]{:S(2)}, u32[]{:S(2)}) collective-permute-start(f32[2,128,512]{2,1,0:T(8,128)S(1)} %bitcast.71), channel_id=1, source_target_pairs={{0,1},{1,0},{2,3},{3,2},{4,5},{5,4},{6,7},{7,6},{8,9},{9,8},{10,11... | collective-permute-start | bytes 1572872 | tf_op jit(solution)/shard_map/ppermute | solution.py:237
  44.7 21.3 %copy-start.7 = (f32[2,128,512]{2,1,0:T(8,128)}, f32[2,128,512]{2,1,0:T(8,128)S(1)}, u32[]{:S(2)}) copy-start(f32[2,128,512]{2,1,0:T(8,128)S(1)} %collective-permute-done.9.rest_2_) | copy-start | bytes 1572868
  44.7 21.3 %collective-permute-start.10 = (f32[2,128,512]{2,1,0:T(8,128)S(1)}, f32[2,128,512]{2,1,0:T(8,128)S(1)}, u32[]{:S(2)}, u32[]{:S(2)}) collective-permute-start(f32[2,128,512]{2,1,0:T(8,128)S(1)} %collective-permute-done.9.rest_2_), channel_id=1, source_target_pairs={{0,1},{1,0},{2,3},{3,2},{4,5},{5,4},{6,7},{7,6},{8,9},{9,8},{10,11... | collective-permute-start | bytes 1572872 | tf_op jit(solution)/shard_map/ppermute | solution.py:237
  49.0 17.0 %collective-permute-start.8 = (f32[2,128,512]{2,1,0:T(8,128)S(1)}, f32[2,128,512]{2,1,0:T(8,128)S(1)}, u32[]{:S(2)}, u32[]{:S(2)}) collective-permute-start(f32[2,128,512]{2,1,0:T(8,128)S(1)} %collective-permute-done.7.rest_4_), channel_id=1, source_target_pairs={{0,1},{1,0},{2,3},{3,2},{4,5},{5,4},{6,7},{7,6},{8,9},{9,8},{10,11... | collective-permute-start | bytes 1572872 | tf_op jit(solution)/shard_map/ppermute | solution.py:237
  51.2 14.8 %copy-start.5 = (f32[2,128,512]{2,1,0:T(8,128)}, f32[2,128,512]{2,1,0:T(8,128)S(1)}, u32[]{:S(2)}) copy-start(f32[2,128,512]{2,1,0:T(8,128)S(1)} %collective-permute-done.5.rest_6_) | copy-start | bytes 1572868
  51.2 14.8 %collective-permute-start.6 = (f32[2,128,512]{2,1,0:T(8,128)S(1)}, f32[2,128,512]{2,1,0:T(8,128)S(1)}, u32[]{:S(2)}, u32[]{:S(2)}) collective-permute-start(f32[2,128,512]{2,1,0:T(8,128)S(1)} %collective-permute-done.5.rest_6_), channel_id=1, source_target_pairs={{0,1},{1,0},{2,3},{3,2},{4,5},{5,4},{6,7},{7,6},{8,9},{9,8},{10,11... | collective-permute-start | bytes 1572872 | tf_op jit(solution)/shard_map/ppermute | solution.py:237
  55.9 2.2 %copy-start.1 = (bf16[2,1,2,128,4096]{4,3,2,1,0:T(8,128)(2,1)S(1)}, bf16[2,1,2,128,4096]{4,3,2,1,0:T(8,128)(2,1)}, u32[]{:S(2)}) copy-start(bf16[2,1,2,128,4096]{4,3,2,1,0:T(8,128)(2,1)} %src.9) | copy-start | bytes 12582916
  70.1 0.8 copy-start.8
  70.9 0.8 copy-start.9
  71.7 0.8 copy-start.10
  74.9 18.5 %all-to-all-start.1 = ((f32[2,2,8,1024]{3,1,0,2:T(2,128)}), f32[2,2,8,1024]{3,1,0,2:T(2,128)S(1)}, u32[]{:S(2)}, u32[]{:S(2)}) async-start(f32[2,2,8,1024]{3,1,0,2:T(2,128)} %copy.51), calls=%async_computation.1 | async-start | bytes 262144 | tf_op jit(solution)/shard_map/all_to_all | solution.py:284
  82.3 2.2 %copy-start.2 = (bf16[2,1,2,128,4096]{4,3,2,1,0:T(8,128)(2,1)S(1)}, bf16[2,1,2,128,4096]{4,3,2,1,0:T(8,128)(2,1)}, u32[]{:S(2)}) copy-start(bf16[2,1,2,128,4096]{4,3,2,1,0:T(8,128)(2,1)} %src.9) | copy-start | bytes 12582916
  84.4 7.9 %copy-start.6 = (f32[2,128,512]{2,1,0:T(8,128)S(1)}, f32[2,128,512]{2,1,0:T(8,128)}, u32[]{:S(2)}) copy-start(f32[2,128,512]{2,1,0:T(8,128)} %copy-done.5) | copy-start | bytes 1572868
  84.4 7.9 %copy-start.11 = (f32[2,128,512]{2,1,0:T(8,128)S(1)}, f32[2,128,512]{2,1,0:T(8,128)}, u32[]{:S(2)}) copy-start(f32[2,128,512]{2,1,0:T(8,128)} %copy-done.10) | copy-start | bytes 1572868
  94.8 24.1 %all-to-all-start.2 = ((f32[64,2,1024]{2,1,0:T(2,128)}), f32[64,2,1024]{2,1,0:T(2,128)}, u32[]{:S(2)}, u32[]{:S(2)}) async-start(f32[64,2,1024]{2,1,0:T(2,128)} %copy.52), calls=%async_computation.2 | async-start | bytes 1048576 | tf_op jit(solution)/shard_map/all_to_all | solution.py:288
  100.9 2.2 %copy-start.3 = (bf16[2,1,2,128,4096]{4,3,2,1,0:T(8,128)(2,1)S(1)}, bf16[2,1,2,128,4096]{4,3,2,1,0:T(8,128)(2,1)}, u32[]{:S(2)}) copy-start(bf16[2,1,2,128,4096]{4,3,2,1,0:T(8,128)(2,1)} %src.9) | copy-start | bytes 12582916
  103.1 7.9 %copy-start.4 = (f32[2,2,128,512]{3,2,1,0:T(8,128)S(1)}, f32[2,2,128,512]{3,2,1,0:T(8,128)}, u32[]{:S(2)}) copy-start(f32[2,2,128,512]{3,2,1,0:T(8,128)} %pad_maximum_fusion.slab) | copy-start | bytes 3145732

commit v2 on v1

v2 whole, which is shorter than its diff:
```python
import functools
import math

import jax
import jax.numpy as jnp
from jax import lax
from jax.experimental import pallas as pl
from jax.experimental.pallas import tpu as pltpu
from jax.sharding import PartitionSpec as P

DEPTH = 2
TILE_DEV = 4
BLOCK = 128
TILE = 512
VMEM = 48 * 1024 * 1024
SIN = (4.442867755889893, -7.307443618774414, 3.594788074493408, -0.7843739986419678)
COS = (1.4142135381698608, -6.978850841522217, 5.7394609451293945, -1.8835630416870117, 0.31069818139076233)


def poly(u, coefs):
    total = coefs[-1] * u + coefs[-2]
    for c in coefs[-3::-1]:
        total = total * u + c
    return total


def sincos(turns):
    r = turns - jnp.round(turns)
    u = r * r
    s = r * poly(u, SIN)
    c = poly(u, COS)
    return s * c, 1.0 - s * s


def quad(a, b, c, d):
    a, b, c, d = (v.astype(jnp.bfloat16) for v in (a, b, c, d))
    return jnp.concatenate([jnp.concatenate([a, b], 1), jnp.concatenate([c, d], 1)], 0)


def advance(parts, phases, wx, wy):
    freqs, blocks = len(parts), len(parts[0])
    height, width = parts[0][0][0].shape
    out = [[None] * blocks for _ in range(freqs)]
    for f in range(freqs):
        for b in range(blocks):
            sr, si, rr, ri = parts[f][b]
            sin, cos = sincos(phases[f][b])
            out[f][b] = (sr * cos - si * sin, sr * sin + si * cos, rr * cos - ri * sin, rr * sin + ri * cos)
    for f in range(freqs):
        left = jnp.concatenate([quad(*out[f][b]) for b in range(blocks)], 0)
        prod = jnp.dot(left, wx[f], preferred_element_type=jnp.float32)
        for b in range(blocks):
            x = prod[b * 2 * height : (b + 1) * 2 * height]
            sr, si, rr, ri = out[f][b]
            out[f][b] = (
                sr + x[:height, :width],
                si + x[:height, width:],
                rr + x[height:, :width],
                ri + x[height:, width:],
            )
    for f in range(freqs):
        right = jnp.concatenate([quad(v[0], v[2], v[1], v[3]) for v in out[f]], 1)
        prod = jnp.dot(wy[f], right, preferred_element_type=jnp.float32)
        for b in range(blocks):
            y = prod[:, b * 2 * width : (b + 1) * 2 * width]
            sr, si, rr, ri = out[f][b]
            out[f][b] = (
                sr + y[:height, :width],
                si + y[height:, :width],
                rr + y[:height, width:],
                ri + y[height:, width:],
            )
    return out


def load_parts(src, rcv, cols):
    f32 = jnp.float32
    return [
        [
            (
                src[f, 0, 0, :, c].astype(f32),
                src[f, 0, 1, :, c].astype(f32),
                rcv[f, 0, 0, :, c].astype(f32),
                -rcv[f, 0, 1, :, c].astype(f32),
            )
            for c in cols
        ]
        for f in range(src.shape[0])
    ]


def slab_view(slab, d, cols):
    rows = slab[:, d, :, cols]
    return rows.reshape(rows.shape[0] * rows.shape[1], rows.shape[2])


def march_body(where, turns, wx, wy, src, rcv, *rest, count, per):
    slabs, so, ro = rest[:count], rest[-2], rest[-1]
    freqs, tile = src.shape[0], src.shape[-1]
    cols = [slice(c, c + BLOCK) for c in range(0, tile, BLOCK)]
    i = pl.program_id(0)

    def run(slab, offset):
        parts = load_parts(src, rcv, cols)
        for d in range(slab.shape[1]):
            views = [slab_view(slab, d, slice(offset + c.start, offset + c.stop)) for c in cols]
            parts = advance(parts, [[v * turns[f] for v in views] for f in range(freqs)], wx, wy)
        for f in range(freqs):
            for b, c in enumerate(cols):
                sr, si, rr, ri = parts[f][b]
                so[f, 0, 0, :, c] = sr.astype(so.dtype)
                so[f, 0, 1, :, c] = si.astype(so.dtype)
                ro[f, 0, 0, :, c] = rr.astype(ro.dtype)
                ro[f, 0, 1, :, c] = (-ri).astype(ro.dtype)

    for k, slab in enumerate(slabs):
        for part in range(per):

            @pl.when(i == k * per + part)
            def _():
                run(slab, part * tile)


def march(where, turns, slabs, wx, wy, src, rcv, done=()):
    count, cols = len(slabs), slabs[0].shape[-1]
    freqs, height = src.shape[0], src.shape[3]
    tile = min(cols, TILE)
    per = cols // tile
    field = pl.BlockSpec((freqs, 1, 2, height, tile), lambda i, w: (0, 0, 0, 0, w[lax.div(i, per)] * per + lax.rem(i, per)))
    whole = lambda a: pl.BlockSpec(a.shape, lambda i, w: (0,) * a.ndim)
    args = [turns, wx, wy, src, rcv, *slabs]
    in_specs = [pl.BlockSpec(memory_space=pltpu.SMEM), whole(wx), whole(wy), field, field] + [whole(s) for s in slabs]
    alias = {len(args) + 1 + i: i for i in range(len(done))}
    cells = count * cols * height * freqs
    return pl.pallas_call(
        functools.partial(march_body, count=count, per=per),
        grid_spec=pltpu.PrefetchScalarGridSpec(
            num_scalar_prefetch=1,
            grid=(count * per,),
            in_specs=in_specs + [pl.BlockSpec(memory_space=pl.ANY)] * len(done),
            out_specs=[field, field],
        ),
        out_shape=[jax.ShapeDtypeStruct(src.shape, src.dtype), jax.ShapeDtypeStruct(rcv.shape, rcv.dtype)],
        input_output_aliases=alias,
        cost_estimate=pl.CostEstimate(
            flops=cells * DEPTH * 4 * 2 * 4 * BLOCK * 3, bytes_accessed=cells * 16, transcendentals=0
        ),
        compiler_params=pltpu.CompilerParams(vmem_limit_bytes=VMEM),
    )(where, *args, *done)


def image_body(tiles, slot, turns, wx, wy, *rest, scale, per, aper, count):
    fields, slabs, out, held, sems = rest[: 2 * aper], rest[2 * aper : -3], rest[-3], rest[-2], rest[-1]
    copies = []
    for a in range(aper):
        column = pl.multiple_of(lax.rem(lax.div(tiles[a], 2), per) * BLOCK, BLOCK)
        for k, slab in enumerate(slabs):

            @pl.when(slot[a] == k)
            def _():
                pltpu.make_async_copy(slab.at[:, :, :, pl.ds(column, BLOCK)], held.at[a], sems.at[a]).start()

    for a in range(aper):
        pltpu.make_async_copy(slabs[0].at[:, :, :, pl.ds(0, BLOCK)], held.at[a], sems.at[a]).wait()
    freqs = fields[0].shape[0]
    cols = [slice(0, BLOCK)]
    loaded = [load_parts(fields[2 * a], fields[2 * a + 1], cols) for a in range(aper)]
    parts = [[loaded[a][f][0] for a in range(aper)] for f in range(freqs)]
    half = BLOCK // 2
    for d in range(held.shape[2]):
        views = [slab_view(held.at[a], d, slice(0, BLOCK)) for a in range(aper)]
        parts = advance(parts, [[v * turns[f] for v in views] for f in range(freqs)], wx, wy)
        picked = []
        for a in range(aper):
            sr, si, rr, ri = parts[0][a]
            term = sr * rr - si * ri
            for f in range(1, freqs):
                sr, si, rr, ri = parts[f][a]
                term += sr * rr - si * ri
            odd = lax.rem(tiles[a], 2) == 1
            picked.append(jnp.where(odd, term[:, half:], term[:, :half]) * scale)
        both = jnp.concatenate(picked, 1)
        out[:, d] = both.reshape(count, both.shape[0] // count, both.shape[1])


def image_terms(tiles, slot, turns, wx, wy, src, rcv, slabs, scale, count):
    steps, cols = slabs[0].shape[1], slabs[0].shape[-1]
    freqs, height = src.shape[0], src.shape[3]
    aper = tiles.shape[0]
    whole = lambda a: pl.BlockSpec(a.shape, lambda i, t, s: (0,) * a.ndim)
    field = lambda a: pl.BlockSpec((freqs, 1, 2, height, BLOCK), lambda i, t, s: (0, 0, 0, 0, lax.div(t[a], 2)))
    lanes = aper * BLOCK // 2
    shape = (count, steps, height // count, lanes)
    return pl.pallas_call(
        functools.partial(image_body, scale=scale, per=cols // BLOCK, aper=aper, count=count),
        grid_spec=pltpu.PrefetchScalarGridSpec(
            num_scalar_prefetch=2,
            grid=(1,),
            in_specs=[pl.BlockSpec(memory_space=pltpu.SMEM), whole(wx), whole(wy)]
            + [field(a) for a in range(aper) for _ in range(2)]
            + [pl.BlockSpec(memory_space=pl.ANY)] * len(slabs),
            out_specs=pl.BlockSpec(shape, lambda i, t, s: (0, 0, 0, 0)),
            scratch_shapes=[
                pltpu.VMEM((aper,) + slabs[0].shape[:3] + (BLOCK,), jnp.float32),
                pltpu.SemaphoreType.DMA((aper,)),
            ],
        ),
        out_shape=jax.ShapeDtypeStruct(shape, jnp.float32),
        cost_estimate=pl.CostEstimate(
            flops=aper * BLOCK * height * freqs * steps * 4 * 2 * 4 * BLOCK * 3, bytes_accessed=1 << 21, transcendentals=0
        ),
        compiler_params=pltpu.CompilerParams(vmem_limit_bytes=VMEM),
    )(tiles, slot, turns, wx, wy, *[v for _ in range(aper) for v in (src, rcv)], *slabs)


def deal_body(tiles, order, parts, out, *, per):
    total = jnp.sum(parts[...], axis=0)
    half = BLOCK // 2
    swapped = jnp.concatenate([total[..., half:], total[..., :half]], -1)
    low = lax.broadcasted_iota(jnp.int32, total.shape, 2) < half
    zero = jnp.zeros_like(total)
    for j in range(out.shape[0]):
        for q in range(per // 2):
            p = j * per + 2 * q
            straight = (low & (order[p] == tiles[0])) | (~low & (order[p + 1] == tiles[1]))
            crossed = (low & (order[p] == tiles[1])) | (~low & (order[p + 1] == tiles[0]))
            out[j, :, :, q * BLOCK : (q + 1) * BLOCK] = jnp.where(straight, total, zero) + jnp.where(crossed, swapped, zero)


def deal(tiles, order, parts, shots):
    per = order.shape[0] // shots
    _, steps, lines, lanes = parts.shape
    return pl.pallas_call(
        functools.partial(deal_body, per=per),
        in_specs=[pl.BlockSpec(memory_space=pltpu.SMEM)] * 2 + [pl.BlockSpec(memory_space=pltpu.VMEM)],
        out_specs=pl.BlockSpec(memory_space=pltpu.VMEM),
        out_shape=jax.ShapeDtypeStruct((shots, steps, lines, per * BLOCK // 2), jnp.float32),
    )(tiles, order, parts)


def sweep_weights(xc, yc):
    xr, xi = xc[:, 0], xc[:, 1]
    yr, yi = jnp.swapaxes(yc[:, 0], 1, 2), jnp.swapaxes(yc[:, 1], 1, 2)
    join = lambda a, b, c, d: jnp.concatenate([jnp.concatenate([a, b], 2), jnp.concatenate([c, d], 2)], 1)
    return join(xr, xi, -xi, xr), join(yr, -yi, yi, yr)


AXES = ("freq", "shot")
YS = 4
XS = 4
CORES = 2


def pairs(mesh_shape, move):
    freq, shot = mesh_shape
    at = lambda zh, y, zl, x, c: ((zh * YS + y) * shot) + (zl * XS + x) * CORES + c
    out = []
    for zh in range(freq // YS):
        for y in range(YS):
            for zl in range(shot // (XS * CORES)):
                for x in range(XS):
                    for c in range(CORES):
                        out.append((at(zh, y, zl, x, c), at(*move(zh, y, zl, x, c))))
    return out


def row_groups(mesh_shape):
    freq, shot = mesh_shape
    zhs, zls = freq // YS, shot // (XS * CORES)
    at = lambda zh, y, zl, x, c: ((zh * YS + y) * shot) + (zl * XS + x) * CORES + c
    every = [(zl, zh) for zl in range(zls) for zh in range(zhs)]
    out = [[at(zh, y, zl, x, 0) for zl, zh in every for x in range(XS)] for y in range(YS)]
    return out + [[at(zh, y, zl, x, 1) for zl, zh in every for y in range(YS)] for x in range(XS)]


def local(
    source_field,
    receiver_field,
    angular_freq,
    x_correction,
    y_correction,
    velocity,
    slab_owner,
    apertures,
    tile_order,
):
    freqs_dev, shots = lax.axis_size("freq"), lax.axis_size("shot")
    freq_total = angular_freq.shape[0] * freqs_dev
    height, width = velocity.shape[1:]
    f_id, s_id = lax.axis_index("freq"), lax.axis_index("shot")
    zh, y = lax.div(f_id, YS), lax.rem(f_id, YS)
    zl, x, core = lax.div(s_id, XS * CORES), lax.rem(lax.div(s_id, CORES), XS), lax.rem(s_id, CORES)
    zhs, zls = freq // YS, shot // (XS * CORES)
    at = lambda zh, y, zl, x, c: ((zh * YS + y) * shot) + (zl * XS + x) * CORES + c
    every = [(zl, zh) for zl in range(zls) for zh in range(zhs)]
    out = [[at(zh, y, zl, x, 0) for zl, zh in every for x in range(XS)] for y in range(YS)]
    return out + [[at(zh, y, zl, x, 1) for zl, zh in every for y in range(YS)] for x in range(XS)]


def local(
    source_field,
    receiver_field,
    angular_freq,
    x_correction,
    y_correction,
    velocity,
    slab_owner,
    apertures,
    tile_order,
):
    freqs_dev, shots = lax.axis_size("freq"), lax.axis_size("shot")
    freq_total = angular_freq.shape[0] * freqs_dev
    height, width = velocity.shape[1:]
    f_id, s_id = lax.axis_index("freq"), lax.axis_index("shot")
    zh, y = f_id // YS, f_id % YS
    zl, x, core = s_id // (XS * CORES), (s_id // CORES) % XS, s_id % CORES
    zhs, zls = freqs_dev // YS, shots // (XS * CORES)
    first = core == 0
    cols = width // (CORES * XS)
    rows = height // (zls * zhs * XS)
    send = lambda v, move: lax.ppermute(v, AXES, pairs((freqs_dev, shots), move))

    half = width // CORES
    slab = velocity[0].reshape(zls, zhs, XS, rows, width)
    slab = lax.dynamic_index_in_dim(slab, zh, 1, keepdims=False)
    to_first = lax.dynamic_slice_in_dim(slab, y * cols, cols, 3)
    to_second = lax.dynamic_index_in_dim(slab, y, 1, keepdims=False)[..., half:]
    to_second = jnp.swapaxes(to_second.reshape(zls, rows, XS, cols), 1, 2)
    outgoing = jnp.stack([to_first, to_second], axis=2).reshape(shots, rows, cols)
    arrived = lax.all_to_all(outgoing, "shot", 0, 0, tiled=True)
    mine = jnp.stack([lax.dynamic_index_in_dim(arrived, slab_owner[d], 0, keepdims=False) for d in range(DEPTH)])

    groups = row_groups((freqs_dev, shots))
    members = len(groups[0])
    own = jnp.broadcast_to(mine[None], (members,) + mine.shape)
    own = lax.all_to_all(own, AXES, 0, 0, axis_index_groups=groups, tiled=True)

    column = jnp.where(first, y, x)
    partner_column = jnp.where(first, x, y)
    shift = lambda k: lambda zh, y, zl, x, c: (zh, (y + k) % YS, zl, x, c) if c == 0 else (zh, y, zl, (x + k) % XS, c)
    swap = lambda zh, y, zl, x, c: (zh, y, zl, x, 1 - c)
    place = lambda k: core * XS + lax.rem(column + XS - k, XS)
    partner_place = lambda k: (1 - core) * XS + lax.rem(partner_column + XS - k, XS)
    wx, wy = sweep_weights(x_correction, y_correction)
    turns = angular_freq * (0.5 / math.pi)
    src = pltpu.with_memory_space_constraint(source_field, pltpu.HBM)
    rcv = pltpu.with_memory_space_constraint(receiver_field, pltpu.HBM)

    def forward(places, slabs, done=()):
        return march(jnp.stack(places).astype(jnp.int32), turns, slabs, wx, wy, src, rcv, tuple(done))

    own_p = send(own, swap)
    s1, s3, s2 = (send(own, shift(k)) for k in (1, 3, 2))
    fields = forward([place(0), partner_place(0)], [own, own_p])
    s1, s3, *fields = lax.optimization_barrier((s1, s3, *fields))
    s1_p, s3_p = send(s1, swap), send(s3, swap)
    fields = forward([place(1), place(3)], [s1, s3], fields)
    s2, *fields = lax.optimization_barrier((s2, *fields))
    s2_p = send(s2, swap)
    fields = forward([partner_place(1)], [s1_p], fields)
    s2_p, s3_p, *fields = lax.optimization_barrier((s2_p, s3_p, *fields))

    tiles = apertures[0]
    held = lax.div(tiles * (width // (TILE_DEV * shots)), cols)
    slabs = [own, own_p, s1, s3, s2, s1_p, s3_p, s2_p]
    places = jnp.stack([place(0), partner_place(0), place(1), place(3), place(2)] + [partner_place(k) for k in (1, 3, 2)])
    slot = jnp.argmax(places[None, :] == held[:, None], axis=1).astype(jnp.int32)
    terms = image_terms(tiles, slot, turns, wx, wy, src, rcv, slabs, 1.0 / freq_total, freqs_dev)
    terms = lax.all_to_all(terms, "freq", 0, 0, tiled=True)
    fields = forward([partner_place(3), place(2)], [s3_p, s2], fields)
    terms, *fields = lax.optimization_barrier((terms, *fields))
    dense = lax.all_to_all(deal(tiles, tile_order, terms, shots), "shot", 0, 0, tiled=True)
    fields = forward([partner_place(2)], [s2_p], fields)
    image = jnp.sum(dense, axis=0)
    image = image.reshape(DEPTH, image.shape[1], TILE_DEV, -1)
    image = jnp.transpose(image, (2, 0, 1, 3)).reshape(TILE_DEV, DEPTH, -1)
    return (*fields, image)


def solution(mesh):
    in_specs = (
        P("freq", "shot", None, None, None),
        P("freq", "shot", None, None, None),
        P("freq"),
        P("freq", None, None, None),
        P("freq", None, None, None),
        P("shot", None, None),
        P(),
        P("shot", None),
        P(),
    )
    out_specs = (
        P("freq", "shot", None, None, None),
        P("freq", "shot", None, None, None),
        P("shot", None, "freq"),
    )
    return jax.shard_map(local, mesh=mesh, in_specs=in_specs, out_specs=out_specs, check_vma=False)
```

time: 122 us -> 108 us (0.89)
  starting transfers between devices: 46.5 us -> 28.8 us
  waiting for transfers between devices: 7.59 us -> 20.5 us
  local copies, waits for them, and re-layouts: 17.9 us -> 9.41 us
  other arithmetic: 8.29 us -> 3.72 us
  Pallas kernels: 35.6 us -> 39.4 us
    ppermute x12 -> x7, starting transfers between devices: 28.4 us -> 6.49 us  [local(): lax.ppermute(v, AXES, pairs((freqs_dev, shots), move))]
    all_to_all x2 -> x3, waiting for transfers between devices: 0.01 us -> 14.7 us  [the longest x1 9.51 us: local(): own = lax.all_to_all(own, AXES, 0, 0, axis_index_groups=groups, tiled=True)]
    unnamed x32 -> x24, local copies, waits for them, and re-layouts: 10.7 us -> 5.31 us
    all_to_all x2 -> x3, starting transfers between devices: 11 us -> 15.2 us  [the longest x1 7.46 us: local(): own = lax.all_to_all(own, AXES, 0, 0, axis_index_groups=groups, tiled=True)]
    pallas_call x4 -> x6, Pallas kernels: 31.5 us -> 35.5 us  [the longest x5 33.6 us: march(): pl.pallas_call(functools.partial(march_body, count=count, per=per), grid_...]
    another operation x8 -> x3, other arithmetic: 3.87 us -> 0.16 us  [the longest x2 0.15 us: forward(): jnp.stack(places).astype(jnp.int32)]
    ppermute x12 -> x7, waiting for transfers between devices: 7.59 us -> 5.72 us  [local(): lax.ppermute(v, AXES, pairs((freqs_dev, shots), move))]
    reshape x2, local copies, waits for them, and re-layouts: 2.45 us -> 0.8 us  [the longest x1 0.71 us: local(): image = jnp.transpose(image, (2, 0, 1, 3)).reshape(TILE_DEV, DEPTH, -1)]
  transfers between devices with their start and end apart: 15 -> 11, of which waited for: 4 -> 4; matrix products, arithmetic and copies ran while one was open for 8% -> 4% of each run, Pallas kernels for 26% -> 31%
where the time goes in v2:
time: 108 us; the launch traced here: 107 us
  Pallas kernels  39.4 us (36%)
  starting transfers between devices  28.8 us (27%)
  waiting for transfers between devices  20.5 us (19%)
  local copies, waits for them, and re-layouts  9.41 us (9%)
  between operations  4.87 us (5%)
  other arithmetic  3.72 us (3%)
    pallas_call x5, Pallas kernels, march(): pl.pallas_call(functools.partial(march_body, count=count, per=per), grid_...  33.6 us
    all_to_all x1, waiting for transfers between devices, local(): own = lax.all_to_all(own, AXES, 0, 0, axis_index_groups=groups, tiled=True)  9.51 us
    all_to_all x1, starting transfers between devices, local(): own = lax.all_to_all(own, AXES, 0, 0, axis_index_groups=groups, tiled=True)  7.46 us
    all_to_all x1, starting transfers between devices, local(): arrived = lax.all_to_all(outgoing, 'shot', 0, 0, tiled=True)  7.17 us
    ppermute x7, starting transfers between devices, local(): lax.ppermute(v, AXES, pairs((freqs_dev, shots), move))  6.49 us
    ppermute x7, waiting for transfers between devices, local(): lax.ppermute(v, AXES, pairs((freqs_dev, shots), move))  5.72 us
    unnamed x24, local copies, waits for them, and re-layouts  5.31 us
    all_to_all x1, waiting for transfers between devices, local(): lax.all_to_all(deal(tiles, tile_order, terms, shots), 'shot', 0, 0, tiled...  5.15 us
  transfers between devices with their start and end apart: 11, of which 4 were waited for; matrix products, arithmetic and copies ran while one was open for 4% of the time, Pallas kernels for 31%

profile of v2, /device:TPU:1, one launch (start us, length us, event | category | flops | bytes accessed | tf_op | source)
XLA Modules:
  0.0 106.7 jit_solution(7322689721568670494)
XLA Ops:
  0.6 0.0 copy-start
  0.6 0.0 copy-start.9
  0.7 0.0 copy-start.10
  0.7 0.0 copy-start.7
  0.7 1.5 %copy-done = f32[1,128,4096]{2,1,0:T(8,128)S(1)} copy-done((f32[1,128,4096]{2,1,0:T(8,128)S(1)}, f32[1,128,4096]{2,1,0:T(8,128)}, u32[]{:S(2)}) %copy-start) | copy-done | bytes 2097176
  2.2 0.1 dynamic-slice_bitcast_fusion.1
  2.4 0.7 pad_maximum_fusion
  3.1 7.2 %all-to-all-start = ((f32[16,8,512]{2,1,0:T(8,128)}), f32[16,8,512]{2,1,0:T(8,128)S(1)}, u32[]{:S(2)}, u32[]{:S(2)}) async-start(f32[16,8,512]{2,1,0:T(8,128)} %bitcast.15), calls=%async_computation | async-start | bytes 524288 | tf_op jit(solution)/shard_map/all_to_all | solution.py:330
  10.3 0.9 fusion.2
  11.2 1.3 %fusion.3 = (s32[1]{0:T(128)}, s32[1]{0:T(128)}) fusion(s32[2]{0:T(128)} %param.15), kind=kLoop, calls=%fused_computation.21 | loop fusion | bytes 16 | tf_op jit(solution)/shard_map/slice | solution.py:331
  15.1 0.1 copy.41
  16.5 0.9 fusion.1
  17.4 0.1 all-to-all-done
  17.5 0.9 broadcast_in_dim.2
  18.3 7.5 %all-to-all-start.1 = ((f32[16,2,8,512]{3,2,1,0:T(8,128)}), f32[16,2,8,512]{3,2,1,0:T(8,128)S(1)}, u32[]{:S(2)}, u32[]{:S(2)}) async-start(f32[16,2,8,512]{3,2,1,0:T(8,128)} %broadcast_in_dim.2), calls=%async_computation.1 | async-start | bytes 1048576 | tf_op jit(solution)/shard_map/all_to_all | solution.py:336
  25.9 0.1 copy.40
  26.0 0.1 stack.72
  26.1 0.1 pad_add_fusion.2.where
  26.2 0.0 copy-done.9
  26.2 0.1 maximum_maximum_fusion
  26.3 9.5 %all-to-all-done.1.rest_0_.rest_4_ = f32[16,2,8,512]{3,2,1,0:T(8,128)S(1)} async-done(((f32[16,2,8,512]{3,2,1,0:T(8,128)}), f32[16,2,8,512]{3,2,1,0:T(8,128)S(1)}, u32[]{:S(2)}, u32[]{:S(2)}) %all-to-all-start.1) | async-done | bytes 524320 | tf_op jit(solution)/shard_map/all_to_all | solution.py:336
  35.8 0.0 copy-start.1
  35.8 1.4 %collective-permute-start.3 = (f32[16,2,8,512]{3,2,1,0:T(8,128)S(1)}, f32[16,2,8,512]{3,2,1,0:T(8,128)S(1)}, u32[]{:S(2)}, u32[]{:S(2)}) collective-permute-start(f32[16,2,8,512]{3,2,1,0:T(8,128)S(1)} %all-to-all-done.1.rest_0_.rest_4_), channel_id=1, source_target_pairs={{0,1},{1,0},{2,3},{3,2},{4,5},{5,4},{6,7},{7,6},{8,9},{9,8},{10,11... | collective-permute-start | bytes 1572872 | tf_op jit(solution)/shard_map/ppermute | solution.py:321
  37.2 0.1 pad_add_fusion.1.where
  37.3 0.0 copy-done.10
  37.3 0.0 copy-done.7
  37.3 0.1 compare_select_fusion
  37.3 1.3 %collective-permute-start.2 = (f32[16,2,8,512]{3,2,1,0:T(8,128)S(1)}, f32[16,2,8,512]{3,2,1,0:T(8,128)S(1)}, u32[]{:S(2)}, u32[]{:S(2)}) collective-permute-start(f32[16,2,8,512]{3,2,1,0:T(8,128)S(1)} %all-to-all-done.1.rest_0_.rest_4_), channel_id=1, source_target_pairs={{0,48},{1,7},{2,50},{3,1},{4,52},{5,3},{6,54},{7,5},{8,56},{9,15},... | collective-permute-start | bytes 1572872 | tf_op jit(solution)/shard_map/ppermute | solution.py:321
  38.7 0.1 collective-permute-start.1
  38.8 1.3 %collective-permute-start = (f32[16,2,8,512]{3,2,1,0:T(8,128)S(1)}, f32[16,2,8,512]{3,2,1,0:T(8,128)S(1)}, u32[]{:S(2)}, u32[]{:S(2)}) collective-permute-start(f32[16,2,8,512]{3,2,1,0:T(8,128)S(1)} %all-to-all-done.1.rest_0_.rest_4_), channel_id=1, source_target_pairs={{0,32},{1,5},{2,34},{3,7},{4,36},{5,1},{6,38},{7,3},{8,40},{9,13},... | collective-permute-start | bytes 1572872 | tf_op jit(solution)/shard_map/ppermute | solution.py:321
  40.1 0.0 collective-permute-done.3.rest_1_.rest_5_
  40.1 8.0 %shard_map.112 = (bf16[2,1,2,128,4096]{4,3,2,1,0:T(8,128)(2,1)}, bf16[2,1,2,128,4096]{4,3,2,1,0:T(8,128)(2,1)}) custom-call(s32[2]{0:T(128)S(1)} %pad_add_fusion.1.where, f32[2]{0:T(128)S(1)} %broadcast_multiply_fusion.turns, bf16[2,256,256]{2,1,0:T(8,128)(2,1)S(1)} %get-tuple-element.63.wx, bf16[2,256,256]{2,1,0:T(8,128)(2,1)S(1)} %get-tuple-element.64.wy, ...), custom_call_target="tpu_custom_call" | custom-call | flops 6442450944 | bytes 4194304 | tf_op jit(solution)/shard_map/pallas_call | solution.py:135
  48.1 0.0 copy-done.1
  48.1 0.0 collective-permute-done.2.rest_1_.rest_7_
  48.1 5.7 %collective-permute-done.1.rest_0_.rest_6_ = f32[16,2,8,512]{3,2,1,0:T(8,128)S(1)} collective-permute-done((f32[16,2,8,512]{3,2,1,0:T(8,128)S(1)}, f32[16,2,8,512]{3,2,1,0:T(8,128)S(1)}, u32[]{:S(2)}, u32[]{:S(2)}) %collective-permute-start.1) | collective-permute-done | bytes 524320 | tf_op jit(solution)/shard_map/ppermute | solution.py:321
  53.8 1.7 %collective-permute-start.6 = (f32[16,2,8,512]{3,2,1,0:T(8,128)S(1)}, f32[16,2,8,512]{3,2,1,0:T(8,128)S(1)}, u32[]{:S(2)}, u32[]{:S(2)}) collective-permute-start(f32[16,2,8,512]{3,2,1,0:T(8,128)S(1)} %collective-permute-done.1.rest_0_.rest_6_), channel_id=1, source_target_pairs={{0,1},{1,0},{2,3},{3,2},{4,5},{5,4},{6,7},{7,6},{8,9},{9,8},{10,11... | collective-permute-start | bytes 1572872 | tf_op jit(solution)/shard_map/ppermute | solution.py:321
  55.6 0.0 collective-permute-start.5
  55.6 8.0 %shard_map.113 = (bf16[2,1,2,128,4096]{4,3,2,1,0:T(8,128)(2,1)}, bf16[2,1,2,128,4096]{4,3,2,1,0:T(8,128)(2,1)}) custom-call(s32[2]{0:T(128)S(1)} %get-tuple-element.62.where, f32[2]{0:T(128)S(1)} %broadcast_multiply_fusion.turns, bf16[2,256,256]{2,1,0:T(8,128)(2,1)S(1)} %get-tuple-element.63.wx, ...), custom_call_target="tpu_custom_call", output_to_operand_aliasing={{0}: (8, {}), {1}: (9, {})} | custom-call | flops 6442450944 | bytes 4194304 | tf_op jit(solution)/shard_map/pallas_call | solution.py:135
  63.6 0.0 collective-permute-done.rest_8_.rest_1_
  63.6 0.6 collective-permute-start.4
  64.2 0.8 compare_reduce_fusion
  64.9 0.0 collective-permute-done.6.rest_0_.rest_9_
  64.9 4.8 %shard_map.114 = (bf16[2,1,2,128,4096]{4,3,2,1,0:T(8,128)(2,1)}, bf16[2,1,2,128,4096]{4,3,2,1,0:T(8,128)(2,1)}) custom-call(s32[1]{0:T(128)} %bitcast.22.where, f32[2]{0:T(128)S(1)} %broadcast_multiply_fusion.turns, bf16[2,256,256]{2,1,0:T(8,128)(2,1)S(1)} %get-tuple-element.63.wx, ...), custom_call_target="tpu_custom_call", output_to_operand_aliasing={{0}: (7, {}), {1}: (8, {})} | custom-call | flops 3221225472 | bytes 2097152 | tf_op jit(solution)/shard_map/pallas_call | solution.py:135
  69.7 0.0 collective-permute-done.4.rest_11_.rest_0_
  69.7 0.0 collective-permute-done.5.rest_10_.rest_0_
  69.7 0.0 copy-done.3
  69.8 0.0 copy-done.2
  69.8 3.9 %shard_map.115 = f32[8,2,16,128]{3,2,1,0:T(8,128)} custom-call(s32[2]{0:T(128)S(1)} %bitcast.46, s32[2]{0:T(128)S(1)} %get-tuple-element.42.slot, f32[2]{0:T(128)S(1)} %broadcast_multiply_fusion.turns, bf16[2,256,256]{2,1,0:T(8,128)(2,1)S(1)} %get-tuple-element.63.wx, bf16[2,256,256]{2,1,0:T(8,128)(2,1)S(1)} %get-tuple-element.64.wy, ...), custom_call_target="tpu_custom_call" | custom-call | flops 1610612736 | bytes 2097152 | tf_op jit(solution)/shard_map/pallas_call | solution.py:194
  73.7 0.0 copy-start.5
  73.7 0.8 copy-done.5
  74.5 3.6 %all-to-all-start.2 = ((f32[8,2,16,128]{3,2,1,0:T(8,128)}), f32[8,2,16,128]{3,2,1,0:T(8,128)S(1)}, u32[]{:S(2)}, u32[]{:S(2)}) async-start(f32[8,2,16,128]{3,2,1,0:T(8,128)} %shard_map.115), calls=%async_computation.2 | async-start | bytes 262144 | tf_op jit(solution)/shard_map/all_to_all | solution.py:369
  78.1 0.0 copy-start.4
  78.1 1.0 copy-done.4
  79.1 1.0 copy-done.6
  80.2 8.0 %shard_map.116 = (bf16[2,1,2,128,4096]{4,3,2,1,0:T(8,128)(2,1)}, bf16[2,1,2,128,4096]{4,3,2,1,0:T(8,128)(2,1)}) custom-call(s32[2]{0:T(128)S(1)} %pad_add_fusion.2.where, f32[2]{0:T(128)S(1)} %broadcast_multiply_fusion.turns, bf16[2,256,256]{2,1,0:T(8,128)(2,1)S(1)} %get-tuple-element.63.wx, ...), custom_call_target="tpu_custom_call", output_to_operand_aliasing={{0}: (8, {}), {1}: (9, {})} | custom-call | flops 6442450944 | bytes 4194304 | tf_op jit(solution)/shard_map/pallas_call | solution.py:135
  88.2 0.0 all-to-all-done.2.parts
  88.2 0.7 copy-done.8
  88.8 1.9 %shard_map.118 = f32[16,2,16,256]{3,2,1,0:T(8,128)} custom-call(s32[2]{0:T(128)} %bitcast.45, s32[64]{0:T(128)} %order.1, f32[8,2,16,128]{3,2,1,0:T(8,128)} %copy-done.8), custom_call_target="tpu_custom_call" | custom-call | tf_op jit(solution)/shard_map/pallas_call | solution.py:233
  90.8 4.1 %all-to-all-start.3 = ((f32[16,2,16,256]{3,2,1,0:T(8,128)}), f32[16,2,16,256]{3,2,1,0:T(8,128)}, u32[]{:S(2)}, u32[]{:S(2)}) async-start(f32[16,2,16,256]{3,2,1,0:T(8,128)} %shard_map.118), calls=%async_computation.3 | async-start | bytes 1048576 | tf_op jit(solution)/shard_map/all_to_all | solution.py:372
  94.9 4.8 %shard_map.117 = (bf16[2,1,2,128,4096]{4,3,2,1,0:T(8,128)(2,1)}, bf16[2,1,2,128,4096]{4,3,2,1,0:T(8,128)(2,1)}) custom-call(s32[1]{0:T(128)} %bitcast.where, f32[2]{0:T(128)S(1)} %broadcast_multiply_fusion.turns, bf16[2,256,256]{2,1,0:T(8,128)(2,1)S(1)} %get-tuple-element.63.wx, ...), custom_call_target="tpu_custom_call", output_to_operand_aliasing={{0}: (7, {}), {1}: (8, {})} | custom-call | flops 3221225472 | bytes 2097152 | tf_op jit(solution)/shard_map/pallas_call | solution.py:135
  99.7 5.1 %all-to-all-done.3 = f32[16,2,16,256]{3,2,1,0:T(8,128)} async-done(((f32[16,2,16,256]{3,2,1,0:T(8,128)}), f32[16,2,16,256]{3,2,1,0:T(8,128)}, u32[]{:S(2)}, u32[]{:S(2)}) %all-to-all-start.3) | async-done | bytes 524320 | tf_op jit(solution)/shard_map/all_to_all | solution.py:372
  104.8 1.1 %reduce_sum.9 = f32[2,16,256]{2,1,0:T(8,128)S(1)} reduce(f32[16,2,16,256]{3,2,1,0:T(8,128)} %all-to-all-done.3, f32[]{:T(128)} %constant.168.clone.1), dimensions={0}, to_apply=%region_1.2 | reduce | flops 122880 | bytes 557060 | tf_op jit(solution)/shard_map/reduce_sum | solution.py:374
  105.9 0.1 reshape.37
  106.0 0.7 reshape.38
  (12 shorter events, 0.1 us)
Async XLA Ops:
  0.6 1.6 %copy-start = (f32[1,128,4096]{2,1,0:T(8,128)S(1)}, f32[1,128,4096]{2,1,0:T(8,128)}, u32[]{:S(2)}) copy-start(f32[1,128,4096]{2,1,0:T(8,128)} %param.14) | copy-start | bytes 6291460
  0.6 25.5 %copy-start.9 = (bf16[2,2,128,128]{3,2,1,0:T(8,128)(2,1)S(1)}, bf16[2,2,128,128]{3,2,1,0:T(8,128)(2,1)}, u32[]{:S(2)}) copy-start(bf16[2,2,128,128]{3,2,1,0:T(8,128)(2,1)} %param.12) | copy-start | bytes 393220
  0.7 36.6 %copy-start.10 = (f32[2]{0:T(128)S(1)}, f32[2]{0:T(128)}, u32[]{:S(2)}) copy-start(f32[2]{0:T(128)} %param.11) | copy-start | bytes 28
  0.7 36.6 %copy-start.7 = (s32[1,2]{1,0:T(1,128)S(1)}, s32[1,2]{1,0:T(1,128)}, u32[]{:S(2)}) copy-start(s32[1,2]{1,0:T(1,128)} %param.16) | copy-start | bytes 28
  3.1 14.3 %all-to-all-start = ((f32[16,8,512]{2,1,0:T(8,128)}), f32[16,8,512]{2,1,0:T(8,128)S(1)}, u32[]{:S(2)}, u32[]{:S(2)}) async-start(f32[16,8,512]{2,1,0:T(8,128)} %bitcast.15), calls=%async_computation | async-start | bytes 524288 | tf_op jit(solution)/shard_map/all_to_all | solution.py:330
  18.3 17.5 %all-to-all-start.1 = ((f32[16,2,8,512]{3,2,1,0:T(8,128)}), f32[16,2,8,512]{3,2,1,0:T(8,128)S(1)}, u32[]{:S(2)}, u32[]{:S(2)}) async-start(f32[16,2,8,512]{3,2,1,0:T(8,128)} %broadcast_in_dim.2), calls=%async_computation.1 | async-start | bytes 1048576 | tf_op jit(solution)/shard_map/all_to_all | solution.py:336
  35.8 12.3 %copy-start.1 = (f32[16,2,8,512]{3,2,1,0:T(8,128)}, f32[16,2,8,512]{3,2,1,0:T(8,128)S(1)}, u32[]{:S(2)}) copy-start(f32[16,2,8,512]{3,2,1,0:T(8,128)S(1)} %all-to-all-done.1.rest_0_.rest_4_) | copy-start | bytes 1572868
  35.8 4.3 %collective-permute-start.3 = (f32[16,2,8,512]{3,2,1,0:T(8,128)S(1)}, f32[16,2,8,512]{3,2,1,0:T(8,128)S(1)}, u32[]{:S(2)}, u32[]{:S(2)}) collective-permute-start(f32[16,2,8,512]{3,2,1,0:T(8,128)S(1)} %all-to-all-done.1.rest_0_.rest_4_), channel_id=1, source_target_pairs={{0,1},{1,0},{2,3},{3,2},{4,5},{5,4},{6,7},{7,6},{8,9},{9,8},{10,11... | collective-permute-start | bytes 1572872 | tf_op jit(solution)/shard_map/ppermute | solution.py:321
  37.3 10.8 %collective-permute-start.2 = (f32[16,2,8,512]{3,2,1,0:T(8,128)S(1)}, f32[16,2,8,512]{3,2,1,0:T(8,128)S(1)}, u32[]{:S(2)}, u32[]{:S(2)}) collective-permute-start(f32[16,2,8,512]{3,2,1,0:T(8,128)S(1)} %all-to-all-done.1.rest_0_.rest_4_), channel_id=1, source_target_pairs={{0,48},{1,7},{2,50},{3,1},{4,52},{5,3},{6,54},{7,5},{8,56},{9,15},... | collective-permute-start | bytes 1572872 | tf_op jit(solution)/shard_map/ppermute | solution.py:321
  38.7 15.2 %collective-permute-start.1 = (f32[16,2,8,512]{3,2,1,0:T(8,128)S(1)}, f32[16,2,8,512]{3,2,1,0:T(8,128)S(1)}, u32[]{:S(2)}, u32[]{:S(2)}) collective-permute-start(f32[16,2,8,512]{3,2,1,0:T(8,128)S(1)} %all-to-all-done.1.rest_0_.rest_4_), channel_id=1, source_target_pairs={{0,16},{1,3},{2,18},{3,5},{4,20},{5,7},{6,22},{7,1},{8,24},{9,11},... | collective-permute-start | bytes 1572872 | tf_op jit(solution)/shard_map/ppermute | solution.py:321
  38.8 24.7 %collective-permute-start = (f32[16,2,8,512]{3,2,1,0:T(8,128)S(1)}, f32[16,2,8,512]{3,2,1,0:T(8,128)S(1)}, u32[]{:S(2)}, u32[]{:S(2)}) collective-permute-start(f32[16,2,8,512]{3,2,1,0:T(8,128)S(1)} %all-to-all-done.1.rest_0_.rest_4_), channel_id=1, source_target_pairs={{0,32},{1,5},{2,34},{3,7},{4,36},{5,1},{6,38},{7,3},{8,40},{9,13},... | collective-permute-start | bytes 1572872 | tf_op jit(solution)/shard_map/ppermute | solution.py:321
  53.8 11.1 %collective-permute-start.6 = (f32[16,2,8,512]{3,2,1,0:T(8,128)S(1)}, f32[16,2,8,512]{3,2,1,0:T(8,128)S(1)}, u32[]{:S(2)}, u32[]{:S(2)}) collective-permute-start(f32[16,2,8,512]{3,2,1,0:T(8,128)S(1)} %collective-permute-done.1.rest_0_.rest_6_), channel_id=1, source_target_pairs={{0,1},{1,0},{2,3},{3,2},{4,5},{5,4},{6,7},{7,6},{8,9},{9,8},{10,11... | collective-permute-start | bytes 1572872 | tf_op jit(solution)/shard_map/ppermute | solution.py:321
  55.6 14.2 %collective-permute-start.5 = (f32[16,2,8,512]{3,2,1,0:T(8,128)S(1)}, f32[16,2,8,512]{3,2,1,0:T(8,128)S(1)}, u32[]{:S(2)}, u32[]{:S(2)}) collective-permute-start(f32[16,2,8,512]{3,2,1,0:T(8,128)S(1)} %collective-permute-done.2.rest_1_.rest_7_), channel_id=1, source_target_pairs={{0,1},{1,0},{2,3},{3,2},{4,5},{5,4},{6,7},{7,6},{8,9},{9,8},{10,11... | collective-permute-start | bytes 1572872 | tf_op jit(solution)/shard_map/ppermute | solution.py:321
  63.6 6.2 %copy-start.3 = (f32[16,2,8,512]{3,2,1,0:T(8,128)}, f32[16,2,8,512]{3,2,1,0:T(8,128)S(1)}, u32[]{:S(2)}) copy-start(f32[16,2,8,512]{3,2,1,0:T(8,128)S(1)} %collective-permute-done.rest_8_.rest_1_) | copy-start | bytes 1572868
  63.6 6.2 %collective-permute-start.4 = (f32[16,2,8,512]{3,2,1,0:T(8,128)S(1)}, f32[16,2,8,512]{3,2,1,0:T(8,128)S(1)}, u32[]{:S(2)}, u32[]{:S(2)}) collective-permute-start(f32[16,2,8,512]{3,2,1,0:T(8,128)S(1)} %collective-permute-done.rest_8_.rest_1_), channel_id=1, source_target_pairs={{0,1},{1,0},{2,3},{3,2},{4,5},{5,4},{6,7},{7,6},{8,9},{9,8},{10,11... | collective-permute-start | bytes 1572872 | tf_op jit(solution)/shard_map/ppermute | solution.py:321
  64.9 4.8 %copy-start.2 = (f32[16,2,8,512]{3,2,1,0:T(8,128)S(1)}, f32[16,2,8,512]{3,2,1,0:T(8,128)}, u32[]{:S(2)}) copy-start(f32[16,2,8,512]{3,2,1,0:T(8,128)} %copy-done.1) | copy-start | bytes 1572868
  73.7 0.8 copy-start.5
  74.5 13.7 %all-to-all-start.2 = ((f32[8,2,16,128]{3,2,1,0:T(8,128)}), f32[8,2,16,128]{3,2,1,0:T(8,128)S(1)}, u32[]{:S(2)}, u32[]{:S(2)}) async-start(f32[8,2,16,128]{3,2,1,0:T(8,128)} %shard_map.115), calls=%async_computation.2 | async-start | bytes 262144 | tf_op jit(solution)/shard_map/all_to_all | solution.py:369
  78.1 1.0 copy-start.4
  79.1 1.0 copy-start.6
  88.2 0.7 copy-start.8
  90.8 14.1 %all-to-all-start.3 = ((f32[16,2,16,256]{3,2,1,0:T(8,128)}), f32[16,2,16,256]{3,2,1,0:T(8,128)}, u32[]{:S(2)}, u32[]{:S(2)}) async-start(f32[16,2,16,256]{3,2,1,0:T(8,128)} %shard_map.118), calls=%async_computation.3 | async-start | bytes 1048576 | tf_op jit(solution)/shard_map/all_to_all | solution.py:372

commit v3 on v2

--- a/solution.py
+++ b/solution.py
@@ -12,7 +12,7 @@
 TILE_DEV = 4
 BLOCK = 128
 TILE = 512
-VMEM = 48 * 1024 * 1024
+VMEM = 24 * 1024 * 1024
 SIN = (4.442867755889893, -7.307443618774414, 3.594788074493408, -0.7843739986419678)
 COS = (1.4142135381698608, -6.978850841522217, 5.7394609451293945, -1.8835630416870117, 0.31069818139076233)
 
@@ -150,7 +150,8 @@
 
 
 def image_body(tiles, slot, turns, wx, wy, *rest, scale, per, aper, count):
-    fields, slabs, out, held, sems = rest[: 2 * aper], rest[2 * aper : -3], rest[-3], rest[-2], rest[-1]
+    fields, slabs = rest[: 2 * aper], rest[2 * aper : -4]
+    out, held, lines, sems = rest[-4:]
     copies = []
     for a in range(aper):
         column = pl.multiple_of(lax.rem(lax.div(tiles[a], 2), per) * BLOCK, BLOCK)
@@ -170,7 +171,6 @@
     for d in range(held.shape[2]):
         views = [slab_view(held.at[a], d, slice(0, BLOCK)) for a in range(aper)]
         parts = advance(parts, [[v * turns[f] for v in views] for f in range(freqs)], wx, wy)
-        picked = []
         for a in range(aper):
             sr, si, rr, ri = parts[0][a]
             term = sr * rr - si * ri
@@ -178,9 +178,11 @@
                 sr, si, rr, ri = parts[f][a]
                 term += sr * rr - si * ri
             odd = lax.rem(tiles[a], 2) == 1
-            picked.append(jnp.where(odd, term[:, half:], term[:, :half]) * scale)
-        both = jnp.concatenate(picked, 1)
-        out[:, d] = both.reshape(count, both.shape[0] // count, both.shape[1])
+            lines[a, :, :half] = jnp.where(odd, term[:, half:], term[:, :half]) * scale
+            pairs_of = lines.shape[1] // 2
+            even_odd = [lines[a, pl.ds(k, pairs_of, stride=2), :half] for k in range(2)]
+            both = jnp.concatenate(even_odd, 1)
+            out[:, a, d] = both.reshape(count, pairs_of // count, BLOCK)
 
 
 def image_terms(tiles, slot, turns, wx, wy, src, rcv, slabs, scale, count):
@@ -189,8 +191,7 @@
     aper = tiles.shape[0]
     whole = lambda a: pl.BlockSpec(a.shape, lambda i, t, s: (0,) * a.ndim)
     field = lambda a: pl.BlockSpec((freqs, 1, 2, height, BLOCK), lambda i, t, s: (0, 0, 0, 0, lax.div(t[a], 2)))
-    lanes = aper * BLOCK // 2
-    shape = (count, steps, height // count, lanes)
+    shape = (count, aper, steps, height // 2 // count, BLOCK)
     return pl.pallas_call(
         functools.partial(image_body, scale=scale, per=cols // BLOCK, aper=aper, count=count),
         grid_spec=pltpu.PrefetchScalarGridSpec(
@@ -199,9 +200,10 @@
             in_specs=[pl.BlockSpec(memory_space=pltpu.SMEM), whole(wx), whole(wy)]
             + [field(a) for a in range(aper) for _ in range(2)]
             + [pl.BlockSpec(memory_space=pl.ANY)] * len(slabs),
-            out_specs=pl.BlockSpec(shape, lambda i, t, s: (0, 0, 0, 0)),
+            out_specs=pl.BlockSpec(shape, lambda i, t, s: (0,) * len(shape)),
             scratch_shapes=[
                 pltpu.VMEM((aper,) + slabs[0].shape[:3] + (BLOCK,), jnp.float32),
+                pltpu.VMEM((aper, height, BLOCK), jnp.float32),
                 pltpu.SemaphoreType.DMA((aper,)),
             ],
         ),
@@ -213,29 +215,77 @@
     )(tiles, slot, turns, wx, wy, *[v for _ in range(aper) for v in (src, rcv)], *slabs)
 
 
-def deal_body(tiles, order, parts, out, *, per):
+def deal_body(tiles, parts, out):
     total = jnp.sum(parts[...], axis=0)
-    half = BLOCK // 2
-    swapped = jnp.concatenate([total[..., half:], total[..., :half]], -1)
-    low = lax.broadcasted_iota(jnp.int32, total.shape, 2) < half
-    zero = jnp.zeros_like(total)
+    ids = [jnp.full((1, BLOCK), tiles[a], jnp.int32).astype(jnp.float32) for a in range(tiles.shape[0])]
+    spare = out.shape[1] - total.shape[0] - len(ids)
+    total = jnp.concatenate([total] + ids + [jnp.zeros((spare, BLOCK), jnp.float32)], 0)
     for j in range(out.shape[0]):
-        for q in range(per // 2):
-            p = j * per + 2 * q
-            straight = (low & (order[p] == tiles[0])) | (~low & (order[p + 1] == tiles[1]))
-            crossed = (low & (order[p] == tiles[1])) | (~low & (order[p + 1] == tiles[0]))
-            out[j, :, :, q * BLOCK : (q + 1) * BLOCK] = jnp.where(straight, total, zero) + jnp.where(crossed, swapped, zero)
-
-
-def deal(tiles, order, parts, shots):
-    per = order.shape[0] // shots
-    _, steps, lines, lanes = parts.shape
+        out[j] = total
+
+
+def deal(tiles, parts, shots):
+    rows = parts.shape[1] + 8
     return pl.pallas_call(
-        functools.partial(deal_body, per=per),
-        in_specs=[pl.BlockSpec(memory_space=pltpu.SMEM)] * 2 + [pl.BlockSpec(memory_space=pltpu.VMEM)],
+        deal_body,
+        in_specs=[pl.BlockSpec(memory_space=pltpu.SMEM), pl.BlockSpec(memory_space=pltpu.VMEM)],
         out_specs=pl.BlockSpec(memory_space=pltpu.VMEM),
-        out_shape=jax.ShapeDtypeStruct((shots, steps, lines, per * BLOCK // 2), jnp.float32),
-    )(tiles, order, parts)
+        out_shape=jax.ShapeDtypeStruct((shots, rows, BLOCK), jnp.float32),
+    )(tiles, parts)
+
+
+def collect_body(entries, parts, out, *, aper):
+    steps = out.shape[1]
+    rows = out.shape[2] // BLOCK
+    size = steps * rows
+    for p in range(out.shape[0]):
+        total = jnp.zeros((size, BLOCK), jnp.float32)
+        for s in range(parts.shape[0]):
+            for a in range(aper):
+                at = aper * size + a
+                named = parts[s, at : at + 1].astype(jnp.int32) == entries[p]
+                total += jnp.where(named, parts[s, a * size : (a + 1) * size], 0.0)
+        for d in range(steps):
+            for r in range(rows):
+                out[p, d, r * BLOCK : (r + 1) * BLOCK] = total[d * rows + r]
+
+
+def collect(entries, parts, aper, steps, length):
+    return pl.pallas_call(
+        functools.partial(collect_body, aper=aper),
+        in_specs=[pl.BlockSpec(memory_space=pltpu.SMEM), pl.BlockSpec(memory_space=pltpu.VMEM)],
+        out_specs=pl.BlockSpec(memory_space=pltpu.VMEM),
+        out_shape=jax.ShapeDtypeStruct((entries.shape[0], steps, length), jnp.float32),
+    )(entries, parts)
+
+
+def cut_body(spot, slab, out, sems, *, cols):
+    y = spot[0]
+    xs = out.shape[1]
+    copies = [
+        pltpu.make_async_copy(
+            slab.at[:, :, :, pl.ds(pl.multiple_of(y * cols, BLOCK), cols)], out.at[:, :, 0], sems.at[xs]
+        )
+    ]
+    for x in range(xs):
+        copies.append(
+            pltpu.make_async_copy(slab.at[:, y, :, pl.ds((xs + x) * cols, cols)], out.at[:, x, 1], sems.at[x])
+        )
+    for c in copies:
+        c.start()
+    for c in copies:
+        c.wait()
+
+
+def cut(y, slab, cols):
+    zls, xs, rows, _ = slab.shape
+    return pl.pallas_call(
+        functools.partial(cut_body, cols=cols),
+        in_specs=[pl.BlockSpec(memory_space=pltpu.SMEM), pl.BlockSpec(memory_space=pltpu.HBM)],
+        out_specs=pl.BlockSpec(memory_space=pltpu.HBM),
+        out_shape=jax.ShapeDtypeStruct((zls, xs, CORES, rows, cols), slab.dtype),
+        scratch_shapes=[pltpu.SemaphoreType.DMA((xs + 1,))],
+    )(y, slab)
 
 
 def sweep_weights(xc, yc):
@@ -268,9 +318,8 @@
     freq, shot = mesh_shape
     zhs, zls = freq // YS, shot // (XS * CORES)
     at = lambda zh, y, zl, x, c: ((zh * YS + y) * shot) + (zl * XS + x) * CORES + c
-    every = [(zl, zh) for zl in range(zls) for zh in range(zhs)]
-    out = [[at(zh, y, zl, x, 0) for zl, zh in every for x in range(XS)] for y in range(YS)]
-    return out + [[at(zh, y, zl, x, 1) for zl, zh in every for y in range(YS)] for x in range(XS)]
+    out = [[at(zh, y, zl, x, 0) for zl in range(zls) for x in range(XS)] for zh in range(zhs) for y in range(YS)]
+    return out + [[at(zh, y, zl, x, 1) for zl in range(zls) for y in range(YS)] for zh in range(zhs) for x in range(XS)]
 
 
 def local(
@@ -288,7 +337,7 @@
     freq_total = angular_freq.shape[0] * freqs_dev
     height, width = velocity.shape[1:]
     f_id, s_id = lax.axis_index("freq"), lax.axis_index("shot")
-    zh, y = lax.div(f_id, YS), lax.rem(f_id, YS)
+    y = lax.rem(f_id, YS)
     zl, x, core = lax.div(s_id, XS * CORES), lax.rem(lax.div(s_id, CORES), XS), lax.rem(s_id, CORES)
     zhs, zls = freq // YS, shot // (XS * CORES)
     at = lambda zh, y, zl, x, c: ((zh * YS + y) * shot) + (zl * XS + x) * CORES + c
@@ -317,16 +366,10 @@
     zhs, zls = freqs_dev // YS, shots // (XS * CORES)
     first = core == 0
     cols = width // (CORES * XS)
-    rows = height // (zls * zhs * XS)
+    rows = height // (zls * XS)
     send = lambda v, move: lax.ppermute(v, AXES, pairs((freqs_dev, shots), move))
 
-    half = width // CORES
-    slab = velocity[0].reshape(zls, zhs, XS, rows, width)
-    slab = lax.dynamic_index_in_dim(slab, zh, 1, keepdims=False)
-    to_first = lax.dynamic_slice_in_dim(slab, y * cols, cols, 3)
-    to_second = lax.dynamic_index_in_dim(slab, y, 1, keepdims=False)[..., half:]
-    to_second = jnp.swapaxes(to_second.reshape(zls, rows, XS, cols), 1, 2)
-    outgoing = jnp.stack([to_first, to_second], axis=2).reshape(shots, rows, cols)
+    outgoing = cut(y[None], velocity.reshape(zls, XS, rows, width), cols).reshape(shots, rows, cols)
     arrived = lax.all_to_all(outgoing, "shot", 0, 0, tiled=True)
     mine = jnp.stack([lax.dynamic_index_in_dim(arrived, slab_owner[d], 0, keepdims=False) for d in range(DEPTH)])
 
@@ -350,15 +393,15 @@
         return march(jnp.stack(places).astype(jnp.int32), turns, slabs, wx, wy, src, rcv, tuple(done))
 
     own_p = send(own, swap)
-    s1, s3, s2 = (send(own, shift(k)) for k in (1, 3, 2))
+    s1, s3 = send(own, shift(1)), send(own, shift(3))
+    later, own_p = lax.optimization_barrier((own, own_p))
+    s2 = send(later, shift(2))
     fields = forward([place(0), partner_place(0)], [own, own_p])
     s1, s3, *fields = lax.optimization_barrier((s1, s3, *fields))
     s1_p, s3_p = send(s1, swap), send(s3, swap)
     fields = forward([place(1), place(3)], [s1, s3], fields)
     s2, *fields = lax.optimization_barrier((s2, *fields))
     s2_p = send(s2, swap)
-    fields = forward([partner_place(1)], [s1_p], fields)
-    s2_p, s3_p, *fields = lax.optimization_barrier((s2_p, s3_p, *fields))
 
     tiles = apertures[0]
     held = lax.div(tiles * (width // (TILE_DEV * shots)), cols)
@@ -366,14 +409,14 @@
     places = jnp.stack([place(0), partner_place(0), place(1), place(3), place(2)] + [partner_place(k) for k in (1, 3, 2)])
     slot = jnp.argmax(places[None, :] == held[:, None], axis=1).astype(jnp.int32)
     terms = image_terms(tiles, slot, turns, wx, wy, src, rcv, slabs, 1.0 / freq_total, freqs_dev)
-    terms = lax.all_to_all(terms, "freq", 0, 0, tiled=True)
-    fields = forward([partner_place(3), place(2)], [s3_p, s2], fields)
+    length = terms.shape[3] * terms.shape[4]
+    terms = lax.all_to_all(terms.reshape(freqs_dev, -1, BLOCK), "freq", 0, 0, tiled=True)
+    fields = forward([partner_place(1), partner_place(3)], [s1_p, s3_p], fields)
     terms, *fields = lax.optimization_barrier((terms, *fields))
-    dense = lax.all_to_all(deal(tiles, tile_order, terms, shots), "shot", 0, 0, tiled=True)
-    fields = forward([partner_place(2)], [s2_p], fields)
-    image = jnp.sum(dense, axis=0)
-    image = image.reshape(DEPTH, image.shape[1], TILE_DEV, -1)
-    image = jnp.transpose(image, (2, 0, 1, 3)).reshape(TILE_DEV, DEPTH, -1)
+    dealt = lax.all_to_all(deal(tiles, terms, shots), "shot", 0, 0, tiled=True)
+    fields = forward([place(2), partner_place(2)], [s2, s2_p], fields)
+    entries = lax.dynamic_slice_in_dim(tile_order, s_id * TILE_DEV, TILE_DEV)
+    image = collect(entries, dealt, tiles.shape[0], DEPTH, length)
     return (*fields, image)
 
 

time: 108 us -> 113 us (1.046)
  Pallas kernels: 39.4 us -> 56.4 us
  local copies, waits for them, and re-layouts: 9.41 us -> 5.5 us
  waiting for transfers between devices: 20.5 us -> 16.9 us
  other arithmetic: 3.72 us -> 1.09 us
  starting transfers between devices: 28.8 us -> 27.2 us
    pallas_call x1 -> x3, Pallas kernels: 1.92 us -> 20.5 us  [the longest x1 17 us: cut(): pl.pallas_call(functools.partial(cut_body, cols=cols), in_specs=[pl.Block...]
    all_to_all x2, waiting for transfers between devices: 5.15 us -> 0.01 us  [the longest x1 0.01 us: local(): dealt = lax.all_to_all(deal(tiles, terms, shots), 'shot', 0, 0, tiled=True)]
    unnamed x24 -> x14, local copies, waits for them, and re-layouts: 5.31 us -> 1.62 us
    all_to_all x1, waiting for transfers between devices: 0.09 us -> 3.42 us  [local(): arrived = lax.all_to_all(outgoing, 'shot', 0, 0, tiled=True)]
    all_to_all x1, starting transfers between devices: 7.46 us -> 4.81 us  [local(): own = lax.all_to_all(own, AXES, 0, 0, axis_index_groups=groups, tiled=True)]
    all_to_all x1, waiting for transfers between devices: 9.51 us -> 7.35 us  [local(): own = lax.all_to_all(own, AXES, 0, 0, axis_index_groups=groups, tiled=True)]
    pallas_call x5 -> x4, Pallas kernels: 33.6 us -> 31.8 us  [march(): pl.pallas_call(functools.partial(march_body, count=count, per=per), grid_...]
  transfers between devices with their start and end apart: 11 -> 11, of which waited for: 4 -> 4; matrix products, arithmetic and copies ran while one was open for 4% -> 4% of each run, Pallas kernels for 31% -> 28%
where the time goes in v3:
time: 113 us; the launch traced here: 112 us
  Pallas kernels  56.4 us (50%)
  starting transfers between devices  27.2 us (24%)
  waiting for transfers between devices  16.9 us (15%)
  local copies, waits for them, and re-layouts  5.5 us (5%)
  between operations  4.82 us (4%)
    pallas_call x4, Pallas kernels, march(): pl.pallas_call(functools.partial(march_body, count=count, per=per), grid_...  31.8 us
    pallas_call x1, Pallas kernels, cut(): pl.pallas_call(functools.partial(cut_body, cols=cols), in_specs=[pl.Block...  17 us
    all_to_all x1, waiting for transfers between devices, local(): own = lax.all_to_all(own, AXES, 0, 0, axis_index_groups=groups, tiled=True)  7.35 us
    all_to_all x1, starting transfers between devices, local(): arrived = lax.all_to_all(outgoing, 'shot', 0, 0, tiled=True)  7.18 us
    ppermute x7, starting transfers between devices, local(): lax.ppermute(v, AXES, pairs((freqs_dev, shots), move))  6.49 us
    ppermute x7, waiting for transfers between devices, local(): lax.ppermute(v, AXES, pairs((freqs_dev, shots), move))  6.12 us
    all_to_all x1, starting transfers between devices, local(): own = lax.all_to_all(own, AXES, 0, 0, axis_index_groups=groups, tiled=True)  4.81 us
    all_to_all x1, starting transfers between devices, local(): lax.all_to_all(terms.reshape(freqs_dev, -1, BLOCK), 'freq', 0, 0, tiled=T...  4.59 us
  transfers between devices with their start and end apart: 11, of which 4 were waited for; matrix products, arithmetic and copies ran while one was open for 4% of the time, Pallas kernels for 28%

profile of v3, /device:TPU:1, one launch (start us, length us, event | category | flops | bytes accessed | tf_op | source)
XLA Modules:
  0.0 111.9 jit_solution(16274938687496786357)
XLA Ops:
  0.6 0.0 copy-start.4
  0.6 0.0 copy-start.3
  0.7 0.0 copy-start.5
  0.7 17.0 %shard_map.112 = f32[2,4,2,16,512]{4,3,2,1,0:T(8,128)} custom-call(s32[1]{0:T(128)} %bitcast.10.spot, f32[2,4,16,4096]{3,2,1,0:T(8,128)} %bitcast.35), custom_call_target="tpu_custom_call" | custom-call | tf_op jit(solution)/shard_map/pallas_call | solution.py:282
  17.7 7.2 %all-to-all-start = ((f32[16,16,512]{2,1,0:T(8,128)}), f32[16,16,512]{2,1,0:T(8,128)S(1)}, u32[]{:S(2)}, u32[]{:S(2)}) async-start(f32[16,16,512]{2,1,0:T(8,128)} %bitcast.36), calls=%async_computation | async-start | bytes 1048576 | tf_op jit(solution)/shard_map/all_to_all | solution.py:373
  24.9 1.4 %fusion.3 = (s32[1]{0:T(128)}, s32[1]{0:T(128)}) fusion(s32[2]{0:T(128)} %param.15), kind=kLoop, calls=%fused_computation.19 | loop fusion | bytes 16 | tf_op jit(solution)/shard_map/slice | solution.py:374
  30.3 0.1 pad_add_fusion.3.where
  30.4 0.1 pad_add_fusion.1.where
  30.5 0.9 fusion.2
  31.4 3.4 %all-to-all-done = f32[16,16,512]{2,1,0:T(8,128)S(1)} async-done(((f32[16,16,512]{2,1,0:T(8,128)}), f32[16,16,512]{2,1,0:T(8,128)S(1)}, u32[]{:S(2)}, u32[]{:S(2)}) %all-to-all-start) | async-done | bytes 524320 | tf_op jit(solution)/shard_map/all_to_all | solution.py:373
  34.8 0.9 broadcast_in_dim.5
  35.7 4.8 %all-to-all-start.1 = ((f32[8,2,16,512]{3,2,1,0:T(8,128)}), f32[8,2,16,512]{3,2,1,0:T(8,128)S(1)}, u32[]{:S(2)}, u32[]{:S(2)}) async-start(f32[8,2,16,512]{3,2,1,0:T(8,128)} %broadcast_in_dim.5), calls=%async_computation.1 | async-start | bytes 1048576 | tf_op jit(solution)/shard_map/all_to_all | solution.py:379
  40.5 0.1 pad_add_fusion.2.where
  40.5 0.1 copy.29
  40.7 0.1 copy.28
  40.8 0.0 copy-done.4
  40.8 0.7 dynamic_slice.12.entries
  41.5 0.1 stack.64
  41.5 0.0 copy-done.3
  41.6 7.4 %all-to-all-done.1.rest_0_.rest_4_ = f32[8,2,16,512]{3,2,1,0:T(8,128)S(1)} async-done(((f32[8,2,16,512]{3,2,1,0:T(8,128)}), f32[8,2,16,512]{3,2,1,0:T(8,128)S(1)}, u32[]{:S(2)}, u32[]{:S(2)}) %all-to-all-start.1) | async-done | bytes 524320 | tf_op jit(solution)/shard_map/all_to_all | solution.py:379
  48.9 0.9 collective-permute-start
  49.8 0.1 maximum_maximum_fusion
  49.9 0.0 copy-done.5
  49.9 1.2 %collective-permute-start.3 = (f32[8,2,16,512]{3,2,1,0:T(8,128)S(1)}, f32[8,2,16,512]{3,2,1,0:T(8,128)S(1)}, u32[]{:S(2)}, u32[]{:S(2)}) collective-permute-start(f32[8,2,16,512]{3,2,1,0:T(8,128)S(1)} %all-to-all-done.1.rest_0_.rest_4_), channel_id=1, source_target_pairs={{0,48},{1,7},{2,50},{3,1},{4,52},{5,3},{6,54},{7,5},{8,56},{9,15},... | collective-permute-start | bytes 1572872 | tf_op jit(solution)/shard_map/ppermute | solution.py:370
  51.0 0.4 collective-permute-start.2
  51.4 0.0 collective-permute-done.rest_1_.rest_5_
  51.4 1.4 %collective-permute-start.1 = (f32[8,2,16,512]{3,2,1,0:T(8,128)S(1)}, f32[8,2,16,512]{3,2,1,0:T(8,128)S(1)}, u32[]{:S(2)}, u32[]{:S(2)}) collective-permute-start(f32[8,2,16,512]{3,2,1,0:T(8,128)S(1)} %all-to-all-done.1.rest_0_.rest_4_), channel_id=1, source_target_pairs={{0,32},{1,5},{2,34},{3,7},{4,36},{5,1},{6,38},{7,3},{8,40},{9,13},... | collective-permute-start | bytes 1572872 | tf_op jit(solution)/shard_map/ppermute | solution.py:370
  52.9 8.0 %shard_map.113 = (bf16[2,1,2,128,4096]{4,3,2,1,0:T(8,128)(2,1)}, bf16[2,1,2,128,4096]{4,3,2,1,0:T(8,128)(2,1)}) custom-call(s32[2]{0:T(128)S(1)} %pad_add_fusion.2.where, f32[2]{0:T(128)S(1)} %broadcast_multiply_fusion.turns, bf16[2,256,256]{2,1,0:T(8,128)(2,1)S(1)} %get-tuple-element.53.wx, bf16[2,256,256]{2,1,0:T(8,128)(2,1)S(1)} %get-tuple-element.54.wy, ...), custom_call_target="tpu_custom_call" | custom-call | flops 6442450944 | bytes 4194304 | tf_op jit(solution)/shard_map/pallas_call | solution.py:135
  60.8 0.0 collective-permute-done.3.rest_1_.rest_7_
  60.8 5.4 %collective-permute-done.2.rest_0_.rest_6_ = f32[8,2,16,512]{3,2,1,0:T(8,128)S(1)} collective-permute-done((f32[8,2,16,512]{3,2,1,0:T(8,128)S(1)}, f32[8,2,16,512]{3,2,1,0:T(8,128)S(1)}, u32[]{:S(2)}, u32[]{:S(2)}) %collective-permute-start.2) | collective-permute-done | bytes 524320 | tf_op jit(solution)/shard_map/ppermute | solution.py:370
  66.2 0.0 copy-start
  66.2 2.1 %collective-permute-start.5 = (f32[8,2,16,512]{3,2,1,0:T(8,128)S(1)}, f32[8,2,16,512]{3,2,1,0:T(8,128)S(1)}, u32[]{:S(2)}, u32[]{:S(2)}) collective-permute-start(f32[8,2,16,512]{3,2,1,0:T(8,128)S(1)} %collective-permute-done.2.rest_0_.rest_6_), channel_id=1, source_target_pairs={{0,1},{1,0},{2,3},{3,2},{4,5},{5,4},{6,7},{7,6},{8,9},{9,8},{10,11... | collective-permute-start | bytes 1572872 | tf_op jit(solution)/shard_map/ppermute | solution.py:370
  68.3 0.0 collective-permute-start.6
  68.3 7.9 %shard_map.114 = (bf16[2,1,2,128,4096]{4,3,2,1,0:T(8,128)(2,1)}, bf16[2,1,2,128,4096]{4,3,2,1,0:T(8,128)(2,1)}) custom-call(s32[2]{0:T(128)S(1)} %pad_add_fusion.1.where, f32[2]{0:T(128)S(1)} %broadcast_multiply_fusion.turns, bf16[2,256,256]{2,1,0:T(8,128)(2,1)S(1)} %get-tuple-element.53.wx, ...), custom_call_target="tpu_custom_call", output_to_operand_aliasing={{0}: (8, {}), {1}: (9, {})} | custom-call | flops 6442450944 | bytes 4194304 | tf_op jit(solution)/shard_map/pallas_call | solution.py:135
  76.3 0.0 collective-permute-done.1.rest_8_.rest_0_
  76.3 0.5 collective-permute-start.4
  76.8 0.1 pad_add_fusion.where
  76.9 0.0 copy-done
  76.9 0.7 compare_reduce_fusion
  77.6 0.0 collective-permute-done.5.rest_9_.rest_0_
  77.6 0.0 collective-permute-done.6.rest_10_.rest_1_
  77.6 0.7 collective-permute-done.4.rest_11_.rest_1_
  78.3 4.0 %shard_map.115 = f32[8,2,2,8,128]{4,3,2,1,0:T(8,128)} custom-call(s32[2]{0:T(128)S(1)} %bitcast.34, s32[2]{0:T(128)S(1)} %get-tuple-element.35.slot, f32[2]{0:T(128)S(1)} %broadcast_multiply_fusion.turns, bf16[2,256,256]{2,1,0:T(8,128)(2,1)S(1)} %get-tuple-element.53.wx, bf16[2,256,256]{2,1,0:T(8,128)(2,1)S(1)} %get-tuple-element.54.wy, ...), custom_call_target="tpu_custom_call" | custom-call | flops 1610612736 | bytes 2097152 | tf_op jit(solution)/shard_map/pallas_call | solution.py:195
  82.4 4.6 %all-to-all-start.2 = ((f32[8,32,128]{2,1,0:T(8,128)}), f32[8,32,128]{2,1,0:T(8,128)S(1)}, u32[]{:S(2)}, u32[]{:S(2)}) async-start(f32[8,32,128]{2,1,0:T(8,128)} %bitcast.22), calls=%async_computation.2 | async-start | bytes 262144 | tf_op jit(solution)/shard_map/all_to_all | solution.py:413
  87.0 8.0 %shard_map.116 = (bf16[2,1,2,128,4096]{4,3,2,1,0:T(8,128)(2,1)}, bf16[2,1,2,128,4096]{4,3,2,1,0:T(8,128)(2,1)}) custom-call(s32[2]{0:T(128)S(1)} %pad_add_fusion.3.where, f32[2]{0:T(128)S(1)} %broadcast_multiply_fusion.turns, bf16[2,256,256]{2,1,0:T(8,128)(2,1)S(1)} %get-tuple-element.53.wx, ...), custom_call_target="tpu_custom_call", output_to_operand_aliasing={{0}: (8, {}), {1}: (9, {})} | custom-call | flops 6442450944 | bytes 4194304 | tf_op jit(solution)/shard_map/pallas_call | solution.py:135
  94.9 0.0 all-to-all-done.2.parts
  94.9 0.0 copy-start.2
  95.0 0.6 copy-done.2
  95.6 1.7 %shard_map.118 = f32[16,40,128]{2,1,0:T(8,128)} custom-call(s32[2]{0:T(128)} %bitcast.33, f32[8,32,128]{2,1,0:T(8,128)} %copy-done.2), custom_call_target="tpu_custom_call" | custom-call | tf_op jit(solution)/shard_map/pallas_call | solution.py:229
  97.3 4.1 %all-to-all-start.3 = ((f32[16,40,128]{2,1,0:T(8,128)}), f32[16,40,128]{2,1,0:T(8,128)S(1)}, u32[]{:S(2)}, u32[]{:S(2)}) async-start(f32[16,40,128]{2,1,0:T(8,128)} %shard_map.118), calls=%async_computation.3 | async-start | bytes 655360 | tf_op jit(solution)/shard_map/all_to_all | solution.py:416
  101.4 7.9 %shard_map.117 = (bf16[2,1,2,128,4096]{4,3,2,1,0:T(8,128)(2,1)}, bf16[2,1,2,128,4096]{4,3,2,1,0:T(8,128)(2,1)}) custom-call(s32[2]{0:T(128)S(1)} %pad_add_fusion.where, f32[2]{0:T(128)S(1)} %broadcast_multiply_fusion.turns, bf16[2,256,256]{2,1,0:T(8,128)(2,1)S(1)} %get-tuple-element.53.wx, ...), custom_call_target="tpu_custom_call", output_to_operand_aliasing={{0}: (8, {}), {1}: (9, {})} | custom-call | flops 6442450944 | bytes 4194304 | tf_op jit(solution)/shard_map/pallas_call | solution.py:135
  109.3 0.0 all-to-all-done.3.parts
  109.3 0.0 copy-start.1
  109.3 0.7 copy-done.1
  110.0 1.8 %shard_map.119 = f32[4,2,1024]{2,1,0:T(2,128)} custom-call(s32[4]{0:T(128)} %dynamic_slice.12.entries, f32[16,40,128]{2,1,0:T(8,128)} %copy-done.1), custom_call_target="tpu_custom_call" | custom-call | tf_op jit(solution)/shard_map/pallas_call | solution.py:254
  (7 shorter events, 0.1 us)
Async XLA Ops:
  0.6 40.2 %copy-start.4 = (s32[64]{0:T(128)S(1)}, s32[64]{0:T(128)}, u32[]{:S(2)}) copy-start(s32[64]{0:T(128)} %param.17) | copy-start | bytes 772
  0.6 40.9 %copy-start.3 = (bf16[2,2,128,128]{3,2,1,0:T(8,128)(2,1)S(1)}, bf16[2,2,128,128]{3,2,1,0:T(8,128)(2,1)}, u32[]{:S(2)}) copy-start(bf16[2,2,128,128]{3,2,1,0:T(8,128)(2,1)} %param.12) | copy-start | bytes 393220
  0.7 49.2 %copy-start.5 = (f32[2]{0:T(128)S(1)}, f32[2]{0:T(128)}, u32[]{:S(2)}) copy-start(f32[2]{0:T(128)} %param.11) | copy-start | bytes 28
  17.7 17.1 %all-to-all-start = ((f32[16,16,512]{2,1,0:T(8,128)}), f32[16,16,512]{2,1,0:T(8,128)S(1)}, u32[]{:S(2)}, u32[]{:S(2)}) async-start(f32[16,16,512]{2,1,0:T(8,128)} %bitcast.36), calls=%async_computation | async-start | bytes 1048576 | tf_op jit(solution)/shard_map/all_to_all | solution.py:373
  35.7 13.3 %all-to-all-start.1 = ((f32[8,2,16,512]{3,2,1,0:T(8,128)}), f32[8,2,16,512]{3,2,1,0:T(8,128)S(1)}, u32[]{:S(2)}, u32[]{:S(2)}) async-start(f32[8,2,16,512]{3,2,1,0:T(8,128)} %broadcast_in_dim.5), calls=%async_computation.1 | async-start | bytes 1048576 | tf_op jit(solution)/shard_map/all_to_all | solution.py:379
  48.9 2.5 %collective-permute-start = (f32[8,2,16,512]{3,2,1,0:T(8,128)S(1)}, f32[8,2,16,512]{3,2,1,0:T(8,128)S(1)}, u32[]{:S(2)}, u32[]{:S(2)}) collective-permute-start(f32[8,2,16,512]{3,2,1,0:T(8,128)S(1)} %all-to-all-done.1.rest_0_.rest_4_), channel_id=1, source_target_pairs={{0,1},{1,0},{2,3},{3,2},{4,5},{5,4},{6,7},{7,6},{8,9},{9,8},{10,11... | collective-permute-start | bytes 1572872 | tf_op jit(solution)/shard_map/ppermute | solution.py:370
  49.9 11.0 %collective-permute-start.3 = (f32[8,2,16,512]{3,2,1,0:T(8,128)S(1)}, f32[8,2,16,512]{3,2,1,0:T(8,128)S(1)}, u32[]{:S(2)}, u32[]{:S(2)}) collective-permute-start(f32[8,2,16,512]{3,2,1,0:T(8,128)S(1)} %all-to-all-done.1.rest_0_.rest_4_), channel_id=1, source_target_pairs={{0,48},{1,7},{2,50},{3,1},{4,52},{5,3},{6,54},{7,5},{8,56},{9,15},... | collective-permute-start | bytes 1572872 | tf_op jit(solution)/shard_map/ppermute | solution.py:370
  51.0 15.2 %collective-permute-start.2 = (f32[8,2,16,512]{3,2,1,0:T(8,128)S(1)}, f32[8,2,16,512]{3,2,1,0:T(8,128)S(1)}, u32[]{:S(2)}, u32[]{:S(2)}) collective-permute-start(f32[8,2,16,512]{3,2,1,0:T(8,128)S(1)} %all-to-all-done.1.rest_0_.rest_4_), channel_id=1, source_target_pairs={{0,16},{1,3},{2,18},{3,5},{4,20},{5,7},{6,22},{7,1},{8,24},{9,11},... | collective-permute-start | bytes 1572872 | tf_op jit(solution)/shard_map/ppermute | solution.py:370
  51.4 24.8 %collective-permute-start.1 = (f32[8,2,16,512]{3,2,1,0:T(8,128)S(1)}, f32[8,2,16,512]{3,2,1,0:T(8,128)S(1)}, u32[]{:S(2)}, u32[]{:S(2)}) collective-permute-start(f32[8,2,16,512]{3,2,1,0:T(8,128)S(1)} %all-to-all-done.1.rest_0_.rest_4_), channel_id=1, source_target_pairs={{0,32},{1,5},{2,34},{3,7},{4,36},{5,1},{6,38},{7,3},{8,40},{9,13},... | collective-permute-start | bytes 1572872 | tf_op jit(solution)/shard_map/ppermute | solution.py:370
  66.2 10.7 %copy-start = (s32[1,2]{1,0:T(1,128)S(1)}, s32[1,2]{1,0:T(1,128)}, u32[]{:S(2)}) copy-start(s32[1,2]{1,0:T(1,128)} %param.16) | copy-start | bytes 28
  66.2 11.4 %collective-permute-start.5 = (f32[8,2,16,512]{3,2,1,0:T(8,128)S(1)}, f32[8,2,16,512]{3,2,1,0:T(8,128)S(1)}, u32[]{:S(2)}, u32[]{:S(2)}) collective-permute-start(f32[8,2,16,512]{3,2,1,0:T(8,128)S(1)} %collective-permute-done.2.rest_0_.rest_6_), channel_id=1, source_target_pairs={{0,1},{1,0},{2,3},{3,2},{4,5},{5,4},{6,7},{7,6},{8,9},{9,8},{10,11... | collective-permute-start | bytes 1572872 | tf_op jit(solution)/shard_map/ppermute | solution.py:370
  68.3 9.3 %collective-permute-start.6 = (f32[8,2,16,512]{3,2,1,0:T(8,128)S(1)}, f32[8,2,16,512]{3,2,1,0:T(8,128)S(1)}, u32[]{:S(2)}, u32[]{:S(2)}) collective-permute-start(f32[8,2,16,512]{3,2,1,0:T(8,128)S(1)} %collective-permute-done.3.rest_1_.rest_7_), channel_id=1, source_target_pairs={{0,1},{1,0},{2,3},{3,2},{4,5},{5,4},{6,7},{7,6},{8,9},{9,8},{10,11... | collective-permute-start | bytes 1572872 | tf_op jit(solution)/shard_map/ppermute | solution.py:370
  76.3 2.1 %collective-permute-start.4 = (f32[8,2,16,512]{3,2,1,0:T(8,128)S(1)}, f32[8,2,16,512]{3,2,1,0:T(8,128)S(1)}, u32[]{:S(2)}, u32[]{:S(2)}) collective-permute-start(f32[8,2,16,512]{3,2,1,0:T(8,128)S(1)} %collective-permute-done.1.rest_8_.rest_0_), channel_id=1, source_target_pairs={{0,1},{1,0},{2,3},{3,2},{4,5},{5,4},{6,7},{7,6},{8,9},{9,8},{10,11... | collective-permute-start | bytes 1572872 | tf_op jit(solution)/shard_map/ppermute | solution.py:370
  82.4 12.5 %all-to-all-start.2 = ((f32[8,32,128]{2,1,0:T(8,128)}), f32[8,32,128]{2,1,0:T(8,128)S(1)}, u32[]{:S(2)}, u32[]{:S(2)}) async-start(f32[8,32,128]{2,1,0:T(8,128)} %bitcast.22), calls=%async_computation.2 | async-start | bytes 262144 | tf_op jit(solution)/shard_map/all_to_all | solution.py:413
  94.9 0.6 copy-start.2
  97.3 12.1 %all-to-all-start.3 = ((f32[16,40,128]{2,1,0:T(8,128)}), f32[16,40,128]{2,1,0:T(8,128)S(1)}, u32[]{:S(2)}, u32[]{:S(2)}) async-start(f32[16,40,128]{2,1,0:T(8,128)} %shard_map.118), calls=%async_computation.3 | async-start | bytes 655360 | tf_op jit(solution)/shard_map/all_to_all | solution.py:416
  109.3 0.7 copy-start.1

commit v4 on v3

--- a/solution.py
+++ b/solution.py
@@ -13,6 +13,7 @@
 BLOCK = 128
 TILE = 512
 VMEM = 24 * 1024 * 1024
+NEAREST = 12582912.0
 SIN = (4.442867755889893, -7.307443618774414, 3.594788074493408, -0.7843739986419678)
 COS = (1.4142135381698608, -6.978850841522217, 5.7394609451293945, -1.8835630416870117, 0.31069818139076233)
 
@@ -25,15 +26,22 @@
 
 
 def sincos(turns):
-    r = turns - jnp.round(turns)
+    r = turns - ((turns + NEAREST) - NEAREST)
     u = r * r
     s = r * poly(u, SIN)
     c = poly(u, COS)
     return s * c, 1.0 - s * s
 
 
+def rounded(parts):
+    return tuple(v.astype(jnp.bfloat16) for v in parts)
+
+
+def widened(parts):
+    return tuple(v.astype(jnp.float32) for v in parts)
+
+
 def quad(a, b, c, d):
-    a, b, c, d = (v.astype(jnp.bfloat16) for v in (a, b, c, d))
     return jnp.concatenate([jnp.concatenate([a, b], 1), jnp.concatenate([c, d], 1)], 0)
 
 
@@ -43,27 +51,31 @@
     out = [[None] * blocks for _ in range(freqs)]
     for f in range(freqs):
         for b in range(blocks):
-            sr, si, rr, ri = parts[f][b]
+            sr, si, rr, ri = widened(parts[f][b])
             sin, cos = sincos(phases[f][b])
-            out[f][b] = (sr * cos - si * sin, sr * sin + si * cos, rr * cos - ri * sin, rr * sin + ri * cos)
+            out[f][b] = rounded(
+                (sr * cos - si * sin, sr * sin + si * cos, rr * cos - ri * sin, rr * sin + ri * cos)
+            )
     for f in range(freqs):
         left = jnp.concatenate([quad(*out[f][b]) for b in range(blocks)], 0)
         prod = jnp.dot(left, wx[f], preferred_element_type=jnp.float32)
         for b in range(blocks):
             x = prod[b * 2 * height : (b + 1) * 2 * height]
-            sr, si, rr, ri = out[f][b]
-            out[f][b] = (
-                sr + x[:height, :width],
-                si + x[:height, width:],
-                rr + x[height:, :width],
-                ri + x[height:, width:],
+            sr, si, rr, ri = widened(out[f][b])
+            out[f][b] = rounded(
+                (
+                    sr + x[:height, :width],
+                    si + x[:height, width:],
+                    rr + x[height:, :width],
+                    ri + x[height:, width:],
+                )
             )
     for f in range(freqs):
         right = jnp.concatenate([quad(v[0], v[2], v[1], v[3]) for v in out[f]], 1)
         prod = jnp.dot(wy[f], right, preferred_element_type=jnp.float32)
         for b in range(blocks):
             y = prod[:, b * 2 * width : (b + 1) * 2 * width]
-            sr, si, rr, ri = out[f][b]
+            sr, si, rr, ri = widened(out[f][b])
             out[f][b] = (
                 sr + y[:height, :width],
                 si + y[height:, :width],
@@ -73,18 +85,10 @@
     return out
 
 
-def load_parts(src, rcv, cols):
-    f32 = jnp.float32
+def load_parts(src, rcv, starts):
+    at = [pl.ds(pl.multiple_of(c, BLOCK), BLOCK) for c in starts]
     return [
-        [
-            (
-                src[f, 0, 0, :, c].astype(f32),
-                src[f, 0, 1, :, c].astype(f32),
-                rcv[f, 0, 0, :, c].astype(f32),
-                -rcv[f, 0, 1, :, c].astype(f32),
-            )
-            for c in cols
-        ]
+        [(src[f, 0, 0, :, c], src[f, 0, 1, :, c], rcv[f, 0, 0, :, c], -rcv[f, 0, 1, :, c]) for c in at]
         for f in range(src.shape[0])
     ]
 
@@ -94,16 +98,16 @@
     return rows.reshape(rows.shape[0] * rows.shape[1], rows.shape[2])
 
 
-def march_body(where, turns, wx, wy, src, rcv, *rest, count, per):
+def march_body(where, turns, wx, wy, src, rcv, *rest, count):
     slabs, so, ro = rest[:count], rest[-2], rest[-1]
-    freqs, tile = src.shape[0], src.shape[-1]
+    freqs, tile = src.shape[0], so.shape[-1]
     cols = [slice(c, c + BLOCK) for c in range(0, tile, BLOCK)]
     i = pl.program_id(0)
 
-    def run(slab, offset):
-        parts = load_parts(src, rcv, cols)
+    def run(slab):
+        parts = load_parts(src, rcv, [where[i] * tile + c.start for c in cols])
         for d in range(slab.shape[1]):
-            views = [slab_view(slab, d, slice(offset + c.start, offset + c.stop)) for c in cols]
+            views = [slab_view(slab, d, c) for c in cols]
             parts = advance(parts, [[v * turns[f] for v in views] for f in range(freqs)], wx, wy)
         for f in range(freqs):
             for b, c in enumerate(cols):
@@ -114,29 +118,25 @@
                 ro[f, 0, 1, :, c] = (-ri).astype(ro.dtype)
 
     for k, slab in enumerate(slabs):
-        for part in range(per):
-
-            @pl.when(i == k * per + part)
-            def _():
-                run(slab, part * tile)
+
+        @pl.when(i == k)
+        def _():
+            run(slab)
 
 
 def march(where, turns, slabs, wx, wy, src, rcv, done=()):
     count, cols = len(slabs), slabs[0].shape[-1]
     freqs, height = src.shape[0], src.shape[3]
-    tile = min(cols, TILE)
-    per = cols // tile
-    field = pl.BlockSpec((freqs, 1, 2, height, tile), lambda i, w: (0, 0, 0, 0, w[lax.div(i, per)] * per + lax.rem(i, per)))
-    whole = lambda a: pl.BlockSpec(a.shape, lambda i, w: (0,) * a.ndim)
+    field = pl.BlockSpec((freqs, 1, 2, height, cols), lambda i, w: (0, 0, 0, 0, w[i]))
     args = [turns, wx, wy, src, rcv, *slabs]
-    in_specs = [pl.BlockSpec(memory_space=pltpu.SMEM), whole(wx), whole(wy), field, field] + [whole(s) for s in slabs]
+    in_specs = [pl.BlockSpec(memory_space=pltpu.SMEM)] + [pl.BlockSpec(memory_space=pltpu.VMEM)] * (len(args) - 1)
     alias = {len(args) + 1 + i: i for i in range(len(done))}
     cells = count * cols * height * freqs
     return pl.pallas_call(
-        functools.partial(march_body, count=count, per=per),
+        functools.partial(march_body, count=count),
         grid_spec=pltpu.PrefetchScalarGridSpec(
             num_scalar_prefetch=1,
-            grid=(count * per,),
+            grid=(count,),
             in_specs=in_specs + [pl.BlockSpec(memory_space=pl.ANY)] * len(done),
             out_specs=[field, field],
         ),
@@ -149,24 +149,19 @@
     )(where, *args, *done)
 
 
-def image_body(tiles, slot, turns, wx, wy, *rest, scale, per, aper, count):
-    fields, slabs = rest[: 2 * aper], rest[2 * aper : -4]
-    out, held, lines, sems = rest[-4:]
-    copies = []
+def image_body(tiles, slot, turns, wx, wy, src, rcv, *rest, scale, per, count):
+    slabs, out, held, lines = rest[:-3], rest[-3], rest[-2], rest[-1]
+    aper = tiles.shape[0]
     for a in range(aper):
         column = pl.multiple_of(lax.rem(lax.div(tiles[a], 2), per) * BLOCK, BLOCK)
         for k, slab in enumerate(slabs):
 
             @pl.when(slot[a] == k)
             def _():
-                pltpu.make_async_copy(slab.at[:, :, :, pl.ds(column, BLOCK)], held.at[a], sems.at[a]).start()
-
-    for a in range(aper):
-        pltpu.make_async_copy(slabs[0].at[:, :, :, pl.ds(0, BLOCK)], held.at[a], sems.at[a]).wait()
-    freqs = fields[0].shape[0]
-    cols = [slice(0, BLOCK)]
-    loaded = [load_parts(fields[2 * a], fields[2 * a + 1], cols) for a in range(aper)]
-    parts = [[loaded[a][f][0] for a in range(aper)] for f in range(freqs)]
+                held[a] = slab[:, :, :, pl.ds(column, BLOCK)]
+
+    freqs = src.shape[0]
+    parts = load_parts(src, rcv, [lax.div(tiles[a], 2) * BLOCK for a in range(aper)])
     half = BLOCK // 2
     for d in range(held.shape[2]):
         views = [slab_view(held.at[a], d, slice(0, BLOCK)) for a in range(aper)]
@@ -189,30 +184,22 @@
     steps, cols = slabs[0].shape[1], slabs[0].shape[-1]
     freqs, height = src.shape[0], src.shape[3]
     aper = tiles.shape[0]
-    whole = lambda a: pl.BlockSpec(a.shape, lambda i, t, s: (0,) * a.ndim)
-    field = lambda a: pl.BlockSpec((freqs, 1, 2, height, BLOCK), lambda i, t, s: (0, 0, 0, 0, lax.div(t[a], 2)))
     shape = (count, aper, steps, height // 2 // count, BLOCK)
     return pl.pallas_call(
-        functools.partial(image_body, scale=scale, per=cols // BLOCK, aper=aper, count=count),
-        grid_spec=pltpu.PrefetchScalarGridSpec(
-            num_scalar_prefetch=2,
-            grid=(1,),
-            in_specs=[pl.BlockSpec(memory_space=pltpu.SMEM), whole(wx), whole(wy)]
-            + [field(a) for a in range(aper) for _ in range(2)]
-            + [pl.BlockSpec(memory_space=pl.ANY)] * len(slabs),
-            out_specs=pl.BlockSpec(shape, lambda i, t, s: (0,) * len(shape)),
-            scratch_shapes=[
-                pltpu.VMEM((aper,) + slabs[0].shape[:3] + (BLOCK,), jnp.float32),
-                pltpu.VMEM((aper, height, BLOCK), jnp.float32),
-                pltpu.SemaphoreType.DMA((aper,)),
-            ],
-        ),
+        functools.partial(image_body, scale=scale, per=cols // BLOCK, count=count),
+        in_specs=[pl.BlockSpec(memory_space=pltpu.SMEM)] * 3
+        + [pl.BlockSpec(memory_space=pltpu.VMEM)] * (4 + len(slabs)),
+        out_specs=pl.BlockSpec(memory_space=pltpu.VMEM),
         out_shape=jax.ShapeDtypeStruct(shape, jnp.float32),
+        scratch_shapes=[
+            pltpu.VMEM((aper,) + slabs[0].shape[:3] + (BLOCK,), jnp.float32),
+            pltpu.VMEM((aper, height, BLOCK), jnp.float32),
+        ],
         cost_estimate=pl.CostEstimate(
             flops=aper * BLOCK * height * freqs * steps * 4 * 2 * 4 * BLOCK * 3, bytes_accessed=1 << 21, transcendentals=0
         ),
         compiler_params=pltpu.CompilerParams(vmem_limit_bytes=VMEM),
-    )(tiles, slot, turns, wx, wy, *[v for _ in range(aper) for v in (src, rcv)], *slabs)
+    )(tiles, slot, turns, wx, wy, src, rcv, *slabs)
 
 
 def deal_body(tiles, parts, out):
@@ -279,13 +266,39 @@
 
 def cut(y, slab, cols):
     zls, xs, rows, _ = slab.shape
+    slab = pltpu.with_memory_space_constraint(slab, pltpu.HBM)
     return pl.pallas_call(
         functools.partial(cut_body, cols=cols),
         in_specs=[pl.BlockSpec(memory_space=pltpu.SMEM), pl.BlockSpec(memory_space=pltpu.HBM)],
-        out_specs=pl.BlockSpec(memory_space=pltpu.HBM),
+        out_specs=pl.BlockSpec(memory_space=pltpu.VMEM),
         out_shape=jax.ShapeDtypeStruct((zls, xs, CORES, rows, cols), slab.dtype),
         scratch_shapes=[pltpu.SemaphoreType.DMA((xs + 1,))],
     )(y, slab)
+
+
+def stage_body(*refs):
+    count = len(refs) // 2
+    sems = refs[-1]
+    copies = [pltpu.make_async_copy(refs[i], refs[count + i], sems.at[i]) for i in range(count)]
+    for c in copies:
+        c.start()
+    for c in copies:
+        c.wait()
+
+
+def stage(*arrays):
+    arrays = [pltpu.with_memory_space_constraint(a, pltpu.HBM) for a in arrays]
+    return pl.pallas_call(
+        stage_body,
+        in_specs=[pl.BlockSpec(memory_space=pltpu.HBM)] * len(arrays),
+        out_specs=[pl.BlockSpec(memory_space=pltpu.VMEM)] * len(arrays),
+        out_shape=[pltpu.VMEM(a.shape, a.dtype) for a in arrays],
+        scratch_shapes=[pltpu.SemaphoreType.DMA((len(arrays),))],
+        cost_estimate=pl.CostEstimate(
+            flops=0, bytes_accessed=sum(2 * a.size * a.dtype.itemsize for a in arrays), transcendentals=0
+        ),
+        compiler_params=pltpu.CompilerParams(vmem_limit_bytes=VMEM),
+    )(*arrays)
 
 
 def sweep_weights(xc, yc):
@@ -386,18 +399,16 @@
     partner_place = lambda k: (1 - core) * XS + lax.rem(partner_column + XS - k, XS)
     wx, wy = sweep_weights(x_correction, y_correction)
     turns = angular_freq * (0.5 / math.pi)
-    src = pltpu.with_memory_space_constraint(source_field, pltpu.HBM)
-    rcv = pltpu.with_memory_space_constraint(receiver_field, pltpu.HBM)
+    src, rcv = stage(source_field, receiver_field)
 
     def forward(places, slabs, done=()):
         return march(jnp.stack(places).astype(jnp.int32), turns, slabs, wx, wy, src, rcv, tuple(done))
 
     own_p = send(own, swap)
     s1, s3 = send(own, shift(1)), send(own, shift(3))
-    later, own_p = lax.optimization_barrier((own, own_p))
+    fields = forward([place(0), partner_place(0)], [own, own_p])
+    s1, s3, later, *fields = lax.optimization_barrier((s1, s3, own, *fields))
     s2 = send(later, shift(2))
-    fields = forward([place(0), partner_place(0)], [own, own_p])
-    s1, s3, *fields = lax.optimization_barrier((s1, s3, *fields))
     s1_p, s3_p = send(s1, swap), send(s3, swap)
     fields = forward([place(1), place(3)], [s1, s3], fields)
     s2, *fields = lax.optimization_barrier((s2, *fields))

time: 113 us -> 104 us (0.920)
  local copies, waits for them, and re-layouts: 5.5 us -> 22.5 us
  Pallas kernels: 56.4 us -> 40.3 us
  waiting for transfers between devices: 16.9 us -> 4.51 us
  starting transfers between devices: 27.2 us -> 30.3 us
    unnamed x14 -> x30, local copies, waits for them, and re-layouts: 1.62 us -> 18.8 us
    pallas_call x1, Pallas kernels: 17 us -> 1.86 us  [cut(): pl.pallas_call(functools.partial(cut_body, cols=cols), in_specs=[pl.Block...]
    all_to_all x1, waiting for transfers between devices: 7.35 us -> 0.01 us  [local(): own = lax.all_to_all(own, AXES, 0, 0, axis_index_groups=groups, tiled=True)]
    ppermute x7, waiting for transfers between devices: 6.12 us -> 0.98 us  [local(): lax.ppermute(v, AXES, pairs((freqs_dev, shots), move))]
    all_to_all x1, starting transfers between devices: 4.59 us -> 5.93 us  [local(): lax.all_to_all(terms.reshape(freqs_dev, -1, BLOCK), 'freq', 0, 0, tiled=T...]
    pallas_call x4 -> x5, Pallas kernels: 31.8 us -> 32 us  [the longest x4 28.5 us: march(): pl.pallas_call(functools.partial(march_body, count=count), grid_spec=pltp...]
  transfers between devices with their start and end apart: 11 -> 11, of which waited for: 4 -> 3; matrix products, arithmetic and copies ran while one was open for 4% -> 4% of each run, Pallas kernels for 28% -> 31%
where the time goes in v4:
time: 104 us
  Pallas kernels  40.3 us (39%)
  starting transfers between devices  30.3 us (29%)
  local copies, waits for them, and re-layouts  22.5 us (22%)
  between operations  4.81 us (5%)
  waiting for transfers between devices  4.51 us (4%)
  other arithmetic  1.09 us (1%)
    pallas_call x4, Pallas kernels, march(): pl.pallas_call(functools.partial(march_body, count=count), grid_spec=pltp...  28.5 us
    unnamed x30, local copies, waits for them, and re-layouts  18.8 us
    ppermute x7, starting transfers between devices, local(): lax.ppermute(v, AXES, pairs((freqs_dev, shots), move))  7.43 us
    all_to_all x1, starting transfers between devices, local(): arrived = lax.all_to_all(outgoing, 'shot', 0, 0, tiled=True)  7.18 us
    all_to_all x1, starting transfers between devices, local(): lax.all_to_all(terms.reshape(freqs_dev, -1, BLOCK), 'freq', 0, 0, tiled=T...  5.93 us
    all_to_all x1, starting transfers between devices, local(): dealt = lax.all_to_all(deal(tiles, terms, shots), 'shot', 0, 0, tiled=True)  4.91 us
    all_to_all x1, starting transfers between devices, local(): own = lax.all_to_all(own, AXES, 0, 0, axis_index_groups=groups, tiled=True)  4.81 us
    all_to_all x1, waiting for transfers between devices, local(): arrived = lax.all_to_all(outgoing, 'shot', 0, 0, tiled=True)  3.52 us
  transfers between devices with their start and end apart: 11, of which 3 were waited for; matrix products, arithmetic and copies ran while one was open for 4% of the time, Pallas kernels for 31%

profile of v4, /device:TPU:1, one launch (start us, length us, event | category | flops | bytes accessed | tf_op | source)
XLA Modules:
  0.0 103.5 jit_solution(7927064304109940290)
XLA Ops:
  0.6 1.9 %shard_map.113 = f32[2,4,2,16,512]{4,3,2,1,0:T(8,128)} custom-call(s32[1]{0:T(128)} %bitcast.10.spot, f32[2,4,16,4096]{3,2,1,0:T(8,128)} %bitcast.35), custom_call_target="tpu_custom_call" | custom-call | tf_op jit(solution)/shard_map/pallas_call | solution.py:270
  2.5 7.2 %all-to-all-start = ((f32[16,16,512]{2,1,0:T(8,128)}), f32[16,16,512]{2,1,0:T(8,128)S(1)}, u32[]{:S(2)}, u32[]{:S(2)}) async-start(f32[16,16,512]{2,1,0:T(8,128)} %bitcast.36), calls=%async_computation | async-start | bytes 1048576 | tf_op jit(solution)/shard_map/all_to_all | solution.py:386
  9.7 1.3 %fusion.3 = (s32[1]{0:T(128)}, s32[1]{0:T(128)}) fusion(s32[2]{0:T(128)} %param.15), kind=kLoop, calls=%fused_computation.19 | loop fusion | bytes 16 | tf_op jit(solution)/shard_map/slice | solution.py:387
  15.0 0.1 pad_add_fusion.where
  15.1 0.1 pad_add_fusion.1.where
  15.2 0.9 fusion.2
  16.1 3.5 %all-to-all-done = f32[16,16,512]{2,1,0:T(8,128)S(1)} async-done(((f32[16,16,512]{2,1,0:T(8,128)}), f32[16,16,512]{2,1,0:T(8,128)S(1)}, u32[]{:S(2)}, u32[]{:S(2)}) %all-to-all-start) | async-done | bytes 524320 | tf_op jit(solution)/shard_map/all_to_all | solution.py:386
  19.6 0.9 broadcast_in_dim.5
  20.4 4.8 %all-to-all-start.1 = ((f32[8,2,16,512]{3,2,1,0:T(8,128)}), f32[8,2,16,512]{3,2,1,0:T(8,128)S(1)}, u32[]{:S(2)}, u32[]{:S(2)}) async-start(f32[8,2,16,512]{3,2,1,0:T(8,128)} %broadcast_in_dim.5), calls=%async_computation.1 | async-start | bytes 1048576 | tf_op jit(solution)/shard_map/all_to_all | solution.py:392
  25.3 0.1 pad_add_fusion.2.where
  25.3 0.1 copy.28
  25.5 0.1 copy.29
  25.6 0.0 copy-start.12
  25.6 0.0 copy-start.11
  25.6 0.0 copy-start.13
  25.6 3.5 %shard_map.112 = (bf16[2,1,2,128,4096]{4,3,2,1,0:T(8,128)(2,1)S(1)}, bf16[2,1,2,128,4096]{4,3,2,1,0:T(8,128)(2,1)S(1)}) custom-call(bf16[2,1,2,128,4096]{4,3,2,1,0:T(8,128)(2,1)} %refs_0_.1, bf16[2,1,2,128,4096]{4,3,2,1,0:T(8,128)(2,1)} %refs_1_.1), custom_call_target="tpu_custom_call" | custom-call | bytes 16777216 | tf_op jit(solution)/shard_map/pallas_call | solution.py:291
  29.2 0.0 copy-start
  29.2 1.9 %copy-done = bf16[2,1,2,128,4096]{4,3,2,1,0:T(8,128)(2,1)} copy-done((bf16[2,1,2,128,4096]{4,3,2,1,0:T(8,128)(2,1)}, bf16[2,1,2,128,4096]{4,3,2,1,0:T(8,128)(2,1)S(1)}, u32[]{:S(2)}) %copy-start) | copy-done | bytes 4194328
  31.1 0.0 copy-start.4
  31.1 2.0 %copy-done.4 = bf16[2,1,2,128,4096]{4,3,2,1,0:T(8,128)(2,1)} copy-done((bf16[2,1,2,128,4096]{4,3,2,1,0:T(8,128)(2,1)}, bf16[2,1,2,128,4096]{4,3,2,1,0:T(8,128)(2,1)S(1)}, u32[]{:S(2)}) %copy-start.4) | copy-done | bytes 4194328
  33.1 0.1 stack.64
  33.2 0.0 copy-done.12
  33.2 0.6 dynamic_slice.12.entries
  33.8 0.0 copy-done.11
  33.9 0.0 all-to-all-done.1.rest_0_
  33.9 0.7 collective-permute-start.2
  34.6 0.1 maximum_maximum_fusion
  34.7 0.0 copy-done.13
  34.7 0.8 collective-permute-start
  35.5 1.9 %collective-permute-start.1 = (f32[8,2,16,512]{3,2,1,0:T(8,128)S(1)}, f32[8,2,16,512]{3,2,1,0:T(8,128)S(1)}, u32[]{:S(2)}, u32[]{:S(2)}) collective-permute-start(f32[8,2,16,512]{3,2,1,0:T(8,128)S(1)} %all-to-all-done.1.rest_0_), channel_id=1, source_target_pairs={{0,48},{1,7},{2,50},{3,1},{4,52},{5,3},{6,54},{7,5},{8,56},{9,15},... | collective-permute-start | bytes 1572872 | tf_op jit(solution)/shard_map/ppermute | solution.py:383
  37.4 0.0 collective-permute-done.2.rest_1_
  37.4 2.2 %copy-done.1 = bf16[2,1,2,128,4096]{4,3,2,1,0:T(8,128)(2,1)S(1)} copy-done((bf16[2,1,2,128,4096]{4,3,2,1,0:T(8,128)(2,1)S(1)}, bf16[2,1,2,128,4096]{4,3,2,1,0:T(8,128)(2,1)}, u32[]{:S(2)}) %copy-start.1) | copy-done | bytes 4194328
  39.6 2.2 %copy-done.5 = bf16[2,1,2,128,4096]{4,3,2,1,0:T(8,128)(2,1)S(1)} copy-done((bf16[2,1,2,128,4096]{4,3,2,1,0:T(8,128)(2,1)S(1)}, bf16[2,1,2,128,4096]{4,3,2,1,0:T(8,128)(2,1)}, u32[]{:S(2)}) %copy-start.5) | copy-done | bytes 4194328
  41.8 7.1 %shard_map.114 = (bf16[2,1,2,128,4096]{4,3,2,1,0:T(8,128)(2,1)}, bf16[2,1,2,128,4096]{4,3,2,1,0:T(8,128)(2,1)}) custom-call(s32[2]{0:T(128)S(1)} %pad_add_fusion.1.where, f32[2]{0:T(128)S(1)} %broadcast_multiply_fusion.turns, bf16[2,256,256]{2,1,0:T(8,128)(2,1)S(1)} %get-tuple-element.55.wx, bf16[2,256,256]{2,1,0:T(8,128)(2,1)S(1)} %get-tuple-element.56.wy, ...), custom_call_target="tpu_custom_call" | custom-call | flops 6442450944 | bytes 4194304 | tf_op jit(solution)/shard_map/pallas_call | solution.py:135
  48.9 0.0 collective-permute-done.rest_0_.rest_2_
  48.9 0.0 collective-permute-done.1.rest_1_.rest_3_
  48.9 0.0 copy-start.8
  48.9 1.2 %collective-permute-start.3 = (f32[8,2,16,512]{3,2,1,0:T(8,128)S(1)}, f32[8,2,16,512]{3,2,1,0:T(8,128)S(1)}, u32[]{:S(2)}, u32[]{:S(2)}) collective-permute-start(f32[8,2,16,512]{3,2,1,0:T(8,128)S(1)} %all-to-all-done.1.rest_0_), channel_id=1, source_target_pairs={{0,32},{1,5},{2,34},{3,7},{4,36},{5,1},{6,38},{7,3},{8,40},{9,13},... | collective-permute-start | bytes 1572872 | tf_op jit(solution)/shard_map/ppermute | solution.py:383
  50.1 1.4 %collective-permute-start.5 = (f32[8,2,16,512]{3,2,1,0:T(8,128)S(1)}, f32[8,2,16,512]{3,2,1,0:T(8,128)S(1)}, u32[]{:S(2)}, u32[]{:S(2)}) collective-permute-start(f32[8,2,16,512]{3,2,1,0:T(8,128)S(1)} %collective-permute-done.rest_0_.rest_2_), channel_id=1, source_target_pairs={{0,1},{1,0},{2,3},{3,2},{4,5},{5,4},{6,7},{7,6},{8,9},{9,8},{10,11... | collective-permute-start | bytes 1572872 | tf_op jit(solution)/shard_map/ppermute | solution.py:383
  51.5 0.0 collective-permute-start.6
  51.5 7.1 %shard_map.115 = (bf16[2,1,2,128,4096]{4,3,2,1,0:T(8,128)(2,1)}, bf16[2,1,2,128,4096]{4,3,2,1,0:T(8,128)(2,1)}) custom-call(s32[2]{0:T(128)S(1)} %pad_add_fusion.2.where, f32[2]{0:T(128)S(1)} %broadcast_multiply_fusion.turns, bf16[2,256,256]{2,1,0:T(8,128)(2,1)S(1)} %get-tuple-element.55.wx, ...), custom_call_target="tpu_custom_call", output_to_operand_aliasing={{0}: (8, {}), {1}: (9, {})} | custom-call | flops 6442450944 | bytes 4194304 | tf_op jit(solution)/shard_map/pallas_call | solution.py:135
  58.6 0.2 collective-permute-done.3.rest_4_.rest_0_
  58.9 1.4 %collective-permute-start.4 = (f32[8,2,16,512]{3,2,1,0:T(8,128)S(1)}, f32[8,2,16,512]{3,2,1,0:T(8,128)S(1)}, u32[]{:S(2)}, u32[]{:S(2)}) collective-permute-start(f32[8,2,16,512]{3,2,1,0:T(8,128)S(1)} %collective-permute-done.3.rest_4_.rest_0_), channel_id=1, source_target_pairs={{0,1},{1,0},{2,3},{3,2},{4,5},{5,4},{6,7},{7,6},{8,9},{9,8},{10,11... | collective-permute-start | bytes 1572872 | tf_op jit(solution)/shard_map/ppermute | solution.py:383
  60.3 0.1 pad_add_fusion.3.where
  60.4 0.0 copy-done.8
  60.4 0.7 compare_reduce_fusion
  61.1 0.0 collective-permute-done.5.rest_5_.rest_0_
  61.1 0.0 collective-permute-done.6.rest_6_.rest_1_
  61.1 0.7 collective-permute-done.4.rest_7_.rest_1_
  61.8 3.0 %shard_map.116 = f32[8,2,2,8,128]{4,3,2,1,0:T(8,128)} custom-call(s32[2]{0:T(128)S(1)} %bitcast.34, s32[2]{0:T(128)S(1)} %get-tuple-element.37.slot, f32[2]{0:T(128)S(1)} %broadcast_multiply_fusion.turns, bf16[2,256,256]{2,1,0:T(8,128)(2,1)S(1)} %get-tuple-element.55.wx, bf16[2,256,256]{2,1,0:T(8,128)(2,1)S(1)} %get-tuple-element.56.wy, ...), custom_call_target="tpu_custom_call" | custom-call | flops 1610612736 | bytes 2097152 | tf_op jit(solution)/shard_map/pallas_call | solution.py:188
  64.8 5.9 %all-to-all-start.2 = ((f32[8,32,128]{2,1,0:T(8,128)}), f32[8,32,128]{2,1,0:T(8,128)S(1)}, u32[]{:S(2)}, u32[]{:S(2)}) async-start(f32[8,32,128]{2,1,0:T(8,128)} %bitcast.22), calls=%async_computation.2 | async-start | bytes 262144 | tf_op jit(solution)/shard_map/all_to_all | solution.py:424
  70.7 2.2 %copy-done.2 = bf16[2,1,2,128,4096]{4,3,2,1,0:T(8,128)(2,1)S(1)} copy-done((bf16[2,1,2,128,4096]{4,3,2,1,0:T(8,128)(2,1)S(1)}, bf16[2,1,2,128,4096]{4,3,2,1,0:T(8,128)(2,1)}, u32[]{:S(2)}) %copy-start.2) | copy-done | bytes 4194328
  72.9 2.2 %copy-done.6 = bf16[2,1,2,128,4096]{4,3,2,1,0:T(8,128)(2,1)S(1)} copy-done((bf16[2,1,2,128,4096]{4,3,2,1,0:T(8,128)(2,1)S(1)}, bf16[2,1,2,128,4096]{4,3,2,1,0:T(8,128)(2,1)}, u32[]{:S(2)}) %copy-start.6) | copy-done | bytes 4194328
  75.1 7.1 %shard_map.117 = (bf16[2,1,2,128,4096]{4,3,2,1,0:T(8,128)(2,1)}, bf16[2,1,2,128,4096]{4,3,2,1,0:T(8,128)(2,1)}) custom-call(s32[2]{0:T(128)S(1)} %pad_add_fusion.3.where, f32[2]{0:T(128)S(1)} %broadcast_multiply_fusion.turns, bf16[2,256,256]{2,1,0:T(8,128)(2,1)S(1)} %get-tuple-element.55.wx, ...), custom_call_target="tpu_custom_call", output_to_operand_aliasing={{0}: (8, {}), {1}: (9, {})} | custom-call | flops 6442450944 | bytes 4194304 | tf_op jit(solution)/shard_map/pallas_call | solution.py:135
  82.2 0.0 all-to-all-done.2.parts
  82.2 0.7 copy-done.10
  82.9 1.7 %shard_map.119 = f32[16,40,128]{2,1,0:T(8,128)} custom-call(s32[2]{0:T(128)} %bitcast.33, f32[8,32,128]{2,1,0:T(8,128)} %copy-done.10), custom_call_target="tpu_custom_call" | custom-call | tf_op jit(solution)/shard_map/pallas_call | solution.py:216
  84.6 4.9 %all-to-all-start.3 = ((f32[16,40,128]{2,1,0:T(8,128)}), f32[16,40,128]{2,1,0:T(8,128)S(1)}, u32[]{:S(2)}, u32[]{:S(2)}) async-start(f32[16,40,128]{2,1,0:T(8,128)} %shard_map.119), calls=%async_computation.3 | async-start | bytes 655360 | tf_op jit(solution)/shard_map/all_to_all | solution.py:427
  89.5 2.2 %copy-done.3 = bf16[2,1,2,128,4096]{4,3,2,1,0:T(8,128)(2,1)S(1)} copy-done((bf16[2,1,2,128,4096]{4,3,2,1,0:T(8,128)(2,1)S(1)}, bf16[2,1,2,128,4096]{4,3,2,1,0:T(8,128)(2,1)}, u32[]{:S(2)}) %copy-start.3) | copy-done | bytes 4194328
  91.7 2.2 %copy-done.7 = bf16[2,1,2,128,4096]{4,3,2,1,0:T(8,128)(2,1)S(1)} copy-done((bf16[2,1,2,128,4096]{4,3,2,1,0:T(8,128)(2,1)S(1)}, bf16[2,1,2,128,4096]{4,3,2,1,0:T(8,128)(2,1)}, u32[]{:S(2)}) %copy-start.7) | copy-done | bytes 4194328
  93.9 7.1 %shard_map.118 = (bf16[2,1,2,128,4096]{4,3,2,1,0:T(8,128)(2,1)}, bf16[2,1,2,128,4096]{4,3,2,1,0:T(8,128)(2,1)}) custom-call(s32[2]{0:T(128)S(1)} %pad_add_fusion.where, f32[2]{0:T(128)S(1)} %broadcast_multiply_fusion.turns, bf16[2,256,256]{2,1,0:T(8,128)(2,1)S(1)} %get-tuple-element.55.wx, ...), custom_call_target="tpu_custom_call", output_to_operand_aliasing={{0}: (8, {}), {1}: (9, {})} | custom-call | flops 6442450944 | bytes 4194304 | tf_op jit(solution)/shard_map/pallas_call | solution.py:135
  101.0 0.0 all-to-all-done.3.parts
  101.0 0.7 copy-done.9
  101.7 1.8 %shard_map.120 = f32[4,2,1024]{2,1,0:T(2,128)} custom-call(s32[4]{0:T(128)} %dynamic_slice.12.entries, f32[16,40,128]{2,1,0:T(8,128)} %copy-done.9), custom_call_target="tpu_custom_call" | custom-call | tf_op jit(solution)/shard_map/pallas_call | solution.py:241
  (15 shorter events, 0.1 us)
Async XLA Ops:
  2.5 17.1 %all-to-all-start = ((f32[16,16,512]{2,1,0:T(8,128)}), f32[16,16,512]{2,1,0:T(8,128)S(1)}, u32[]{:S(2)}, u32[]{:S(2)}) async-start(f32[16,16,512]{2,1,0:T(8,128)} %bitcast.36), calls=%async_computation | async-start | bytes 1048576 | tf_op jit(solution)/shard_map/all_to_all | solution.py:386
  20.4 13.4 %all-to-all-start.1 = ((f32[8,2,16,512]{3,2,1,0:T(8,128)}), f32[8,2,16,512]{3,2,1,0:T(8,128)S(1)}, u32[]{:S(2)}, u32[]{:S(2)}) async-start(f32[8,2,16,512]{3,2,1,0:T(8,128)} %broadcast_in_dim.5), calls=%async_computation.1 | async-start | bytes 1048576 | tf_op jit(solution)/shard_map/all_to_all | solution.py:392
  25.6 7.6 %copy-start.12 = (s32[64]{0:T(128)S(1)}, s32[64]{0:T(128)}, u32[]{:S(2)}) copy-start(s32[64]{0:T(128)} %param.17) | copy-start | bytes 772
  25.6 8.2 %copy-start.11 = (bf16[2,2,128,128]{3,2,1,0:T(8,128)(2,1)S(1)}, bf16[2,2,128,128]{3,2,1,0:T(8,128)(2,1)}, u32[]{:S(2)}) copy-start(bf16[2,2,128,128]{3,2,1,0:T(8,128)(2,1)} %param.12) | copy-start | bytes 393220
  25.6 9.0 %copy-start.13 = (f32[2]{0:T(128)S(1)}, f32[2]{0:T(128)}, u32[]{:S(2)}) copy-start(f32[2]{0:T(128)} %param.11) | copy-start | bytes 28
  29.2 1.9 %copy-start = (bf16[2,1,2,128,4096]{4,3,2,1,0:T(8,128)(2,1)}, bf16[2,1,2,128,4096]{4,3,2,1,0:T(8,128)(2,1)S(1)}, u32[]{:S(2)}) copy-start(bf16[2,1,2,128,4096]{4,3,2,1,0:T(8,128)(2,1)S(1)} %get-tuple-element.25.src) | copy-start | bytes 12582916
  31.1 2.0 %copy-start.4 = (bf16[2,1,2,128,4096]{4,3,2,1,0:T(8,128)(2,1)}, bf16[2,1,2,128,4096]{4,3,2,1,0:T(8,128)(2,1)S(1)}, u32[]{:S(2)}) copy-start(bf16[2,1,2,128,4096]{4,3,2,1,0:T(8,128)(2,1)S(1)} %get-tuple-element.26.rcv) | copy-start | bytes 12582916
  33.9 3.6 %collective-permute-start.2 = (f32[8,2,16,512]{3,2,1,0:T(8,128)S(1)}, f32[8,2,16,512]{3,2,1,0:T(8,128)S(1)}, u32[]{:S(2)}, u32[]{:S(2)}) collective-permute-start(f32[8,2,16,512]{3,2,1,0:T(8,128)S(1)} %all-to-all-done.1.rest_0_), channel_id=1, source_target_pairs={{0,1},{1,0},{2,3},{3,2},{4,5},{5,4},{6,7},{7,6},{8,9},{9,8},{10,11... | collective-permute-start | bytes 1572872 | tf_op jit(solution)/shard_map/ppermute | solution.py:383
  34.7 14.2 %collective-permute-start = (f32[8,2,16,512]{3,2,1,0:T(8,128)S(1)}, f32[8,2,16,512]{3,2,1,0:T(8,128)S(1)}, u32[]{:S(2)}, u32[]{:S(2)}) collective-permute-start(f32[8,2,16,512]{3,2,1,0:T(8,128)S(1)} %all-to-all-done.1.rest_0_), channel_id=1, source_target_pairs={{0,16},{1,3},{2,18},{3,5},{4,20},{5,7},{6,22},{7,1},{8,24},{9,11},... | collective-permute-start | bytes 1572872 | tf_op jit(solution)/shard_map/ppermute | solution.py:383
  35.5 13.4 %collective-permute-start.1 = (f32[8,2,16,512]{3,2,1,0:T(8,128)S(1)}, f32[8,2,16,512]{3,2,1,0:T(8,128)S(1)}, u32[]{:S(2)}, u32[]{:S(2)}) collective-permute-start(f32[8,2,16,512]{3,2,1,0:T(8,128)S(1)} %all-to-all-done.1.rest_0_), channel_id=1, source_target_pairs={{0,48},{1,7},{2,50},{3,1},{4,52},{5,3},{6,54},{7,5},{8,56},{9,15},... | collective-permute-start | bytes 1572872 | tf_op jit(solution)/shard_map/ppermute | solution.py:383
  37.4 2.2 %copy-start.1 = (bf16[2,1,2,128,4096]{4,3,2,1,0:T(8,128)(2,1)S(1)}, bf16[2,1,2,128,4096]{4,3,2,1,0:T(8,128)(2,1)}, u32[]{:S(2)}) copy-start(bf16[2,1,2,128,4096]{4,3,2,1,0:T(8,128)(2,1)} %copy-done) | copy-start | bytes 12582916
  39.6 2.2 %copy-start.5 = (bf16[2,1,2,128,4096]{4,3,2,1,0:T(8,128)(2,1)S(1)}, bf16[2,1,2,128,4096]{4,3,2,1,0:T(8,128)(2,1)}, u32[]{:S(2)}) copy-start(bf16[2,1,2,128,4096]{4,3,2,1,0:T(8,128)(2,1)} %copy-done.4) | copy-start | bytes 12582916
  48.9 11.4 %copy-start.8 = (s32[1,2]{1,0:T(1,128)S(1)}, s32[1,2]{1,0:T(1,128)}, u32[]{:S(2)}) copy-start(s32[1,2]{1,0:T(1,128)} %param.16) | copy-start | bytes 28
  48.9 9.9 %collective-permute-start.3 = (f32[8,2,16,512]{3,2,1,0:T(8,128)S(1)}, f32[8,2,16,512]{3,2,1,0:T(8,128)S(1)}, u32[]{:S(2)}, u32[]{:S(2)}) collective-permute-start(f32[8,2,16,512]{3,2,1,0:T(8,128)S(1)} %all-to-all-done.1.rest_0_), channel_id=1, source_target_pairs={{0,32},{1,5},{2,34},{3,7},{4,36},{5,1},{6,38},{7,3},{8,40},{9,13},... | collective-permute-start | bytes 1572872 | tf_op jit(solution)/shard_map/ppermute | solution.py:383
  50.1 11.0 %collective-permute-start.5 = (f32[8,2,16,512]{3,2,1,0:T(8,128)S(1)}, f32[8,2,16,512]{3,2,1,0:T(8,128)S(1)}, u32[]{:S(2)}, u32[]{:S(2)}) collective-permute-start(f32[8,2,16,512]{3,2,1,0:T(8,128)S(1)} %collective-permute-done.rest_0_.rest_2_), channel_id=1, source_target_pairs={{0,1},{1,0},{2,3},{3,2},{4,5},{5,4},{6,7},{7,6},{8,9},{9,8},{10,11... | collective-permute-start | bytes 1572872 | tf_op jit(solution)/shard_map/ppermute | solution.py:383
  51.5 9.6 %collective-permute-start.6 = (f32[8,2,16,512]{3,2,1,0:T(8,128)S(1)}, f32[8,2,16,512]{3,2,1,0:T(8,128)S(1)}, u32[]{:S(2)}, u32[]{:S(2)}) collective-permute-start(f32[8,2,16,512]{3,2,1,0:T(8,128)S(1)} %collective-permute-done.1.rest_1_.rest_3_), channel_id=1, source_target_pairs={{0,1},{1,0},{2,3},{3,2},{4,5},{5,4},{6,7},{7,6},{8,9},{9,8},{10,11... | collective-permute-start | bytes 1572872 | tf_op jit(solution)/shard_map/ppermute | solution.py:383
  58.9 3.0 %collective-permute-start.4 = (f32[8,2,16,512]{3,2,1,0:T(8,128)S(1)}, f32[8,2,16,512]{3,2,1,0:T(8,128)S(1)}, u32[]{:S(2)}, u32[]{:S(2)}) collective-permute-start(f32[8,2,16,512]{3,2,1,0:T(8,128)S(1)} %collective-permute-done.3.rest_4_.rest_0_), channel_id=1, source_target_pairs={{0,1},{1,0},{2,3},{3,2},{4,5},{5,4},{6,7},{7,6},{8,9},{9,8},{10,11... | collective-permute-start | bytes 1572872 | tf_op jit(solution)/shard_map/ppermute | solution.py:383
  64.8 17.4 %all-to-all-start.2 = ((f32[8,32,128]{2,1,0:T(8,128)}), f32[8,32,128]{2,1,0:T(8,128)S(1)}, u32[]{:S(2)}, u32[]{:S(2)}) async-start(f32[8,32,128]{2,1,0:T(8,128)} %bitcast.22), calls=%async_computation.2 | async-start | bytes 262144 | tf_op jit(solution)/shard_map/all_to_all | solution.py:424
  70.7 2.2 %copy-start.2 = (bf16[2,1,2,128,4096]{4,3,2,1,0:T(8,128)(2,1)S(1)}, bf16[2,1,2,128,4096]{4,3,2,1,0:T(8,128)(2,1)}, u32[]{:S(2)}) copy-start(bf16[2,1,2,128,4096]{4,3,2,1,0:T(8,128)(2,1)} %copy-done) | copy-start | bytes 12582916
  72.9 2.2 %copy-start.6 = (bf16[2,1,2,128,4096]{4,3,2,1,0:T(8,128)(2,1)S(1)}, bf16[2,1,2,128,4096]{4,3,2,1,0:T(8,128)(2,1)}, u32[]{:S(2)}) copy-start(bf16[2,1,2,128,4096]{4,3,2,1,0:T(8,128)(2,1)} %copy-done.4) | copy-start | bytes 12582916
  82.2 0.7 copy-start.10
  84.6 16.4 %all-to-all-start.3 = ((f32[16,40,128]{2,1,0:T(8,128)}), f32[16,40,128]{2,1,0:T(8,128)S(1)}, u32[]{:S(2)}, u32[]{:S(2)}) async-start(f32[16,40,128]{2,1,0:T(8,128)} %shard_map.119), calls=%async_computation.3 | async-start | bytes 655360 | tf_op jit(solution)/shard_map/all_to_all | solution.py:427
  89.5 2.2 %copy-start.3 = (bf16[2,1,2,128,4096]{4,3,2,1,0:T(8,128)(2,1)S(1)}, bf16[2,1,2,128,4096]{4,3,2,1,0:T(8,128)(2,1)}, u32[]{:S(2)}) copy-start(bf16[2,1,2,128,4096]{4,3,2,1,0:T(8,128)(2,1)} %copy-done) | copy-start | bytes 12582916
  91.7 2.2 %copy-start.7 = (bf16[2,1,2,128,4096]{4,3,2,1,0:T(8,128)(2,1)S(1)}, bf16[2,1,2,128,4096]{4,3,2,1,0:T(8,128)(2,1)}, u32[]{:S(2)}) copy-start(bf16[2,1,2,128,4096]{4,3,2,1,0:T(8,128)(2,1)} %copy-done.4) | copy-start | bytes 12582916
  101.0 0.7 copy-start.9

commit v5 on v4

--- a/solution.py
+++ b/solution.py
@@ -86,7 +86,7 @@
 
 
 def load_parts(src, rcv, starts):
-    at = [pl.ds(pl.multiple_of(c, BLOCK), BLOCK) for c in starts]
+    at = [slice(c, c + BLOCK) for c in starts]
     return [
         [(src[f, 0, 0, :, c], src[f, 0, 1, :, c], rcv[f, 0, 0, :, c], -rcv[f, 0, 1, :, c]) for c in at]
         for f in range(src.shape[0])
@@ -105,7 +105,7 @@
     i = pl.program_id(0)
 
     def run(slab):
-        parts = load_parts(src, rcv, [where[i] * tile + c.start for c in cols])
+        parts = load_parts(src, rcv, [c.start for c in cols])
         for d in range(slab.shape[1]):
             views = [slab_view(slab, d, c) for c in cols]
             parts = advance(parts, [[v * turns[f] for v in views] for f in range(freqs)], wx, wy)
@@ -129,7 +129,8 @@
     freqs, height = src.shape[0], src.shape[3]
     field = pl.BlockSpec((freqs, 1, 2, height, cols), lambda i, w: (0, 0, 0, 0, w[i]))
     args = [turns, wx, wy, src, rcv, *slabs]
-    in_specs = [pl.BlockSpec(memory_space=pltpu.SMEM)] + [pl.BlockSpec(memory_space=pltpu.VMEM)] * (len(args) - 1)
+    vmem = pl.BlockSpec(memory_space=pltpu.VMEM)
+    in_specs = [pl.BlockSpec(memory_space=pltpu.SMEM), vmem, vmem, field, field] + [vmem] * count
     alias = {len(args) + 1 + i: i for i in range(len(done))}
     cells = count * cols * height * freqs
     return pl.pallas_call(
@@ -149,9 +150,9 @@
     )(where, *args, *done)
 
 
-def image_body(tiles, slot, turns, wx, wy, src, rcv, *rest, scale, per, count):
-    slabs, out, held, lines = rest[:-3], rest[-3], rest[-2], rest[-1]
+def image_body(tiles, slot, turns, wx, wy, *rest, scale, per, count):
     aper = tiles.shape[0]
+    fields, slabs, out, held, lines = rest[: 2 * aper], rest[2 * aper : -3], rest[-3], rest[-2], rest[-1]
     for a in range(aper):
         column = pl.multiple_of(lax.rem(lax.div(tiles[a], 2), per) * BLOCK, BLOCK)
         for k, slab in enumerate(slabs):
@@ -160,8 +161,9 @@
             def _():
                 held[a] = slab[:, :, :, pl.ds(column, BLOCK)]
 
-    freqs = src.shape[0]
-    parts = load_parts(src, rcv, [lax.div(tiles[a], 2) * BLOCK for a in range(aper)])
+    freqs = fields[0].shape[0]
+    loaded = [load_parts(fields[2 * a], fields[2 * a + 1], [0]) for a in range(aper)]
+    parts = [[loaded[a][f][0] for a in range(aper)] for f in range(freqs)]
     half = BLOCK // 2
     for d in range(held.shape[2]):
         views = [slab_view(held.at[a], d, slice(0, BLOCK)) for a in range(aper)]
@@ -184,22 +186,29 @@
     steps, cols = slabs[0].shape[1], slabs[0].shape[-1]
     freqs, height = src.shape[0], src.shape[3]
     aper = tiles.shape[0]
+    vmem = pl.BlockSpec(memory_space=pltpu.VMEM)
+    field = lambda a: pl.BlockSpec((freqs, 1, 2, height, BLOCK), lambda i, t, s: (0, 0, 0, 0, lax.div(t[a], 2)))
     shape = (count, aper, steps, height // 2 // count, BLOCK)
     return pl.pallas_call(
         functools.partial(image_body, scale=scale, per=cols // BLOCK, count=count),
-        in_specs=[pl.BlockSpec(memory_space=pltpu.SMEM)] * 3
-        + [pl.BlockSpec(memory_space=pltpu.VMEM)] * (4 + len(slabs)),
-        out_specs=pl.BlockSpec(memory_space=pltpu.VMEM),
+        grid_spec=pltpu.PrefetchScalarGridSpec(
+            num_scalar_prefetch=2,
+            grid=(1,),
+            in_specs=[pl.BlockSpec(memory_space=pltpu.SMEM), vmem, vmem]
+            + [field(a) for a in range(aper) for _ in range(2)]
+            + [vmem] * len(slabs),
+            out_specs=pl.BlockSpec(shape, lambda i, t, s: (0,) * len(shape)),
+            scratch_shapes=[
+                pltpu.VMEM((aper,) + slabs[0].shape[:3] + (BLOCK,), jnp.float32),
+                pltpu.VMEM((aper, height, BLOCK), jnp.float32),
+            ],
+        ),
         out_shape=jax.ShapeDtypeStruct(shape, jnp.float32),
-        scratch_shapes=[
-            pltpu.VMEM((aper,) + slabs[0].shape[:3] + (BLOCK,), jnp.float32),
-            pltpu.VMEM((aper, height, BLOCK), jnp.float32),
-        ],
         cost_estimate=pl.CostEstimate(
             flops=aper * BLOCK * height * freqs * steps * 4 * 2 * 4 * BLOCK * 3, bytes_accessed=1 << 21, transcendentals=0
         ),
         compiler_params=pltpu.CompilerParams(vmem_limit_bytes=VMEM),
-    )(tiles, slot, turns, wx, wy, src, rcv, *slabs)
+    )(tiles, slot, turns, wx, wy, *[v for _ in range(aper) for v in (src, rcv)], *slabs)
 
 
 def deal_body(tiles, parts, out):
@@ -218,7 +227,7 @@
         in_specs=[pl.BlockSpec(memory_space=pltpu.SMEM), pl.BlockSpec(memory_space=pltpu.VMEM)],
         out_specs=pl.BlockSpec(memory_space=pltpu.VMEM),
         out_shape=jax.ShapeDtypeStruct((shots, rows, BLOCK), jnp.float32),
-    )(tiles, parts)
+    )(tiles, pltpu.with_memory_space_constraint(parts, pltpu.VMEM))
 
 
 def collect_body(entries, parts, out, *, aper):
@@ -243,7 +252,7 @@
         in_specs=[pl.BlockSpec(memory_space=pltpu.SMEM), pl.BlockSpec(memory_space=pltpu.VMEM)],
         out_specs=pl.BlockSpec(memory_space=pltpu.VMEM),
         out_shape=jax.ShapeDtypeStruct((entries.shape[0], steps, length), jnp.float32),
-    )(entries, parts)
+    )(entries, pltpu.with_memory_space_constraint(parts, pltpu.VMEM))
 
 
 def cut_body(spot, slab, out, sems, *, cols):
@@ -274,31 +283,6 @@
         out_shape=jax.ShapeDtypeStruct((zls, xs, CORES, rows, cols), slab.dtype),
         scratch_shapes=[pltpu.SemaphoreType.DMA((xs + 1,))],
     )(y, slab)
-
-
-def stage_body(*refs):
-    count = len(refs) // 2
-    sems = refs[-1]
-    copies = [pltpu.make_async_copy(refs[i], refs[count + i], sems.at[i]) for i in range(count)]
-    for c in copies:
-        c.start()
-    for c in copies:
-        c.wait()
-
-
-def stage(*arrays):
-    arrays = [pltpu.with_memory_space_constraint(a, pltpu.HBM) for a in arrays]
-    return pl.pallas_call(
-        stage_body,
-        in_specs=[pl.BlockSpec(memory_space=pltpu.HBM)] * len(arrays),
-        out_specs=[pl.BlockSpec(memory_space=pltpu.VMEM)] * len(arrays),
-        out_shape=[pltpu.VMEM(a.shape, a.dtype) for a in arrays],
-        scratch_shapes=[pltpu.SemaphoreType.DMA((len(arrays),))],
-        cost_estimate=pl.CostEstimate(
-            flops=0, bytes_accessed=sum(2 * a.size * a.dtype.itemsize for a in arrays), transcendentals=0
-        ),
-        compiler_params=pltpu.CompilerParams(vmem_limit_bytes=VMEM),
-    )(*arrays)
 
 
 def sweep_weights(xc, yc):
@@ -399,7 +383,8 @@
     partner_place = lambda k: (1 - core) * XS + lax.rem(partner_column + XS - k, XS)
     wx, wy = sweep_weights(x_correction, y_correction)
     turns = angular_freq * (0.5 / math.pi)
-    src, rcv = stage(source_field, receiver_field)
+    src = pltpu.with_memory_space_constraint(source_field, pltpu.HBM)
+    rcv = pltpu.with_memory_space_constraint(receiver_field, pltpu.HBM)
 
     def forward(places, slabs, done=()):
         return march(jnp.stack(places).astype(jnp.int32), turns, slabs, wx, wy, src, rcv, tuple(done))

time: 104 us -> 92.3 us (0.89)
  local copies, waits for them, and re-layouts: 22.5 us -> 4.1 us
  waiting for transfers between devices: 4.51 us -> 11.8 us
    unnamed x30 -> x10, local copies, waits for them, and re-layouts: 18.8 us -> 0.26 us
    all_to_all x1, waiting for transfers between devices: 0.01 us -> 7.34 us  [local(): own = lax.all_to_all(own, AXES, 0, 0, axis_index_groups=groups, tiled=True)]
    pallas_call x1 -> x0, Pallas kernels: 3.52 us -> none  [stage(): pl.pallas_call(stage_body, in_specs=[pl.BlockSpec(memory_space=pltpu.HBM)...]
    pallas_call x4, Pallas kernels: 28.5 us -> 31.1 us  [march(): pl.pallas_call(functools.partial(march_body, count=count), grid_spec=pltp...]
    pallas_call x1, Pallas kernels: 2.98 us -> 4.06 us  [image_terms(): pl.pallas_call(functools.partial(image_body, scale=scale, per=cols // BLO...]
  transfers between devices with their start and end apart: 11 -> 11, of which waited for: 3 -> 3; matrix products, arithmetic and copies ran while one was open for 4% -> 5% of each run, Pallas kernels for 31% -> 34%
where the time goes in v5:
time: 92.3 us; the launch traced here: 91.5 us
  Pallas kernels  39.9 us (43%)
  starting transfers between devices  30 us (33%)
  waiting for transfers between devices  11.8 us (13%)
  between operations  4.58 us (5%)
  local copies, waits for them, and re-layouts  4.1 us (4%)
  other arithmetic  1.09 us (1%)
    pallas_call x4, Pallas kernels, march(): pl.pallas_call(functools.partial(march_body, count=count), grid_spec=pltp...  31.1 us
    all_to_all x1, waiting for transfers between devices, local(): own = lax.all_to_all(own, AXES, 0, 0, axis_index_groups=groups, tiled=True)  7.34 us
    all_to_all x1, starting transfers between devices, local(): arrived = lax.all_to_all(outgoing, 'shot', 0, 0, tiled=True)  7.18 us
    ppermute x7, starting transfers between devices, local(): lax.ppermute(v, AXES, pairs((freqs_dev, shots), move))  7.16 us
    all_to_all x1, starting transfers between devices, local(): lax.all_to_all(terms.reshape(freqs_dev, -1, BLOCK), 'freq', 0, 0, tiled=T...  6.52 us
    all_to_all x1, starting transfers between devices, local(): own = lax.all_to_all(own, AXES, 0, 0, axis_index_groups=groups, tiled=True)  4.81 us
    all_to_all x1, starting transfers between devices, local(): dealt = lax.all_to_all(deal(tiles, terms, shots), 'shot', 0, 0, tiled=True)  4.3 us
    pallas_call x1, Pallas kernels, image_terms(): pl.pallas_call(functools.partial(image_body, scale=scale, per=cols // BLO...  4.06 us
  transfers between devices with their start and end apart: 11, of which 3 were waited for; matrix products, arithmetic and copies ran while one was open for 5% of the time, Pallas kernels for 34%

profile of v5, /device:TPU:1, one launch (start us, length us, event | category | flops | bytes accessed | tf_op | source)
XLA Modules:
  0.0 91.5 jit_solution(13662382132205032005)
XLA Ops:
  0.6 0.0 copy-start.2
  0.6 0.0 copy-start.1
  0.7 0.0 copy-start.3
  0.7 1.9 %shard_map.112 = f32[2,4,2,16,512]{4,3,2,1,0:T(8,128)} custom-call(s32[1]{0:T(128)} %bitcast.10.spot, f32[2,4,16,4096]{3,2,1,0:T(8,128)} %bitcast.35), custom_call_target="tpu_custom_call" | custom-call | tf_op jit(solution)/shard_map/pallas_call | solution.py:279
  2.6 7.2 %all-to-all-start = ((f32[16,16,512]{2,1,0:T(8,128)}), f32[16,16,512]{2,1,0:T(8,128)S(1)}, u32[]{:S(2)}, u32[]{:S(2)}) async-start(f32[16,16,512]{2,1,0:T(8,128)} %bitcast.36), calls=%async_computation | async-start | bytes 1048576 | tf_op jit(solution)/shard_map/all_to_all | solution.py:370
  9.8 1.3 %fusion.3 = (s32[1]{0:T(128)}, s32[1]{0:T(128)}) fusion(s32[2]{0:T(128)} %param.15), kind=kLoop, calls=%fused_computation.19 | loop fusion | bytes 16 | tf_op jit(solution)/shard_map/slice | solution.py:371
  14.9 0.1 pad_add_fusion.where
  15.0 0.1 pad_add_fusion.1.where
  15.1 0.9 fusion.2
  15.9 3.7 %all-to-all-done = f32[16,16,512]{2,1,0:T(8,128)S(1)} async-done(((f32[16,16,512]{2,1,0:T(8,128)}), f32[16,16,512]{2,1,0:T(8,128)S(1)}, u32[]{:S(2)}, u32[]{:S(2)}) %all-to-all-start) | async-done | bytes 524320 | tf_op jit(solution)/shard_map/all_to_all | solution.py:370
  19.7 0.9 broadcast_in_dim.5
  20.5 4.8 %all-to-all-start.1 = ((f32[8,2,16,512]{3,2,1,0:T(8,128)}), f32[8,2,16,512]{3,2,1,0:T(8,128)S(1)}, u32[]{:S(2)}, u32[]{:S(2)}) async-start(f32[8,2,16,512]{3,2,1,0:T(8,128)} %broadcast_in_dim.5), calls=%async_computation.1 | async-start | bytes 1048576 | tf_op jit(solution)/shard_map/all_to_all | solution.py:376
  25.3 0.1 pad_add_fusion.2.where
  25.4 0.1 copy.28
  25.5 0.1 copy.29
  25.7 0.1 stack.64
  25.8 0.0 copy-done.2
  25.8 0.7 dynamic_slice.12.entries
  26.4 0.0 copy-done.1
  26.5 7.3 %all-to-all-done.1.rest_0_.rest_4_ = f32[8,2,16,512]{3,2,1,0:T(8,128)S(1)} async-done(((f32[8,2,16,512]{3,2,1,0:T(8,128)}), f32[8,2,16,512]{3,2,1,0:T(8,128)S(1)}, u32[]{:S(2)}, u32[]{:S(2)}) %all-to-all-start.1) | async-done | bytes 524320 | tf_op jit(solution)/shard_map/all_to_all | solution.py:376
  33.8 0.9 collective-permute-start.2
  34.7 0.1 maximum_maximum_fusion
  34.7 0.0 copy-done.3
  34.8 0.3 collective-permute-start
  35.1 2.4 %collective-permute-start.1 = (f32[8,2,16,512]{3,2,1,0:T(8,128)S(1)}, f32[8,2,16,512]{3,2,1,0:T(8,128)S(1)}, u32[]{:S(2)}, u32[]{:S(2)}) collective-permute-start(f32[8,2,16,512]{3,2,1,0:T(8,128)S(1)} %all-to-all-done.1.rest_0_.rest_4_), channel_id=1, source_target_pairs={{0,48},{1,7},{2,50},{3,1},{4,52},{5,3},{6,54},{7,5},{8,56},{9,15},... | collective-permute-start | bytes 1572872 | tf_op jit(solution)/shard_map/ppermute | solution.py:367
  37.5 0.0 collective-permute-done.2.rest_1_.rest_5_
  37.5 7.8 %shard_map.113 = (bf16[2,1,2,128,4096]{4,3,2,1,0:T(8,128)(2,1)}, bf16[2,1,2,128,4096]{4,3,2,1,0:T(8,128)(2,1)}) custom-call(s32[2]{0:T(128)S(1)} %pad_add_fusion.1.where, f32[2]{0:T(128)S(1)} %broadcast_multiply_fusion.turns, bf16[2,256,256]{2,1,0:T(8,128)(2,1)S(1)} %get-tuple-element.51.wx, bf16[2,256,256]{2,1,0:T(8,128)(2,1)S(1)} %get-tuple-element.52.wy, ...), custom_call_target="tpu_custom_call" | custom-call | flops 6442450944 | bytes 4194304 | tf_op jit(solution)/shard_map/pallas_call | solution.py:136
  45.3 0.0 collective-permute-done.rest_0_.rest_6_
  45.3 0.0 collective-permute-done.1.rest_1_.rest_7_
  45.3 0.0 copy-start
  45.3 0.3 collective-permute-start.3
  45.6 2.2 %collective-permute-start.5 = (f32[8,2,16,512]{3,2,1,0:T(8,128)S(1)}, f32[8,2,16,512]{3,2,1,0:T(8,128)S(1)}, u32[]{:S(2)}, u32[]{:S(2)}) collective-permute-start(f32[8,2,16,512]{3,2,1,0:T(8,128)S(1)} %collective-permute-done.rest_0_.rest_6_), channel_id=1, source_target_pairs={{0,1},{1,0},{2,3},{3,2},{4,5},{5,4},{6,7},{7,6},{8,9},{9,8},{10,11... | collective-permute-start | bytes 1572872 | tf_op jit(solution)/shard_map/ppermute | solution.py:367
  47.8 0.0 collective-permute-start.6
  47.8 7.8 %shard_map.114 = (bf16[2,1,2,128,4096]{4,3,2,1,0:T(8,128)(2,1)}, bf16[2,1,2,128,4096]{4,3,2,1,0:T(8,128)(2,1)}) custom-call(s32[2]{0:T(128)S(1)} %pad_add_fusion.2.where, f32[2]{0:T(128)S(1)} %broadcast_multiply_fusion.turns, bf16[2,256,256]{2,1,0:T(8,128)(2,1)S(1)} %get-tuple-element.51.wx, ...), custom_call_target="tpu_custom_call", output_to_operand_aliasing={{0}: (8, {}), {1}: (9, {})} | custom-call | flops 6442450944 | bytes 4194304 | tf_op jit(solution)/shard_map/pallas_call | solution.py:136
  55.6 0.0 collective-permute-done.3.rest_8_.rest_0_
  55.6 1.0 %collective-permute-start.4 = (f32[8,2,16,512]{3,2,1,0:T(8,128)S(1)}, f32[8,2,16,512]{3,2,1,0:T(8,128)S(1)}, u32[]{:S(2)}, u32[]{:S(2)}) collective-permute-start(f32[8,2,16,512]{3,2,1,0:T(8,128)S(1)} %collective-permute-done.3.rest_8_.rest_0_), channel_id=1, source_target_pairs={{0,1},{1,0},{2,3},{3,2},{4,5},{5,4},{6,7},{7,6},{8,9},{9,8},{10,11... | collective-permute-start | bytes 1572872 | tf_op jit(solution)/shard_map/ppermute | solution.py:367
  56.6 0.1 pad_add_fusion.3.where
  56.7 0.0 copy-done
  56.7 0.7 compare_reduce_fusion
  57.4 0.0 collective-permute-done.5.rest_9_.rest_0_
  57.4 0.0 collective-permute-done.6.rest_10_.rest_1_
  57.4 0.7 collective-permute-done.4.rest_11_.rest_1_
  58.2 4.1 %shard_map.115 = f32[8,2,2,8,128]{4,3,2,1,0:T(8,128)} custom-call(s32[2]{0:T(128)S(1)} %bitcast.34, s32[2]{0:T(128)S(1)} %get-tuple-element.33.slot, f32[2]{0:T(128)S(1)} %broadcast_multiply_fusion.turns, bf16[2,256,256]{2,1,0:T(8,128)(2,1)S(1)} %get-tuple-element.51.wx, bf16[2,256,256]{2,1,0:T(8,128)(2,1)S(1)} %get-tuple-element.52.wy, ...), custom_call_target="tpu_custom_call" | custom-call | flops 1610612736 | bytes 2097152 | tf_op jit(solution)/shard_map/pallas_call | solution.py:192
  62.2 6.5 %all-to-all-start.2 = ((f32[8,32,128]{2,1,0:T(8,128)}), f32[8,32,128]{2,1,0:T(8,128)S(1)}, u32[]{:S(2)}, u32[]{:S(2)}) async-start(f32[8,32,128]{2,1,0:T(8,128)} %bitcast.22), calls=%async_computation.2 | async-start | bytes 262144 | tf_op jit(solution)/shard_map/all_to_all | solution.py:409
  68.8 7.8 %shard_map.116 = (bf16[2,1,2,128,4096]{4,3,2,1,0:T(8,128)(2,1)}, bf16[2,1,2,128,4096]{4,3,2,1,0:T(8,128)(2,1)}) custom-call(s32[2]{0:T(128)S(1)} %pad_add_fusion.3.where, f32[2]{0:T(128)S(1)} %broadcast_multiply_fusion.turns, bf16[2,256,256]{2,1,0:T(8,128)(2,1)S(1)} %get-tuple-element.51.wx, ...), custom_call_target="tpu_custom_call", output_to_operand_aliasing={{0}: (8, {}), {1}: (9, {})} | custom-call | flops 6442450944 | bytes 4194304 | tf_op jit(solution)/shard_map/pallas_call | solution.py:136
  76.5 0.0 all-to-all-done.2.parts
  76.5 1.4 %shard_map.118 = f32[16,40,128]{2,1,0:T(8,128)} custom-call(s32[2]{0:T(128)} %bitcast.33, f32[8,32,128]{2,1,0:T(8,128)S(1)} %all-to-all-done.2.parts), custom_call_target="tpu_custom_call" | custom-call | tf_op jit(solution)/shard_map/pallas_call | solution.py:225
  77.9 4.3 %all-to-all-start.3 = ((f32[16,40,128]{2,1,0:T(8,128)}), f32[16,40,128]{2,1,0:T(8,128)S(1)}, u32[]{:S(2)}, u32[]{:S(2)}) async-start(f32[16,40,128]{2,1,0:T(8,128)} %shard_map.118), calls=%async_computation.3 | async-start | bytes 655360 | tf_op jit(solution)/shard_map/all_to_all | solution.py:412
  82.2 7.8 %shard_map.117 = (bf16[2,1,2,128,4096]{4,3,2,1,0:T(8,128)(2,1)}, bf16[2,1,2,128,4096]{4,3,2,1,0:T(8,128)(2,1)}) custom-call(s32[2]{0:T(128)S(1)} %pad_add_fusion.where, f32[2]{0:T(128)S(1)} %broadcast_multiply_fusion.turns, bf16[2,256,256]{2,1,0:T(8,128)(2,1)S(1)} %get-tuple-element.51.wx, ...), custom_call_target="tpu_custom_call", output_to_operand_aliasing={{0}: (8, {}), {1}: (9, {})} | custom-call | flops 6442450944 | bytes 4194304 | tf_op jit(solution)/shard_map/pallas_call | solution.py:136
  90.0 0.0 all-to-all-done.3.parts
  90.0 1.5 %shard_map.119 = f32[4,2,1024]{2,1,0:T(2,128)} custom-call(s32[4]{0:T(128)} %dynamic_slice.12.entries, f32[16,40,128]{2,1,0:T(8,128)S(1)} %all-to-all-done.3.parts), custom_call_target="tpu_custom_call" | custom-call | tf_op jit(solution)/shard_map/pallas_call | solution.py:250
  (7 shorter events, 0.1 us)
Async XLA Ops:
  0.6 25.1 %copy-start.2 = (s32[64]{0:T(128)S(1)}, s32[64]{0:T(128)}, u32[]{:S(2)}) copy-start(s32[64]{0:T(128)} %param.17) | copy-start | bytes 772
  0.6 25.8 %copy-start.1 = (bf16[2,2,128,128]{3,2,1,0:T(8,128)(2,1)S(1)}, bf16[2,2,128,128]{3,2,1,0:T(8,128)(2,1)}, u32[]{:S(2)}) copy-start(bf16[2,2,128,128]{3,2,1,0:T(8,128)(2,1)} %param.12) | copy-start | bytes 393220
  0.7 34.1 %copy-start.3 = (f32[2]{0:T(128)S(1)}, f32[2]{0:T(128)}, u32[]{:S(2)}) copy-start(f32[2]{0:T(128)} %param.11) | copy-start | bytes 28
  2.6 17.1 %all-to-all-start = ((f32[16,16,512]{2,1,0:T(8,128)}), f32[16,16,512]{2,1,0:T(8,128)S(1)}, u32[]{:S(2)}, u32[]{:S(2)}) async-start(f32[16,16,512]{2,1,0:T(8,128)} %bitcast.36), calls=%async_computation | async-start | bytes 1048576 | tf_op jit(solution)/shard_map/all_to_all | solution.py:370
  20.5 13.3 %all-to-all-start.1 = ((f32[8,2,16,512]{3,2,1,0:T(8,128)}), f32[8,2,16,512]{3,2,1,0:T(8,128)S(1)}, u32[]{:S(2)}, u32[]{:S(2)}) async-start(f32[8,2,16,512]{3,2,1,0:T(8,128)} %broadcast_in_dim.5), calls=%async_computation.1 | async-start | bytes 1048576 | tf_op jit(solution)/shard_map/all_to_all | solution.py:376
  33.8 3.7 %collective-permute-start.2 = (f32[8,2,16,512]{3,2,1,0:T(8,128)S(1)}, f32[8,2,16,512]{3,2,1,0:T(8,128)S(1)}, u32[]{:S(2)}, u32[]{:S(2)}) collective-permute-start(f32[8,2,16,512]{3,2,1,0:T(8,128)S(1)} %all-to-all-done.1.rest_0_.rest_4_), channel_id=1, source_target_pairs={{0,1},{1,0},{2,3},{3,2},{4,5},{5,4},{6,7},{7,6},{8,9},{9,8},{10,11... | collective-permute-start | bytes 1572872 | tf_op jit(solution)/shard_map/ppermute | solution.py:367
  34.8 10.5 %collective-permute-start = (f32[8,2,16,512]{3,2,1,0:T(8,128)S(1)}, f32[8,2,16,512]{3,2,1,0:T(8,128)S(1)}, u32[]{:S(2)}, u32[]{:S(2)}) collective-permute-start(f32[8,2,16,512]{3,2,1,0:T(8,128)S(1)} %all-to-all-done.1.rest_0_.rest_4_), channel_id=1, source_target_pairs={{0,16},{1,3},{2,18},{3,5},{4,20},{5,7},{6,22},{7,1},{8,24},{9,11},... | collective-permute-start | bytes 1572872 | tf_op jit(solution)/shard_map/ppermute | solution.py:367
  35.1 10.2 %collective-permute-start.1 = (f32[8,2,16,512]{3,2,1,0:T(8,128)S(1)}, f32[8,2,16,512]{3,2,1,0:T(8,128)S(1)}, u32[]{:S(2)}, u32[]{:S(2)}) collective-permute-start(f32[8,2,16,512]{3,2,1,0:T(8,128)S(1)} %all-to-all-done.1.rest_0_.rest_4_), channel_id=1, source_target_pairs={{0,48},{1,7},{2,50},{3,1},{4,52},{5,3},{6,54},{7,5},{8,56},{9,15},... | collective-permute-start | bytes 1572872 | tf_op jit(solution)/shard_map/ppermute | solution.py:367
  45.3 11.4 %copy-start = (s32[1,2]{1,0:T(1,128)S(1)}, s32[1,2]{1,0:T(1,128)}, u32[]{:S(2)}) copy-start(s32[1,2]{1,0:T(1,128)} %param.16) | copy-start | bytes 28
  45.3 10.3 %collective-permute-start.3 = (f32[8,2,16,512]{3,2,1,0:T(8,128)S(1)}, f32[8,2,16,512]{3,2,1,0:T(8,128)S(1)}, u32[]{:S(2)}, u32[]{:S(2)}) collective-permute-start(f32[8,2,16,512]{3,2,1,0:T(8,128)S(1)} %all-to-all-done.1.rest_0_.rest_4_), channel_id=1, source_target_pairs={{0,32},{1,5},{2,34},{3,7},{4,36},{5,1},{6,38},{7,3},{8,40},{9,13},... | collective-permute-start | bytes 1572872 | tf_op jit(solution)/shard_map/ppermute | solution.py:367
  45.6 11.8 %collective-permute-start.5 = (f32[8,2,16,512]{3,2,1,0:T(8,128)S(1)}, f32[8,2,16,512]{3,2,1,0:T(8,128)S(1)}, u32[]{:S(2)}, u32[]{:S(2)}) collective-permute-start(f32[8,2,16,512]{3,2,1,0:T(8,128)S(1)} %collective-permute-done.rest_0_.rest_6_), channel_id=1, source_target_pairs={{0,1},{1,0},{2,3},{3,2},{4,5},{5,4},{6,7},{7,6},{8,9},{9,8},{10,11... | collective-permute-start | bytes 1572872 | tf_op jit(solution)/shard_map/ppermute | solution.py:367
  47.8 9.6 %collective-permute-start.6 = (f32[8,2,16,512]{3,2,1,0:T(8,128)S(1)}, f32[8,2,16,512]{3,2,1,0:T(8,128)S(1)}, u32[]{:S(2)}, u32[]{:S(2)}) collective-permute-start(f32[8,2,16,512]{3,2,1,0:T(8,128)S(1)} %collective-permute-done.1.rest_1_.rest_7_), channel_id=1, source_target_pairs={{0,1},{1,0},{2,3},{3,2},{4,5},{5,4},{6,7},{7,6},{8,9},{9,8},{10,11... | collective-permute-start | bytes 1572872 | tf_op jit(solution)/shard_map/ppermute | solution.py:367
  55.6 2.6 %collective-permute-start.4 = (f32[8,2,16,512]{3,2,1,0:T(8,128)S(1)}, f32[8,2,16,512]{3,2,1,0:T(8,128)S(1)}, u32[]{:S(2)}, u32[]{:S(2)}) collective-permute-start(f32[8,2,16,512]{3,2,1,0:T(8,128)S(1)} %collective-permute-done.3.rest_8_.rest_0_), channel_id=1, source_target_pairs={{0,1},{1,0},{2,3},{3,2},{4,5},{5,4},{6,7},{7,6},{8,9},{9,8},{10,11... | collective-permute-start | bytes 1572872 | tf_op jit(solution)/shard_map/ppermute | solution.py:367
  62.2 14.3 %all-to-all-start.2 = ((f32[8,32,128]{2,1,0:T(8,128)}), f32[8,32,128]{2,1,0:T(8,128)S(1)}, u32[]{:S(2)}, u32[]{:S(2)}) async-start(f32[8,32,128]{2,1,0:T(8,128)} %bitcast.22), calls=%async_computation.2 | async-start | bytes 262144 | tf_op jit(solution)/shard_map/all_to_all | solution.py:409
  77.9 12.1 %all-to-all-start.3 = ((f32[16,40,128]{2,1,0:T(8,128)}), f32[16,40,128]{2,1,0:T(8,128)S(1)}, u32[]{:S(2)}, u32[]{:S(2)}) async-start(f32[16,40,128]{2,1,0:T(8,128)} %shard_map.118), calls=%async_computation.3 | async-start | bytes 655360 | tf_op jit(solution)/shard_map/all_to_all | solution.py:412

commit v6 on v5

--- a/solution.py
+++ b/solution.py
@@ -46,51 +46,29 @@
 
 
 def advance(parts, phases, wx, wy):
-    freqs, blocks = len(parts), len(parts[0])
-    height, width = parts[0][0][0].shape
-    out = [[None] * blocks for _ in range(freqs)]
-    for f in range(freqs):
-        for b in range(blocks):
-            sr, si, rr, ri = widened(parts[f][b])
-            sin, cos = sincos(phases[f][b])
-            out[f][b] = rounded(
-                (sr * cos - si * sin, sr * sin + si * cos, rr * cos - ri * sin, rr * sin + ri * cos)
-            )
-    for f in range(freqs):
-        left = jnp.concatenate([quad(*out[f][b]) for b in range(blocks)], 0)
-        prod = jnp.dot(left, wx[f], preferred_element_type=jnp.float32)
-        for b in range(blocks):
-            x = prod[b * 2 * height : (b + 1) * 2 * height]
-            sr, si, rr, ri = widened(out[f][b])
-            out[f][b] = rounded(
-                (
-                    sr + x[:height, :width],
-                    si + x[:height, width:],
-                    rr + x[height:, :width],
-                    ri + x[height:, width:],
-                )
-            )
-    for f in range(freqs):
-        right = jnp.concatenate([quad(v[0], v[2], v[1], v[3]) for v in out[f]], 1)
-        prod = jnp.dot(wy[f], right, preferred_element_type=jnp.float32)
-        for b in range(blocks):
-            y = prod[:, b * 2 * width : (b + 1) * 2 * width]
-            sr, si, rr, ri = widened(out[f][b])
-            out[f][b] = (
-                sr + y[:height, :width],
-                si + y[height:, :width],
-                rr + y[:height, width:],
-                ri + y[height:, width:],
-            )
+    height, width = parts[0][0].shape
+    out = []
+    for part, phase in zip(parts, phases):
+        sr, si, rr, ri = widened(part)
+        sin, cos = sincos(phase)
+        out.append(rounded((sr * cos - si * sin, sr * sin + si * cos, rr * cos - ri * sin, rr * sin + ri * cos)))
+    prod = jnp.dot(jnp.concatenate([quad(*v) for v in out], 0), wx, preferred_element_type=jnp.float32)
+    for b, (sr, si, rr, ri) in enumerate(out):
+        x = prod[b * 2 * height : (b + 1) * 2 * height]
+        x = rounded((x[:height, :width], x[:height, width:], x[height:, :width], x[height:, width:]))
+        out[b] = (sr + x[0], si + x[1], rr + x[2], ri + x[3])
+    right = jnp.concatenate([quad(v[0], v[2], v[1], v[3]) for v in out], 1)
+    prod = jnp.dot(wy, right, preferred_element_type=jnp.float32)
+    for b, part in enumerate(out):
+        y = prod[:, b * 2 * width : (b + 1) * 2 * width]
+        sr, si, rr, ri = widened(part)
+        out[b] = (
+            sr + y[:height, :width],
+            si + y[height:, :width],
+            rr + y[:height, width:],
+            ri + y[height:, width:],
+        )
     return out
-
-
-def load_parts(src, rcv, starts):
-    at = [slice(c, c + BLOCK) for c in starts]
-    return [
-        [(src[f, 0, 0, :, c], src[f, 0, 1, :, c], rcv[f, 0, 0, :, c], -rcv[f, 0, 1, :, c]) for c in at]
-        for f in range(src.shape[0])
-    ]
 
 
 def slab_view(slab, d, cols):
@@ -98,48 +76,117 @@
     return rows.reshape(rows.shape[0] * rows.shape[1], rows.shape[2])
 
 
-def march_body(where, turns, wx, wy, src, rcv, *rest, count):
-    slabs, so, ro = rest[:count], rest[-2], rest[-1]
-    freqs, tile = src.shape[0], so.shape[-1]
+def fetch_body(blocks, tiles, src, rcv, *rest, steps, cols):
+    firsts, wanted, sems = rest[:steps], rest[steps], rest[steps + 1]
+    copies = []
+
+    def copy(source, target):
+        copies.append(pltpu.make_async_copy(source, target, sems.at[len(copies)]))
+
+    for k in range(steps):
+        at = pl.ds(pl.multiple_of(blocks[k] * cols, BLOCK), cols)
+        for i, field in enumerate((src, rcv)):
+            copy(field.at[0, 0, :, :, at], firsts[k].at[i])
+    for a in range(wanted.shape[0]):
+        at = pl.ds(pl.multiple_of(lax.div(tiles[a], 2) * BLOCK, BLOCK), BLOCK)
+        for i, field in enumerate((src, rcv)):
+            copy(field.at[:, 0, :, :, at], wanted.at[a, i])
+    for c in copies:
+        c.start()
+    for c in copies:
+        c.wait()
+
+
+def fetch(blocks, tiles, src, rcv, cols):
+    steps, aper = blocks.shape[0], tiles.shape[0]
+    freqs, _, _, height, _ = src.shape
+    shapes = [(2, 2, height, cols)] * steps + [(aper, 2, freqs, 2, height, BLOCK)]
+    vmem = pl.BlockSpec(memory_space=pltpu.VMEM)
+    out = pl.pallas_call(
+        functools.partial(fetch_body, steps=steps, cols=cols),
+        in_specs=[pl.BlockSpec(memory_space=pltpu.SMEM)] * 2 + [pl.BlockSpec(memory_space=pltpu.HBM)] * 2,
+        out_specs=[vmem] * len(shapes),
+        out_shape=[pltpu.VMEM(s, src.dtype) for s in shapes],
+        scratch_shapes=[pltpu.SemaphoreType.DMA((2 * (steps + aper),))],
+        cost_estimate=pl.CostEstimate(flops=0, bytes_accessed=1 << 23, transcendentals=0),
+        compiler_params=pltpu.CompilerParams(vmem_limit_bytes=VMEM),
+    )(blocks, tiles, src, rcv)
+    return out[:-1], out[-1]
+
+
+def march_body(where, turns, wx, wy, first, src, rcv, *rest, count, freqs):
+    slabs, (so, ro, held, sems) = rest[:count], rest[-4:]
+    tile = so.shape[-1]
     cols = [slice(c, c + BLOCK) for c in range(0, tile, BLOCK)]
-    i = pl.program_id(0)
+    unit = pl.program_id(0)
+    block, f = lax.div(unit, freqs), lax.rem(unit, freqs)
+
+    def copies(u):
+        at = pl.ds(pl.multiple_of(where[lax.div(u, freqs)] * tile, BLOCK), tile)
+        slot = lax.rem(u, 2)
+        return [
+            pltpu.make_async_copy(field.at[lax.rem(u, freqs), 0, :, :, at], held.at[slot, i], sems.at[slot, i])
+            for i, field in enumerate((src, rcv))
+        ]
+
+    @pl.when(unit + 1 < count * freqs)
+    def _():
+        for c in copies(unit + 1):
+            c.start()
+
+    @pl.when(unit == 0)
+    def _():
+        held[0] = first[...]
+
+    @pl.when(unit > 0)
+    def _():
+        for c in copies(unit):
+            c.wait()
+
+    slot = lax.rem(unit, 2)
 
     def run(slab):
-        parts = load_parts(src, rcv, [c.start for c in cols])
+        parts = [
+            (held[slot, 0, 0, :, c], held[slot, 0, 1, :, c], held[slot, 1, 0, :, c], -held[slot, 1, 1, :, c])
+            for c in cols
+        ]
         for d in range(slab.shape[1]):
-            views = [slab_view(slab, d, c) for c in cols]
-            parts = advance(parts, [[v * turns[f] for v in views] for f in range(freqs)], wx, wy)
-        for f in range(freqs):
-            for b, c in enumerate(cols):
-                sr, si, rr, ri = parts[f][b]
-                so[f, 0, 0, :, c] = sr.astype(so.dtype)
-                so[f, 0, 1, :, c] = si.astype(so.dtype)
-                ro[f, 0, 0, :, c] = rr.astype(ro.dtype)
-                ro[f, 0, 1, :, c] = (-ri).astype(ro.dtype)
+            parts = advance(parts, [slab_view(slab, d, c) * turns[f] for c in cols], wx[f], wy[f])
+        for (sr, si, rr, ri), c in zip(parts, cols):
+            so[0, 0, 0, :, c] = sr.astype(so.dtype)
+            so[0, 0, 1, :, c] = si.astype(so.dtype)
+            ro[0, 0, 0, :, c] = rr.astype(ro.dtype)
+            ro[0, 0, 1, :, c] = (-ri).astype(ro.dtype)
 
     for k, slab in enumerate(slabs):
 
-        @pl.when(i == k)
+        @pl.when(block == k)
         def _():
             run(slab)
 
 
-def march(where, turns, slabs, wx, wy, src, rcv, done=()):
+def march(where, turns, slabs, wx, wy, first, src, rcv, done=()):
     count, cols = len(slabs), slabs[0].shape[-1]
     freqs, height = src.shape[0], src.shape[3]
-    field = pl.BlockSpec((freqs, 1, 2, height, cols), lambda i, w: (0, 0, 0, 0, w[i]))
-    args = [turns, wx, wy, src, rcv, *slabs]
-    vmem = pl.BlockSpec(memory_space=pltpu.VMEM)
-    in_specs = [pl.BlockSpec(memory_space=pltpu.SMEM), vmem, vmem, field, field] + [vmem] * count
+    vmem, hbm = pl.BlockSpec(memory_space=pltpu.VMEM), pl.BlockSpec(memory_space=pltpu.HBM)
+    field = pl.BlockSpec(
+        (1, 1, 2, height, cols), lambda u, w: (lax.rem(u, freqs), 0, 0, 0, w[lax.div(u, freqs)])
+    )
+    args = [turns, wx, wy, first, src, rcv, *slabs]
+    in_specs = [pl.BlockSpec(memory_space=pltpu.SMEM), vmem, vmem, vmem, hbm, hbm] + [vmem] * count
     alias = {len(args) + 1 + i: i for i in range(len(done))}
     cells = count * cols * height * freqs
     return pl.pallas_call(
-        functools.partial(march_body, count=count),
+        functools.partial(march_body, count=count, freqs=freqs),
         grid_spec=pltpu.PrefetchScalarGridSpec(
             num_scalar_prefetch=1,
-            grid=(count,),
+            grid=(count * freqs,),
             in_specs=in_specs + [pl.BlockSpec(memory_space=pl.ANY)] * len(done),
             out_specs=[field, field],
+            scratch_shapes=[
+                pltpu.VMEM((2, 2, 2, height, cols), src.dtype),
+                pltpu.SemaphoreType.DMA((2, 2)),
+            ],
         ),
         out_shape=[jax.ShapeDtypeStruct(src.shape, src.dtype), jax.ShapeDtypeStruct(rcv.shape, rcv.dtype)],
         input_output_aliases=alias,
@@ -150,30 +197,29 @@
     )(where, *args, *done)
 
 
-def image_body(tiles, slot, turns, wx, wy, *rest, scale, per, count):
+def image_body(tiles, places, turns, wx, wy, wanted, *rest, scale, per, count):
+    slabs, out, held, lines = rest[:-3], rest[-3], rest[-2], rest[-1]
     aper = tiles.shape[0]
-    fields, slabs, out, held, lines = rest[: 2 * aper], rest[2 * aper : -3], rest[-3], rest[-2], rest[-1]
     for a in range(aper):
-        column = pl.multiple_of(lax.rem(lax.div(tiles[a], 2), per) * BLOCK, BLOCK)
+        x_block = lax.div(tiles[a], 2)
+        column = pl.multiple_of(lax.rem(x_block, per) * BLOCK, BLOCK)
         for k, slab in enumerate(slabs):
 
-            @pl.when(slot[a] == k)
+            @pl.when(places[k] == lax.div(x_block, per))
             def _():
                 held[a] = slab[:, :, :, pl.ds(column, BLOCK)]
 
-    freqs = fields[0].shape[0]
-    loaded = [load_parts(fields[2 * a], fields[2 * a + 1], [0]) for a in range(aper)]
-    parts = [[loaded[a][f][0] for a in range(aper)] for f in range(freqs)]
+    freqs = wanted.shape[2]
+    parts = [
+        [(wanted[a, 0, f, 0], wanted[a, 0, f, 1], wanted[a, 1, f, 0], -wanted[a, 1, f, 1]) for a in range(aper)]
+        for f in range(freqs)
+    ]
     half = BLOCK // 2
     for d in range(held.shape[2]):
         views = [slab_view(held.at[a], d, slice(0, BLOCK)) for a in range(aper)]
-        parts = advance(parts, [[v * turns[f] for v in views] for f in range(freqs)], wx, wy)
+        parts = [advance(parts[f], [v * turns[f] for v in views], wx[f], wy[f]) for f in range(freqs)]
         for a in range(aper):
-            sr, si, rr, ri = parts[0][a]
-            term = sr * rr - si * ri
-            for f in range(1, freqs):
-                sr, si, rr, ri = parts[f][a]
-                term += sr * rr - si * ri
+            term = sum(sr * rr - si * ri for sr, si, rr, ri in (widened(rounded(p[a])) for p in parts))
             odd = lax.rem(tiles[a], 2) == 1
             lines[a, :, :half] = jnp.where(odd, term[:, half:], term[:, :half]) * scale
             pairs_of = lines.shape[1] // 2
@@ -182,33 +228,25 @@
             out[:, a, d] = both.reshape(count, pairs_of // count, BLOCK)
 
 
-def image_terms(tiles, slot, turns, wx, wy, src, rcv, slabs, scale, count):
+def image_terms(tiles, places, turns, wx, wy, wanted, slabs, scale, count):
     steps, cols = slabs[0].shape[1], slabs[0].shape[-1]
-    freqs, height = src.shape[0], src.shape[3]
-    aper = tiles.shape[0]
-    vmem = pl.BlockSpec(memory_space=pltpu.VMEM)
-    field = lambda a: pl.BlockSpec((freqs, 1, 2, height, BLOCK), lambda i, t, s: (0, 0, 0, 0, lax.div(t[a], 2)))
+    aper, _, freqs, _, height, _ = wanted.shape
+    smem, vmem = pl.BlockSpec(memory_space=pltpu.SMEM), pl.BlockSpec(memory_space=pltpu.VMEM)
     shape = (count, aper, steps, height // 2 // count, BLOCK)
     return pl.pallas_call(
         functools.partial(image_body, scale=scale, per=cols // BLOCK, count=count),
-        grid_spec=pltpu.PrefetchScalarGridSpec(
-            num_scalar_prefetch=2,
-            grid=(1,),
-            in_specs=[pl.BlockSpec(memory_space=pltpu.SMEM), vmem, vmem]
-            + [field(a) for a in range(aper) for _ in range(2)]
-            + [vmem] * len(slabs),
-            out_specs=pl.BlockSpec(shape, lambda i, t, s: (0,) * len(shape)),
-            scratch_shapes=[
-                pltpu.VMEM((aper,) + slabs[0].shape[:3] + (BLOCK,), jnp.float32),
-                pltpu.VMEM((aper, height, BLOCK), jnp.float32),
-            ],
-        ),
+        in_specs=[smem] * 3 + [vmem] * (3 + len(slabs)),
+        out_specs=vmem,
         out_shape=jax.ShapeDtypeStruct(shape, jnp.float32),
+        scratch_shapes=[
+            pltpu.VMEM((aper,) + slabs[0].shape[:3] + (BLOCK,), jnp.float32),
+            pltpu.VMEM((aper, height, BLOCK), jnp.float32),
+        ],
         cost_estimate=pl.CostEstimate(
             flops=aper * BLOCK * height * freqs * steps * 4 * 2 * 4 * BLOCK * 3, bytes_accessed=1 << 21, transcendentals=0
         ),
         compiler_params=pltpu.CompilerParams(vmem_limit_bytes=VMEM),
-    )(tiles, slot, turns, wx, wy, *[v for _ in range(aper) for v in (src, rcv)], *slabs)
+    )(tiles, places, turns, wx, wy, wanted, *slabs)
 
 
 def deal_body(tiles, parts, out):
@@ -227,6 +265,7 @@
         in_specs=[pl.BlockSpec(memory_space=pltpu.SMEM), pl.BlockSpec(memory_space=pltpu.VMEM)],
         out_specs=pl.BlockSpec(memory_space=pltpu.VMEM),
         out_shape=jax.ShapeDtypeStruct((shots, rows, BLOCK), jnp.float32),
+        compiler_params=pltpu.CompilerParams(vmem_limit_bytes=VMEM),
     )(tiles, pltpu.with_memory_space_constraint(parts, pltpu.VMEM))
 
 
@@ -252,6 +291,7 @@
         in_specs=[pl.BlockSpec(memory_space=pltpu.SMEM), pl.BlockSpec(memory_space=pltpu.VMEM)],
         out_specs=pl.BlockSpec(memory_space=pltpu.VMEM),
         out_shape=jax.ShapeDtypeStruct((entries.shape[0], steps, length), jnp.float32),
+        compiler_params=pltpu.CompilerParams(vmem_limit_bytes=VMEM),
     )(entries, pltpu.with_memory_space_constraint(parts, pltpu.VMEM))
 
 
@@ -282,6 +322,7 @@
         out_specs=pl.BlockSpec(memory_space=pltpu.VMEM),
         out_shape=jax.ShapeDtypeStruct((zls, xs, CORES, rows, cols), slab.dtype),
         scratch_shapes=[pltpu.SemaphoreType.DMA((xs + 1,))],
+        compiler_params=pltpu.CompilerParams(vmem_limit_bytes=VMEM),
     )(y, slab)
 
 
@@ -386,31 +427,38 @@
     src = pltpu.with_memory_space_constraint(source_field, pltpu.HBM)
     rcv = pltpu.with_memory_space_constraint(receiver_field, pltpu.HBM)
 
-    def forward(places, slabs, done=()):
-        return march(jnp.stack(places).astype(jnp.int32), turns, slabs, wx, wy, src, rcv, tuple(done))
+    tiles = apertures[0]
+    order = [
+        (place(0), partner_place(0)),
+        (place(1), place(3)),
+        (partner_place(1), partner_place(3)),
+        (place(2), partner_place(2)),
+    ]
+    order = [jnp.stack(p).astype(jnp.int32) for p in order]
+    firsts, wanted = fetch(jnp.stack([p[0] for p in order]), tiles, src, rcv, cols)
+
+    def forward(call, slabs, done=()):
+        return march(order[call], turns, slabs, wx, wy, firsts[call], src, rcv, tuple(done))
 
     own_p = send(own, swap)
     s1, s3 = send(own, shift(1)), send(own, shift(3))
-    fields = forward([place(0), partner_place(0)], [own, own_p])
+    fields = forward(0, [own, own_p])
     s1, s3, later, *fields = lax.optimization_barrier((s1, s3, own, *fields))
     s2 = send(later, shift(2))
     s1_p, s3_p = send(s1, swap), send(s3, swap)
-    fields = forward([place(1), place(3)], [s1, s3], fields)
+    fields = forward(1, [s1, s3], fields)
     s2, *fields = lax.optimization_barrier((s2, *fields))
     s2_p = send(s2, swap)
 
-    tiles = apertures[0]
-    held = lax.div(tiles * (width // (TILE_DEV * shots)), cols)
-    slabs = [own, own_p, s1, s3, s2, s1_p, s3_p, s2_p]
-    places = jnp.stack([place(0), partner_place(0), place(1), place(3), place(2)] + [partner_place(k) for k in (1, 3, 2)])
-    slot = jnp.argmax(places[None, :] == held[:, None], axis=1).astype(jnp.int32)
-    terms = image_terms(tiles, slot, turns, wx, wy, src, rcv, slabs, 1.0 / freq_total, freqs_dev)
+    slabs = [own, own_p, s1, s3, s1_p, s3_p, s2, s2_p]
+    places = jnp.concatenate(order)
+    terms = image_terms(tiles, places, turns, wx, wy, wanted, slabs, 1.0 / freq_total, freqs_dev)
     length = terms.shape[3] * terms.shape[4]
     terms = lax.all_to_all(terms.reshape(freqs_dev, -1, BLOCK), "freq", 0, 0, tiled=True)
-    fields = forward([partner_place(1), partner_place(3)], [s1_p, s3_p], fields)
+    fields = forward(2, [s1_p, s3_p], fields)
     terms, *fields = lax.optimization_barrier((terms, *fields))
     dealt = lax.all_to_all(deal(tiles, terms, shots), "shot", 0, 0, tiled=True)
-    fields = forward([place(2), partner_place(2)], [s2, s2_p], fields)
+    fields = forward(3, [s2, s2_p], fields)
     entries = lax.dynamic_slice_in_dim(tile_order, s_id * TILE_DEV, TILE_DEV)
     image = collect(entries, dealt, tiles.shape[0], DEPTH, length)
     return (*fields, image)

time: 92.3 us -> 92.7 us (level)
  waiting for transfers between devices: 11.8 us -> 9.6 us
  local copies, waits for them, and re-layouts: 4.1 us -> 6.12 us
  Pallas kernels: 39.9 us -> 41.5 us
    all_to_all x1, waiting for transfers between devices: 7.34 us -> 4.11 us  [local(): own = lax.all_to_all(own, AXES, 0, 0, axis_index_groups=groups, tiled=True)]
    unnamed x10 -> x18, local copies, waits for them, and re-layouts: 0.26 us -> 2.91 us
    pallas_call x4 -> x5, Pallas kernels: 31.1 us -> 32.8 us  [the longest x4 30.4 us: march(): pl.pallas_call(functools.partial(march_body, count=count, freqs=freqs), g...]
  transfers between devices with their start and end apart: 11 -> 11, of which waited for: 3 -> 3; matrix products, arithmetic and copies ran while one was open for 5% -> 3% of each run, Pallas kernels for 34% -> 36%
where the time goes in v6:
time: 92.7 us; the launch traced here: 91.9 us
  Pallas kernels  41.5 us (45%)
  starting transfers between devices  29.7 us (32%)
  waiting for transfers between devices  9.6 us (10%)
  local copies, waits for them, and re-layouts  6.12 us (7%)
  between operations  4.51 us (5%)
    pallas_call x4, Pallas kernels, march(): pl.pallas_call(functools.partial(march_body, count=count, freqs=freqs), g...  30.4 us
    ppermute x7, starting transfers between devices, local(): lax.ppermute(v, AXES, pairs((freqs_dev, shots), move))  7.22 us
    all_to_all x1, starting transfers between devices, local(): arrived = lax.all_to_all(outgoing, 'shot', 0, 0, tiled=True)  7.18 us
    all_to_all x1, starting transfers between devices, local(): lax.all_to_all(terms.reshape(freqs_dev, -1, BLOCK), 'freq', 0, 0, tiled=T...  6.22 us
    all_to_all x1, starting transfers between devices, local(): own = lax.all_to_all(own, AXES, 0, 0, axis_index_groups=groups, tiled=True)  4.81 us
    all_to_all x1, starting transfers between devices, local(): dealt = lax.all_to_all(deal(tiles, terms, shots), 'shot', 0, 0, tiled=True)  4.29 us
    pallas_call x1, Pallas kernels, image_terms(): pl.pallas_call(functools.partial(image_body, scale=scale, per=cols // BLO...  4.21 us
    all_to_all x1, waiting for transfers between devices, local(): own = lax.all_to_all(own, AXES, 0, 0, axis_index_groups=groups, tiled=True)  4.11 us
  transfers between devices with their start and end apart: 11, of which 3 were waited for; matrix products, arithmetic and copies ran while one was open for 3% of the time, Pallas kernels for 36%

profile of v6, /device:TPU:1, one launch (start us, length us, event | category | flops | bytes accessed | tf_op | source)
XLA Modules:
  0.0 91.9 jit_solution(10642646236069883410)
XLA Ops:
  0.6 0.0 copy-start
  0.7 1.9 %shard_map.113 = f32[2,4,2,16,512]{4,3,2,1,0:T(8,128)} custom-call(s32[1]{0:T(128)} %bitcast.14.spot, f32[2,4,16,4096]{3,2,1,0:T(8,128)} %bitcast.35), custom_call_target="tpu_custom_call" | custom-call | tf_op jit(solution)/shard_map/pallas_call | solution.py:319
  2.5 7.2 %all-to-all-start = ((f32[16,16,512]{2,1,0:T(8,128)}), f32[16,16,512]{2,1,0:T(8,128)S(1)}, u32[]{:S(2)}, u32[]{:S(2)}) async-start(f32[16,16,512]{2,1,0:T(8,128)} %bitcast.16), calls=%async_computation | async-start | bytes 1048576 | tf_op jit(solution)/shard_map/all_to_all | solution.py:411
  9.7 1.3 %fusion.2 = (s32[1]{0:T(128)}, s32[1]{0:T(128)}) fusion(s32[2]{0:T(128)} %param.15), kind=kLoop, calls=%fused_computation.16 | loop fusion | bytes 16 | tf_op jit(solution)/shard_map/slice | solution.py:412
  14.7 0.1 pad_add_fusion.2.where
  14.8 0.1 pad_add_fusion.3.where
  14.8 0.9 fusion.1
  15.7 3.9 %all-to-all-done = f32[16,16,512]{2,1,0:T(8,128)S(1)} async-done(((f32[16,16,512]{2,1,0:T(8,128)}), f32[16,16,512]{2,1,0:T(8,128)S(1)}, u32[]{:S(2)}, u32[]{:S(2)}) %all-to-all-start) | async-done | bytes 524320 | tf_op jit(solution)/shard_map/all_to_all | solution.py:411
  19.6 0.9 broadcast_in_dim.10
  20.5 4.8 %all-to-all-start.1 = ((f32[8,2,16,512]{3,2,1,0:T(8,128)}), f32[8,2,16,512]{3,2,1,0:T(8,128)S(1)}, u32[]{:S(2)}, u32[]{:S(2)}) async-start(f32[8,2,16,512]{3,2,1,0:T(8,128)} %broadcast_in_dim.10), calls=%async_computation.1 | async-start | bytes 1048576 | tf_op jit(solution)/shard_map/all_to_all | solution.py:417
  25.3 0.1 pad_add_fusion.1.blocks
  25.3 0.1 copy.24
  25.5 0.1 copy.25
  25.6 0.0 copy-done
  25.6 0.0 copy-start.5
  25.6 0.0 copy-start.6
  25.6 2.3 %shard_map.112 = (bf16[2,2,128,512]{3,2,1,0:T(8,128)(2,1)S(1)}, bf16[2,2,128,512]{3,2,1,0:T(8,128)(2,1)S(1)}, bf16[2,2,128,512]{3,2,1,0:T(8,128)(2,1)S(1)}, bf16...) custom-call(s32[4]{0:T(128)S(1)} %pad_add_fusion.1.blocks, s32[2]{0:T(128)S(1)} %bitcast.32, ...), custom_call_target="tpu_custom_call" | custom-call | bytes 8388608 | tf_op jit(solution)/shard_map/pallas_call | solution.py:105
  28.0 0.0 copy-start.1
  28.0 0.8 copy-done.1
  28.8 0.0 copy-start.3
  28.8 0.8 copy-done.3
  29.6 0.0 copy-done.5
  29.6 4.1 %all-to-all-done.1.rest_0_ = f32[8,2,16,512]{3,2,1,0:T(8,128)S(1)} async-done(((f32[8,2,16,512]{3,2,1,0:T(8,128)}), f32[8,2,16,512]{3,2,1,0:T(8,128)S(1)}, u32[]{:S(2)}, u32[]{:S(2)}) %all-to-all-start.1) | async-done | bytes 524320 | tf_op jit(solution)/shard_map/all_to_all | solution.py:417
  33.7 0.9 collective-permute-start.2
  34.6 0.1 maximum_maximum_fusion
  34.7 0.0 copy-done.6
  34.7 0.3 collective-permute-start
  35.0 2.4 %collective-permute-start.1 = (f32[8,2,16,512]{3,2,1,0:T(8,128)S(1)}, f32[8,2,16,512]{3,2,1,0:T(8,128)}, u32[]{:S(2)}, u32[]{:S(2)}) collective-permute-start(f32[8,2,16,512]{3,2,1,0:T(8,128)S(1)} %all-to-all-done.1.rest_0_), channel_id=1, source_target_pairs={{0,48},{1,7},{2,50},{3,1},{4,52},{5,3},{6,54},{7,5},{8,56},{9,15},... | collective-permute-start | bytes 1572872 | tf_op jit(solution)/shard_map/ppermute | solution.py:408
  37.4 0.0 collective-permute-done.2.rest_1_
  37.4 0.0 copy-start.4
  37.4 1.0 %copy-done.4 = bf16[2,2,128,512]{3,2,1,0:T(8,128)(2,1)S(1)} copy-done((bf16[2,2,128,512]{3,2,1,0:T(8,128)(2,1)S(1)}, bf16[2,2,128,512]{3,2,1,0:T(8,128)(2,1)}, u32[]{:S(2)}) %copy-start.4) | copy-done | bytes 524312
  38.5 0.0 copy-start.2
  38.5 7.1 %shard_map.114 = (bf16[2,1,2,128,4096]{4,3,2,1,0:T(8,128)(2,1)}, bf16[2,1,2,128,4096]{4,3,2,1,0:T(8,128)(2,1)}) custom-call(s32[2]{0:T(128)S(1)} %pad_add_fusion.2.where, f32[2]{0:T(128)S(1)} %broadcast_multiply_fusion.turns, bf16[2,256,256]{2,1,0:T(8,128)(2,1)S(1)} %get-tuple-element.59.wx, bf16[2,256,256]{2,1,0:T(8,128)(2,1)S(1)} %get-tuple-element.60.wy, ...), custom_call_target="tpu_custom_call" | custom-call | flops 6442450944 | bytes 4194304 | tf_op jit(solution)/shard_map/pallas_call | solution.py:179
  45.6 0.0 collective-permute-done.rest_0_.rest_2_
  45.6 0.0 collective-permute-done.1.rest_1_.rest_3_
  45.7 0.3 collective-permute-start.3
  46.0 1.9 %collective-permute-start.5 = (f32[8,2,16,512]{3,2,1,0:T(8,128)}, f32[8,2,16,512]{3,2,1,0:T(8,128)}, u32[]{:S(2)}, u32[]{:S(2)}) collective-permute-start(f32[8,2,16,512]{3,2,1,0:T(8,128)} %collective-permute-done.rest_0_.rest_2_), channel_id=1, source_target_pairs={{0,1},{1,0},{2,3},{3,2},{4,5},{5,4},{6,7},{7,6},{8,9},{9,8},{10,11... | collective-permute-start | bytes 1572872 | tf_op jit(solution)/shard_map/ppermute | solution.py:408
  47.9 0.0 collective-permute-start.6
  47.9 0.0 copy-done.2
  47.9 0.0 copy-start.7
  47.9 7.8 %shard_map.115 = (bf16[2,1,2,128,4096]{4,3,2,1,0:T(8,128)(2,1)}, bf16[2,1,2,128,4096]{4,3,2,1,0:T(8,128)(2,1)}) custom-call(s32[2]{0:T(128)S(1)} %pad_add_fusion.3.where, f32[2]{0:T(128)S(1)} %broadcast_multiply_fusion.turns, bf16[2,256,256]{2,1,0:T(8,128)(2,1)S(1)} %get-tuple-element.59.wx, ...), custom_call_target="tpu_custom_call", output_to_operand_aliasing={{0}: (9, {}), {1}: (10, {})} | custom-call | flops 6442450944 | bytes 4194304 | tf_op jit(solution)/shard_map/pallas_call | solution.py:179
  55.6 0.0 collective-permute-done.3.rest_6_.rest_0_
  55.7 1.4 %collective-permute-start.4 = (f32[8,2,16,512]{3,2,1,0:T(8,128)}, f32[8,2,16,512]{3,2,1,0:T(8,128)}, u32[]{:S(2)}, u32[]{:S(2)}) collective-permute-start(f32[8,2,16,512]{3,2,1,0:T(8,128)} %collective-permute-done.3.rest_6_.rest_0_), channel_id=1, source_target_pairs={{0,1},{1,0},{2,3},{3,2},{4,5},{5,4},{6,7},{7,6},{8,9},{9,8},{10,11... | collective-permute-start | bytes 1572872 | tf_op jit(solution)/shard_map/ppermute | solution.py:408
  57.1 0.1 concatenate.28.places
  57.2 0.0 copy-done.7
  57.2 0.1 dynamic_slice.12.entries
  57.2 0.1 pad_add_fusion.where
  57.3 0.1 pad_add_fusion.4.where
  57.4 0.0 collective-permute-done.5.rest_4_.rest_0_
  57.4 0.0 collective-permute-done.6.rest_5_.rest_1_
  57.4 1.6 %collective-permute-done.4.rest_7_.rest_1_ = f32[8,2,16,512]{3,2,1,0:T(8,128)} collective-permute-done((f32[8,2,16,512]{3,2,1,0:T(8,128)}, f32[8,2,16,512]{3,2,1,0:T(8,128)}, u32[]{:S(2)}, u32[]{:S(2)}) %collective-permute-start.4) | collective-permute-done | bytes 524320 | tf_op jit(solution)/shard_map/ppermute | solution.py:408
  59.0 4.2 %shard_map.116 = f32[8,2,2,8,128]{4,3,2,1,0:T(8,128)} custom-call(s32[2]{0:T(128)S(1)} %bitcast.33, s32[8]{0:T(128)S(1)} %concatenate.28.places, f32[2]{0:T(128)S(1)} %broadcast_multiply_fusion.turns, bf16[2,256,256]{2,1,0:T(8,128)(2,1)S(1)} %get-tuple-element.59.wx, bf16[2,256,256]{2,1,0:T(8,128)(2,1)S(1)} %get-tuple-element.60.wy, ...), custom_call_target="tpu_custom_call" | custom-call | flops 1610612736 | bytes 2097152 | tf_op jit(solution)/shard_map/pallas_call | solution.py:236
  63.2 6.2 %all-to-all-start.2 = ((f32[8,32,128]{2,1,0:T(8,128)}), f32[8,32,128]{2,1,0:T(8,128)S(1)}, u32[]{:S(2)}, u32[]{:S(2)}) async-start(f32[8,32,128]{2,1,0:T(8,128)} %bitcast.22), calls=%async_computation.2 | async-start | bytes 262144 | tf_op jit(solution)/shard_map/all_to_all | solution.py:457
  69.4 7.8 %shard_map.117 = (bf16[2,1,2,128,4096]{4,3,2,1,0:T(8,128)(2,1)}, bf16[2,1,2,128,4096]{4,3,2,1,0:T(8,128)(2,1)}) custom-call(s32[2]{0:T(128)S(1)} %pad_add_fusion.4.where, f32[2]{0:T(128)S(1)} %broadcast_multiply_fusion.turns, bf16[2,256,256]{2,1,0:T(8,128)(2,1)S(1)} %get-tuple-element.59.wx, ...), custom_call_target="tpu_custom_call", output_to_operand_aliasing={{0}: (9, {}), {1}: (10, {})} | custom-call | flops 6442450944 | bytes 4194304 | tf_op jit(solution)/shard_map/pallas_call | solution.py:179
  77.2 0.0 all-to-all-done.2.parts
  77.2 1.3 %shard_map.119 = f32[16,40,128]{2,1,0:T(8,128)} custom-call(s32[2]{0:T(128)S(1)} %bitcast.34, f32[8,32,128]{2,1,0:T(8,128)S(1)} %all-to-all-done.2.parts), custom_call_target="tpu_custom_call" | custom-call | tf_op jit(solution)/shard_map/pallas_call | solution.py:263
  78.5 4.3 %all-to-all-start.3 = ((f32[16,40,128]{2,1,0:T(8,128)}), f32[16,40,128]{2,1,0:T(8,128)S(1)}, u32[]{:S(2)}, u32[]{:S(2)}) async-start(f32[16,40,128]{2,1,0:T(8,128)} %shard_map.119), calls=%async_computation.3 | async-start | bytes 655360 | tf_op jit(solution)/shard_map/all_to_all | solution.py:460
  82.8 7.8 %shard_map.118 = (bf16[2,1,2,128,4096]{4,3,2,1,0:T(8,128)(2,1)}, bf16[2,1,2,128,4096]{4,3,2,1,0:T(8,128)(2,1)}) custom-call(s32[2]{0:T(128)S(1)} %pad_add_fusion.where, f32[2]{0:T(128)S(1)} %broadcast_multiply_fusion.turns, bf16[2,256,256]{2,1,0:T(8,128)(2,1)S(1)} %get-tuple-element.59.wx, ...), custom_call_target="tpu_custom_call", output_to_operand_aliasing={{0}: (9, {}), {1}: (10, {})} | custom-call | flops 6442450944 | bytes 4194304 | tf_op jit(solution)/shard_map/pallas_call | solution.py:179
  90.5 0.0 all-to-all-done.3.parts
  90.5 1.4 %shard_map.120 = f32[4,2,1024]{2,1,0:T(2,128)} custom-call(s32[4]{0:T(128)S(1)} %dynamic_slice.12.entries, f32[16,40,128]{2,1,0:T(8,128)S(1)} %all-to-all-done.3.parts), custom_call_target="tpu_custom_call" | custom-call | tf_op jit(solution)/shard_map/pallas_call | solution.py:289
  (6 shorter events, 0.0 us)
Async XLA Ops:
  0.6 25.0 %copy-start = (s32[1,2]{1,0:T(1,128)S(1)}, s32[1,2]{1,0:T(1,128)}, u32[]{:S(2)}) copy-start(s32[1,2]{1,0:T(1,128)} %param.16) | copy-start | bytes 28
  2.5 17.1 %all-to-all-start = ((f32[16,16,512]{2,1,0:T(8,128)}), f32[16,16,512]{2,1,0:T(8,128)S(1)}, u32[]{:S(2)}, u32[]{:S(2)}) async-start(f32[16,16,512]{2,1,0:T(8,128)} %bitcast.16), calls=%async_computation | async-start | bytes 1048576 | tf_op jit(solution)/shard_map/all_to_all | solution.py:411
  20.5 13.3 %all-to-all-start.1 = ((f32[8,2,16,512]{3,2,1,0:T(8,128)}), f32[8,2,16,512]{3,2,1,0:T(8,128)S(1)}, u32[]{:S(2)}, u32[]{:S(2)}) async-start(f32[8,2,16,512]{3,2,1,0:T(8,128)} %broadcast_in_dim.10), calls=%async_computation.1 | async-start | bytes 1048576 | tf_op jit(solution)/shard_map/all_to_all | solution.py:417
  25.6 4.0 %copy-start.5 = (bf16[2,2,128,128]{3,2,1,0:T(8,128)(2,1)S(1)}, bf16[2,2,128,128]{3,2,1,0:T(8,128)(2,1)}, u32[]{:S(2)}) copy-start(bf16[2,2,128,128]{3,2,1,0:T(8,128)(2,1)} %param.12) | copy-start | bytes 393220
  25.6 9.0 %copy-start.6 = (f32[2]{0:T(128)S(1)}, f32[2]{0:T(128)}, u32[]{:S(2)}) copy-start(f32[2]{0:T(128)} %param.11) | copy-start | bytes 28
  28.0 0.8 copy-start.1
  28.8 0.8 copy-start.3
  33.7 3.7 %collective-permute-start.2 = (f32[8,2,16,512]{3,2,1,0:T(8,128)S(1)}, f32[8,2,16,512]{3,2,1,0:T(8,128)S(1)}, u32[]{:S(2)}, u32[]{:S(2)}) collective-permute-start(f32[8,2,16,512]{3,2,1,0:T(8,128)S(1)} %all-to-all-done.1.rest_0_), channel_id=1, source_target_pairs={{0,1},{1,0},{2,3},{3,2},{4,5},{5,4},{6,7},{7,6},{8,9},{9,8},{10,11... | collective-permute-start | bytes 1572872 | tf_op jit(solution)/shard_map/ppermute | solution.py:408
  34.7 10.9 %collective-permute-start = (f32[8,2,16,512]{3,2,1,0:T(8,128)S(1)}, f32[8,2,16,512]{3,2,1,0:T(8,128)}, u32[]{:S(2)}, u32[]{:S(2)}) collective-permute-start(f32[8,2,16,512]{3,2,1,0:T(8,128)S(1)} %all-to-all-done.1.rest_0_), channel_id=1, source_target_pairs={{0,16},{1,3},{2,18},{3,5},{4,20},{5,7},{6,22},{7,1},{8,24},{9,11},... | collective-permute-start | bytes 1572872 | tf_op jit(solution)/shard_map/ppermute | solution.py:408
  35.0 10.7 %collective-permute-start.1 = (f32[8,2,16,512]{3,2,1,0:T(8,128)S(1)}, f32[8,2,16,512]{3,2,1,0:T(8,128)}, u32[]{:S(2)}, u32[]{:S(2)}) collective-permute-start(f32[8,2,16,512]{3,2,1,0:T(8,128)S(1)} %all-to-all-done.1.rest_0_), channel_id=1, source_target_pairs={{0,48},{1,7},{2,50},{3,1},{4,52},{5,3},{6,54},{7,5},{8,56},{9,15},... | collective-permute-start | bytes 1572872 | tf_op jit(solution)/shard_map/ppermute | solution.py:408
  37.4 1.0 %copy-start.4 = (bf16[2,2,128,512]{3,2,1,0:T(8,128)(2,1)S(1)}, bf16[2,2,128,512]{3,2,1,0:T(8,128)(2,1)}, u32[]{:S(2)}) copy-start(bf16[2,2,128,512]{3,2,1,0:T(8,128)(2,1)} %copy-done.3) | copy-start | bytes 1572868
  38.5 9.4 %copy-start.2 = (bf16[2,2,128,512]{3,2,1,0:T(8,128)(2,1)S(1)}, bf16[2,2,128,512]{3,2,1,0:T(8,128)(2,1)}, u32[]{:S(2)}) copy-start(bf16[2,2,128,512]{3,2,1,0:T(8,128)(2,1)} %copy-done.1) | copy-start | bytes 1572868
  45.7 10.0 %collective-permute-start.3 = (f32[8,2,16,512]{3,2,1,0:T(8,128)S(1)}, f32[8,2,16,512]{3,2,1,0:T(8,128)}, u32[]{:S(2)}, u32[]{:S(2)}) collective-permute-start(f32[8,2,16,512]{3,2,1,0:T(8,128)S(1)} %all-to-all-done.1.rest_0_), channel_id=1, source_target_pairs={{0,32},{1,5},{2,34},{3,7},{4,36},{5,1},{6,38},{7,3},{8,40},{9,13},... | collective-permute-start | bytes 1572872 | tf_op jit(solution)/shard_map/ppermute | solution.py:408
  46.0 11.4 %collective-permute-start.5 = (f32[8,2,16,512]{3,2,1,0:T(8,128)}, f32[8,2,16,512]{3,2,1,0:T(8,128)}, u32[]{:S(2)}, u32[]{:S(2)}) collective-permute-start(f32[8,2,16,512]{3,2,1,0:T(8,128)} %collective-permute-done.rest_0_.rest_2_), channel_id=1, source_target_pairs={{0,1},{1,0},{2,3},{3,2},{4,5},{5,4},{6,7},{7,6},{8,9},{9,8},{10,11... | collective-permute-start | bytes 1572872 | tf_op jit(solution)/shard_map/ppermute | solution.py:408
  47.9 9.6 %collective-permute-start.6 = (f32[8,2,16,512]{3,2,1,0:T(8,128)}, f32[8,2,16,512]{3,2,1,0:T(8,128)}, u32[]{:S(2)}, u32[]{:S(2)}) collective-permute-start(f32[8,2,16,512]{3,2,1,0:T(8,128)} %collective-permute-done.1.rest_1_.rest_3_), channel_id=1, source_target_pairs={{0,1},{1,0},{2,3},{3,2},{4,5},{5,4},{6,7},{7,6},{8,9},{9,8},{10,11... | collective-permute-start | bytes 1572872 | tf_op jit(solution)/shard_map/ppermute | solution.py:408
  47.9 9.3 %copy-start.7 = (s32[64]{0:T(128)S(1)}, s32[64]{0:T(128)}, u32[]{:S(2)}) copy-start(s32[64]{0:T(128)} %param.17) | copy-start | bytes 772
  55.7 3.3 %collective-permute-start.4 = (f32[8,2,16,512]{3,2,1,0:T(8,128)}, f32[8,2,16,512]{3,2,1,0:T(8,128)}, u32[]{:S(2)}, u32[]{:S(2)}) collective-permute-start(f32[8,2,16,512]{3,2,1,0:T(8,128)} %collective-permute-done.3.rest_6_.rest_0_), channel_id=1, source_target_pairs={{0,1},{1,0},{2,3},{3,2},{4,5},{5,4},{6,7},{7,6},{8,9},{9,8},{10,11... | collective-permute-start | bytes 1572872 | tf_op jit(solution)/shard_map/ppermute | solution.py:408
  63.2 14.0 %all-to-all-start.2 = ((f32[8,32,128]{2,1,0:T(8,128)}), f32[8,32,128]{2,1,0:T(8,128)S(1)}, u32[]{:S(2)}, u32[]{:S(2)}) async-start(f32[8,32,128]{2,1,0:T(8,128)} %bitcast.22), calls=%async_computation.2 | async-start | bytes 262144 | tf_op jit(solution)/shard_map/all_to_all | solution.py:457
  78.5 12.1 %all-to-all-start.3 = ((f32[16,40,128]{2,1,0:T(8,128)}), f32[16,40,128]{2,1,0:T(8,128)S(1)}, u32[]{:S(2)}, u32[]{:S(2)}) async-start(f32[16,40,128]{2,1,0:T(8,128)} %shard_map.119), calls=%async_computation.3 | async-start | bytes 655360 | tf_op jit(solution)/shard_map/all_to_all | solution.py:460

commit v7 on v6

v7 whole, which is shorter than its diff:
```python
import functools
import math

import jax
import jax.numpy as jnp
from jax import lax
from jax.experimental import pallas as pl
from jax.experimental.pallas import tpu as pltpu
from jax.sharding import PartitionSpec as P

DEPTH = 2
TILE_DEV = 4
AXES = ("freq", "shot")
YS = 4
XS = 4
CORES = 2
BLOCK = 128
VMEM = 24 * 1024 * 1024
NEAREST = 12582912.0
SIN = (4.442867755889893, -7.307443618774414, 3.594788074493408, -0.7843739986419678)
COS = (1.4142135381698608, -6.978850841522217, 5.7394609451293945, -1.8835630416870117, 0.31069818139076233)


def poly(u, coefs):
    total = coefs[-1] * u + coefs[-2]
    for c in coefs[-3::-1]:
        total = total * u + c
    return total


def sincos(turns):
    r = turns - ((turns + NEAREST) - NEAREST)
    u = r * r
    s = r * poly(u, SIN)
    c = poly(u, COS)
    return s * c, 1.0 - s * s


def rounded(parts):
    return tuple(v.astype(jnp.bfloat16) for v in parts)


def widened(parts):
    return tuple(v.astype(jnp.float32) for v in parts)


def quad(a, b, c, d):
    return jnp.concatenate([jnp.concatenate([a, b], 1), jnp.concatenate([c, d], 1)], 0)


def advance(parts, phases, wx, wy):
    height, width = parts[0][0].shape
    out = []
    for part, phase in zip(parts, phases):
        sr, si, rr, ri = widened(part)
        sin, cos = sincos(phase)
        out.append(rounded((sr * cos - si * sin, sr * sin + si * cos, rr * cos - ri * sin, rr * sin + ri * cos)))
    prod = jnp.dot(jnp.concatenate([quad(*v) for v in out], 0), wx, preferred_element_type=jnp.float32)
    for b, part in enumerate(out):
        x = prod[b * 2 * height : (b + 1) * 2 * height]
        sr, si, rr, ri = widened(part)
        out[b] = rounded(
            (
                sr + x[:height, :width],
                si + x[:height, width:],
                rr + x[height:, :width],
                ri + x[height:, width:],
            )
        )
    right = jnp.concatenate([quad(v[0], v[2], v[1], v[3]) for v in out], 1)
    prod = jnp.dot(wy, right, preferred_element_type=jnp.float32)
    for b, part in enumerate(out):
        y = prod[:, b * 2 * width : (b + 1) * 2 * width]
        sr, si, rr, ri = widened(part)
        out[b] = (
            sr + y[:height, :width],
            si + y[height:, :width],
            rr + y[:height, width:],
            ri + y[height:, width:],
        )
    return out


def slab_view(slab, d, cols):
    rows = slab[:, d, :, cols]
    return rows.reshape(rows.shape[0] * rows.shape[1], rows.shape[2])


def here():
    f_id, s_id = lax.axis_index("freq"), lax.axis_index("shot")
    return lax.rem(f_id, YS), lax.rem(lax.div(s_id, CORES), XS), lax.rem(s_id, CORES)


def column_blocks(k):
    y, x, core = here()
    first = core == 0
    mine = core * XS + lax.rem(jnp.where(first, y, x) + XS - k, XS)
    theirs = (1 - core) * XS + lax.rem(jnp.where(first, x, y) + XS - k, XS)
    return mine, theirs


def blocks_of(names):
    return [column_blocks(k)[theirs] for k, theirs in names]


def field_copies(src, rcv, target, sems, block, f):
    cols = target.shape[-1]
    at = pl.ds(pl.multiple_of(block * cols, BLOCK), cols)
    return [
        pltpu.make_async_copy(field.at[f, 0, :, :, at], target.at[i], sems.at[i])
        for i, field in enumerate((src, rcv))
    ]


def fetch_body(src, rcv, first, sems, *, name):
    copies = field_copies(src, rcv, first, sems, blocks_of([name])[0], 0)
    for c in copies:
        c.start()
    for c in copies:
        c.wait()


def fetch(name, src, rcv, cols):
    height = src.shape[3]
    hbm = pl.BlockSpec(memory_space=pltpu.HBM)
    return pl.pallas_call(
        functools.partial(fetch_body, name=name),
        in_specs=[hbm, hbm],
        out_specs=pl.BlockSpec(memory_space=pltpu.VMEM),
        out_shape=pltpu.VMEM((2, 2, height, cols), src.dtype),
        scratch_shapes=[pltpu.SemaphoreType.DMA((2,))],
        cost_estimate=pl.CostEstimate(flops=0, bytes_accessed=1 << 22, transcendentals=0),
        compiler_params=pltpu.CompilerParams(vmem_limit_bytes=VMEM),
    )(src, rcv)


def march_body(turns, wx, wy, src, rcv, *rest, names, freqs, given):
    count = len(names)
    slabs, rest = rest[:count], rest[count:]
    so, ro, held, made, in_sems, out_sems = rest[-6:]
    cols = [slice(c, c + BLOCK) for c in range(0, held.shape[-1], BLOCK)]
    unit = pl.program_id(0)
    units = count * freqs
    where = blocks_of(names)
    slot = lax.rem(unit, 2)

    def block_of(u):
        block, i = where[0], lax.div(u, freqs)
        for k in range(1, count):
            block = jnp.where(i == k, where[k], block)
        return block

    def loads(u):
        at = lax.rem(u, 2)
        return field_copies(src, rcv, held.at[at], in_sems.at[at], block_of(u), lax.rem(u, freqs))

    def stores(u):
        at = lax.rem(u, 2)
        width = made.shape[-1]
        spot = pl.ds(pl.multiple_of(block_of(u) * width, BLOCK), width)
        return [
            pltpu.make_async_copy(made.at[at, i], field.at[lax.rem(u, freqs), 0, :, :, spot], out_sems.at[at, i])
            for i, field in enumerate((so, ro))
        ]

    def each(copies, what):
        for c in copies:
            c.start() if what == "start" else c.wait()

    if not given:

        @pl.when(unit == 0)
        def _():
            each(loads(unit), "start")

    @pl.when(unit + 1 < units)
    def _():
        each(loads(unit + 1), "start")

    if given:
        first = rest[0]

        @pl.when(unit == 0)
        def _():
            held[0] = first[...]

        @pl.when(unit > 0)
        def _():
            each(loads(unit), "wait")

    else:
        each(loads(unit), "wait")

    @pl.when(unit >= 2)
    def _():
        each(stores(unit - 2), "wait")

    f = lax.rem(unit, freqs)

    def run(slab):
        parts = [
            (held[slot, 0, 0, :, c], held[slot, 0, 1, :, c], held[slot, 1, 0, :, c], -held[slot, 1, 1, :, c])
            for c in cols
        ]
        turn = turns[f]
        for d in range(slab.shape[1]):
            parts = advance(parts, [slab_view(slab, d, c) * turn for c in cols], wx[f], wy[f])
        for (sr, si, rr, ri), c in zip(parts, cols):
            made[slot, 0, 0, :, c] = sr.astype(made.dtype)
            made[slot, 0, 1, :, c] = si.astype(made.dtype)
            made[slot, 1, 0, :, c] = rr.astype(made.dtype)
            made[slot, 1, 1, :, c] = (-ri).astype(made.dtype)

    for k, slab in enumerate(slabs):

        @pl.when(lax.div(unit, freqs) == k)
        def _():
            run(slab)

    each(stores(unit), "start")

    @pl.when(unit == units - 1)
    def _():
        if units > 1:
            each(stores(unit - 1), "wait")
        each(stores(unit), "wait")


def march(names, turns, slabs, wx, wy, src, rcv, first=None, done=()):
    count, cols = len(slabs), slabs[0].shape[-1]
    freqs, height = src.shape[0], src.shape[3]
    vmem, hbm = pl.BlockSpec(memory_space=pltpu.VMEM), pl.BlockSpec(memory_space=pltpu.HBM)
    given = first is not None
    args = [turns, wx, wy, src, rcv, *slabs] + [first] * given
    in_specs = [vmem, vmem, vmem, hbm, hbm] + [vmem] * (count + given)
    cells = count * cols * height * freqs
    return pl.pallas_call(
        functools.partial(march_body, names=names, freqs=freqs, given=given),
        grid=(count * freqs,),
        in_specs=in_specs + [hbm] * len(done),
        out_specs=[hbm, hbm],
        scratch_shapes=[
            pltpu.VMEM((2, 2, 2, height, cols), src.dtype),
            pltpu.VMEM((2, 2, 2, height, cols), src.dtype),
            pltpu.SemaphoreType.DMA((2, 2)),
            pltpu.SemaphoreType.DMA((2, 2)),
        ],
        out_shape=[jax.ShapeDtypeStruct(src.shape, src.dtype), jax.ShapeDtypeStruct(rcv.shape, rcv.dtype)],
        input_output_aliases={len(args) + i: i for i in range(len(done))},
        cost_estimate=pl.CostEstimate(
            flops=cells * DEPTH * 4 * 2 * 4 * BLOCK * 3, bytes_accessed=cells * 16, transcendentals=0
        ),
        compiler_params=pltpu.CompilerParams(vmem_limit_bytes=VMEM),
    )(*args, *done)


def image_body(tiles, turns, wx, wy, src, rcv, *rest, names, scale, per, count):
    slabs, out, wanted, held, lines, sems = rest[:-5], *rest[-5:]
    aper = tiles.shape[0]
    x_blocks = [lax.div(tiles[a], 2) for a in range(aper)]
    copies = []
    for a in range(aper):
        at = pl.ds(pl.multiple_of(x_blocks[a] * BLOCK, BLOCK), BLOCK)
        for i, field in enumerate((src, rcv)):
            copies.append(pltpu.make_async_copy(field.at[:, 0, :, :, at], wanted.at[a, i], sems.at[a, i]))
    for c in copies:
        c.start()
    places = blocks_of(names)
    for a in range(aper):
        column = pl.multiple_of(lax.rem(x_blocks[a], per) * BLOCK, BLOCK)
        for k, slab in enumerate(slabs):

            @pl.when(places[k] == lax.div(x_blocks[a], per))
            def _():
                held[a] = slab[:, :, :, pl.ds(column, BLOCK)]

    for c in copies:
        c.wait()
    freqs = wanted.shape[2]
    parts = [
        [(wanted[a, 0, f, 0], wanted[a, 0, f, 1], wanted[a, 1, f, 0], -wanted[a, 1, f, 1]) for a in range(aper)]
        for f in range(freqs)
    ]
    half = BLOCK // 2
    for d in range(held.shape[2]):
        views = [slab_view(held.at[a], d, slice(0, BLOCK)) for a in range(aper)]
        parts = [advance(parts[f], [v * turns[f] for v in views], wx[f], wy[f]) for f in range(freqs)]
        for a in range(aper):
            term = sum(sr * rr - si * ri for sr, si, rr, ri in (p[a] for p in parts))
            odd = lax.rem(tiles[a], 2) == 1
            lines[a, :, :half] = jnp.where(odd, term[:, half:], term[:, :half]) * scale
            pairs_of = lines.shape[1] // 2
            even_odd = [lines[a, pl.ds(k, pairs_of, stride=2), :half] for k in range(2)]
            both = jnp.concatenate(even_odd, 1)
            out[:, a, d] = both.reshape(count, pairs_of // count, BLOCK)


def image_terms(tiles, names, turns, wx, wy, src, rcv, slabs, scale, count):
    steps, cols = slabs[0].shape[1], slabs[0].shape[-1]
    freqs, _, _, height, _ = src.shape
    aper = tiles.shape[0]
    vmem, hbm = pl.BlockSpec(memory_space=pltpu.VMEM), pl.BlockSpec(memory_space=pltpu.HBM)
    shape = (count, aper, steps, height // 2 // count, BLOCK)
    return pl.pallas_call(
        functools.partial(image_body, names=names, scale=scale, per=cols // BLOCK, count=count),
        in_specs=[pl.BlockSpec(memory_space=pltpu.SMEM), vmem, vmem, vmem, hbm, hbm] + [vmem] * len(slabs),
        out_specs=vmem,
        out_shape=jax.ShapeDtypeStruct(shape, jnp.float32),
        scratch_shapes=[
            pltpu.VMEM((aper, 2, freqs, 2, height, BLOCK), src.dtype),
            pltpu.VMEM((aper,) + slabs[0].shape[:3] + (BLOCK,), jnp.float32),
            pltpu.VMEM((aper, height, BLOCK), jnp.float32),
            pltpu.SemaphoreType.DMA((aper, 2)),
        ],
        cost_estimate=pl.CostEstimate(
            flops=aper * BLOCK * height * freqs * steps * 4 * 2 * 4 * BLOCK * 3, bytes_accessed=1 << 21, transcendentals=0
        ),
        compiler_params=pltpu.CompilerParams(vmem_limit_bytes=VMEM),
    )(tiles, turns, wx, wy, src, rcv, *slabs)


def deal_body(ids, parts, out):
    total = jnp.sum(parts[...], axis=0)
    spare = out.shape[1] - total.shape[0] - ids.shape[0]
    total = jnp.concatenate([total, ids[...], jnp.zeros((spare, BLOCK), jnp.float32)], 0)
    for j in range(out.shape[0]):
        out[j] = total


def deal(ids, parts, shots):
    rows = parts.shape[1] + 8
    return pl.pallas_call(
        deal_body,
        in_specs=[pl.BlockSpec(memory_space=pltpu.VMEM)] * 2,
        out_specs=pl.BlockSpec(memory_space=pltpu.VMEM),
        out_shape=jax.ShapeDtypeStruct((shots, rows, BLOCK), jnp.float32),
        compiler_params=pltpu.CompilerParams(vmem_limit_bytes=VMEM),
    )(ids, pltpu.with_memory_space_constraint(parts, pltpu.VMEM))


def collect_body(entries, parts, out, *, aper):
    steps = out.shape[1]
    rows = out.shape[2] // BLOCK
    size = steps * rows
    for p in range(out.shape[0]):
        total = jnp.zeros((size, BLOCK), jnp.float32)
        for s in range(parts.shape[0]):
            for a in range(aper):
                at = aper * size + a
                named = parts[s, at : at + 1] == entries[p : p + 1]
                total += jnp.where(named, parts[s, a * size : (a + 1) * size], 0.0)
        for d in range(steps):
            for r in range(rows):
                out[p, d, r * BLOCK : (r + 1) * BLOCK] = total[d * rows + r]


def collect(entries, parts, aper, steps, length):
    return pl.pallas_call(
        functools.partial(collect_body, aper=aper),
        in_specs=[pl.BlockSpec(memory_space=pltpu.VMEM)] * 2,
        out_specs=pl.BlockSpec(memory_space=pltpu.VMEM),
        out_shape=jax.ShapeDtypeStruct((entries.shape[0], steps, length), jnp.float32),
        compiler_params=pltpu.CompilerParams(vmem_limit_bytes=VMEM),
    )(entries, pltpu.with_memory_space_constraint(parts, pltpu.VMEM))


def cut_body(slab, out, sems, *, cols):
    y = here()[0]
    xs = out.shape[1]
    copies = [
        pltpu.make_async_copy(
            slab.at[:, :, :, pl.ds(pl.multiple_of(y * cols, BLOCK), cols)], out.at[:, :, 0], sems.at[xs]
        )
    ]
    for x in range(xs):
        copies.append(
            pltpu.make_async_copy(slab.at[:, y, :, pl.ds((xs + x) * cols, cols)], out.at[:, x, 1], sems.at[x])
        )
    for c in copies:
        c.start()
    for c in copies:
        c.wait()


def cut(slab, cols):
    zls, xs, rows, _ = slab.shape
    slab = pltpu.with_memory_space_constraint(slab, pltpu.HBM)
    return pl.pallas_call(
        functools.partial(cut_body, cols=cols),
        in_specs=[pl.BlockSpec(memory_space=pltpu.HBM)],
        out_specs=pl.BlockSpec(memory_space=pltpu.VMEM),
        out_shape=jax.ShapeDtypeStruct((zls, xs, CORES, rows, cols), slab.dtype),
        scratch_shapes=[pltpu.SemaphoreType.DMA((xs + 1,))],
        compiler_params=pltpu.CompilerParams(vmem_limit_bytes=VMEM),
    )(slab)


def sweep_weights(xc, yc):
    xr, xi = xc[:, 0], xc[:, 1]
    yr, yi = jnp.swapaxes(yc[:, 0], 1, 2), jnp.swapaxes(yc[:, 1], 1, 2)
    join = lambda a, b, c, d: jnp.concatenate([jnp.concatenate([a, b], 2), jnp.concatenate([c, d], 2)], 1)
    return join(xr, xi, -xi, xr), join(yr, -yi, yi, yr)


def pairs(mesh_shape, move):
    freq, shot = mesh_shape
    at = lambda zh, y, zl, x, c: ((zh * YS + y) * shot) + (zl * XS + x) * CORES + c
    out = []
    for zh in range(freq // YS):
        for y in range(YS):
            for zl in range(shot // (XS * CORES)):
                for x in range(XS):
                    for c in range(CORES):
                        out.append((at(zh, y, zl, x, c), at(*move(zh, y, zl, x, c))))
    return out


def row_groups(mesh_shape):
    freq, shot = mesh_shape
    zhs, zls = freq // YS, shot // (XS * CORES)
    at = lambda zh, y, zl, x, c: ((zh * YS + y) * shot) + (zl * XS + x) * CORES + c
    out = [[at(zh, y, zl, x, 0) for zl in range(zls) for x in range(XS)] for zh in range(zhs) for y in range(YS)]
    return out + [[at(zh, y, zl, x, 1) for zl in range(zls) for y in range(YS)] for zh in range(zhs) for x in range(XS)]


def local(
    source_field,
    receiver_field,
    angular_freq,
    x_correction,
    y_correction,
    velocity,
    slab_owner,
    apertures,
    tile_order,
):
    freqs_dev, shots = lax.axis_size("freq"), lax.axis_size("shot")
    freq_total = angular_freq.shape[0] * freqs_dev
    height, width = velocity.shape[1:]
    zls = shots // (XS * CORES)
    cols = width // (CORES * XS)
    rows = height // (zls * XS)
    send = lambda v, move: lax.ppermute(v, AXES, pairs((freqs_dev, shots), move))

    outgoing = cut(velocity.reshape(zls, XS, rows, width), cols).reshape(shots, rows, cols)
    arrived = lax.all_to_all(outgoing, "shot", 0, 0, tiled=True)
    mine = jnp.stack([lax.dynamic_index_in_dim(arrived, slab_owner[d], 0, keepdims=False) for d in range(DEPTH)])

    groups = row_groups((freqs_dev, shots))
    members = len(groups[0])
    own = jnp.broadcast_to(mine[None], (members,) + mine.shape)
    own = lax.all_to_all(own, AXES, 0, 0, axis_index_groups=groups, tiled=True)

    shift = lambda k: lambda zh, y, zl, x, c: (zh, (y + k) % YS, zl, x, c) if c == 0 else (zh, y, zl, (x + k) % XS, c)
    swap = lambda zh, y, zl, x, c: (zh, y, zl, x, 1 - c)
    wx, wy = sweep_weights(x_correction, y_correction)
    turns = jnp.broadcast_to((angular_freq * (0.5 / math.pi))[:, None, None], (angular_freq.shape[0], 1, BLOCK))
    src = pltpu.with_memory_space_constraint(source_field, pltpu.HBM)
    rcv = pltpu.with_memory_space_constraint(receiver_field, pltpu.HBM)

    order = [[(0, 0), (0, 1)], [(1, 0), (3, 0)], [(1, 1), (3, 1)], [(2, 0), (2, 1)]]
    first = fetch(order[0][0], src, rcv, cols)

    def forward(call, slabs, first=None, done=()):
        return march(order[call], turns, slabs, wx, wy, src, rcv, first, tuple(done))

    own_p = send(own, swap)
    s1, s3 = send(own, shift(1)), send(own, shift(3))
    fields = forward(0, [own, own_p], first)
    s1, s3, later, *fields = lax.optimization_barrier((s1, s3, own, *fields))
    s2 = send(later, shift(2))
    s1_p, s3_p = send(s1, swap), send(s3, swap)
    fields = forward(1, [s1, s3], done=fields)
    s2, *fields = lax.optimization_barrier((s2, *fields))
    s2_p = send(s2, swap)

    rows_of = lambda ids: jnp.broadcast_to(ids.astype(jnp.float32)[:, None], (ids.shape[0], BLOCK))
    slabs = [own, own_p, s1, s3, s1_p, s3_p, s2, s2_p]
    tiles = apertures[0]
    names = [name for names in order for name in names]
    terms = image_terms(tiles, names, turns, wx, wy, src, rcv, slabs, 1.0 / freq_total, freqs_dev)
    length = terms.shape[3] * terms.shape[4]
    terms = lax.all_to_all(terms.reshape(freqs_dev, -1, BLOCK), "freq", 0, 0, tiled=True)
    fields = forward(2, [s1_p, s3_p], done=fields)
    terms, *fields = lax.optimization_barrier((terms, *fields))
    dealt = lax.all_to_all(deal(rows_of(tiles), terms, shots), "shot", 0, 0, tiled=True)
    fields = forward(3, [s2, s2_p], done=fields)
    entries = lax.dynamic_slice_in_dim(tile_order, lax.axis_index("shot") * TILE_DEV, TILE_DEV)
    image = collect(rows_of(entries), dealt, tiles.shape[0], DEPTH, length)
    return (*fields, image)


def solution(mesh):
    in_specs = (
        P("freq", "shot", None, None, None),
        P("freq", "shot", None, None, None),
        P("freq"),
        P("freq", None, None, None),
        P("freq", None, None, None),
        P("shot", None, None),
        P(),
        P("shot", None),
        P(),
    )
    out_specs = (
        P("freq", "shot", None, None, None),
        P("freq", "shot", None, None, None),
        P("shot", None, "freq"),
    )
    return jax.shard_map(local, mesh=mesh, in_specs=in_specs, out_specs=out_specs, check_vma=False)
```

time: 92.7 us -> 92.6 us (level)
  waiting for transfers between devices: 9.6 us -> 13.9 us
  local copies, waits for them, and re-layouts: 6.12 us -> 2.67 us
  Pallas kernels: 41.5 us -> 39.2 us
  starting transfers between devices: 29.7 us -> 31.2 us
    all_to_all x1, waiting for transfers between devices: 4.11 us -> 7 us  [local(): own = lax.all_to_all(own, AXES, 0, 0, axis_index_groups=groups, tiled=True)]
    unnamed x18 -> x12, local copies, waits for them, and re-layouts: 2.91 us -> 0.27 us
    pallas_call x7, Pallas kernels: 38.3 us -> 36.4 us  [the longest x4 29.9 us: march(): pl.pallas_call(functools.partial(march_body, names=names, freqs=freqs, gi...]
    all_to_all x1, starting transfers between devices: 6.22 us -> 7.19 us  [local(): lax.all_to_all(terms.reshape(freqs_dev, -1, BLOCK), 'freq', 0, 0, tiled=T...]
  transfers between devices with their start and end apart: 11 -> 11, of which waited for: 3 -> 4; matrix products, arithmetic and copies ran while one was open for 3% -> 2% of each run, Pallas kernels for 36% -> 34%
where the time goes in v7:
time: 92.6 us; the launch traced here: 91.8 us
  Pallas kernels  39.2 us (42%)
  starting transfers between devices  31.2 us (34%)
  waiting for transfers between devices  13.9 us (15%)
  between operations  4.71 us (5%)
  local copies, waits for them, and re-layouts  2.67 us (3%)
    pallas_call x4, Pallas kernels, march(): pl.pallas_call(functools.partial(march_body, names=names, freqs=freqs, gi...  29.9 us
    ppermute x7, starting transfers between devices, local(): lax.ppermute(v, AXES, pairs((freqs_dev, shots), move))  8.05 us
    all_to_all x1, starting transfers between devices, local(): lax.all_to_all(terms.reshape(freqs_dev, -1, BLOCK), 'freq', 0, 0, tiled=T...  7.19 us
    all_to_all x1, starting transfers between devices, local(): arrived = lax.all_to_all(outgoing, 'shot', 0, 0, tiled=True)  7.18 us
    all_to_all x1, waiting for transfers between devices, local(): own = lax.all_to_all(own, AXES, 0, 0, axis_index_groups=groups, tiled=True)  7 us
    all_to_all x1, starting transfers between devices, local(): own = lax.all_to_all(own, AXES, 0, 0, axis_index_groups=groups, tiled=True)  4.81 us
    pallas_call x1, Pallas kernels, image_terms(): pl.pallas_call(functools.partial(image_body, names=names, scale=scale, pe...  4.7 us
    all_to_all x1, waiting for transfers between devices, local(): arrived = lax.all_to_all(outgoing, 'shot', 0, 0, tiled=True)  4.69 us
  transfers between devices with their start and end apart: 11, of which 4 were waited for; matrix products, arithmetic and copies ran while one was open for 2% of the time, Pallas kernels for 34%

profile of v7, /device:TPU:1, one launch (start us, length us, event | category | flops | bytes accessed | tf_op | source)
XLA Modules:
  0.0 91.8 jit_solution(3176346369906824404)
XLA Ops:
  0.6 0.0 copy-start.2
  0.6 1.9 %shard_map.112 = f32[2,4,2,16,512]{4,3,2,1,0:T(8,128)} custom-call(f32[2,4,16,4096]{3,2,1,0:T(8,128)} %bitcast.25), custom_call_target="tpu_custom_call" | custom-call | tf_op jit(solution)/shard_map/pallas_call | solution.py:388
  2.5 7.2 %all-to-all-start = ((f32[16,16,512]{2,1,0:T(8,128)}), f32[16,16,512]{2,1,0:T(8,128)S(1)}, u32[]{:S(2)}, u32[]{:S(2)}) async-start(f32[16,16,512]{2,1,0:T(8,128)} %bitcast.9), calls=%async_computation | async-start | bytes 1048576 | tf_op jit(solution)/shard_map/all_to_all | solution.py:446
  9.7 1.3 %fusion.2 = (s32[1]{0:T(128)}, s32[1]{0:T(128)}) fusion(s32[2]{0:T(128)} %param.15), kind=kLoop, calls=%fused_computation.13 | loop fusion | bytes 16 | tf_op jit(solution)/shard_map/slice | solution.py:447
  14.9 4.7 %all-to-all-done = f32[16,16,512]{2,1,0:T(8,128)S(1)} async-done(((f32[16,16,512]{2,1,0:T(8,128)}), f32[16,16,512]{2,1,0:T(8,128)S(1)}, u32[]{:S(2)}, u32[]{:S(2)}) %all-to-all-start) | async-done | bytes 524320 | tf_op jit(solution)/shard_map/all_to_all | solution.py:446
  19.6 0.9 broadcast_in_dim.9
  20.5 4.8 %all-to-all-start.1 = ((f32[8,2,16,512]{3,2,1,0:T(8,128)}), f32[8,2,16,512]{3,2,1,0:T(8,128)S(1)}, u32[]{:S(2)}, u32[]{:S(2)}) async-start(f32[8,2,16,512]{3,2,1,0:T(8,128)} %broadcast_in_dim.9), calls=%async_computation.1 | async-start | bytes 1048576 | tf_op jit(solution)/shard_map/all_to_all | solution.py:452
  25.3 0.0 copy-done.2
  25.3 0.1 copy.24
  25.4 0.1 copy.25
  25.6 0.0 copy-start.1
  25.6 0.0 copy-start.3
  25.6 1.1 %shard_map.113.rest_2_ = bf16[2,2,128,512]{3,2,1,0:T(8,128)(2,1)S(1)} custom-call(bf16[2,1,2,128,4096]{4,3,2,1,0:T(8,128)(2,1)} %src.11, bf16[2,1,2,128,4096]{4,3,2,1,0:T(8,128)(2,1)} %rcv.11), custom_call_target="tpu_custom_call" | custom-call | bytes 4194304 | tf_op jit(solution)/shard_map/pallas_call | solution.py:126
  26.7 0.0 copy-done.1
  26.8 7.0 %all-to-all-done.1.rest_0_ = f32[8,2,16,512]{3,2,1,0:T(8,128)S(1)} async-done(((f32[8,2,16,512]{3,2,1,0:T(8,128)}), f32[8,2,16,512]{3,2,1,0:T(8,128)S(1)}, u32[]{:S(2)}, u32[]{:S(2)}) %all-to-all-start.1) | async-done | bytes 524320 | tf_op jit(solution)/shard_map/all_to_all | solution.py:452
  33.8 0.9 collective-permute-start.2
  34.6 0.1 maximum_maximum_fusion
  34.7 0.0 copy-done.3
  34.7 0.3 collective-permute-start
  35.0 2.4 %collective-permute-start.1 = (f32[8,2,16,512]{3,2,1,0:T(8,128)S(1)}, f32[8,2,16,512]{3,2,1,0:T(8,128)S(1)}, u32[]{:S(2)}, u32[]{:S(2)}) collective-permute-start(f32[8,2,16,512]{3,2,1,0:T(8,128)S(1)} %all-to-all-done.1.rest_0_), channel_id=1, source_target_pairs={{0,48},{1,7},{2,50},{3,1},{4,52},{5,3},{6,54},{7,5},{8,56},{9,15},... | collective-permute-start | bytes 1572872 | tf_op jit(solution)/shard_map/ppermute | solution.py:443
  37.5 0.0 collective-permute-done.2.rest_1_
  37.5 0.1 broadcast_in_dim.8.turns
  37.5 6.2 %shard_map.114 = (bf16[2,1,2,128,4096]{4,3,2,1,0:T(8,128)(2,1)}, bf16[2,1,2,128,4096]{4,3,2,1,0:T(8,128)(2,1)}) custom-call(f32[2,1,128]{2,1,0:T(1,128)S(1)} %broadcast_in_dim.8.turns, bf16[2,256,256]{2,1,0:T(8,128)(2,1)S(1)} %get-tuple-element.49.wx, bf16[2,256,256]{2,1,0:T(8,128)(2,1)S(1)} %get-tuple-element.50.wy, bf16[2,1,2,128,4096]{4,3,2,1,0:T(8,128)(2,1)} %src.11, ...), custom_call_target="tpu_custom_call" | custom-call | flops 6442450944 | bytes 4194304 | tf_op jit(solution)/shard_map/pallas_call | solution.py:237
  43.7 0.6 collective-permute-done.rest_0_.rest_2_
  44.3 0.0 collective-permute-done.1.rest_1_.rest_3_
  44.3 0.0 copy-start.4
  44.3 0.0 copy-start
  44.3 1.2 %collective-permute-start.3 = (f32[8,2,16,512]{3,2,1,0:T(8,128)S(1)}, f32[8,2,16,512]{3,2,1,0:T(8,128)S(1)}, u32[]{:S(2)}, u32[]{:S(2)}) collective-permute-start(f32[8,2,16,512]{3,2,1,0:T(8,128)S(1)} %all-to-all-done.1.rest_0_), channel_id=1, source_target_pairs={{0,32},{1,5},{2,34},{3,7},{4,36},{5,1},{6,38},{7,3},{8,40},{9,13},... | collective-permute-start | bytes 1572872 | tf_op jit(solution)/shard_map/ppermute | solution.py:443
  45.5 2.3 %collective-permute-start.5 = (f32[8,2,16,512]{3,2,1,0:T(8,128)S(1)}, f32[8,2,16,512]{3,2,1,0:T(8,128)}, u32[]{:S(2)}, u32[]{:S(2)}) collective-permute-start(f32[8,2,16,512]{3,2,1,0:T(8,128)S(1)} %collective-permute-done.rest_0_.rest_2_), channel_id=1, source_target_pairs={{0,1},{1,0},{2,3},{3,2},{4,5},{5,4},{6,7},{7,6},{8,9},{9,8},{10,11... | collective-permute-start | bytes 1572872 | tf_op jit(solution)/shard_map/ppermute | solution.py:443
  47.8 0.0 collective-permute-start.6
  47.8 7.1 %shard_map.115 = (bf16[2,1,2,128,4096]{4,3,2,1,0:T(8,128)(2,1)}, bf16[2,1,2,128,4096]{4,3,2,1,0:T(8,128)(2,1)}) custom-call(f32[2,1,128]{2,1,0:T(1,128)S(1)} %broadcast_in_dim.8.turns, bf16[2,256,256]{2,1,0:T(8,128)(2,1)S(1)} %get-tuple-element.49.wx, bf16[2,256,256]{2,1,0:T(8,128)(2,1)S(1)} %get-tuple-element.50.wy, ...), custom_call_target="tpu_custom_call", output_to_operand_aliasing={{0}: (7, {}), {1}: (8, {})} | custom-call | flops 6442450944 | bytes 4194304 | tf_op jit(solution)/shard_map/pallas_call | solution.py:237
  54.9 0.0 collective-permute-done.3.rest_6_.rest_0_
  54.9 1.0 %collective-permute-start.4 = (f32[8,2,16,512]{3,2,1,0:T(8,128)S(1)}, f32[8,2,16,512]{3,2,1,0:T(8,128)}, u32[]{:S(2)}, u32[]{:S(2)}) collective-permute-start(f32[8,2,16,512]{3,2,1,0:T(8,128)S(1)} %collective-permute-done.3.rest_6_.rest_0_), channel_id=1, source_target_pairs={{0,1},{1,0},{2,3},{3,2},{4,5},{5,4},{6,7},{7,6},{8,9},{9,8},{10,11... | collective-permute-start | bytes 1572872 | tf_op jit(solution)/shard_map/ppermute | solution.py:443
  56.0 0.0 copy-done.4
  56.0 0.1 dynamic-slice_convert_fusion
  56.0 0.0 copy-done
  56.0 0.0 collective-permute-done.5.rest_4_.rest_0_
  56.0 0.0 collective-permute-done.6.rest_5_.rest_1_
  56.0 1.6 %collective-permute-done.4.rest_7_.rest_1_ = f32[8,2,16,512]{3,2,1,0:T(8,128)} collective-permute-done((f32[8,2,16,512]{3,2,1,0:T(8,128)S(1)}, f32[8,2,16,512]{3,2,1,0:T(8,128)}, u32[]{:S(2)}, u32[]{:S(2)}) %collective-permute-start.4) | collective-permute-done | bytes 524320 | tf_op jit(solution)/shard_map/ppermute | solution.py:443
  57.6 4.7 %shard_map.116 = f32[8,2,2,8,128]{4,3,2,1,0:T(8,128)} custom-call(s32[2]{0:T(128)S(1)} %bitcast.24, f32[2,1,128]{2,1,0:T(1,128)S(1)} %broadcast_in_dim.8.turns, bf16[2,256,256]{2,1,0:T(8,128)(2,1)S(1)} %get-tuple-element.49.wx, bf16[2,256,256]{2,1,0:T(8,128)(2,1)S(1)} %get-tuple-element.50.wy, bf16[2,1,2,128,4096]{4,3,2,1,0:T(8,128)(2,1)} %src.11, ...), custom_call_target="tpu_custom_call" | custom-call | flops 1610612736 | bytes 2097152 | tf_op jit(solution)/shard_map/pallas_call | solution.py:304
  62.3 7.2 %all-to-all-start.2 = ((f32[8,32,128]{2,1,0:T(8,128)}), f32[8,32,128]{2,1,0:T(8,128)S(1)}, u32[]{:S(2)}, u32[]{:S(2)}) async-start(f32[8,32,128]{2,1,0:T(8,128)} %bitcast.13), calls=%async_computation.2 | async-start | bytes 262144 | tf_op jit(solution)/shard_map/all_to_all | solution.py:483
  69.5 8.4 %shard_map.117 = (bf16[2,1,2,128,4096]{4,3,2,1,0:T(8,128)(2,1)}, bf16[2,1,2,128,4096]{4,3,2,1,0:T(8,128)(2,1)}) custom-call(f32[2,1,128]{2,1,0:T(1,128)S(1)} %broadcast_in_dim.8.turns, bf16[2,256,256]{2,1,0:T(8,128)(2,1)S(1)} %get-tuple-element.49.wx, bf16[2,256,256]{2,1,0:T(8,128)(2,1)S(1)} %get-tuple-element.50.wy, ...), custom_call_target="tpu_custom_call", output_to_operand_aliasing={{0}: (7, {}), {1}: (8, {})} | custom-call | flops 6442450944 | bytes 4194304 | tf_op jit(solution)/shard_map/pallas_call | solution.py:237
  77.9 0.0 all-to-all-done.2.parts
  77.9 0.1 broadcast_in_dim.11.ids
  78.0 0.8 shard_map.119
  78.7 4.0 %all-to-all-start.3 = ((f32[16,40,128]{2,1,0:T(8,128)}), f32[16,40,128]{2,1,0:T(8,128)S(1)}, u32[]{:S(2)}, u32[]{:S(2)}) async-start(f32[16,40,128]{2,1,0:T(8,128)} %shard_map.119), calls=%async_computation.3 | async-start | bytes 655360 | tf_op jit(solution)/shard_map/all_to_all | solution.py:486
  82.7 8.2 %shard_map.118 = (bf16[2,1,2,128,4096]{4,3,2,1,0:T(8,128)(2,1)}, bf16[2,1,2,128,4096]{4,3,2,1,0:T(8,128)(2,1)}) custom-call(f32[2,1,128]{2,1,0:T(1,128)S(1)} %broadcast_in_dim.8.turns, bf16[2,256,256]{2,1,0:T(8,128)(2,1)S(1)} %get-tuple-element.49.wx, bf16[2,256,256]{2,1,0:T(8,128)(2,1)S(1)} %get-tuple-element.50.wy, ...), custom_call_target="tpu_custom_call", output_to_operand_aliasing={{0}: (7, {}), {1}: (8, {})} | custom-call | flops 6442450944 | bytes 4194304 | tf_op jit(solution)/shard_map/pallas_call | solution.py:237
  90.9 0.0 all-to-all-done.3.parts
  90.9 0.1 broadcast_in_dim.10.entries
  91.0 0.8 shard_map.120
  (8 shorter events, 0.1 us)
Async XLA Ops:
  0.6 24.7 %copy-start.2 = (bf16[2,2,128,128]{3,2,1,0:T(8,128)(2,1)S(1)}, bf16[2,2,128,128]{3,2,1,0:T(8,128)(2,1)}, u32[]{:S(2)}) copy-start(bf16[2,2,128,128]{3,2,1,0:T(8,128)(2,1)} %param.13) | copy-start | bytes 393220
  2.5 17.1 %all-to-all-start = ((f32[16,16,512]{2,1,0:T(8,128)}), f32[16,16,512]{2,1,0:T(8,128)S(1)}, u32[]{:S(2)}, u32[]{:S(2)}) async-start(f32[16,16,512]{2,1,0:T(8,128)} %bitcast.9), calls=%async_computation | async-start | bytes 1048576 | tf_op jit(solution)/shard_map/all_to_all | solution.py:446
  20.5 13.3 %all-to-all-start.1 = ((f32[8,2,16,512]{3,2,1,0:T(8,128)}), f32[8,2,16,512]{3,2,1,0:T(8,128)S(1)}, u32[]{:S(2)}, u32[]{:S(2)}) async-start(f32[8,2,16,512]{3,2,1,0:T(8,128)} %broadcast_in_dim.9), calls=%async_computation.1 | async-start | bytes 1048576 | tf_op jit(solution)/shard_map/all_to_all | solution.py:452
  25.6 1.1 %copy-start.1 = (bf16[2,2,128,128]{3,2,1,0:T(8,128)(2,1)S(1)}, bf16[2,2,128,128]{3,2,1,0:T(8,128)(2,1)}, u32[]{:S(2)}) copy-start(bf16[2,2,128,128]{3,2,1,0:T(8,128)(2,1)} %param.12) | copy-start | bytes 393220
  25.6 9.1 %copy-start.3 = (f32[2]{0:T(128)S(1)}, f32[2]{0:T(128)}, u32[]{:S(2)}) copy-start(f32[2]{0:T(128)} %param.11) | copy-start | bytes 28
  33.8 3.7 %collective-permute-start.2 = (f32[8,2,16,512]{3,2,1,0:T(8,128)S(1)}, f32[8,2,16,512]{3,2,1,0:T(8,128)S(1)}, u32[]{:S(2)}, u32[]{:S(2)}) collective-permute-start(f32[8,2,16,512]{3,2,1,0:T(8,128)S(1)} %all-to-all-done.1.rest_0_), channel_id=1, source_target_pairs={{0,1},{1,0},{2,3},{3,2},{4,5},{5,4},{6,7},{7,6},{8,9},{9,8},{10,11... | collective-permute-start | bytes 1572872 | tf_op jit(solution)/shard_map/ppermute | solution.py:443
  34.7 9.6 %collective-permute-start = (f32[8,2,16,512]{3,2,1,0:T(8,128)S(1)}, f32[8,2,16,512]{3,2,1,0:T(8,128)S(1)}, u32[]{:S(2)}, u32[]{:S(2)}) collective-permute-start(f32[8,2,16,512]{3,2,1,0:T(8,128)S(1)} %all-to-all-done.1.rest_0_), channel_id=1, source_target_pairs={{0,16},{1,3},{2,18},{3,5},{4,20},{5,7},{6,22},{7,1},{8,24},{9,11},... | collective-permute-start | bytes 1572872 | tf_op jit(solution)/shard_map/ppermute | solution.py:443
  35.0 9.3 %collective-permute-start.1 = (f32[8,2,16,512]{3,2,1,0:T(8,128)S(1)}, f32[8,2,16,512]{3,2,1,0:T(8,128)S(1)}, u32[]{:S(2)}, u32[]{:S(2)}) collective-permute-start(f32[8,2,16,512]{3,2,1,0:T(8,128)S(1)} %all-to-all-done.1.rest_0_), channel_id=1, source_target_pairs={{0,48},{1,7},{2,50},{3,1},{4,52},{5,3},{6,54},{7,5},{8,56},{9,15},... | collective-permute-start | bytes 1572872 | tf_op jit(solution)/shard_map/ppermute | solution.py:443
  44.3 11.6 %copy-start.4 = (s32[64]{0:T(128)S(1)}, s32[64]{0:T(128)}, u32[]{:S(2)}) copy-start(s32[64]{0:T(128)} %param.17) | copy-start | bytes 772
  44.3 11.7 %copy-start = (s32[1,2]{1,0:T(1,128)S(1)}, s32[1,2]{1,0:T(1,128)}, u32[]{:S(2)}) copy-start(s32[1,2]{1,0:T(1,128)} %param.16) | copy-start | bytes 28
  44.3 10.6 %collective-permute-start.3 = (f32[8,2,16,512]{3,2,1,0:T(8,128)S(1)}, f32[8,2,16,512]{3,2,1,0:T(8,128)S(1)}, u32[]{:S(2)}, u32[]{:S(2)}) collective-permute-start(f32[8,2,16,512]{3,2,1,0:T(8,128)S(1)} %all-to-all-done.1.rest_0_), channel_id=1, source_target_pairs={{0,32},{1,5},{2,34},{3,7},{4,36},{5,1},{6,38},{7,3},{8,40},{9,13},... | collective-permute-start | bytes 1572872 | tf_op jit(solution)/shard_map/ppermute | solution.py:443
  45.5 10.5 %collective-permute-start.5 = (f32[8,2,16,512]{3,2,1,0:T(8,128)S(1)}, f32[8,2,16,512]{3,2,1,0:T(8,128)}, u32[]{:S(2)}, u32[]{:S(2)}) collective-permute-start(f32[8,2,16,512]{3,2,1,0:T(8,128)S(1)} %collective-permute-done.rest_0_.rest_2_), channel_id=1, source_target_pairs={{0,1},{1,0},{2,3},{3,2},{4,5},{5,4},{6,7},{7,6},{8,9},{9,8},{10,11... | collective-permute-start | bytes 1572872 | tf_op jit(solution)/shard_map/ppermute | solution.py:443
  47.8 8.3 %collective-permute-start.6 = (f32[8,2,16,512]{3,2,1,0:T(8,128)S(1)}, f32[8,2,16,512]{3,2,1,0:T(8,128)}, u32[]{:S(2)}, u32[]{:S(2)}) collective-permute-start(f32[8,2,16,512]{3,2,1,0:T(8,128)S(1)} %collective-permute-done.1.rest_1_.rest_3_), channel_id=1, source_target_pairs={{0,1},{1,0},{2,3},{3,2},{4,5},{5,4},{6,7},{7,6},{8,9},{9,8},{10,11... | collective-permute-start | bytes 1572872 | tf_op jit(solution)/shard_map/ppermute | solution.py:443
  54.9 2.7 %collective-permute-start.4 = (f32[8,2,16,512]{3,2,1,0:T(8,128)S(1)}, f32[8,2,16,512]{3,2,1,0:T(8,128)}, u32[]{:S(2)}, u32[]{:S(2)}) collective-permute-start(f32[8,2,16,512]{3,2,1,0:T(8,128)S(1)} %collective-permute-done.3.rest_6_.rest_0_), channel_id=1, source_target_pairs={{0,1},{1,0},{2,3},{3,2},{4,5},{5,4},{6,7},{7,6},{8,9},{9,8},{10,11... | collective-permute-start | bytes 1572872 | tf_op jit(solution)/shard_map/ppermute | solution.py:443
  62.3 15.6 %all-to-all-start.2 = ((f32[8,32,128]{2,1,0:T(8,128)}), f32[8,32,128]{2,1,0:T(8,128)S(1)}, u32[]{:S(2)}, u32[]{:S(2)}) async-start(f32[8,32,128]{2,1,0:T(8,128)} %bitcast.13), calls=%async_computation.2 | async-start | bytes 262144 | tf_op jit(solution)/shard_map/all_to_all | solution.py:483
  78.7 12.2 %all-to-all-start.3 = ((f32[16,40,128]{2,1,0:T(8,128)}), f32[16,40,128]{2,1,0:T(8,128)S(1)}, u32[]{:S(2)}, u32[]{:S(2)}) async-start(f32[16,40,128]{2,1,0:T(8,128)} %shard_map.119), calls=%async_computation.3 | async-start | bytes 655360 | tf_op jit(solution)/shard_map/all_to_all | solution.py:486

commit v8 on v7

--- a/solution.py
+++ b/solution.py
@@ -15,6 +15,7 @@
 XS = 4
 CORES = 2
 BLOCK = 128
+EARLY = 2
 VMEM = 24 * 1024 * 1024
 NEAREST = 12582912.0
 SIN = (4.442867755889893, -7.307443618774414, 3.594788074493408, -0.7843739986419678)
@@ -86,6 +87,10 @@
     return rows.reshape(rows.shape[0] * rows.shape[1], rows.shape[2])
 
 
+def in_vmem(arrays):
+    return [pltpu.with_memory_space_constraint(a, pltpu.VMEM) for a in arrays]
+
+
 def here():
     f_id, s_id = lax.axis_index("freq"), lax.axis_index("shot")
     return lax.rem(f_id, YS), lax.rem(lax.div(s_id, CORES), XS), lax.rem(s_id, CORES)
@@ -231,6 +236,7 @@
     freqs, height = src.shape[0], src.shape[3]
     vmem, hbm = pl.BlockSpec(memory_space=pltpu.VMEM), pl.BlockSpec(memory_space=pltpu.HBM)
     given = first is not None
+    slabs = in_vmem(slabs)
     args = [turns, wx, wy, src, rcv, *slabs] + [first] * given
     in_specs = [vmem, vmem, vmem, hbm, hbm] + [vmem] * (count + given)
     cells = count * cols * height * freqs
@@ -297,6 +303,7 @@
 
 def image_terms(tiles, names, turns, wx, wy, src, rcv, slabs, scale, count):
     steps, cols = slabs[0].shape[1], slabs[0].shape[-1]
+    slabs = in_vmem(slabs)
     freqs, _, _, height, _ = src.shape
     aper = tiles.shape[0]
     vmem, hbm = pl.BlockSpec(memory_space=pltpu.VMEM), pl.BlockSpec(memory_space=pltpu.HBM)
@@ -458,35 +465,39 @@
     src = pltpu.with_memory_space_constraint(source_field, pltpu.HBM)
     rcv = pltpu.with_memory_space_constraint(receiver_field, pltpu.HBM)
 
+    tiles = apertures[0]
+    rows_of = lambda ids: jnp.broadcast_to(ids.astype(jnp.float32)[:, None], (ids.shape[0], BLOCK))
+    entries = lax.dynamic_slice_in_dim(tile_order, lax.axis_index("shot") * TILE_DEV, TILE_DEV)
     order = [[(0, 0), (0, 1)], [(1, 0), (3, 0)], [(1, 1), (3, 1)], [(2, 0), (2, 1)]]
-    first = fetch(order[0][0], src, rcv, cols)
-
-    def forward(call, slabs, first=None, done=()):
-        return march(order[call], turns, slabs, wx, wy, src, rcv, first, tuple(done))
+    firsts = [fetch(blocks[0], src, rcv, cols) for blocks in order[:EARLY]]
+    own, wx, wy, turns, named, entries, *firsts = lax.optimization_barrier(
+        (own, wx, wy, turns, rows_of(tiles), rows_of(entries), *firsts)
+    )
+    firsts += [None] * (len(order) - len(firsts))
+
+    def forward(call, slabs, done=()):
+        return march(order[call], turns, slabs, wx, wy, src, rcv, firsts[call], tuple(done))
 
     own_p = send(own, swap)
     s1, s3 = send(own, shift(1)), send(own, shift(3))
-    fields = forward(0, [own, own_p], first)
+    fields = forward(0, [own, own_p])
     s1, s3, later, *fields = lax.optimization_barrier((s1, s3, own, *fields))
     s2 = send(later, shift(2))
     s1_p, s3_p = send(s1, swap), send(s3, swap)
-    fields = forward(1, [s1, s3], done=fields)
+    fields = forward(1, [s1, s3], fields)
     s2, *fields = lax.optimization_barrier((s2, *fields))
     s2_p = send(s2, swap)
 
-    rows_of = lambda ids: jnp.broadcast_to(ids.astype(jnp.float32)[:, None], (ids.shape[0], BLOCK))
     slabs = [own, own_p, s1, s3, s1_p, s3_p, s2, s2_p]
-    tiles = apertures[0]
     names = [name for names in order for name in names]
     terms = image_terms(tiles, names, turns, wx, wy, src, rcv, slabs, 1.0 / freq_total, freqs_dev)
     length = terms.shape[3] * terms.shape[4]
     terms = lax.all_to_all(terms.reshape(freqs_dev, -1, BLOCK), "freq", 0, 0, tiled=True)
-    fields = forward(2, [s1_p, s3_p], done=fields)
+    fields = forward(2, [s1_p, s3_p], fields)
     terms, *fields = lax.optimization_barrier((terms, *fields))
-    dealt = lax.all_to_all(deal(rows_of(tiles), terms, shots), "shot", 0, 0, tiled=True)
-    fields = forward(3, [s2, s2_p], done=fields)
-    entries = lax.dynamic_slice_in_dim(tile_order, lax.axis_index("shot") * TILE_DEV, TILE_DEV)
-    image = collect(rows_of(entries), dealt, tiles.shape[0], DEPTH, length)
+    dealt = lax.all_to_all(deal(named, terms, shots), "shot", 0, 0, tiled=True)
+    fields = forward(3, [s2, s2_p], fields)
+    image = collect(entries, dealt, tiles.shape[0], DEPTH, length)
     return (*fields, image)
 
 

time: 92.6 us -> 90.7 us (0.979)
  Pallas kernels: 39.2 us -> 36.2 us
  waiting for transfers between devices: 13.9 us -> 11.6 us
  starting transfers between devices: 31.2 us -> 32.9 us
    pallas_call x4, Pallas kernels: 29.9 us -> 26.7 us  [march(): pl.pallas_call(functools.partial(march_body, names=names, freqs=freqs, gi...]
    all_to_all x1, waiting for transfers between devices: 4.69 us -> 2.55 us  [local(): arrived = lax.all_to_all(outgoing, 'shot', 0, 0, tiled=True)]
    pallas_call x1 -> x2, Pallas kernels: 1.11 us -> 2.12 us  [fetch(): pl.pallas_call(functools.partial(fetch_body, name=name), in_specs=[hbm, h...]
  transfers between devices with their start and end apart: 11 -> 11, of which waited for: 4 -> 6; matrix products, arithmetic and copies ran while one was open for 2% -> 4% of each run, Pallas kernels for 34% -> 32%
where the time goes in v8:
time: 90.7 us; the launch traced here: 90 us
  Pallas kernels  36.2 us (40%)
  starting transfers between devices  32.9 us (36%)
  waiting for transfers between devices  11.6 us (13%)
  between operations  4.74 us (5%)
  local copies, waits for them, and re-layouts  3.55 us (4%)
  other arithmetic  1.02 us (1%)
    pallas_call x4, Pallas kernels, march(): pl.pallas_call(functools.partial(march_body, names=names, freqs=freqs, gi...  26.7 us
    ppermute x7, starting transfers between devices, local(): lax.ppermute(v, AXES, pairs((freqs_dev, shots), move))  8.69 us
    all_to_all x1, starting transfers between devices, local(): lax.all_to_all(terms.reshape(freqs_dev, -1, BLOCK), 'freq', 0, 0, tiled=T...  7.26 us
    all_to_all x1, starting transfers between devices, local(): arrived = lax.all_to_all(outgoing, 'shot', 0, 0, tiled=True)  7.18 us
    all_to_all x1, waiting for transfers between devices, local(): own = lax.all_to_all(own, AXES, 0, 0, axis_index_groups=groups, tiled=True)  6.19 us
    all_to_all x1, starting transfers between devices, local(): dealt = lax.all_to_all(deal(named, terms, shots), 'shot', 0, 0, tiled=True)  4.91 us
    all_to_all x1, starting transfers between devices, local(): own = lax.all_to_all(own, AXES, 0, 0, axis_index_groups=groups, tiled=True)  4.81 us
    pallas_call x1, Pallas kernels, image_terms(): pl.pallas_call(functools.partial(image_body, names=names, scale=scale, pe...  3.87 us
  transfers between devices with their start and end apart: 11, of which 6 were waited for; matrix products, arithmetic and copies ran while one was open for 4% of the time, Pallas kernels for 32%

profile of v8, /device:TPU:1, one launch (start us, length us, event | category | flops | bytes accessed | tf_op | source)
XLA Modules:
  0.0 90.0 jit_solution(8261772072419990122)
XLA Ops:
  0.6 0.0 copy-start.1
  0.6 0.0 copy-start.2
  0.7 1.9 %shard_map.112 = f32[2,4,2,16,512]{4,3,2,1,0:T(8,128)} custom-call(f32[2,4,16,4096]{3,2,1,0:T(8,128)} %bitcast.25), custom_call_target="tpu_custom_call" | custom-call | tf_op jit(solution)/shard_map/pallas_call | solution.py:395
  2.6 7.2 %all-to-all-start = ((f32[16,16,512]{2,1,0:T(8,128)}), f32[16,16,512]{2,1,0:T(8,128)S(1)}, u32[]{:S(2)}, u32[]{:S(2)}) async-start(f32[16,16,512]{2,1,0:T(8,128)} %bitcast.1), calls=%async_computation | async-start | bytes 1048576 | tf_op jit(solution)/shard_map/all_to_all | solution.py:453
  9.8 1.3 %fusion.2 = (s32[1]{0:T(128)}, s32[1]{0:T(128)}) fusion(s32[2]{0:T(128)} %param.15), kind=kLoop, calls=%fused_computation.13 | loop fusion | bytes 16 | tf_op jit(solution)/shard_map/slice | solution.py:454
  13.7 0.9 fusion
  14.5 0.9 fusion.1
  15.4 0.1 copy.24
  15.5 0.1 copy.25
  17.0 0.0 copy-done.1
  17.0 0.1 maximum_maximum_fusion
  17.1 2.6 %all-to-all-done = f32[16,16,512]{2,1,0:T(8,128)S(1)} async-done(((f32[16,16,512]{2,1,0:T(8,128)}), f32[16,16,512]{2,1,0:T(8,128)S(1)}, u32[]{:S(2)}, u32[]{:S(2)}) %all-to-all-start) | async-done | bytes 524320 | tf_op jit(solution)/shard_map/all_to_all | solution.py:453
  19.7 0.9 broadcast_in_dim.8
  20.5 4.8 %all-to-all-start.1 = ((f32[8,2,16,512]{3,2,1,0:T(8,128)}), f32[8,2,16,512]{3,2,1,0:T(8,128)S(1)}, u32[]{:S(2)}, u32[]{:S(2)}) async-start(f32[8,2,16,512]{3,2,1,0:T(8,128)} %broadcast_in_dim.8), calls=%async_computation.1 | async-start | bytes 1048576 | tf_op jit(solution)/shard_map/all_to_all | solution.py:459
  25.3 0.0 copy-done.2
  25.3 0.1 dynamic-slice_convert_fusion
  25.4 1.0 %shard_map.113.rest_2_ = bf16[2,2,128,512]{3,2,1,0:T(8,128)(2,1)S(1)} custom-call(bf16[2,1,2,128,4096]{4,3,2,1,0:T(8,128)(2,1)} %src.13, bf16[2,1,2,128,4096]{4,3,2,1,0:T(8,128)(2,1)} %rcv.13), custom_call_target="tpu_custom_call" | custom-call | bytes 4194304 | tf_op jit(solution)/shard_map/pallas_call | solution.py:131
  26.5 0.0 copy-start.3
  26.5 0.0 copy-start
  26.5 1.1 %shard_map.114.rest_2_ = bf16[2,2,128,512]{3,2,1,0:T(8,128)(2,1)S(1)} custom-call(bf16[2,1,2,128,4096]{4,3,2,1,0:T(8,128)(2,1)} %src.13, bf16[2,1,2,128,4096]{4,3,2,1,0:T(8,128)(2,1)} %rcv.13), custom_call_target="tpu_custom_call" | custom-call | bytes 4194304 | tf_op jit(solution)/shard_map/pallas_call | solution.py:131
  27.6 0.0 copy-done.3
  27.6 0.0 copy-done
  27.6 6.2 %all-to-all-done.1.rest_0_ = f32[8,2,16,512]{3,2,1,0:T(8,128)S(1)} async-done(((f32[8,2,16,512]{3,2,1,0:T(8,128)}), f32[8,2,16,512]{3,2,1,0:T(8,128)S(1)}, u32[]{:S(2)}, u32[]{:S(2)}) %all-to-all-start.1) | async-done | bytes 524320 | tf_op jit(solution)/shard_map/all_to_all | solution.py:459
  33.8 0.1 broadcast_in_dim.9.turns
  33.9 0.1 broadcast_in_dim.10.ids
  33.9 0.1 broadcast_in_dim.11.entries
  34.0 0.9 collective-permute-start.2
  34.9 0.2 collective-permute-start
  35.1 2.4 %collective-permute-start.1 = (f32[8,2,16,512]{3,2,1,0:T(8,128)S(1)}, f32[8,2,16,512]{3,2,1,0:T(8,128)S(1)}, u32[]{:S(2)}, u32[]{:S(2)}) collective-permute-start(f32[8,2,16,512]{3,2,1,0:T(8,128)S(1)} %all-to-all-done.1.rest_0_), channel_id=1, source_target_pairs={{0,48},{1,7},{2,50},{3,1},{4,52},{5,3},{6,54},{7,5},{8,56},{9,15},... | collective-permute-start | bytes 1572872 | tf_op jit(solution)/shard_map/ppermute | solution.py:450
  37.5 0.0 collective-permute-done.2.rest_1_
  37.5 6.2 %shard_map.115 = (bf16[2,1,2,128,4096]{4,3,2,1,0:T(8,128)(2,1)}, bf16[2,1,2,128,4096]{4,3,2,1,0:T(8,128)(2,1)}) custom-call(f32[2,1,128]{2,1,0:T(1,128)S(1)} %broadcast_in_dim.9.turns, bf16[2,256,256]{2,1,0:T(8,128)(2,1)S(1)} %get-tuple-element.31.wx, bf16[2,256,256]{2,1,0:T(8,128)(2,1)S(1)} %get-tuple-element.32.wy, bf16[2,1,2,128,4096]{4,3,2,1,0:T(8,128)(2,1)} %src.13, ...), custom_call_target="tpu_custom_call" | custom-call | flops 6442450944 | bytes 4194304 | tf_op jit(solution)/shard_map/pallas_call | solution.py:243
  43.7 0.7 collective-permute-done.rest_0_.rest_2_
  44.4 0.0 collective-permute-done.1.rest_1_.rest_3_
  44.4 1.2 %collective-permute-start.3 = (f32[8,2,16,512]{3,2,1,0:T(8,128)S(1)}, f32[8,2,16,512]{3,2,1,0:T(8,128)S(1)}, u32[]{:S(2)}, u32[]{:S(2)}) collective-permute-start(f32[8,2,16,512]{3,2,1,0:T(8,128)S(1)} %all-to-all-done.1.rest_0_), channel_id=1, source_target_pairs={{0,32},{1,5},{2,34},{3,7},{4,36},{5,1},{6,38},{7,3},{8,40},{9,13},... | collective-permute-start | bytes 1572872 | tf_op jit(solution)/shard_map/ppermute | solution.py:450
  45.6 2.3 %collective-permute-start.5 = (f32[8,2,16,512]{3,2,1,0:T(8,128)S(1)}, f32[8,2,16,512]{3,2,1,0:T(8,128)S(1)}, u32[]{:S(2)}, u32[]{:S(2)}) collective-permute-start(f32[8,2,16,512]{3,2,1,0:T(8,128)S(1)} %collective-permute-done.rest_0_.rest_2_), channel_id=1, source_target_pairs={{0,1},{1,0},{2,3},{3,2},{4,5},{5,4},{6,7},{7,6},{8,9},{9,8},{10,11... | collective-permute-start | bytes 1572872 | tf_op jit(solution)/shard_map/ppermute | solution.py:450
  47.8 0.0 collective-permute-start.6
  47.8 6.2 %shard_map.116 = (bf16[2,1,2,128,4096]{4,3,2,1,0:T(8,128)(2,1)}, bf16[2,1,2,128,4096]{4,3,2,1,0:T(8,128)(2,1)}) custom-call(f32[2,1,128]{2,1,0:T(1,128)S(1)} %broadcast_in_dim.9.turns, bf16[2,256,256]{2,1,0:T(8,128)(2,1)S(1)} %get-tuple-element.31.wx, bf16[2,256,256]{2,1,0:T(8,128)(2,1)S(1)} %get-tuple-element.32.wy, ...), custom_call_target="tpu_custom_call", output_to_operand_aliasing={{0}: (8, {}), {1}: (9, {})} | custom-call | flops 6442450944 | bytes 4194304 | tf_op jit(solution)/shard_map/pallas_call | solution.py:243
  54.1 0.2 collective-permute-done.3.rest_6_.rest_0_
  54.2 1.7 %collective-permute-start.4 = (f32[8,2,16,512]{3,2,1,0:T(8,128)S(1)}, f32[8,2,16,512]{3,2,1,0:T(8,128)S(1)}, u32[]{:S(2)}, u32[]{:S(2)}) collective-permute-start(f32[8,2,16,512]{3,2,1,0:T(8,128)S(1)} %collective-permute-done.3.rest_6_.rest_0_), channel_id=1, source_target_pairs={{0,1},{1,0},{2,3},{3,2},{4,5},{5,4},{6,7},{7,6},{8,9},{9,8},{10,11... | collective-permute-start | bytes 1572872 | tf_op jit(solution)/shard_map/ppermute | solution.py:450
  55.9 0.0 collective-permute-done.5.rest_4_.rest_0_
  55.9 0.0 collective-permute-done.6.rest_5_.rest_1_
  55.9 1.5 %collective-permute-done.4.rest_7_.rest_1_ = f32[8,2,16,512]{3,2,1,0:T(8,128)S(1)} collective-permute-done((f32[8,2,16,512]{3,2,1,0:T(8,128)S(1)}, f32[8,2,16,512]{3,2,1,0:T(8,128)S(1)}, u32[]{:S(2)}, u32[]{:S(2)}) %collective-permute-start.4) | collective-permute-done | bytes 524320 | tf_op jit(solution)/shard_map/ppermute | solution.py:450
  57.5 3.9 %shard_map.117 = f32[8,2,2,8,128]{4,3,2,1,0:T(8,128)} custom-call(s32[2]{0:T(128)S(1)} %bitcast.24, f32[2,1,128]{2,1,0:T(1,128)S(1)} %broadcast_in_dim.9.turns, bf16[2,256,256]{2,1,0:T(8,128)(2,1)S(1)} %get-tuple-element.31.wx, bf16[2,256,256]{2,1,0:T(8,128)(2,1)S(1)} %get-tuple-element.32.wy, bf16[2,1,2,128,4096]{4,3,2,1,0:T(8,128)(2,1)} %src.13, ...), custom_call_target="tpu_custom_call" | custom-call | flops 1610612736 | bytes 2097152 | tf_op jit(solution)/shard_map/pallas_call | solution.py:311
  61.4 7.3 %all-to-all-start.2 = ((f32[8,32,128]{2,1,0:T(8,128)}), f32[8,32,128]{2,1,0:T(8,128)S(1)}, u32[]{:S(2)}, u32[]{:S(2)}) async-start(f32[8,32,128]{2,1,0:T(8,128)} %bitcast.13), calls=%async_computation.2 | async-start | bytes 262144 | tf_op jit(solution)/shard_map/all_to_all | solution.py:495
  68.6 7.1 %shard_map.118 = (bf16[2,1,2,128,4096]{4,3,2,1,0:T(8,128)(2,1)}, bf16[2,1,2,128,4096]{4,3,2,1,0:T(8,128)(2,1)}) custom-call(f32[2,1,128]{2,1,0:T(1,128)S(1)} %broadcast_in_dim.9.turns, bf16[2,256,256]{2,1,0:T(8,128)(2,1)S(1)} %get-tuple-element.31.wx, bf16[2,256,256]{2,1,0:T(8,128)(2,1)S(1)} %get-tuple-element.32.wy, ...), custom_call_target="tpu_custom_call", output_to_operand_aliasing={{0}: (7, {}), {1}: (8, {})} | custom-call | flops 6442450944 | bytes 4194304 | tf_op jit(solution)/shard_map/pallas_call | solution.py:243
  75.8 0.0 all-to-all-done.2.parts
  75.8 0.8 shard_map.120
  76.5 4.9 %all-to-all-start.3 = ((f32[16,40,128]{2,1,0:T(8,128)}), f32[16,40,128]{2,1,0:T(8,128)S(1)}, u32[]{:S(2)}, u32[]{:S(2)}) async-start(f32[16,40,128]{2,1,0:T(8,128)} %shard_map.120), calls=%async_computation.3 | async-start | bytes 655360 | tf_op jit(solution)/shard_map/all_to_all | solution.py:498
  81.4 7.2 %shard_map.119 = (bf16[2,1,2,128,4096]{4,3,2,1,0:T(8,128)(2,1)}, bf16[2,1,2,128,4096]{4,3,2,1,0:T(8,128)(2,1)}) custom-call(f32[2,1,128]{2,1,0:T(1,128)S(1)} %broadcast_in_dim.9.turns, bf16[2,256,256]{2,1,0:T(8,128)(2,1)S(1)} %get-tuple-element.31.wx, bf16[2,256,256]{2,1,0:T(8,128)(2,1)S(1)} %get-tuple-element.32.wy, ...), custom_call_target="tpu_custom_call", output_to_operand_aliasing={{0}: (7, {}), {1}: (8, {})} | custom-call | flops 6442450944 | bytes 4194304 | tf_op jit(solution)/shard_map/pallas_call | solution.py:243
  88.6 0.6 all-to-all-done.3.parts
  89.2 0.8 shard_map.121
  (6 shorter events, 0.0 us)
Async XLA Ops:
  0.6 16.4 %copy-start.1 = (bf16[2,2,128,128]{3,2,1,0:T(8,128)(2,1)S(1)}, bf16[2,2,128,128]{3,2,1,0:T(8,128)(2,1)}, u32[]{:S(2)}) copy-start(bf16[2,2,128,128]{3,2,1,0:T(8,128)(2,1)} %param.12) | copy-start | bytes 393220
  0.6 24.7 %copy-start.2 = (s32[64]{0:T(128)S(1)}, s32[64]{0:T(128)}, u32[]{:S(2)}) copy-start(s32[64]{0:T(128)} %param.17) | copy-start | bytes 772
  2.6 17.1 %all-to-all-start = ((f32[16,16,512]{2,1,0:T(8,128)}), f32[16,16,512]{2,1,0:T(8,128)S(1)}, u32[]{:S(2)}, u32[]{:S(2)}) async-start(f32[16,16,512]{2,1,0:T(8,128)} %bitcast.1), calls=%async_computation | async-start | bytes 1048576 | tf_op jit(solution)/shard_map/all_to_all | solution.py:453
  20.5 13.3 %all-to-all-start.1 = ((f32[8,2,16,512]{3,2,1,0:T(8,128)}), f32[8,2,16,512]{3,2,1,0:T(8,128)S(1)}, u32[]{:S(2)}, u32[]{:S(2)}) async-start(f32[8,2,16,512]{3,2,1,0:T(8,128)} %broadcast_in_dim.8), calls=%async_computation.1 | async-start | bytes 1048576 | tf_op jit(solution)/shard_map/all_to_all | solution.py:459
  26.5 1.1 %copy-start.3 = (f32[2]{0:T(128)S(1)}, f32[2]{0:T(128)}, u32[]{:S(2)}) copy-start(f32[2]{0:T(128)} %param.11) | copy-start | bytes 28
  26.5 1.1 %copy-start = (s32[1,2]{1,0:T(1,128)S(1)}, s32[1,2]{1,0:T(1,128)}, u32[]{:S(2)}) copy-start(s32[1,2]{1,0:T(1,128)} %param.16) | copy-start | bytes 28
  34.0 3.5 %collective-permute-start.2 = (f32[8,2,16,512]{3,2,1,0:T(8,128)S(1)}, f32[8,2,16,512]{3,2,1,0:T(8,128)S(1)}, u32[]{:S(2)}, u32[]{:S(2)}) collective-permute-start(f32[8,2,16,512]{3,2,1,0:T(8,128)S(1)} %all-to-all-done.1.rest_0_), channel_id=1, source_target_pairs={{0,1},{1,0},{2,3},{3,2},{4,5},{5,4},{6,7},{7,6},{8,9},{9,8},{10,11... | collective-permute-start | bytes 1572872 | tf_op jit(solution)/shard_map/ppermute | solution.py:450
  34.9 9.5 %collective-permute-start = (f32[8,2,16,512]{3,2,1,0:T(8,128)S(1)}, f32[8,2,16,512]{3,2,1,0:T(8,128)S(1)}, u32[]{:S(2)}, u32[]{:S(2)}) collective-permute-start(f32[8,2,16,512]{3,2,1,0:T(8,128)S(1)} %all-to-all-done.1.rest_0_), channel_id=1, source_target_pairs={{0,16},{1,3},{2,18},{3,5},{4,20},{5,7},{6,22},{7,1},{8,24},{9,11},... | collective-permute-start | bytes 1572872 | tf_op jit(solution)/shard_map/ppermute | solution.py:450
  35.1 9.3 %collective-permute-start.1 = (f32[8,2,16,512]{3,2,1,0:T(8,128)S(1)}, f32[8,2,16,512]{3,2,1,0:T(8,128)S(1)}, u32[]{:S(2)}, u32[]{:S(2)}) collective-permute-start(f32[8,2,16,512]{3,2,1,0:T(8,128)S(1)} %all-to-all-done.1.rest_0_), channel_id=1, source_target_pairs={{0,48},{1,7},{2,50},{3,1},{4,52},{5,3},{6,54},{7,5},{8,56},{9,15},... | collective-permute-start | bytes 1572872 | tf_op jit(solution)/shard_map/ppermute | solution.py:450
  44.4 9.8 %collective-permute-start.3 = (f32[8,2,16,512]{3,2,1,0:T(8,128)S(1)}, f32[8,2,16,512]{3,2,1,0:T(8,128)S(1)}, u32[]{:S(2)}, u32[]{:S(2)}) collective-permute-start(f32[8,2,16,512]{3,2,1,0:T(8,128)S(1)} %all-to-all-done.1.rest_0_), channel_id=1, source_target_pairs={{0,32},{1,5},{2,34},{3,7},{4,36},{5,1},{6,38},{7,3},{8,40},{9,13},... | collective-permute-start | bytes 1572872 | tf_op jit(solution)/shard_map/ppermute | solution.py:450
  45.6 10.4 %collective-permute-start.5 = (f32[8,2,16,512]{3,2,1,0:T(8,128)S(1)}, f32[8,2,16,512]{3,2,1,0:T(8,128)S(1)}, u32[]{:S(2)}, u32[]{:S(2)}) collective-permute-start(f32[8,2,16,512]{3,2,1,0:T(8,128)S(1)} %collective-permute-done.rest_0_.rest_2_), channel_id=1, source_target_pairs={{0,1},{1,0},{2,3},{3,2},{4,5},{5,4},{6,7},{7,6},{8,9},{9,8},{10,11... | collective-permute-start | bytes 1572872 | tf_op jit(solution)/shard_map/ppermute | solution.py:450
  47.8 8.1 %collective-permute-start.6 = (f32[8,2,16,512]{3,2,1,0:T(8,128)S(1)}, f32[8,2,16,512]{3,2,1,0:T(8,128)S(1)}, u32[]{:S(2)}, u32[]{:S(2)}) collective-permute-start(f32[8,2,16,512]{3,2,1,0:T(8,128)S(1)} %collective-permute-done.1.rest_1_.rest_3_), channel_id=1, source_target_pairs={{0,1},{1,0},{2,3},{3,2},{4,5},{5,4},{6,7},{7,6},{8,9},{9,8},{10,11... | collective-permute-start | bytes 1572872 | tf_op jit(solution)/shard_map/ppermute | solution.py:450
  54.2 3.2 %collective-permute-start.4 = (f32[8,2,16,512]{3,2,1,0:T(8,128)S(1)}, f32[8,2,16,512]{3,2,1,0:T(8,128)S(1)}, u32[]{:S(2)}, u32[]{:S(2)}) collective-permute-start(f32[8,2,16,512]{3,2,1,0:T(8,128)S(1)} %collective-permute-done.3.rest_6_.rest_0_), channel_id=1, source_target_pairs={{0,1},{1,0},{2,3},{3,2},{4,5},{5,4},{6,7},{7,6},{8,9},{9,8},{10,11... | collective-permute-start | bytes 1572872 | tf_op jit(solution)/shard_map/ppermute | solution.py:450
  61.4 14.4 %all-to-all-start.2 = ((f32[8,32,128]{2,1,0:T(8,128)}), f32[8,32,128]{2,1,0:T(8,128)S(1)}, u32[]{:S(2)}, u32[]{:S(2)}) async-start(f32[8,32,128]{2,1,0:T(8,128)} %bitcast.13), calls=%async_computation.2 | async-start | bytes 262144 | tf_op jit(solution)/shard_map/all_to_all | solution.py:495
  76.5 12.6 %all-to-all-start.3 = ((f32[16,40,128]{2,1,0:T(8,128)}), f32[16,40,128]{2,1,0:T(8,128)S(1)}, u32[]{:S(2)}, u32[]{:S(2)}) async-start(f32[16,40,128]{2,1,0:T(8,128)} %shard_map.120), calls=%async_computation.3 | async-start | bytes 655360 | tf_op jit(solution)/shard_map/all_to_all | solution.py:498

commit v9 on v8

--- a/solution.py
+++ b/solution.py
@@ -15,7 +15,8 @@
 XS = 4
 CORES = 2
 BLOCK = 128
-EARLY = 2
+EARLY = 1
+AHEAD = (0,)
 VMEM = 24 * 1024 * 1024
 NEAREST = 12582912.0
 SIN = (4.442867755889893, -7.307443618774414, 3.594788074493408, -0.7843739986419678)
@@ -139,10 +140,11 @@
     )(src, rcv)
 
 
-def march_body(turns, wx, wy, src, rcv, *rest, names, freqs, given):
+def march_body(turns, wx, wy, src, rcv, *rest, names, freqs, given, ahead):
     count = len(names)
     slabs, rest = rest[:count], rest[count:]
-    so, ro, held, made, in_sems, out_sems = rest[-6:]
+    held, made, in_sems, out_sems, ahead_sems = rest[-5:]
+    so, ro = rest[-7 - (ahead is not None) :][:2]
     cols = [slice(c, c + BLOCK) for c in range(0, held.shape[-1], BLOCK)]
     unit = pl.program_id(0)
     units = count * freqs
@@ -172,6 +174,9 @@
         for c in copies:
             c.start() if what == "start" else c.wait()
 
+    def looks_ahead():
+        return field_copies(src, rcv, rest[-6], ahead_sems, blocks_of([ahead])[0], 0)
+
     if not given:
 
         @pl.when(unit == 0)
@@ -181,6 +186,12 @@
     @pl.when(unit + 1 < units)
     def _():
         each(loads(unit + 1), "start")
+
+    if ahead is not None:
+
+        @pl.when(unit == 0)
+        def _():
+            each(looks_ahead(), "start")
 
     if given:
         first = rest[0]
@@ -229,9 +240,11 @@
         if units > 1:
             each(stores(unit - 1), "wait")
         each(stores(unit), "wait")
-
-
-def march(names, turns, slabs, wx, wy, src, rcv, first=None, done=()):
+        if ahead is not None:
+            each(looks_ahead(), "wait")
+
+
+def march(names, turns, slabs, wx, wy, src, rcv, first=None, done=(), ahead=None):
     count, cols = len(slabs), slabs[0].shape[-1]
     freqs, height = src.shape[0], src.shape[3]
     vmem, hbm = pl.BlockSpec(memory_space=pltpu.VMEM), pl.BlockSpec(memory_space=pltpu.HBM)
@@ -241,17 +254,19 @@
     in_specs = [vmem, vmem, vmem, hbm, hbm] + [vmem] * (count + given)
     cells = count * cols * height * freqs
     return pl.pallas_call(
-        functools.partial(march_body, names=names, freqs=freqs, given=given),
+        functools.partial(march_body, names=names, freqs=freqs, given=given, ahead=ahead),
         grid=(count * freqs,),
         in_specs=in_specs + [hbm] * len(done),
-        out_specs=[hbm, hbm],
+        out_specs=[hbm, hbm] + [vmem] * (ahead is not None),
         scratch_shapes=[
             pltpu.VMEM((2, 2, 2, height, cols), src.dtype),
             pltpu.VMEM((2, 2, 2, height, cols), src.dtype),
             pltpu.SemaphoreType.DMA((2, 2)),
             pltpu.SemaphoreType.DMA((2, 2)),
+            pltpu.SemaphoreType.DMA((2,)),
         ],
-        out_shape=[jax.ShapeDtypeStruct(src.shape, src.dtype), jax.ShapeDtypeStruct(rcv.shape, rcv.dtype)],
+        out_shape=[jax.ShapeDtypeStruct(src.shape, src.dtype), jax.ShapeDtypeStruct(rcv.shape, rcv.dtype)]
+        + [pltpu.VMEM((2, 2, height, cols), src.dtype)] * (ahead is not None),
         input_output_aliases={len(args) + i: i for i in range(len(done))},
         cost_estimate=pl.CostEstimate(
             flops=cells * DEPTH * 4 * 2 * 4 * BLOCK * 3, bytes_accessed=cells * 16, transcendentals=0
@@ -459,6 +474,7 @@
     own = lax.all_to_all(own, AXES, 0, 0, axis_index_groups=groups, tiled=True)
 
     shift = lambda k: lambda zh, y, zl, x, c: (zh, (y + k) % YS, zl, x, c) if c == 0 else (zh, y, zl, (x + k) % XS, c)
+    cross = lambda k: lambda zh, y, zl, x, c: (zh, y, zl, (x + k) % XS, c) if c == 0 else (zh, (y + k) % YS, zl, x, c)
     swap = lambda zh, y, zl, x, c: (zh, y, zl, x, 1 - c)
     wx, wy = sweep_weights(x_correction, y_correction)
     turns = jnp.broadcast_to((angular_freq * (0.5 / math.pi))[:, None, None], (angular_freq.shape[0], 1, BLOCK))
@@ -473,20 +489,21 @@
     own, wx, wy, turns, named, entries, *firsts = lax.optimization_barrier(
         (own, wx, wy, turns, rows_of(tiles), rows_of(entries), *firsts)
     )
-    firsts += [None] * (len(order) - len(firsts))
 
     def forward(call, slabs, done=()):
-        return march(order[call], turns, slabs, wx, wy, src, rcv, firsts[call], tuple(done))
+        ahead = order[call + 1][0] if call in AHEAD else None
+        out = march(order[call], turns, slabs, wx, wy, src, rcv, firsts[call], tuple(done), ahead)
+        firsts.append(out[2] if ahead else None)
+        return out[:2]
 
     own_p = send(own, swap)
     s1, s3 = send(own, shift(1)), send(own, shift(3))
     fields = forward(0, [own, own_p])
-    s1, s3, later, *fields = lax.optimization_barrier((s1, s3, own, *fields))
-    s2 = send(later, shift(2))
+    s1, s3, later, later_p, *fields = lax.optimization_barrier((s1, s3, own, own_p, *fields))
+    s2, s2_p = send(later, shift(2)), send(later_p, cross(2))
     s1_p, s3_p = send(s1, swap), send(s3, swap)
     fields = forward(1, [s1, s3], fields)
-    s2, *fields = lax.optimization_barrier((s2, *fields))
-    s2_p = send(s2, swap)
+    s2, s2_p, *fields = lax.optimization_barrier((s2, s2_p, *fields))
 
     slabs = [own, own_p, s1, s3, s1_p, s3_p, s2, s2_p]
     names = [name for names in order for name in names]

time: 90.7 us -> 93.7 us (1.033)
  waiting for transfers between devices: 11.6 us -> 16.3 us
  Pallas kernels: 36.2 us -> 35.2 us
    ppermute x7, waiting for transfers between devices: 2.35 us -> 5.94 us  [local(): lax.ppermute(v, AXES, pairs((freqs_dev, shots), move))]
    all_to_all x1, waiting for transfers between devices: 6.19 us -> 7.26 us  [local(): own = lax.all_to_all(own, AXES, 0, 0, axis_index_groups=groups, tiled=True)]
    pallas_call x2 -> x1, Pallas kernels: 2.12 us -> 1.08 us  [fetch(): pl.pallas_call(functools.partial(fetch_body, name=name), in_specs=[hbm, h...]
  transfers between devices with their start and end apart: 11 -> 11, of which waited for: 6 -> 6; matrix products, arithmetic and copies ran while one was open for 4% -> 4% of each run, Pallas kernels for 32% -> 30%
where the time goes in v9:
time: 93.7 us; the launch traced here: 92.9 us
  Pallas kernels  35.2 us (38%)
  starting transfers between devices  32.1 us (34%)
  waiting for transfers between devices  16.3 us (17%)
  between operations  4.72 us (5%)
  local copies, waits for them, and re-layouts  3.54 us (4%)
  other arithmetic  1.02 us (1%)
    pallas_call x4, Pallas kernels, march(): pl.pallas_call(functools.partial(march_body, names=names, freqs=freqs, gi...  26.8 us
    ppermute x7, starting transfers between devices, local(): lax.ppermute(v, AXES, pairs((freqs_dev, shots), move))  8.48 us
    all_to_all x1, waiting for transfers between devices, local(): own = lax.all_to_all(own, AXES, 0, 0, axis_index_groups=groups, tiled=True)  7.26 us
    all_to_all x1, starting transfers between devices, local(): arrived = lax.all_to_all(outgoing, 'shot', 0, 0, tiled=True)  7.18 us
    all_to_all x1, starting transfers between devices, local(): lax.all_to_all(terms.reshape(freqs_dev, -1, BLOCK), 'freq', 0, 0, tiled=T...  6.57 us
    ppermute x7, waiting for transfers between devices, local(): lax.ppermute(v, AXES, pairs((freqs_dev, shots), move))  5.94 us
    all_to_all x1, starting transfers between devices, local(): dealt = lax.all_to_all(deal(named, terms, shots), 'shot', 0, 0, tiled=True)  5.08 us
    all_to_all x1, starting transfers between devices, local(): own = lax.all_to_all(own, AXES, 0, 0, axis_index_groups=groups, tiled=True)  4.81 us
  transfers between devices with their start and end apart: 11, of which 6 were waited for; matrix products, arithmetic and copies ran while one was open for 4% of the time, Pallas kernels for 30%

profile of v9, /device:TPU:1, one launch (start us, length us, event | category | flops | bytes accessed | tf_op | source)
XLA Modules:
  0.0 92.9 jit_solution(13381829902021046360)
XLA Ops:
  0.6 0.0 copy-start.1
  0.6 0.0 copy-start.2
  0.7 1.9 %shard_map.112 = f32[2,4,2,16,512]{4,3,2,1,0:T(8,128)} custom-call(f32[2,4,16,4096]{3,2,1,0:T(8,128)} %bitcast.25), custom_call_target="tpu_custom_call" | custom-call | tf_op jit(solution)/shard_map/pallas_call | solution.py:410
  2.6 7.2 %all-to-all-start = ((f32[16,16,512]{2,1,0:T(8,128)}), f32[16,16,512]{2,1,0:T(8,128)S(1)}, u32[]{:S(2)}, u32[]{:S(2)}) async-start(f32[16,16,512]{2,1,0:T(8,128)} %bitcast.1), calls=%async_computation | async-start | bytes 1048576 | tf_op jit(solution)/shard_map/all_to_all | solution.py:468
  9.8 1.3 %fusion.2 = (s32[1]{0:T(128)}, s32[1]{0:T(128)}) fusion(s32[2]{0:T(128)} %param.15), kind=kLoop, calls=%fused_computation.13 | loop fusion | bytes 16 | tf_op jit(solution)/shard_map/slice | solution.py:469
  13.7 0.9 fusion
  14.5 0.9 fusion.1
  15.4 0.1 copy.24
  15.5 0.1 copy.25
  17.0 0.0 copy-done.1
  17.0 0.1 maximum_maximum_fusion
  17.1 2.6 %all-to-all-done = f32[16,16,512]{2,1,0:T(8,128)S(1)} async-done(((f32[16,16,512]{2,1,0:T(8,128)}), f32[16,16,512]{2,1,0:T(8,128)S(1)}, u32[]{:S(2)}, u32[]{:S(2)}) %all-to-all-start) | async-done | bytes 524320 | tf_op jit(solution)/shard_map/all_to_all | solution.py:468
  19.7 0.9 broadcast_in_dim.8
  20.5 4.8 %all-to-all-start.1 = ((f32[8,2,16,512]{3,2,1,0:T(8,128)}), f32[8,2,16,512]{3,2,1,0:T(8,128)S(1)}, u32[]{:S(2)}, u32[]{:S(2)}) async-start(f32[8,2,16,512]{3,2,1,0:T(8,128)} %broadcast_in_dim.8), calls=%async_computation.1 | async-start | bytes 1048576 | tf_op jit(solution)/shard_map/all_to_all | solution.py:474
  25.3 0.0 copy-done.2
  25.3 0.1 dynamic-slice_convert_fusion
  25.4 0.0 copy-start.3
  25.4 0.0 copy-start
  25.4 1.1 %shard_map.113.rest_2_ = bf16[2,2,128,512]{3,2,1,0:T(8,128)(2,1)S(1)} custom-call(bf16[2,1,2,128,4096]{4,3,2,1,0:T(8,128)(2,1)} %src.11, bf16[2,1,2,128,4096]{4,3,2,1,0:T(8,128)(2,1)} %rcv.11), custom_call_target="tpu_custom_call" | custom-call | bytes 4194304 | tf_op jit(solution)/shard_map/pallas_call | solution.py:132
  26.5 0.0 copy-done.3
  26.5 0.0 copy-done
  26.5 7.3 %all-to-all-done.1.rest_0_ = f32[8,2,16,512]{3,2,1,0:T(8,128)S(1)} async-done(((f32[8,2,16,512]{3,2,1,0:T(8,128)}), f32[8,2,16,512]{3,2,1,0:T(8,128)S(1)}, u32[]{:S(2)}, u32[]{:S(2)}) %all-to-all-start.1) | async-done | bytes 524320 | tf_op jit(solution)/shard_map/all_to_all | solution.py:474
  33.8 0.1 broadcast_in_dim.9.turns
  33.9 0.1 broadcast_in_dim.10.ids
  33.9 0.1 broadcast_in_dim.11.entries
  34.0 0.9 collective-permute-start.2
  34.9 0.2 collective-permute-start
  35.1 2.4 %collective-permute-start.1 = (f32[8,2,16,512]{3,2,1,0:T(8,128)S(1)}, f32[8,2,16,512]{3,2,1,0:T(8,128)S(1)}, u32[]{:S(2)}, u32[]{:S(2)}) collective-permute-start(f32[8,2,16,512]{3,2,1,0:T(8,128)S(1)} %all-to-all-done.1.rest_0_), channel_id=1, source_target_pairs={{0,48},{1,7},{2,50},{3,1},{4,52},{5,3},{6,54},{7,5},{8,56},{9,15},... | collective-permute-start | bytes 1572872 | tf_op jit(solution)/shard_map/ppermute | solution.py:465
  37.5 0.0 collective-permute-done.2.rest_1_
  37.5 6.2 %shard_map.114 = (bf16[2,1,2,128,4096]{4,3,2,1,0:T(8,128)(2,1)}, bf16[2,1,2,128,4096]{4,3,2,1,0:T(8,128)(2,1)}, bf16[2,2,128,512]{3,2,1,0:T(8,128)(2,1)S(1)}) custom-call(f32[2,1,128]{2,1,0:T(1,128)S(1)} %broadcast_in_dim.9.turns, bf16[2,256,256]{2,1,0:T(8,128)(2,1)S(1)} %get-tuple-element.33.wx, bf16[2,256,256]{2,1,0:T(8,128)(2,1)S(1)} %get-tuple-element.34.wy, ...), custom_call_target="tpu_custom_call" | custom-call | flops 6442450944 | bytes 4194304 | tf_op jit(solution)/shard_map/pallas_call | solution.py:256
  43.8 0.6 collective-permute-done.rest_0_.rest_2_
  44.4 0.0 collective-permute-done.1.rest_1_.rest_3_
  44.4 1.2 %collective-permute-start.3 = (f32[8,2,16,512]{3,2,1,0:T(8,128)S(1)}, f32[8,2,16,512]{3,2,1,0:T(8,128)S(1)}, u32[]{:S(2)}, u32[]{:S(2)}) collective-permute-start(f32[8,2,16,512]{3,2,1,0:T(8,128)S(1)} %all-to-all-done.1.rest_0_), channel_id=1, source_target_pairs={{0,32},{1,5},{2,34},{3,7},{4,36},{5,1},{6,38},{7,3},{8,40},{9,13},... | collective-permute-start | bytes 1572872 | tf_op jit(solution)/shard_map/ppermute | solution.py:465
  45.6 2.3 %collective-permute-start.4 = (f32[8,2,16,512]{3,2,1,0:T(8,128)S(1)}, f32[8,2,16,512]{3,2,1,0:T(8,128)S(1)}, u32[]{:S(2)}, u32[]{:S(2)}) collective-permute-start(f32[8,2,16,512]{3,2,1,0:T(8,128)S(1)} %collective-permute-done.2.rest_1_), channel_id=1, source_target_pairs={{0,4},{1,33},{2,6},{3,35},{4,0},{5,37},{6,2},{7,39},{8,12},{9,41},... | collective-permute-start | bytes 1572872 | tf_op jit(solution)/shard_map/ppermute | solution.py:465
  47.9 1.5 %collective-permute-start.5 = (f32[8,2,16,512]{3,2,1,0:T(8,128)S(1)}, f32[8,2,16,512]{3,2,1,0:T(8,128)S(1)}, u32[]{:S(2)}, u32[]{:S(2)}) collective-permute-start(f32[8,2,16,512]{3,2,1,0:T(8,128)S(1)} %collective-permute-done.rest_0_.rest_2_), channel_id=1, source_target_pairs={{0,1},{1,0},{2,3},{3,2},{4,5},{5,4},{6,7},{7,6},{8,9},{9,8},{10,11... | collective-permute-start | bytes 1572872 | tf_op jit(solution)/shard_map/ppermute | solution.py:465
  49.3 0.0 collective-permute-start.6
  49.3 6.2 %shard_map.115 = (bf16[2,1,2,128,4096]{4,3,2,1,0:T(8,128)(2,1)}, bf16[2,1,2,128,4096]{4,3,2,1,0:T(8,128)(2,1)}) custom-call(f32[2,1,128]{2,1,0:T(1,128)S(1)} %broadcast_in_dim.9.turns, bf16[2,256,256]{2,1,0:T(8,128)(2,1)S(1)} %get-tuple-element.33.wx, bf16[2,256,256]{2,1,0:T(8,128)(2,1)S(1)} %get-tuple-element.34.wy, ...), custom_call_target="tpu_custom_call", output_to_operand_aliasing={{0}: (8, {}), {1}: (9, {})} | custom-call | flops 6442450944 | bytes 4194304 | tf_op jit(solution)/shard_map/pallas_call | solution.py:256
  55.6 0.3 collective-permute-done.3.rest_6_.rest_0_
  55.9 5.0 %collective-permute-done.4.rest_7_.rest_1_ = f32[8,2,16,512]{3,2,1,0:T(8,128)S(1)} collective-permute-done((f32[8,2,16,512]{3,2,1,0:T(8,128)S(1)}, f32[8,2,16,512]{3,2,1,0:T(8,128)S(1)}, u32[]{:S(2)}, u32[]{:S(2)}) %collective-permute-start.4) | collective-permute-done | bytes 524320 | tf_op jit(solution)/shard_map/ppermute | solution.py:465
  60.9 0.0 collective-permute-done.5.rest_4_.rest_0_
  60.9 0.0 collective-permute-done.6.rest_5_.rest_1_
  60.9 3.9 %shard_map.116 = f32[8,2,2,8,128]{4,3,2,1,0:T(8,128)} custom-call(s32[2]{0:T(128)S(1)} %bitcast.24, f32[2,1,128]{2,1,0:T(1,128)S(1)} %broadcast_in_dim.9.turns, bf16[2,256,256]{2,1,0:T(8,128)(2,1)S(1)} %get-tuple-element.33.wx, bf16[2,256,256]{2,1,0:T(8,128)(2,1)S(1)} %get-tuple-element.34.wy, bf16[2,1,2,128,4096]{4,3,2,1,0:T(8,128)(2,1)} %src.11, ...), custom_call_target="tpu_custom_call" | custom-call | flops 1610612736 | bytes 2097152 | tf_op jit(solution)/shard_map/pallas_call | solution.py:326
  64.8 6.6 %all-to-all-start.2 = ((f32[8,32,128]{2,1,0:T(8,128)}), f32[8,32,128]{2,1,0:T(8,128)S(1)}, u32[]{:S(2)}, u32[]{:S(2)}) async-start(f32[8,32,128]{2,1,0:T(8,128)} %bitcast.13), calls=%async_computation.2 | async-start | bytes 262144 | tf_op jit(solution)/shard_map/all_to_all | solution.py:512
  71.3 7.2 %shard_map.117 = (bf16[2,1,2,128,4096]{4,3,2,1,0:T(8,128)(2,1)}, bf16[2,1,2,128,4096]{4,3,2,1,0:T(8,128)(2,1)}) custom-call(f32[2,1,128]{2,1,0:T(1,128)S(1)} %broadcast_in_dim.9.turns, bf16[2,256,256]{2,1,0:T(8,128)(2,1)S(1)} %get-tuple-element.33.wx, bf16[2,256,256]{2,1,0:T(8,128)(2,1)S(1)} %get-tuple-element.34.wy, ...), custom_call_target="tpu_custom_call", output_to_operand_aliasing={{0}: (7, {}), {1}: (8, {})} | custom-call | flops 6442450944 | bytes 4194304 | tf_op jit(solution)/shard_map/pallas_call | solution.py:256
  78.5 0.0 all-to-all-done.2.parts
  78.5 0.8 shard_map.119
  79.3 5.1 %all-to-all-start.3 = ((f32[16,40,128]{2,1,0:T(8,128)}), f32[16,40,128]{2,1,0:T(8,128)S(1)}, u32[]{:S(2)}, u32[]{:S(2)}) async-start(f32[16,40,128]{2,1,0:T(8,128)} %shard_map.119), calls=%async_computation.3 | async-start | bytes 655360 | tf_op jit(solution)/shard_map/all_to_all | solution.py:515
  84.4 7.2 %shard_map.118 = (bf16[2,1,2,128,4096]{4,3,2,1,0:T(8,128)(2,1)}, bf16[2,1,2,128,4096]{4,3,2,1,0:T(8,128)(2,1)}) custom-call(f32[2,1,128]{2,1,0:T(1,128)S(1)} %broadcast_in_dim.9.turns, bf16[2,256,256]{2,1,0:T(8,128)(2,1)S(1)} %get-tuple-element.33.wx, bf16[2,256,256]{2,1,0:T(8,128)(2,1)S(1)} %get-tuple-element.34.wy, ...), custom_call_target="tpu_custom_call", output_to_operand_aliasing={{0}: (7, {}), {1}: (8, {})} | custom-call | flops 6442450944 | bytes 4194304 | tf_op jit(solution)/shard_map/pallas_call | solution.py:256
  91.5 0.5 all-to-all-done.3.parts
  92.1 0.8 shard_map.120
  (6 shorter events, 0.0 us)
Async XLA Ops:
  0.6 16.4 %copy-start.1 = (bf16[2,2,128,128]{3,2,1,0:T(8,128)(2,1)S(1)}, bf16[2,2,128,128]{3,2,1,0:T(8,128)(2,1)}, u32[]{:S(2)}) copy-start(bf16[2,2,128,128]{3,2,1,0:T(8,128)(2,1)} %param.12) | copy-start | bytes 393220
  0.6 24.7 %copy-start.2 = (s32[64]{0:T(128)S(1)}, s32[64]{0:T(128)}, u32[]{:S(2)}) copy-start(s32[64]{0:T(128)} %param.17) | copy-start | bytes 772
  2.6 17.1 %all-to-all-start = ((f32[16,16,512]{2,1,0:T(8,128)}), f32[16,16,512]{2,1,0:T(8,128)S(1)}, u32[]{:S(2)}, u32[]{:S(2)}) async-start(f32[16,16,512]{2,1,0:T(8,128)} %bitcast.1), calls=%async_computation | async-start | bytes 1048576 | tf_op jit(solution)/shard_map/all_to_all | solution.py:468
  20.5 13.3 %all-to-all-start.1 = ((f32[8,2,16,512]{3,2,1,0:T(8,128)}), f32[8,2,16,512]{3,2,1,0:T(8,128)S(1)}, u32[]{:S(2)}, u32[]{:S(2)}) async-start(f32[8,2,16,512]{3,2,1,0:T(8,128)} %broadcast_in_dim.8), calls=%async_computation.1 | async-start | bytes 1048576 | tf_op jit(solution)/shard_map/all_to_all | solution.py:474
  25.4 1.1 %copy-start.3 = (f32[2]{0:T(128)S(1)}, f32[2]{0:T(128)}, u32[]{:S(2)}) copy-start(f32[2]{0:T(128)} %param.11) | copy-start | bytes 28
  25.4 1.1 %copy-start = (s32[1,2]{1,0:T(1,128)S(1)}, s32[1,2]{1,0:T(1,128)}, u32[]{:S(2)}) copy-start(s32[1,2]{1,0:T(1,128)} %param.16) | copy-start | bytes 28
  34.0 3.5 %collective-permute-start.2 = (f32[8,2,16,512]{3,2,1,0:T(8,128)S(1)}, f32[8,2,16,512]{3,2,1,0:T(8,128)S(1)}, u32[]{:S(2)}, u32[]{:S(2)}) collective-permute-start(f32[8,2,16,512]{3,2,1,0:T(8,128)S(1)} %all-to-all-done.1.rest_0_), channel_id=1, source_target_pairs={{0,1},{1,0},{2,3},{3,2},{4,5},{5,4},{6,7},{7,6},{8,9},{9,8},{10,11... | collective-permute-start | bytes 1572872 | tf_op jit(solution)/shard_map/ppermute | solution.py:465
  34.9 9.5 %collective-permute-start = (f32[8,2,16,512]{3,2,1,0:T(8,128)S(1)}, f32[8,2,16,512]{3,2,1,0:T(8,128)S(1)}, u32[]{:S(2)}, u32[]{:S(2)}) collective-permute-start(f32[8,2,16,512]{3,2,1,0:T(8,128)S(1)} %all-to-all-done.1.rest_0_), channel_id=1, source_target_pairs={{0,16},{1,3},{2,18},{3,5},{4,20},{5,7},{6,22},{7,1},{8,24},{9,11},... | collective-permute-start | bytes 1572872 | tf_op jit(solution)/shard_map/ppermute | solution.py:465
  35.1 9.3 %collective-permute-start.1 = (f32[8,2,16,512]{3,2,1,0:T(8,128)S(1)}, f32[8,2,16,512]{3,2,1,0:T(8,128)S(1)}, u32[]{:S(2)}, u32[]{:S(2)}) collective-permute-start(f32[8,2,16,512]{3,2,1,0:T(8,128)S(1)} %all-to-all-done.1.rest_0_), channel_id=1, source_target_pairs={{0,48},{1,7},{2,50},{3,1},{4,52},{5,3},{6,54},{7,5},{8,56},{9,15},... | collective-permute-start | bytes 1572872 | tf_op jit(solution)/shard_map/ppermute | solution.py:465
  44.4 11.5 %collective-permute-start.3 = (f32[8,2,16,512]{3,2,1,0:T(8,128)S(1)}, f32[8,2,16,512]{3,2,1,0:T(8,128)S(1)}, u32[]{:S(2)}, u32[]{:S(2)}) collective-permute-start(f32[8,2,16,512]{3,2,1,0:T(8,128)S(1)} %all-to-all-done.1.rest_0_), channel_id=1, source_target_pairs={{0,32},{1,5},{2,34},{3,7},{4,36},{5,1},{6,38},{7,3},{8,40},{9,13},... | collective-permute-start | bytes 1572872 | tf_op jit(solution)/shard_map/ppermute | solution.py:465
  45.6 15.3 %collective-permute-start.4 = (f32[8,2,16,512]{3,2,1,0:T(8,128)S(1)}, f32[8,2,16,512]{3,2,1,0:T(8,128)S(1)}, u32[]{:S(2)}, u32[]{:S(2)}) collective-permute-start(f32[8,2,16,512]{3,2,1,0:T(8,128)S(1)} %collective-permute-done.2.rest_1_), channel_id=1, source_target_pairs={{0,4},{1,33},{2,6},{3,35},{4,0},{5,37},{6,2},{7,39},{8,12},{9,41},... | collective-permute-start | bytes 1572872 | tf_op jit(solution)/shard_map/ppermute | solution.py:465
  47.9 13.0 %collective-permute-start.5 = (f32[8,2,16,512]{3,2,1,0:T(8,128)S(1)}, f32[8,2,16,512]{3,2,1,0:T(8,128)S(1)}, u32[]{:S(2)}, u32[]{:S(2)}) collective-permute-start(f32[8,2,16,512]{3,2,1,0:T(8,128)S(1)} %collective-permute-done.rest_0_.rest_2_), channel_id=1, source_target_pairs={{0,1},{1,0},{2,3},{3,2},{4,5},{5,4},{6,7},{7,6},{8,9},{9,8},{10,11... | collective-permute-start | bytes 1572872 | tf_op jit(solution)/shard_map/ppermute | solution.py:465
  49.3 11.6 %collective-permute-start.6 = (f32[8,2,16,512]{3,2,1,0:T(8,128)S(1)}, f32[8,2,16,512]{3,2,1,0:T(8,128)S(1)}, u32[]{:S(2)}, u32[]{:S(2)}) collective-permute-start(f32[8,2,16,512]{3,2,1,0:T(8,128)S(1)} %collective-permute-done.1.rest_1_.rest_3_), channel_id=1, source_target_pairs={{0,1},{1,0},{2,3},{3,2},{4,5},{5,4},{6,7},{7,6},{8,9},{9,8},{10,11... | collective-permute-start | bytes 1572872 | tf_op jit(solution)/shard_map/ppermute | solution.py:465
  64.8 13.7 %all-to-all-start.2 = ((f32[8,32,128]{2,1,0:T(8,128)}), f32[8,32,128]{2,1,0:T(8,128)S(1)}, u32[]{:S(2)}, u32[]{:S(2)}) async-start(f32[8,32,128]{2,1,0:T(8,128)} %bitcast.13), calls=%async_computation.2 | async-start | bytes 262144 | tf_op jit(solution)/shard_map/all_to_all | solution.py:512
  79.3 12.8 %all-to-all-start.3 = ((f32[16,40,128]{2,1,0:T(8,128)}), f32[16,40,128]{2,1,0:T(8,128)S(1)}, u32[]{:S(2)}, u32[]{:S(2)}) async-start(f32[16,40,128]{2,1,0:T(8,128)} %shard_map.119), calls=%async_computation.3 | async-start | bytes 655360 | tf_op jit(solution)/shard_map/all_to_all | solution.py:515

commit v10 on v8

--- a/solution.py
+++ b/solution.py
@@ -260,9 +260,10 @@
     )(*args, *done)
 
 
-def image_body(tiles, turns, wx, wy, src, rcv, *rest, names, scale, per, count):
+def image_body(ids, turns, wx, wy, src, rcv, *rest, names, scale, per, count):
     slabs, out, wanted, held, lines, sems = rest[:-5], *rest[-5:]
-    aper = tiles.shape[0]
+    aper = ids.shape[0]
+    tiles = [jnp.max(ids[a : a + 1]).astype(jnp.int32) for a in range(aper)]
     x_blocks = [lax.div(tiles[a], 2) for a in range(aper)]
     copies = []
     for a in range(aper):
@@ -301,16 +302,16 @@
             out[:, a, d] = both.reshape(count, pairs_of // count, BLOCK)
 
 
-def image_terms(tiles, names, turns, wx, wy, src, rcv, slabs, scale, count):
+def image_terms(ids, names, turns, wx, wy, src, rcv, slabs, scale, count):
     steps, cols = slabs[0].shape[1], slabs[0].shape[-1]
     slabs = in_vmem(slabs)
     freqs, _, _, height, _ = src.shape
-    aper = tiles.shape[0]
+    aper = ids.shape[0]
     vmem, hbm = pl.BlockSpec(memory_space=pltpu.VMEM), pl.BlockSpec(memory_space=pltpu.HBM)
     shape = (count, aper, steps, height // 2 // count, BLOCK)
     return pl.pallas_call(
         functools.partial(image_body, names=names, scale=scale, per=cols // BLOCK, count=count),
-        in_specs=[pl.BlockSpec(memory_space=pltpu.SMEM), vmem, vmem, vmem, hbm, hbm] + [vmem] * len(slabs),
+        in_specs=[vmem, vmem, vmem, vmem, hbm, hbm] + [vmem] * len(slabs),
         out_specs=vmem,
         out_shape=jax.ShapeDtypeStruct(shape, jnp.float32),
         scratch_shapes=[
@@ -323,7 +324,7 @@
             flops=aper * BLOCK * height * freqs * steps * 4 * 2 * 4 * BLOCK * 3, bytes_accessed=1 << 21, transcendentals=0
         ),
         compiler_params=pltpu.CompilerParams(vmem_limit_bytes=VMEM),
-    )(tiles, turns, wx, wy, src, rcv, *slabs)
+    )(ids, turns, wx, wy, src, rcv, *slabs)
 
 
 def deal_body(ids, parts, out):
@@ -371,33 +372,37 @@
     )(entries, pltpu.with_memory_space_constraint(parts, pltpu.VMEM))
 
 
-def cut_body(slab, out, sems, *, cols):
+def cut_body(slab, out, held, in_sems, out_sems, *, cols):
     y = here()[0]
     xs = out.shape[1]
-    copies = [
-        pltpu.make_async_copy(
-            slab.at[:, :, :, pl.ds(pl.multiple_of(y * cols, BLOCK), cols)], out.at[:, :, 0], sems.at[xs]
-        )
-    ]
-    for x in range(xs):
-        copies.append(
-            pltpu.make_async_copy(slab.at[:, y, :, pl.ds((xs + x) * cols, cols)], out.at[:, x, 1], sems.at[x])
-        )
-    for c in copies:
+    first = pl.ds(pl.multiple_of(y * cols, BLOCK), cols)
+    parts = [(slab.at[:, x, :, first], (slice(None), x, 0)) for x in range(xs)]
+    parts += [(slab.at[:, y, :, pl.ds((xs + x) * cols, cols)], (slice(None), x, 1)) for x in range(xs)]
+    loads = [pltpu.make_async_copy(part, held.at[at], in_sems.at[i]) for i, (part, at) in enumerate(parts)]
+    stores = [pltpu.make_async_copy(held.at[at], out.at[at], out_sems.at[i]) for i, (_, at) in enumerate(parts)]
+    for c in loads:
         c.start()
-    for c in copies:
+    for load, store in zip(loads, stores):
+        load.wait()
+        store.start()
+    for c in stores:
         c.wait()
 
 
 def cut(slab, cols):
     zls, xs, rows, _ = slab.shape
     slab = pltpu.with_memory_space_constraint(slab, pltpu.HBM)
+    shape = (zls, xs, CORES, rows, cols)
     return pl.pallas_call(
         functools.partial(cut_body, cols=cols),
         in_specs=[pl.BlockSpec(memory_space=pltpu.HBM)],
-        out_specs=pl.BlockSpec(memory_space=pltpu.VMEM),
-        out_shape=jax.ShapeDtypeStruct((zls, xs, CORES, rows, cols), slab.dtype),
-        scratch_shapes=[pltpu.SemaphoreType.DMA((xs + 1,))],
+        out_specs=pl.BlockSpec(memory_space=pltpu.HBM),
+        out_shape=jax.ShapeDtypeStruct(shape, slab.dtype),
+        scratch_shapes=[
+            pltpu.VMEM(shape, slab.dtype),
+            pltpu.SemaphoreType.DMA((2 * xs,)),
+            pltpu.SemaphoreType.DMA((2 * xs,)),
+        ],
         compiler_params=pltpu.CompilerParams(vmem_limit_bytes=VMEM),
     )(slab)
 
@@ -490,7 +495,7 @@
 
     slabs = [own, own_p, s1, s3, s1_p, s3_p, s2, s2_p]
     names = [name for names in order for name in names]
-    terms = image_terms(tiles, names, turns, wx, wy, src, rcv, slabs, 1.0 / freq_total, freqs_dev)
+    terms = image_terms(named, names, turns, wx, wy, src, rcv, slabs, 1.0 / freq_total, freqs_dev)
     length = terms.shape[3] * terms.shape[4]
     terms = lax.all_to_all(terms.reshape(freqs_dev, -1, BLOCK), "freq", 0, 0, tiled=True)
     fields = forward(2, [s1_p, s3_p], fields)

time: 90.7 us -> 90.3 us (level)
  no operation moved by 1% of the time
where the time goes in v10:
time: 90.3 us; the launch traced here: 89.5 us
  Pallas kernels  35.7 us (40%)
  starting transfers between devices  32.9 us (36%)
  waiting for transfers between devices  11.6 us (13%)
  between operations  4.74 us (5%)
  local copies, waits for them, and re-layouts  3.55 us (4%)
  other arithmetic  1.02 us (1%)
    pallas_call x4, Pallas kernels, march(): pl.pallas_call(functools.partial(march_body, names=names, freqs=freqs, gi...  26.7 us
    ppermute x7, starting transfers between devices, local(): lax.ppermute(v, AXES, pairs((freqs_dev, shots), move))  8.69 us
    all_to_all x1, starting transfers between devices, local(): lax.all_to_all(terms.reshape(freqs_dev, -1, BLOCK), 'freq', 0, 0, tiled=T...  7.26 us
    all_to_all x1, starting transfers between devices, local(): arrived = lax.all_to_all(outgoing, 'shot', 0, 0, tiled=True)  7.18 us
    all_to_all x1, waiting for transfers between devices, local(): own = lax.all_to_all(own, AXES, 0, 0, axis_index_groups=groups, tiled=True)  6.19 us
    all_to_all x1, starting transfers between devices, local(): dealt = lax.all_to_all(deal(named, terms, shots), 'shot', 0, 0, tiled=True)  4.9 us
    all_to_all x1, starting transfers between devices, local(): own = lax.all_to_all(own, AXES, 0, 0, axis_index_groups=groups, tiled=True)  4.81 us
    pallas_call x1, Pallas kernels, image_terms(): pl.pallas_call(functools.partial(image_body, names=names, scale=scale, pe...  3.44 us
  transfers between devices with their start and end apart: 11, of which 6 were waited for; matrix products, arithmetic and copies ran while one was open for 4% of the time, Pallas kernels for 32%

profile of v10, /device:TPU:1, one launch (start us, length us, event | category | flops | bytes accessed | tf_op | source)
XLA Modules:
  0.0 89.5 jit_solution(11072433624325689314)
XLA Ops:
  0.6 0.0 copy-start
  0.6 0.0 copy-start.1
  0.7 1.9 %shard_map.112 = f32[2,4,2,16,512]{4,3,2,1,0:T(8,128)} custom-call(f32[2,4,16,4096]{3,2,1,0:T(8,128)} %bitcast.24), custom_call_target="tpu_custom_call" | custom-call | tf_op jit(solution)/shard_map/pallas_call | solution.py:396
  2.5 7.2 %all-to-all-start = ((f32[16,16,512]{2,1,0:T(8,128)}), f32[16,16,512]{2,1,0:T(8,128)S(1)}, u32[]{:S(2)}, u32[]{:S(2)}) async-start(f32[16,16,512]{2,1,0:T(8,128)} %bitcast.1), calls=%async_computation | async-start | bytes 1048576 | tf_op jit(solution)/shard_map/all_to_all | solution.py:458
  9.7 1.3 %fusion.2 = (s32[1]{0:T(128)}, s32[1]{0:T(128)}) fusion(s32[2]{0:T(128)} %param.15), kind=kLoop, calls=%fused_computation.13 | loop fusion | bytes 16 | tf_op jit(solution)/shard_map/slice | solution.py:459
  13.6 0.9 fusion
  14.5 0.9 fusion.1
  15.4 0.1 copy.24
  15.5 0.1 copy.25
  17.0 0.0 copy-done
  17.0 0.1 maximum_maximum_fusion
  17.1 2.6 %all-to-all-done = f32[16,16,512]{2,1,0:T(8,128)S(1)} async-done(((f32[16,16,512]{2,1,0:T(8,128)}), f32[16,16,512]{2,1,0:T(8,128)S(1)}, u32[]{:S(2)}, u32[]{:S(2)}) %all-to-all-start) | async-done | bytes 524320 | tf_op jit(solution)/shard_map/all_to_all | solution.py:458
  19.6 0.9 broadcast_in_dim.8
  20.5 4.8 %all-to-all-start.1 = ((f32[8,2,16,512]{3,2,1,0:T(8,128)}), f32[8,2,16,512]{3,2,1,0:T(8,128)S(1)}, u32[]{:S(2)}, u32[]{:S(2)}) async-start(f32[8,2,16,512]{3,2,1,0:T(8,128)} %broadcast_in_dim.8), calls=%async_computation.1 | async-start | bytes 1048576 | tf_op jit(solution)/shard_map/all_to_all | solution.py:464
  25.3 0.0 copy-done.1
  25.3 0.1 dynamic-slice_convert_fusion
  25.4 1.0 %shard_map.113.rest_2_ = bf16[2,2,128,512]{3,2,1,0:T(8,128)(2,1)S(1)} custom-call(bf16[2,1,2,128,4096]{4,3,2,1,0:T(8,128)(2,1)} %src.13, bf16[2,1,2,128,4096]{4,3,2,1,0:T(8,128)(2,1)} %rcv.13), custom_call_target="tpu_custom_call" | custom-call | bytes 4194304 | tf_op jit(solution)/shard_map/pallas_call | solution.py:131
  26.4 0.0 copy-start.2
  26.5 0.0 copy-start.3
  26.5 1.1 %shard_map.114.rest_2_ = bf16[2,2,128,512]{3,2,1,0:T(8,128)(2,1)S(1)} custom-call(bf16[2,1,2,128,4096]{4,3,2,1,0:T(8,128)(2,1)} %src.13, bf16[2,1,2,128,4096]{4,3,2,1,0:T(8,128)(2,1)} %rcv.13), custom_call_target="tpu_custom_call" | custom-call | bytes 4194304 | tf_op jit(solution)/shard_map/pallas_call | solution.py:131
  27.5 0.0 copy-done.2
  27.6 0.0 copy-done.3
  27.6 6.2 %all-to-all-done.1.rest_0_ = f32[8,2,16,512]{3,2,1,0:T(8,128)S(1)} async-done(((f32[8,2,16,512]{3,2,1,0:T(8,128)}), f32[8,2,16,512]{3,2,1,0:T(8,128)S(1)}, u32[]{:S(2)}, u32[]{:S(2)}) %all-to-all-start.1) | async-done | bytes 524320 | tf_op jit(solution)/shard_map/all_to_all | solution.py:464
  33.8 0.1 broadcast_in_dim.9.turns
  33.8 0.1 broadcast_in_dim.10.ids
  33.9 0.1 broadcast_in_dim.11.entries
  34.0 0.9 collective-permute-start.2
  34.8 0.2 collective-permute-start
  35.1 2.4 %collective-permute-start.1 = (f32[8,2,16,512]{3,2,1,0:T(8,128)S(1)}, f32[8,2,16,512]{3,2,1,0:T(8,128)S(1)}, u32[]{:S(2)}, u32[]{:S(2)}) collective-permute-start(f32[8,2,16,512]{3,2,1,0:T(8,128)S(1)} %all-to-all-done.1.rest_0_), channel_id=1, source_target_pairs={{0,48},{1,7},{2,50},{3,1},{4,52},{5,3},{6,54},{7,5},{8,56},{9,15},... | collective-permute-start | bytes 1572872 | tf_op jit(solution)/shard_map/ppermute | solution.py:455
  37.5 0.0 collective-permute-done.2.rest_1_
  37.5 6.2 %shard_map.115 = (bf16[2,1,2,128,4096]{4,3,2,1,0:T(8,128)(2,1)}, bf16[2,1,2,128,4096]{4,3,2,1,0:T(8,128)(2,1)}) custom-call(f32[2,1,128]{2,1,0:T(1,128)S(1)} %broadcast_in_dim.9.turns, bf16[2,256,256]{2,1,0:T(8,128)(2,1)S(1)} %get-tuple-element.31.wx, bf16[2,256,256]{2,1,0:T(8,128)(2,1)S(1)} %get-tuple-element.32.wy, bf16[2,1,2,128,4096]{4,3,2,1,0:T(8,128)(2,1)} %src.13, ...), custom_call_target="tpu_custom_call" | custom-call | flops 6442450944 | bytes 4194304 | tf_op jit(solution)/shard_map/pallas_call | solution.py:243
  43.7 0.7 collective-permute-done.rest_0_.rest_2_
  44.4 0.0 collective-permute-done.1.rest_1_.rest_3_
  44.4 1.2 %collective-permute-start.3 = (f32[8,2,16,512]{3,2,1,0:T(8,128)S(1)}, f32[8,2,16,512]{3,2,1,0:T(8,128)S(1)}, u32[]{:S(2)}, u32[]{:S(2)}) collective-permute-start(f32[8,2,16,512]{3,2,1,0:T(8,128)S(1)} %all-to-all-done.1.rest_0_), channel_id=1, source_target_pairs={{0,32},{1,5},{2,34},{3,7},{4,36},{5,1},{6,38},{7,3},{8,40},{9,13},... | collective-permute-start | bytes 1572872 | tf_op jit(solution)/shard_map/ppermute | solution.py:455
  45.6 2.3 %collective-permute-start.5 = (f32[8,2,16,512]{3,2,1,0:T(8,128)S(1)}, f32[8,2,16,512]{3,2,1,0:T(8,128)S(1)}, u32[]{:S(2)}, u32[]{:S(2)}) collective-permute-start(f32[8,2,16,512]{3,2,1,0:T(8,128)S(1)} %collective-permute-done.rest_0_.rest_2_), channel_id=1, source_target_pairs={{0,1},{1,0},{2,3},{3,2},{4,5},{5,4},{6,7},{7,6},{8,9},{9,8},{10,11... | collective-permute-start | bytes 1572872 | tf_op jit(solution)/shard_map/ppermute | solution.py:455
  47.8 0.0 collective-permute-start.6
  47.8 6.2 %shard_map.116 = (bf16[2,1,2,128,4096]{4,3,2,1,0:T(8,128)(2,1)}, bf16[2,1,2,128,4096]{4,3,2,1,0:T(8,128)(2,1)}) custom-call(f32[2,1,128]{2,1,0:T(1,128)S(1)} %broadcast_in_dim.9.turns, bf16[2,256,256]{2,1,0:T(8,128)(2,1)S(1)} %get-tuple-element.31.wx, bf16[2,256,256]{2,1,0:T(8,128)(2,1)S(1)} %get-tuple-element.32.wy, ...), custom_call_target="tpu_custom_call", output_to_operand_aliasing={{0}: (8, {}), {1}: (9, {})} | custom-call | flops 6442450944 | bytes 4194304 | tf_op jit(solution)/shard_map/pallas_call | solution.py:243
  54.0 0.2 collective-permute-done.3.rest_6_.rest_0_
  54.2 1.7 %collective-permute-start.4 = (f32[8,2,16,512]{3,2,1,0:T(8,128)S(1)}, f32[8,2,16,512]{3,2,1,0:T(8,128)S(1)}, u32[]{:S(2)}, u32[]{:S(2)}) collective-permute-start(f32[8,2,16,512]{3,2,1,0:T(8,128)S(1)} %collective-permute-done.3.rest_6_.rest_0_), channel_id=1, source_target_pairs={{0,1},{1,0},{2,3},{3,2},{4,5},{5,4},{6,7},{7,6},{8,9},{9,8},{10,11... | collective-permute-start | bytes 1572872 | tf_op jit(solution)/shard_map/ppermute | solution.py:455
  55.9 0.0 collective-permute-done.5.rest_4_.rest_0_
  55.9 0.0 collective-permute-done.6.rest_5_.rest_1_
  55.9 1.5 %collective-permute-done.4.rest_7_.rest_1_ = f32[8,2,16,512]{3,2,1,0:T(8,128)S(1)} collective-permute-done((f32[8,2,16,512]{3,2,1,0:T(8,128)S(1)}, f32[8,2,16,512]{3,2,1,0:T(8,128)S(1)}, u32[]{:S(2)}, u32[]{:S(2)}) %collective-permute-start.4) | collective-permute-done | bytes 524320 | tf_op jit(solution)/shard_map/ppermute | solution.py:455
  57.5 3.4 %shard_map.117 = f32[8,2,2,8,128]{4,3,2,1,0:T(8,128)} custom-call(f32[2,128]{1,0:T(2,128)S(1)} %broadcast_in_dim.10.ids, f32[2,1,128]{2,1,0:T(1,128)S(1)} %broadcast_in_dim.9.turns, bf16[2,256,256]{2,1,0:T(8,128)(2,1)S(1)} %get-tuple-element.31.wx, bf16[2,256,256]{2,1,0:T(8,128)(2,1)S(1)} %get-tuple-element.32.wy, bf16[2,1,2,128,4096]{4,3,2,1,0:T(8,128)(2,1)} %src.13, ...), custom_call_target="tpu_custom_call" | custom-call | flops 1610612736 | bytes 2097152 | tf_op jit(solution)/shard_map/pallas_call | solution.py:312
  60.9 7.3 %all-to-all-start.2 = ((f32[8,32,128]{2,1,0:T(8,128)}), f32[8,32,128]{2,1,0:T(8,128)S(1)}, u32[]{:S(2)}, u32[]{:S(2)}) async-start(f32[8,32,128]{2,1,0:T(8,128)} %bitcast.13), calls=%async_computation.2 | async-start | bytes 262144 | tf_op jit(solution)/shard_map/all_to_all | solution.py:500
  68.2 7.1 %shard_map.118 = (bf16[2,1,2,128,4096]{4,3,2,1,0:T(8,128)(2,1)}, bf16[2,1,2,128,4096]{4,3,2,1,0:T(8,128)(2,1)}) custom-call(f32[2,1,128]{2,1,0:T(1,128)S(1)} %broadcast_in_dim.9.turns, bf16[2,256,256]{2,1,0:T(8,128)(2,1)S(1)} %get-tuple-element.31.wx, bf16[2,256,256]{2,1,0:T(8,128)(2,1)S(1)} %get-tuple-element.32.wy, ...), custom_call_target="tpu_custom_call", output_to_operand_aliasing={{0}: (7, {}), {1}: (8, {})} | custom-call | flops 6442450944 | bytes 4194304 | tf_op jit(solution)/shard_map/pallas_call | solution.py:243
  75.3 0.0 all-to-all-done.2.parts
  75.3 0.8 shard_map.120
  76.1 4.9 %all-to-all-start.3 = ((f32[16,40,128]{2,1,0:T(8,128)}), f32[16,40,128]{2,1,0:T(8,128)S(1)}, u32[]{:S(2)}, u32[]{:S(2)}) async-start(f32[16,40,128]{2,1,0:T(8,128)} %shard_map.120), calls=%async_computation.3 | async-start | bytes 655360 | tf_op jit(solution)/shard_map/all_to_all | solution.py:503
  81.0 7.2 %shard_map.119 = (bf16[2,1,2,128,4096]{4,3,2,1,0:T(8,128)(2,1)}, bf16[2,1,2,128,4096]{4,3,2,1,0:T(8,128)(2,1)}) custom-call(f32[2,1,128]{2,1,0:T(1,128)S(1)} %broadcast_in_dim.9.turns, bf16[2,256,256]{2,1,0:T(8,128)(2,1)S(1)} %get-tuple-element.31.wx, bf16[2,256,256]{2,1,0:T(8,128)(2,1)S(1)} %get-tuple-element.32.wy, ...), custom_call_target="tpu_custom_call", output_to_operand_aliasing={{0}: (7, {}), {1}: (8, {})} | custom-call | flops 6442450944 | bytes 4194304 | tf_op jit(solution)/shard_map/pallas_call | solution.py:243
  88.2 0.6 all-to-all-done.3.parts
  88.7 0.8 shard_map.121
  (6 shorter events, 0.0 us)
Async XLA Ops:
  0.6 16.4 %copy-start = (bf16[2,2,128,128]{3,2,1,0:T(8,128)(2,1)S(1)}, bf16[2,2,128,128]{3,2,1,0:T(8,128)(2,1)}, u32[]{:S(2)}) copy-start(bf16[2,2,128,128]{3,2,1,0:T(8,128)(2,1)} %param.12) | copy-start | bytes 393220
  0.6 24.7 %copy-start.1 = (s32[64]{0:T(128)S(1)}, s32[64]{0:T(128)}, u32[]{:S(2)}) copy-start(s32[64]{0:T(128)} %param.17) | copy-start | bytes 772
  2.5 17.1 %all-to-all-start = ((f32[16,16,512]{2,1,0:T(8,128)}), f32[16,16,512]{2,1,0:T(8,128)S(1)}, u32[]{:S(2)}, u32[]{:S(2)}) async-start(f32[16,16,512]{2,1,0:T(8,128)} %bitcast.1), calls=%async_computation | async-start | bytes 1048576 | tf_op jit(solution)/shard_map/all_to_all | solution.py:458
  20.5 13.3 %all-to-all-start.1 = ((f32[8,2,16,512]{3,2,1,0:T(8,128)}), f32[8,2,16,512]{3,2,1,0:T(8,128)S(1)}, u32[]{:S(2)}, u32[]{:S(2)}) async-start(f32[8,2,16,512]{3,2,1,0:T(8,128)} %broadcast_in_dim.8), calls=%async_computation.1 | async-start | bytes 1048576 | tf_op jit(solution)/shard_map/all_to_all | solution.py:464
  26.4 1.1 %copy-start.2 = (f32[2]{0:T(128)S(1)}, f32[2]{0:T(128)}, u32[]{:S(2)}) copy-start(f32[2]{0:T(128)} %param.11) | copy-start | bytes 28
  26.5 1.1 %copy-start.3 = (s32[1,2]{1,0:T(1,128)S(1)}, s32[1,2]{1,0:T(1,128)}, u32[]{:S(2)}) copy-start(s32[1,2]{1,0:T(1,128)} %param.16) | copy-start | bytes 28
  34.0 3.5 %collective-permute-start.2 = (f32[8,2,16,512]{3,2,1,0:T(8,128)S(1)}, f32[8,2,16,512]{3,2,1,0:T(8,128)S(1)}, u32[]{:S(2)}, u32[]{:S(2)}) collective-permute-start(f32[8,2,16,512]{3,2,1,0:T(8,128)S(1)} %all-to-all-done.1.rest_0_), channel_id=1, source_target_pairs={{0,1},{1,0},{2,3},{3,2},{4,5},{5,4},{6,7},{7,6},{8,9},{9,8},{10,11... | collective-permute-start | bytes 1572872 | tf_op jit(solution)/shard_map/ppermute | solution.py:455
  34.8 9.5 %collective-permute-start = (f32[8,2,16,512]{3,2,1,0:T(8,128)S(1)}, f32[8,2,16,512]{3,2,1,0:T(8,128)S(1)}, u32[]{:S(2)}, u32[]{:S(2)}) collective-permute-start(f32[8,2,16,512]{3,2,1,0:T(8,128)S(1)} %all-to-all-done.1.rest_0_), channel_id=1, source_target_pairs={{0,16},{1,3},{2,18},{3,5},{4,20},{5,7},{6,22},{7,1},{8,24},{9,11},... | collective-permute-start | bytes 1572872 | tf_op jit(solution)/shard_map/ppermute | solution.py:455
  35.1 9.3 %collective-permute-start.1 = (f32[8,2,16,512]{3,2,1,0:T(8,128)S(1)}, f32[8,2,16,512]{3,2,1,0:T(8,128)S(1)}, u32[]{:S(2)}, u32[]{:S(2)}) collective-permute-start(f32[8,2,16,512]{3,2,1,0:T(8,128)S(1)} %all-to-all-done.1.rest_0_), channel_id=1, source_target_pairs={{0,48},{1,7},{2,50},{3,1},{4,52},{5,3},{6,54},{7,5},{8,56},{9,15},... | collective-permute-start | bytes 1572872 | tf_op jit(solution)/shard_map/ppermute | solution.py:455
  44.4 9.8 %collective-permute-start.3 = (f32[8,2,16,512]{3,2,1,0:T(8,128)S(1)}, f32[8,2,16,512]{3,2,1,0:T(8,128)S(1)}, u32[]{:S(2)}, u32[]{:S(2)}) collective-permute-start(f32[8,2,16,512]{3,2,1,0:T(8,128)S(1)} %all-to-all-done.1.rest_0_), channel_id=1, source_target_pairs={{0,32},{1,5},{2,34},{3,7},{4,36},{5,1},{6,38},{7,3},{8,40},{9,13},... | collective-permute-start | bytes 1572872 | tf_op jit(solution)/shard_map/ppermute | solution.py:455
  45.6 10.4 %collective-permute-start.5 = (f32[8,2,16,512]{3,2,1,0:T(8,128)S(1)}, f32[8,2,16,512]{3,2,1,0:T(8,128)S(1)}, u32[]{:S(2)}, u32[]{:S(2)}) collective-permute-start(f32[8,2,16,512]{3,2,1,0:T(8,128)S(1)} %collective-permute-done.rest_0_.rest_2_), channel_id=1, source_target_pairs={{0,1},{1,0},{2,3},{3,2},{4,5},{5,4},{6,7},{7,6},{8,9},{9,8},{10,11... | collective-permute-start | bytes 1572872 | tf_op jit(solution)/shard_map/ppermute | solution.py:455
  47.8 8.1 %collective-permute-start.6 = (f32[8,2,16,512]{3,2,1,0:T(8,128)S(1)}, f32[8,2,16,512]{3,2,1,0:T(8,128)S(1)}, u32[]{:S(2)}, u32[]{:S(2)}) collective-permute-start(f32[8,2,16,512]{3,2,1,0:T(8,128)S(1)} %collective-permute-done.1.rest_1_.rest_3_), channel_id=1, source_target_pairs={{0,1},{1,0},{2,3},{3,2},{4,5},{5,4},{6,7},{7,6},{8,9},{9,8},{10,11... | collective-permute-start | bytes 1572872 | tf_op jit(solution)/shard_map/ppermute | solution.py:455
  54.2 3.2 %collective-permute-start.4 = (f32[8,2,16,512]{3,2,1,0:T(8,128)S(1)}, f32[8,2,16,512]{3,2,1,0:T(8,128)S(1)}, u32[]{:S(2)}, u32[]{:S(2)}) collective-permute-start(f32[8,2,16,512]{3,2,1,0:T(8,128)S(1)} %collective-permute-done.3.rest_6_.rest_0_), channel_id=1, source_target_pairs={{0,1},{1,0},{2,3},{3,2},{4,5},{5,4},{6,7},{7,6},{8,9},{9,8},{10,11... | collective-permute-start | bytes 1572872 | tf_op jit(solution)/shard_map/ppermute | solution.py:455
  60.9 14.4 %all-to-all-start.2 = ((f32[8,32,128]{2,1,0:T(8,128)}), f32[8,32,128]{2,1,0:T(8,128)S(1)}, u32[]{:S(2)}, u32[]{:S(2)}) async-start(f32[8,32,128]{2,1,0:T(8,128)} %bitcast.13), calls=%async_computation.2 | async-start | bytes 262144 | tf_op jit(solution)/shard_map/all_to_all | solution.py:500
  76.1 12.6 %all-to-all-start.3 = ((f32[16,40,128]{2,1,0:T(8,128)}), f32[16,40,128]{2,1,0:T(8,128)S(1)}, u32[]{:S(2)}, u32[]{:S(2)}) async-start(f32[16,40,128]{2,1,0:T(8,128)} %shard_map.120), calls=%async_computation.3 | async-start | bytes 655360 | tf_op jit(solution)/shard_map/all_to_all | solution.py:503

commit v11 on v10

--- a/solution.py
+++ b/solution.py
@@ -473,7 +473,7 @@
     tiles = apertures[0]
     rows_of = lambda ids: jnp.broadcast_to(ids.astype(jnp.float32)[:, None], (ids.shape[0], BLOCK))
     entries = lax.dynamic_slice_in_dim(tile_order, lax.axis_index("shot") * TILE_DEV, TILE_DEV)
-    order = [[(0, 0), (0, 1)], [(1, 0), (3, 0)], [(1, 1), (3, 1)], [(2, 0), (2, 1)]]
+    order = [[(0, 0), (0, 1)], [(1, 0), (3, 0), (1, 1)], [(3, 1)], [(2, 0), (2, 1)]]
     firsts = [fetch(blocks[0], src, rcv, cols) for blocks in order[:EARLY]]
     own, wx, wy, turns, named, entries, *firsts = lax.optimization_barrier(
         (own, wx, wy, turns, rows_of(tiles), rows_of(entries), *firsts)
@@ -486,10 +486,12 @@
     own_p = send(own, swap)
     s1, s3 = send(own, shift(1)), send(own, shift(3))
     fields = forward(0, [own, own_p])
-    s1, s3, later, *fields = lax.optimization_barrier((s1, s3, own, *fields))
+    s1, *fields = lax.optimization_barrier((s1, *fields))
+    s1_p = send(s1, swap)
+    s3, later, *fields = lax.optimization_barrier((s3, own, *fields))
     s2 = send(later, shift(2))
-    s1_p, s3_p = send(s1, swap), send(s3, swap)
-    fields = forward(1, [s1, s3], fields)
+    s3_p = send(s3, swap)
+    fields = forward(1, [s1, s3, s1_p], fields)
     s2, *fields = lax.optimization_barrier((s2, *fields))
     s2_p = send(s2, swap)
 
@@ -498,7 +500,7 @@
     terms = image_terms(named, names, turns, wx, wy, src, rcv, slabs, 1.0 / freq_total, freqs_dev)
     length = terms.shape[3] * terms.shape[4]
     terms = lax.all_to_all(terms.reshape(freqs_dev, -1, BLOCK), "freq", 0, 0, tiled=True)
-    fields = forward(2, [s1_p, s3_p], fields)
+    fields = forward(2, [s3_p], fields)
     terms, *fields = lax.optimization_barrier((terms, *fields))
     dealt = lax.all_to_all(deal(named, terms, shots), "shot", 0, 0, tiled=True)
     fields = forward(3, [s2, s2_p], fields)

time: 90.3 us -> 91.4 us (1.012)
  waiting for transfers between devices: 11.6 us -> 16.6 us
  starting transfers between devices: 32.9 us -> 29 us
    ppermute x7, starting transfers between devices: 8.69 us -> 6.11 us  [local(): lax.ppermute(v, AXES, pairs((freqs_dev, shots), move))]
    all_to_all x1, waiting for transfers between devices: 0.01 us -> 2.46 us  [local(): lax.all_to_all(terms.reshape(freqs_dev, -1, BLOCK), 'freq', 0, 0, tiled=T...]
    ppermute x7, waiting for transfers between devices: 2.36 us -> 4.8 us  [local(): lax.ppermute(v, AXES, pairs((freqs_dev, shots), move))]
    all_to_all x1, starting transfers between devices: 7.26 us -> 6.04 us  [local(): lax.all_to_all(terms.reshape(freqs_dev, -1, BLOCK), 'freq', 0, 0, tiled=T...]
  transfers between devices with their start and end apart: 11 -> 11, of which waited for: 6 -> 8; matrix products, arithmetic and copies ran while one was open for 4% -> 4% of each run, Pallas kernels for 32% -> 32%
where the time goes in v11:
time: 91.4 us; the launch traced here: 90.7 us
  Pallas kernels  35.8 us (39%)
  starting transfers between devices  29 us (32%)
  waiting for transfers between devices  16.6 us (18%)
  between operations  4.74 us (5%)
  local copies, waits for them, and re-layouts  3.55 us (4%)
  other arithmetic  1.02 us (1%)
    pallas_call x4, Pallas kernels, march(): pl.pallas_call(functools.partial(march_body, names=names, freqs=freqs, gi...  26.7 us
    all_to_all x1, starting transfers between devices, local(): arrived = lax.all_to_all(outgoing, 'shot', 0, 0, tiled=True)  7.18 us
    all_to_all x1, waiting for transfers between devices, local(): own = lax.all_to_all(own, AXES, 0, 0, axis_index_groups=groups, tiled=True)  6.19 us
    ppermute x7, starting transfers between devices, local(): lax.ppermute(v, AXES, pairs((freqs_dev, shots), move))  6.11 us
    all_to_all x1, starting transfers between devices, local(): lax.all_to_all(terms.reshape(freqs_dev, -1, BLOCK), 'freq', 0, 0, tiled=T...  6.04 us
    all_to_all x1, starting transfers between devices, local(): dealt = lax.all_to_all(deal(named, terms, shots), 'shot', 0, 0, tiled=True)  4.91 us
    all_to_all x1, starting transfers between devices, local(): own = lax.all_to_all(own, AXES, 0, 0, axis_index_groups=groups, tiled=True)  4.81 us
    ppermute x7, waiting for transfers between devices, local(): lax.ppermute(v, AXES, pairs((freqs_dev, shots), move))  4.8 us
  transfers between devices with their start and end apart: 11, of which 8 were waited for; matrix products, arithmetic and copies ran while one was open for 4% of the time, Pallas kernels for 32%

profile of v11, /device:TPU:1, one launch (start us, length us, event | category | flops | bytes accessed | tf_op | source)
XLA Modules:
  0.0 90.7 jit_solution(6265417879659025327)
XLA Ops:
  0.6 0.0 copy-start
  0.6 0.0 copy-start.1
  0.7 1.9 %shard_map.112 = f32[2,4,2,16,512]{4,3,2,1,0:T(8,128)} custom-call(f32[2,4,16,4096]{3,2,1,0:T(8,128)} %bitcast.24), custom_call_target="tpu_custom_call" | custom-call | tf_op jit(solution)/shard_map/pallas_call | solution.py:396
  2.5 7.2 %all-to-all-start = ((f32[16,16,512]{2,1,0:T(8,128)}), f32[16,16,512]{2,1,0:T(8,128)S(1)}, u32[]{:S(2)}, u32[]{:S(2)}) async-start(f32[16,16,512]{2,1,0:T(8,128)} %bitcast.1), calls=%async_computation | async-start | bytes 1048576 | tf_op jit(solution)/shard_map/all_to_all | solution.py:458
  9.7 1.3 %fusion.2 = (s32[1]{0:T(128)}, s32[1]{0:T(128)}) fusion(s32[2]{0:T(128)} %param.15), kind=kLoop, calls=%fused_computation.13 | loop fusion | bytes 16 | tf_op jit(solution)/shard_map/slice | solution.py:459
  13.6 0.9 fusion
  14.5 0.9 fusion.1
  15.4 0.1 copy.24
  15.5 0.1 copy.25
  17.0 0.0 copy-done
  17.0 0.1 maximum_maximum_fusion
  17.1 2.6 %all-to-all-done = f32[16,16,512]{2,1,0:T(8,128)S(1)} async-done(((f32[16,16,512]{2,1,0:T(8,128)}), f32[16,16,512]{2,1,0:T(8,128)S(1)}, u32[]{:S(2)}, u32[]{:S(2)}) %all-to-all-start) | async-done | bytes 524320 | tf_op jit(solution)/shard_map/all_to_all | solution.py:458
  19.6 0.9 broadcast_in_dim.8
  20.5 4.8 %all-to-all-start.1 = ((f32[8,2,16,512]{3,2,1,0:T(8,128)}), f32[8,2,16,512]{3,2,1,0:T(8,128)S(1)}, u32[]{:S(2)}, u32[]{:S(2)}) async-start(f32[8,2,16,512]{3,2,1,0:T(8,128)} %broadcast_in_dim.8), calls=%async_computation.1 | async-start | bytes 1048576 | tf_op jit(solution)/shard_map/all_to_all | solution.py:464
  25.3 0.0 copy-done.1
  25.3 0.1 dynamic-slice_convert_fusion
  25.4 1.0 %shard_map.113.rest_2_ = bf16[2,2,128,512]{3,2,1,0:T(8,128)(2,1)S(1)} custom-call(bf16[2,1,2,128,4096]{4,3,2,1,0:T(8,128)(2,1)} %src.13, bf16[2,1,2,128,4096]{4,3,2,1,0:T(8,128)(2,1)} %rcv.13), custom_call_target="tpu_custom_call" | custom-call | bytes 4194304 | tf_op jit(solution)/shard_map/pallas_call | solution.py:131
  26.4 0.0 copy-start.2
  26.5 0.0 copy-start.3
  26.5 1.1 %shard_map.114.rest_3_ = bf16[2,2,128,512]{3,2,1,0:T(8,128)(2,1)S(1)} custom-call(bf16[2,1,2,128,4096]{4,3,2,1,0:T(8,128)(2,1)} %src.13, bf16[2,1,2,128,4096]{4,3,2,1,0:T(8,128)(2,1)} %rcv.13), custom_call_target="tpu_custom_call" | custom-call | bytes 4194304 | tf_op jit(solution)/shard_map/pallas_call | solution.py:131
  27.5 0.0 copy-done.2
  27.6 0.0 copy-done.3
  27.6 6.2 %all-to-all-done.1.rest_0_ = f32[8,2,16,512]{3,2,1,0:T(8,128)S(1)} async-done(((f32[8,2,16,512]{3,2,1,0:T(8,128)}), f32[8,2,16,512]{3,2,1,0:T(8,128)S(1)}, u32[]{:S(2)}, u32[]{:S(2)}) %all-to-all-start.1) | async-done | bytes 524320 | tf_op jit(solution)/shard_map/all_to_all | solution.py:464
  33.8 0.1 broadcast_in_dim.9.turns
  33.8 0.1 broadcast_in_dim.10.ids
  33.9 0.1 broadcast_in_dim.11.entries
  34.0 0.9 collective-permute-start.2
  34.8 1.1 %collective-permute-start = (f32[8,2,16,512]{3,2,1,0:T(8,128)S(1)}, f32[8,2,16,512]{3,2,1,0:T(8,128)S(1)}, u32[]{:S(2)}, u32[]{:S(2)}) collective-permute-start(f32[8,2,16,512]{3,2,1,0:T(8,128)S(1)} %all-to-all-done.1.rest_0_), channel_id=1, source_target_pairs={{0,48},{1,7},{2,50},{3,1},{4,52},{5,3},{6,54},{7,5},{8,56},{9,15},... | collective-permute-start | bytes 1572872 | tf_op jit(solution)/shard_map/ppermute | solution.py:455
  35.9 0.4 collective-permute-start.1
  36.3 0.1 collective-permute-done.2.rest_1_
  36.4 6.2 %shard_map.115 = (bf16[2,1,2,128,4096]{4,3,2,1,0:T(8,128)(2,1)}, bf16[2,1,2,128,4096]{4,3,2,1,0:T(8,128)(2,1)}) custom-call(f32[2,1,128]{2,1,0:T(1,128)S(1)} %broadcast_in_dim.9.turns, bf16[2,256,256]{2,1,0:T(8,128)(2,1)S(1)} %get-tuple-element.33.wx, bf16[2,256,256]{2,1,0:T(8,128)(2,1)S(1)} %get-tuple-element.34.wy, bf16[2,1,2,128,4096]{4,3,2,1,0:T(8,128)(2,1)} %src.13, ...), custom_call_target="tpu_custom_call" | custom-call | flops 6442450944 | bytes 4194304 | tf_op jit(solution)/shard_map/pallas_call | solution.py:243
  42.6 2.9 %collective-permute-done.1.rest_0_.rest_2_ = f32[8,2,16,512]{3,2,1,0:T(8,128)S(1)} collective-permute-done((f32[8,2,16,512]{3,2,1,0:T(8,128)S(1)}, f32[8,2,16,512]{3,2,1,0:T(8,128)S(1)}, u32[]{:S(2)}, u32[]{:S(2)}) %collective-permute-start.1) | collective-permute-done | bytes 524320 | tf_op jit(solution)/shard_map/ppermute | solution.py:455
  45.5 2.1 %collective-permute-start.4 = (f32[8,2,16,512]{3,2,1,0:T(8,128)S(1)}, f32[8,2,16,512]{3,2,1,0:T(8,128)S(1)}, u32[]{:S(2)}, u32[]{:S(2)}) collective-permute-start(f32[8,2,16,512]{3,2,1,0:T(8,128)S(1)} %collective-permute-done.1.rest_0_.rest_2_), channel_id=1, source_target_pairs={{0,1},{1,0},{2,3},{3,2},{4,5},{5,4},{6,7},{7,6},{8,9},{9,8},{10,11... | collective-permute-start | bytes 1572872 | tf_op jit(solution)/shard_map/ppermute | solution.py:455
  47.6 0.0 collective-permute-done.rest_1_.rest_3_
  47.6 1.2 %collective-permute-start.3 = (f32[8,2,16,512]{3,2,1,0:T(8,128)S(1)}, f32[8,2,16,512]{3,2,1,0:T(8,128)S(1)}, u32[]{:S(2)}, u32[]{:S(2)}) collective-permute-start(f32[8,2,16,512]{3,2,1,0:T(8,128)S(1)} %all-to-all-done.1.rest_0_), channel_id=1, source_target_pairs={{0,32},{1,5},{2,34},{3,7},{4,36},{5,1},{6,38},{7,3},{8,40},{9,13},... | collective-permute-start | bytes 1572872 | tf_op jit(solution)/shard_map/ppermute | solution.py:455
  48.8 0.0 collective-permute-start.6
  48.8 0.3 collective-permute-done.4.rest_2_.rest_4_
  49.1 8.9 %shard_map.116 = (bf16[2,1,2,128,4096]{4,3,2,1,0:T(8,128)(2,1)}, bf16[2,1,2,128,4096]{4,3,2,1,0:T(8,128)(2,1)}) custom-call(f32[2,1,128]{2,1,0:T(1,128)S(1)} %broadcast_in_dim.9.turns, bf16[2,256,256]{2,1,0:T(8,128)(2,1)S(1)} %get-tuple-element.33.wx, bf16[2,256,256]{2,1,0:T(8,128)(2,1)S(1)} %get-tuple-element.34.wy, ...), custom_call_target="tpu_custom_call", output_to_operand_aliasing={{0}: (9, {}), {1}: (10, {})} | custom-call | flops 9663676416 | bytes 6291456 | tf_op jit(solution)/shard_map/pallas_call | solution.py:243
  58.0 0.0 collective-permute-done.3.rest_6_.rest_0_
  58.1 0.5 collective-permute-start.5
  58.5 0.0 collective-permute-done.6.rest_5_.rest_0_
  58.5 1.5 %collective-permute-done.5.rest_7_.rest_1_ = f32[8,2,16,512]{3,2,1,0:T(8,128)S(1)} collective-permute-done((f32[8,2,16,512]{3,2,1,0:T(8,128)S(1)}, f32[8,2,16,512]{3,2,1,0:T(8,128)S(1)}, u32[]{:S(2)}, u32[]{:S(2)}) %collective-permute-start.5) | collective-permute-done | bytes 524320 | tf_op jit(solution)/shard_map/ppermute | solution.py:455
  60.0 3.4 %shard_map.117 = f32[8,2,2,8,128]{4,3,2,1,0:T(8,128)} custom-call(f32[2,128]{1,0:T(2,128)S(1)} %broadcast_in_dim.10.ids, f32[2,1,128]{2,1,0:T(1,128)S(1)} %broadcast_in_dim.9.turns, bf16[2,256,256]{2,1,0:T(8,128)(2,1)S(1)} %get-tuple-element.33.wx, bf16[2,256,256]{2,1,0:T(8,128)(2,1)S(1)} %get-tuple-element.34.wy, bf16[2,1,2,128,4096]{4,3,2,1,0:T(8,128)(2,1)} %src.13, ...), custom_call_target="tpu_custom_call" | custom-call | flops 1610612736 | bytes 2097152 | tf_op jit(solution)/shard_map/pallas_call | solution.py:312
  63.5 6.0 %all-to-all-start.2 = ((f32[8,32,128]{2,1,0:T(8,128)}), f32[8,32,128]{2,1,0:T(8,128)S(1)}, u32[]{:S(2)}, u32[]{:S(2)}) async-start(f32[8,32,128]{2,1,0:T(8,128)} %bitcast.13), calls=%async_computation.2 | async-start | bytes 262144 | tf_op jit(solution)/shard_map/all_to_all | solution.py:502
  69.5 4.5 %shard_map.118 = (bf16[2,1,2,128,4096]{4,3,2,1,0:T(8,128)(2,1)}, bf16[2,1,2,128,4096]{4,3,2,1,0:T(8,128)(2,1)}) custom-call(f32[2,1,128]{2,1,0:T(1,128)S(1)} %broadcast_in_dim.9.turns, bf16[2,256,256]{2,1,0:T(8,128)(2,1)S(1)} %get-tuple-element.33.wx, bf16[2,256,256]{2,1,0:T(8,128)(2,1)S(1)} %get-tuple-element.34.wy, ...), custom_call_target="tpu_custom_call", output_to_operand_aliasing={{0}: (6, {}), {1}: (7, {})} | custom-call | flops 3221225472 | bytes 2097152 | tf_op jit(solution)/shard_map/pallas_call | solution.py:243
  74.0 2.5 %all-to-all-done.2.parts = f32[8,32,128]{2,1,0:T(8,128)S(1)} async-done(((f32[8,32,128]{2,1,0:T(8,128)}), f32[8,32,128]{2,1,0:T(8,128)S(1)}, u32[]{:S(2)}, u32[]{:S(2)}) %all-to-all-start.2) | async-done | bytes 131104 | tf_op jit(solution)/shard_map/all_to_all | solution.py:502
  76.5 0.8 shard_map.120
  77.2 4.9 %all-to-all-start.3 = ((f32[16,40,128]{2,1,0:T(8,128)}), f32[16,40,128]{2,1,0:T(8,128)S(1)}, u32[]{:S(2)}, u32[]{:S(2)}) async-start(f32[16,40,128]{2,1,0:T(8,128)} %shard_map.120), calls=%async_computation.3 | async-start | bytes 655360 | tf_op jit(solution)/shard_map/all_to_all | solution.py:505
  82.1 7.1 %shard_map.119 = (bf16[2,1,2,128,4096]{4,3,2,1,0:T(8,128)(2,1)}, bf16[2,1,2,128,4096]{4,3,2,1,0:T(8,128)(2,1)}) custom-call(f32[2,1,128]{2,1,0:T(1,128)S(1)} %broadcast_in_dim.9.turns, bf16[2,256,256]{2,1,0:T(8,128)(2,1)S(1)} %get-tuple-element.33.wx, bf16[2,256,256]{2,1,0:T(8,128)(2,1)S(1)} %get-tuple-element.34.wy, ...), custom_call_target="tpu_custom_call", output_to_operand_aliasing={{0}: (7, {}), {1}: (8, {})} | custom-call | flops 6442450944 | bytes 4194304 | tf_op jit(solution)/shard_map/pallas_call | solution.py:243
  89.3 0.6 all-to-all-done.3.parts
  89.9 0.8 shard_map.121
  (6 shorter events, 0.0 us)
Async XLA Ops:
  0.6 16.4 %copy-start = (bf16[2,2,128,128]{3,2,1,0:T(8,128)(2,1)S(1)}, bf16[2,2,128,128]{3,2,1,0:T(8,128)(2,1)}, u32[]{:S(2)}) copy-start(bf16[2,2,128,128]{3,2,1,0:T(8,128)(2,1)} %param.12) | copy-start | bytes 393220
  0.6 24.7 %copy-start.1 = (s32[64]{0:T(128)S(1)}, s32[64]{0:T(128)}, u32[]{:S(2)}) copy-start(s32[64]{0:T(128)} %param.17) | copy-start | bytes 772
  2.5 17.1 %all-to-all-start = ((f32[16,16,512]{2,1,0:T(8,128)}), f32[16,16,512]{2,1,0:T(8,128)S(1)}, u32[]{:S(2)}, u32[]{:S(2)}) async-start(f32[16,16,512]{2,1,0:T(8,128)} %bitcast.1), calls=%async_computation | async-start | bytes 1048576 | tf_op jit(solution)/shard_map/all_to_all | solution.py:458
  20.5 13.3 %all-to-all-start.1 = ((f32[8,2,16,512]{3,2,1,0:T(8,128)}), f32[8,2,16,512]{3,2,1,0:T(8,128)S(1)}, u32[]{:S(2)}, u32[]{:S(2)}) async-start(f32[8,2,16,512]{3,2,1,0:T(8,128)} %broadcast_in_dim.8), calls=%async_computation.1 | async-start | bytes 1048576 | tf_op jit(solution)/shard_map/all_to_all | solution.py:464
  26.4 1.1 %copy-start.2 = (f32[2]{0:T(128)S(1)}, f32[2]{0:T(128)}, u32[]{:S(2)}) copy-start(f32[2]{0:T(128)} %param.11) | copy-start | bytes 28
  26.5 1.1 %copy-start.3 = (s32[1,2]{1,0:T(1,128)S(1)}, s32[1,2]{1,0:T(1,128)}, u32[]{:S(2)}) copy-start(s32[1,2]{1,0:T(1,128)} %param.16) | copy-start | bytes 28
  34.0 2.4 %collective-permute-start.2 = (f32[8,2,16,512]{3,2,1,0:T(8,128)S(1)}, f32[8,2,16,512]{3,2,1,0:T(8,128)S(1)}, u32[]{:S(2)}, u32[]{:S(2)}) collective-permute-start(f32[8,2,16,512]{3,2,1,0:T(8,128)S(1)} %all-to-all-done.1.rest_0_), channel_id=1, source_target_pairs={{0,1},{1,0},{2,3},{3,2},{4,5},{5,4},{6,7},{7,6},{8,9},{9,8},{10,11... | collective-permute-start | bytes 1572872 | tf_op jit(solution)/shard_map/ppermute | solution.py:455
  34.8 12.7 %collective-permute-start = (f32[8,2,16,512]{3,2,1,0:T(8,128)S(1)}, f32[8,2,16,512]{3,2,1,0:T(8,128)S(1)}, u32[]{:S(2)}, u32[]{:S(2)}) collective-permute-start(f32[8,2,16,512]{3,2,1,0:T(8,128)S(1)} %all-to-all-done.1.rest_0_), channel_id=1, source_target_pairs={{0,48},{1,7},{2,50},{3,1},{4,52},{5,3},{6,54},{7,5},{8,56},{9,15},... | collective-permute-start | bytes 1572872 | tf_op jit(solution)/shard_map/ppermute | solution.py:455
  35.9 9.5 %collective-permute-start.1 = (f32[8,2,16,512]{3,2,1,0:T(8,128)S(1)}, f32[8,2,16,512]{3,2,1,0:T(8,128)S(1)}, u32[]{:S(2)}, u32[]{:S(2)}) collective-permute-start(f32[8,2,16,512]{3,2,1,0:T(8,128)S(1)} %all-to-all-done.1.rest_0_), channel_id=1, source_target_pairs={{0,16},{1,3},{2,18},{3,5},{4,20},{5,7},{6,22},{7,1},{8,24},{9,11},... | collective-permute-start | bytes 1572872 | tf_op jit(solution)/shard_map/ppermute | solution.py:455
  45.5 3.6 %collective-permute-start.4 = (f32[8,2,16,512]{3,2,1,0:T(8,128)S(1)}, f32[8,2,16,512]{3,2,1,0:T(8,128)S(1)}, u32[]{:S(2)}, u32[]{:S(2)}) collective-permute-start(f32[8,2,16,512]{3,2,1,0:T(8,128)S(1)} %collective-permute-done.1.rest_0_.rest_2_), channel_id=1, source_target_pairs={{0,1},{1,0},{2,3},{3,2},{4,5},{5,4},{6,7},{7,6},{8,9},{9,8},{10,11... | collective-permute-start | bytes 1572872 | tf_op jit(solution)/shard_map/ppermute | solution.py:455
  47.6 10.5 %collective-permute-start.3 = (f32[8,2,16,512]{3,2,1,0:T(8,128)S(1)}, f32[8,2,16,512]{3,2,1,0:T(8,128)S(1)}, u32[]{:S(2)}, u32[]{:S(2)}) collective-permute-start(f32[8,2,16,512]{3,2,1,0:T(8,128)S(1)} %all-to-all-done.1.rest_0_), channel_id=1, source_target_pairs={{0,32},{1,5},{2,34},{3,7},{4,36},{5,1},{6,38},{7,3},{8,40},{9,13},... | collective-permute-start | bytes 1572872 | tf_op jit(solution)/shard_map/ppermute | solution.py:455
  48.8 9.7 %collective-permute-start.6 = (f32[8,2,16,512]{3,2,1,0:T(8,128)S(1)}, f32[8,2,16,512]{3,2,1,0:T(8,128)S(1)}, u32[]{:S(2)}, u32[]{:S(2)}) collective-permute-start(f32[8,2,16,512]{3,2,1,0:T(8,128)S(1)} %collective-permute-done.rest_1_.rest_3_), channel_id=1, source_target_pairs={{0,1},{1,0},{2,3},{3,2},{4,5},{5,4},{6,7},{7,6},{8,9},{9,8},{10,11... | collective-permute-start | bytes 1572872 | tf_op jit(solution)/shard_map/ppermute | solution.py:455
  58.1 2.0 %collective-permute-start.5 = (f32[8,2,16,512]{3,2,1,0:T(8,128)S(1)}, f32[8,2,16,512]{3,2,1,0:T(8,128)S(1)}, u32[]{:S(2)}, u32[]{:S(2)}) collective-permute-start(f32[8,2,16,512]{3,2,1,0:T(8,128)S(1)} %collective-permute-done.3.rest_6_.rest_0_), channel_id=1, source_target_pairs={{0,1},{1,0},{2,3},{3,2},{4,5},{5,4},{6,7},{7,6},{8,9},{9,8},{10,11... | collective-permute-start | bytes 1572872 | tf_op jit(solution)/shard_map/ppermute | solution.py:455
  63.5 13.0 %all-to-all-start.2 = ((f32[8,32,128]{2,1,0:T(8,128)}), f32[8,32,128]{2,1,0:T(8,128)S(1)}, u32[]{:S(2)}, u32[]{:S(2)}) async-start(f32[8,32,128]{2,1,0:T(8,128)} %bitcast.13), calls=%async_computation.2 | async-start | bytes 262144 | tf_op jit(solution)/shard_map/all_to_all | solution.py:502
  77.2 12.6 %all-to-all-start.3 = ((f32[16,40,128]{2,1,0:T(8,128)}), f32[16,40,128]{2,1,0:T(8,128)S(1)}, u32[]{:S(2)}, u32[]{:S(2)}) async-start(f32[16,40,128]{2,1,0:T(8,128)} %shard_map.120), calls=%async_computation.3 | async-start | bytes 655360 | tf_op jit(solution)/shard_map/all_to_all | solution.py:505
